TPU v7x, 32 devices: a whole 2x2x4 slice. The times are simulated.
32 devices in a mesh: dp: 4 (over z), row: 2 (over y), col: 4 (over x, core).
Axes of the slice: x: 2, y: 2, z: 4, core: 2. Of those that a mesh axis runs over, the one named last changes fastest.
Arguments:
- tokens: bfloat16 [8192, 2048], P(('dp', 'row'), 'col'), may hold values from -6 to 6
- cotangent: bfloat16 [8192, 2048], P(('dp', 'row'), 'col'), may hold values from -6 to 6
- segment_ids: int32 [8, 1024], P('dp'), may hold values from 0 to 4, never falling along the last dimension, each value on 1 to 800 neighbouring positions
- norm1_gain: float32 [2048], P('col'), may hold values from 0.1 to 1.9
- proj_gate: bfloat16 [2048, 3072], P('col', 'row'), may hold values from -0.125 to 0.125
- proj_conv: bfloat16 [2048, 3072], P('col', 'row'), may hold values from -0.125 to 0.125
- proj_step: bfloat16 [2048, 48], P('col', 'row'), may hold values from -0.125 to 0.125
- proj_shared: bfloat16 [2048, 512], P('col', 'row'), may hold values from -0.125 to 0.125
- proj_query: bfloat16 [2048, 1024], P('col', 'row'), may hold values from -0.125 to 0.125
- proj_key: bfloat16 [2048, 256], P('col', 'row'), may hold values from -0.125 to 0.125
- proj_value: bfloat16 [2048, 256], P('col', 'row'), may hold values from -0.125 to 0.125
- conv_weight: float32 [4, 3072], P(None, ('row', 'col')), may hold values from -3 to 3
- conv_bias: float32 [3072], P(('row', 'col')), may hold values from -3 to 3
- shared_conv: float32 [4, 512], replicated, may hold values from -3 to 3
- shared_bias: float32 [512], replicated, may hold values from -3 to 3
- step_bias: float32 [48], P(('row', 'col')), may hold values from -7 to -2.3
- decay_log: float32 [48], P(('row', 'col')), may hold values from 0 to 2.77
- skip_gain: float32 [48], P(('row', 'col')), may hold values from 0.5 to 1.5
- mamba_out_proj: bfloat16 [3072, 2048], P('row', 'col'), may hold values from -0.109375 to 0.109375
- attn_out_proj: bfloat16 [1024, 2048], P('row', 'col'), may hold values from -0.75 to 0.75
- norm2_gain: float32 [2048], P('col'), may hold values from 0.1 to 1.9
- ffn_gate: bfloat16 [2048, 4096], P('col', 'row'), may hold values from -0.125 to 0.125
- ffn_up: bfloat16 [2048, 4096], P('col', 'row'), may hold values from -0.125 to 0.125
- ffn_down: bfloat16 [4096, 2048], P('row', 'col'), may hold values from -0.09375 to 0.09375
Outputs:
- output: bfloat16 [8192, 2048], P(('dp', 'row'), 'col')
- tokens_grad: bfloat16 [8192, 2048], P(('dp', 'row'), 'col')
- norm1_gain_grad: float32 [2048], P('col')
- proj_gate_grad: float32 [2048, 3072], P('col', 'row')
- proj_conv_grad: float32 [2048, 3072], P('col', 'row')
- proj_step_grad: float32 [2048, 48], P('col', 'row')
- proj_shared_grad: float32 [2048, 512], P('col', 'row')
- proj_query_grad: float32 [2048, 1024], P('col', 'row')
- proj_key_grad: float32 [2048, 256], P('col', 'row')
- proj_value_grad: float32 [2048, 256], P('col', 'row')
- conv_weight_grad: float32 [4, 3072], P(None, ('row', 'col'))
- conv_bias_grad: float32 [3072], P(('row', 'col'))
- shared_conv_grad: float32 [4, 512], replicated
- shared_bias_grad: float32 [512], replicated
- step_bias_grad: float32 [48], P(('row', 'col'))
- decay_log_grad: float32 [48], P(('row', 'col'))
- skip_gain_grad: float32 [48], P(('row', 'col'))
- mamba_out_proj_grad: float32 [3072, 2048], P('row', 'col')
- attn_out_proj_grad: float32 [1024, 2048], P('row', 'col')
- norm2_gain_grad: float32 [2048], P('col')
- ffn_gate_grad: float32 [2048, 4096], P('col', 'row')
- ffn_up_grad: float32 [2048, 4096], P('col', 'row')
- ffn_down_grad: float32 [4096, 2048], P('row', 'col')
Inputs may be any that keep to these rules, and one draw needn't show every extreme that they name: `segment_ids`: along each sequence the ids never fall; a run of equal ids is one document of 1 to 800 tokens, and some document has exactly 800.
All inputs are finite; a program needn't handle non-finite values.
Results may differ from a plain program's by a relative error of at most 0.018.
Values may be sent and summed in bfloat16 or wider, within the bound.
No kernel may reach another device: no remote copies, remote signals or barrier semaphores. Data moves between devices by JAX's collectives and lax.ppermute only.
A program may use at most 384 MiB of HBM per device.

v0:
```python
from functools import partial
import math

import jax
import jax.numpy as jnp
from jax import lax
from jax.sharding import PartitionSpec as P

D = 2048


EPS = 1e-05
ROPE_BASE = 100000000000.0
NEG_DECAY = -10000.0
MASKED = -1e30
HIGHEST = lax.Precision.HIGHEST


def matmul(former, latter):
    return jnp.dot(former, latter, preferred_element_type=jnp.float32)


def matmul_left(former, latter):
    return lax.dot_general(
        former, latter, (((0,), (0,)), ((), ())), preferred_element_type=jnp.float32
    )


def matmul_right(former, latter):
    return lax.dot_general(
        former, latter, (((1,), (1,)), ((), ())), preferred_element_type=jnp.float32
    )


def feature_total(values):
    return lax.psum(values, "col")


def gather_rows(values):
    return lax.all_gather(values, "row", axis=0, tiled=True)


def sum_rows(values):
    return lax.psum_scatter(values, "row", scatter_dimension=0, tiled=True)


def sum_pair(former, latter):
    return (
        lax.psum_scatter(former, "col", scatter_dimension=1, tiled=True),
        lax.psum_scatter(latter, "col", scatter_dimension=1, tiled=True),
    )


def gather_pair(former, latter):
    return (
        lax.all_gather(former, "col", axis=1, tiled=True),
        lax.all_gather(latter, "col", axis=1, tiled=True),
    )


def shared_total(former, latter):
    return lax.psum((former, latter), ("row", "col"))


def norm_forward(values, gain):
    squares = feature_total(jnp.sum(values * values, axis=1))
    factor = lax.rsqrt(squares / D + EPS)
    return (values * factor[:, None] * gain, factor)


def norm_backward(values, factor, gain, grad_normed):
    weighted = grad_normed * gain
    inner_sum = feature_total(jnp.sum(weighted * values, axis=1))
    grad_input = factor[:, None] * weighted - values * (factor**3 * inner_sum / D)[:, None]
    grad_gain = jnp.sum(grad_normed * values * factor[:, None], axis=0)
    return (grad_input, grad_gain)


def doc_layout(segment_ids):
    seq_len = segment_ids.shape[1]
    indices = jnp.arange(seq_len, dtype=jnp.int32)
    earlier = jnp.concatenate([segment_ids[:, :1], segment_ids[:, :-1]], axis=1)
    starts = (indices[None, :] == 0) | (segment_ids != earlier)
    latest = lax.cummax(jnp.where(starts, indices[None, :], 0), axis=1)
    return (starts, indices[None, :] - latest)


def allowed_mask(segment_ids):
    seq_len = segment_ids.shape[1]
    indices = jnp.arange(seq_len, dtype=jnp.int32)
    causal = indices[:, None] >= indices[None, :]
    return causal[None] & (segment_ids[:, :, None] == segment_ids[:, None, :])


def doc_conv(inputs, weight, conv_offset, segment_ids):
    taps = weight.shape[0]
    seq_len = inputs.shape[1]
    running = conv_offset + weight[taps - 1] * inputs
    for offset in range(1, taps):
        shifted = jnp.pad(inputs, ((0, 0), (offset, 0), (0, 0)))[:, :seq_len]
        earlier = jnp.pad(segment_ids, ((0, 0), (offset, 0)), constant_values=-1)[:, :seq_len]
        running = running + weight[taps - 1 - offset] * jnp.where(
            (earlier == segment_ids)[..., None], shifted, 0.0
        )
    return running


def rotate(values, positions, sign):
    half_dim = values.shape[-1] // 2
    frequency = ROPE_BASE ** (-2.0 * jnp.arange(half_dim, dtype=jnp.float32) / values.shape[-1])
    angles = positions.astype(jnp.float32)[..., None] * frequency
    cosine = jnp.cos(angles)[..., None, :]
    sine_term = sign * jnp.sin(angles)[..., None, :]
    front_half = values[..., :half_dim]
    back_half = values[..., half_dim:]
    return jnp.concatenate(
        [front_half * cosine - back_half * sine_term, back_half * cosine + front_half * sine_term],
        axis=-1,
    )


def state_scan(conv_out, b_map, c_map, step_size, log_decay):
    seq_count, length, head_count, head_width = conv_out.shape
    states = b_map.shape[2]
    block_len = min(128, length)
    block_count = length // block_len
    conv_out = conv_out.reshape(seq_count, block_count, block_len, head_count, head_width)
    b_map = b_map.reshape(seq_count, block_count, block_len, states)
    c_map = c_map.reshape(seq_count, block_count, block_len, states)
    step_size = step_size.reshape(seq_count, block_count, block_len, head_count)
    log_decay = log_decay.reshape(seq_count, block_count, block_len, head_count)
    indices = jnp.arange(block_len, dtype=jnp.int32)
    strictly_below = indices[:, None] > indices[None, :]
    causal = indices[:, None] >= indices[None, :]
    gram_matrix = jnp.einsum("abin,abjn->abij", c_map, b_map, precision=HIGHEST)
    decay_heads = jnp.moveaxis(log_decay, 3, 2)
    segsum = jnp.cumsum(jnp.where(strictly_below, decay_heads[..., :, None], 0.0), axis=3)
    weights = (
        jnp.where(causal, gram_matrix[:, :, None] * jnp.exp(segsum), 0.0)
        * jnp.moveaxis(step_size, 3, 2)[..., None, :]
    )
    inner_part = jnp.einsum("abhij,abjhp->abihp", weights, conv_out, precision=HIGHEST)
    prefix = jnp.cumsum(log_decay, axis=2)
    shifted = jnp.concatenate([log_decay[:, :, 1:], jnp.zeros_like(log_decay[:, :, :1])], axis=2)
    suffix = jnp.flip(jnp.cumsum(jnp.flip(shifted, 2), axis=2), 2)
    carried = jnp.einsum(
        "abjn,abjh,abjhp->abhnp", b_map, jnp.exp(suffix) * step_size, conv_out, precision=HIGHEST
    )
    fade_all = jnp.exp(prefix[:, :, -1])

    def advance(state_now, inputs):
        fade_factor, fresh_state = inputs
        return (fade_factor[:, :, None, None] * state_now + fresh_state, state_now)

    start_state = jnp.zeros((seq_count, head_count, states, head_width), jnp.float32)
    unused, previous = lax.scan(
        advance, start_state, (jnp.moveaxis(fade_all, 1, 0), jnp.moveaxis(carried, 1, 0))
    )
    previous = jnp.moveaxis(previous, 0, 1)
    outer_part = (
        jnp.einsum("abin,abhnp->abihp", c_map, previous, precision=HIGHEST)
        * jnp.exp(prefix)[..., None]
    )
    return (inner_part + outer_part).reshape(seq_count, length, head_count, head_width)


def shared_activate(segment_ids, shared_raw, shared_conv, shared_bias):
    seq_count, length = segment_ids.shape
    convolved = doc_conv(
        shared_raw.reshape(seq_count, length, -1), shared_conv, shared_bias, segment_ids
    )
    return jax.nn.silu(convolved).reshape(seq_count * length, -1)


def mamba_core(
    segment_ids,
    starts,
    mixer_gate,
    conv_input,
    step_raw,
    shared_act,
    conv_weight,
    conv_bias,
    step_bias,
    decay_log,
    skip_gain,
):
    seq_count, length = segment_ids.shape
    head_count = step_bias.shape[0]
    states = shared_act.shape[1] // 2
    conv_out = jax.nn.silu(
        doc_conv(conv_input.reshape(seq_count, length, -1), conv_weight, conv_bias, segment_ids)
    )
    conv_out = conv_out.reshape(seq_count, length, head_count, -1)
    step_size = jax.nn.softplus(step_raw.reshape(seq_count, length, head_count) + step_bias)
    log_decay = jnp.where(starts[..., None], NEG_DECAY, step_size * -jnp.exp(decay_log))
    shared = shared_act.reshape(seq_count, length, 2 * states)
    scanned = state_scan(conv_out, shared[..., :states], shared[..., states:], step_size, log_decay)
    combined = (scanned + skip_gain[:, None] * conv_out).reshape(seq_count * length, -1)
    return combined * jax.nn.silu(mixer_gate)


def attend(query_heads, key_heads, value_heads, segment_ids):
    factor = 1.0 / math.sqrt(key_heads.shape[-1])
    scores = (
        jnp.einsum("sqhd,skd->shqk", query_heads, key_heads, preferred_element_type=jnp.float32)
        * factor
    )
    scores = jnp.where(allowed_mask(segment_ids)[:, None], scores, MASKED)
    row_max = jnp.max(scores, axis=-1, keepdims=True)
    unnormed = jnp.exp(scores - row_max)
    running = jnp.sum(unnormed, axis=-1, keepdims=True)
    attn_probs = (unnormed / running).astype(jnp.bfloat16)
    attended = jnp.einsum(
        "shqk,skd->sqhd", attn_probs, value_heads, preferred_element_type=jnp.float32
    )
    return (attended, row_max + jnp.log(running))


def attend_back(query_heads, key_heads, value_heads, segment_ids, log_total, grad_out):
    factor = 1.0 / math.sqrt(key_heads.shape[-1])
    scores = (
        jnp.einsum("sqhd,skd->shqk", query_heads, key_heads, preferred_element_type=jnp.float32)
        * factor
    )
    scores = jnp.where(allowed_mask(segment_ids)[:, None], scores, MASKED)
    attn_probs = jnp.exp(scores - log_total)
    grad_probs = jnp.einsum(
        "sqhd,skd->shqk", grad_out, value_heads, preferred_element_type=jnp.float32
    )
    inner_sum = jnp.sum(attn_probs * grad_probs, axis=-1, keepdims=True)
    grad_scores = (attn_probs * (grad_probs - inner_sum)).astype(jnp.bfloat16)
    grad_query = (
        jnp.einsum("shqk,skd->sqhd", grad_scores, key_heads, preferred_element_type=jnp.float32)
        * factor
    )
    grad_key = (
        jnp.einsum("shqk,sqhd->skd", grad_scores, query_heads, preferred_element_type=jnp.float32)
        * factor
    )
    grad_value = jnp.einsum(
        "shqk,sqhd->skd",
        attn_probs.astype(jnp.bfloat16),
        grad_out,
        preferred_element_type=jnp.float32,
    )
    return (grad_query, grad_key, grad_value)


def on_device(
    tokens,
    cotangent,
    segment_ids,
    norm1_gain,
    proj_gate,
    proj_conv,
    proj_step,
    proj_shared,
    proj_query,
    proj_key,
    proj_value,
    conv_weight,
    conv_bias,
    shared_conv,
    shared_bias,
    step_bias,
    decay_log,
    skip_gain,
    mamba_out_proj,
    attn_out_proj,
    norm2_gain,
    ffn_gate,
    ffn_up,
    ffn_down,
):
    seq_count, length = segment_ids.shape
    group_tokens = seq_count * length
    head_dim = proj_key.shape[1]
    query_count = proj_query.shape[1] // (head_dim * lax.axis_size("col"))
    row_count = lax.axis_size("row")
    row_index = lax.axis_index("row")
    part_cols = proj_shared.shape[1]
    starts, positions = doc_layout(segment_ids)
    slot_mask = (jnp.arange(row_count, dtype=jnp.int32) == row_index).astype(jnp.float32)
    residual = tokens.astype(jnp.float32)
    normed1, factor1 = norm_forward(residual, norm1_gain)
    mixer_rows = gather_rows(normed1.astype(jnp.bfloat16))
    mixer_gate, conv_input, step_raw, query_raw = (
        lax.psum_scatter(matmul(mixer_rows, proj_gate), "col", scatter_dimension=1, tiled=True),
        lax.psum_scatter(matmul(mixer_rows, proj_conv), "col", scatter_dimension=1, tiled=True),
        lax.psum_scatter(matmul(mixer_rows, proj_step), "col", scatter_dimension=1, tiled=True),
        lax.psum_scatter(matmul(mixer_rows, proj_query), "col", scatter_dimension=1, tiled=True),
    )
    key_value = jnp.concatenate(
        [matmul(mixer_rows, proj_key), matmul(mixer_rows, proj_value)], axis=1
    )
    shared_part = lax.dynamic_update_slice_in_dim(
        jnp.zeros((group_tokens, part_cols * row_count), jnp.float32),
        matmul(mixer_rows, proj_shared),
        row_index * part_cols,
        1,
    )
    key_value_all, shared_raw = shared_total(
        slot_mask[None, :, None] * key_value[:, None, :], shared_part
    )
    key_value = lax.dynamic_index_in_dim(key_value_all, row_index, 1, keepdims=False)
    shared_act, shared_back = jax.vjp(
        partial(shared_activate, segment_ids), shared_raw, shared_conv, shared_bias
    )
    mamba_out, mamba_back = jax.vjp(
        partial(mamba_core, segment_ids, starts),
        mixer_gate,
        conv_input,
        step_raw,
        shared_act,
        conv_weight,
        conv_bias,
        step_bias,
        decay_log,
        skip_gain,
    )
    query_heads = rotate(
        query_raw.reshape(seq_count, length, query_count, head_dim), positions, 1.0
    ).astype(jnp.bfloat16)
    key_heads = rotate(
        key_value[:, :head_dim].reshape(seq_count, length, 1, head_dim), positions, 1.0
    )[:, :, 0].astype(jnp.bfloat16)
    value_heads = key_value[:, head_dim:].reshape(seq_count, length, head_dim).astype(jnp.bfloat16)
    attended, log_total = attend(query_heads, key_heads, value_heads, segment_ids)
    mamba_cols, attn_cols = gather_pair(
        mamba_out.astype(jnp.bfloat16), attended.reshape(group_tokens, -1).astype(jnp.bfloat16)
    )
    mixer_sum = sum_rows(matmul(mamba_cols, mamba_out_proj) + matmul(attn_cols, attn_out_proj))
    hidden1 = residual + mixer_sum
    normed2, factor2 = norm_forward(hidden1, norm2_gain)
    ffn_rows = gather_rows(normed2.astype(jnp.bfloat16))
    gate_pre, up_pre = sum_pair(matmul(ffn_rows, ffn_gate), matmul(ffn_rows, ffn_up))
    activated = jax.nn.silu(gate_pre)
    hidden = (activated * up_pre).astype(jnp.bfloat16)
    hidden_all = lax.all_gather(hidden, "col", axis=1, tiled=True)
    output = (hidden1 + sum_rows(matmul(hidden_all, ffn_down))).astype(jnp.bfloat16)
    cot_rows = gather_rows(cotangent)
    grad_ffn_down = matmul_left(hidden_all, cot_rows)
    grad_hidden = lax.psum_scatter(
        matmul_right(cot_rows, ffn_down).astype(jnp.bfloat16),
        "col",
        scatter_dimension=1,
        tiled=True,
    ).astype(jnp.float32)
    sigmoid = jax.nn.sigmoid(gate_pre)
    grad_gate = (grad_hidden * up_pre * sigmoid * (1.0 + gate_pre * (1.0 - sigmoid))).astype(
        jnp.bfloat16
    )
    grad_up = (grad_hidden * activated).astype(jnp.bfloat16)
    gate_rows, up_rows = gather_pair(grad_gate, grad_up)
    grad_ffn_gate = matmul_left(ffn_rows, gate_rows)
    grad_ffn_up = matmul_left(ffn_rows, up_rows)
    grad_normed2 = sum_rows(matmul_right(gate_rows, ffn_gate) + matmul_right(up_rows, ffn_up))
    back_second, grad_gain2 = norm_backward(hidden1, factor2, norm2_gain, grad_normed2)
    grad_hidden1 = cotangent.astype(jnp.float32) + back_second
    mix_rows = gather_rows(grad_hidden1.astype(jnp.bfloat16))
    grad_mamba_proj = matmul_left(mamba_cols, mix_rows)
    grad_attn_proj = matmul_left(attn_cols, mix_rows)
    grad_mamba, grad_attended = sum_pair(
        matmul_right(mix_rows, mamba_out_proj), matmul_right(mix_rows, attn_out_proj)
    )
    grad_query, grad_key, grad_value = attend_back(
        query_heads,
        key_heads,
        value_heads,
        segment_ids,
        log_total,
        grad_attended.reshape(seq_count, length, query_count, head_dim).astype(jnp.bfloat16),
    )
    grad_query_raw = (
        rotate(grad_query, positions, -1.0).reshape(group_tokens, -1).astype(jnp.bfloat16)
    )
    grad_key_raw = rotate(grad_key[:, :, None], positions, -1.0).reshape(group_tokens, head_dim)
    (
        grad_mixer_gate,
        grad_conv_input,
        grad_step_raw,
        grad_shared_act,
        grad_conv_weight,
        grad_conv_bias,
        grad_step_bias,
        grad_decay_log,
        grad_skip_gain,
    ) = mamba_back(grad_mamba)
    key_value_grad = jnp.concatenate(
        [grad_key_raw, grad_value.reshape(group_tokens, head_dim)], axis=1
    )
    key_value_sum, shared_grad = shared_total(
        slot_mask[None, :, None] * key_value_grad[:, None, :], grad_shared_act
    )
    key_value_grad = lax.dynamic_index_in_dim(key_value_sum, row_index, 1, keepdims=False).astype(
        jnp.bfloat16
    )
    key_grad = key_value_grad[:, :head_dim]
    value_grad = key_value_grad[:, head_dim:]
    grad_shared_raw, grad_shared_conv, grad_shared_bias = shared_back(shared_grad)
    shared_rows = lax.dynamic_slice_in_dim(
        grad_shared_raw, row_index * part_cols, part_cols, 1
    ).astype(jnp.bfloat16)
    gate_grad_rows, conv_grad_rows, step_grad_rows, query_grad_rows = (
        lax.all_gather(grad_mixer_gate.astype(jnp.bfloat16), "col", axis=1, tiled=True),
        lax.all_gather(grad_conv_input.astype(jnp.bfloat16), "col", axis=1, tiled=True),
        lax.all_gather(grad_step_raw.astype(jnp.bfloat16), "col", axis=1, tiled=True),
        lax.all_gather(grad_query_raw, "col", axis=1, tiled=True),
    )
    grad_proj_gate = matmul_left(mixer_rows, gate_grad_rows)
    grad_proj_conv = matmul_left(mixer_rows, conv_grad_rows)
    grad_proj_step = matmul_left(mixer_rows, step_grad_rows)
    grad_proj_query = matmul_left(mixer_rows, query_grad_rows)
    grad_proj_key = matmul_left(mixer_rows, key_grad)
    grad_proj_value = matmul_left(mixer_rows, value_grad)
    grad_proj_shared = matmul_left(mixer_rows, shared_rows)
    partial_first = matmul_right(gate_grad_rows, proj_gate) + matmul_right(
        conv_grad_rows, proj_conv
    )
    partial_first = (
        partial_first
        + matmul_right(step_grad_rows, proj_step)
        + matmul_right(query_grad_rows, proj_query)
    )
    partial_first = (
        partial_first + matmul_right(key_grad, proj_key) + matmul_right(value_grad, proj_value)
    )
    partial_first = partial_first + matmul_right(shared_rows, proj_shared)
    grad_normed1 = sum_rows(partial_first)
    back_first, grad_gain1 = norm_backward(residual, factor1, norm1_gain, grad_normed1)
    tokens_grad = (grad_hidden1 + back_first).astype(jnp.bfloat16)
    grad_gain1, grad_gain2 = lax.psum((grad_gain1, grad_gain2), ("dp", "row"))
    summed = (
        lax.psum(grad_proj_gate.astype(jnp.bfloat16), "dp").astype(jnp.float32),
        lax.psum(grad_proj_conv.astype(jnp.bfloat16), "dp").astype(jnp.float32),
        lax.psum(grad_proj_step.astype(jnp.bfloat16), "dp").astype(jnp.float32),
        lax.psum(grad_proj_shared.astype(jnp.bfloat16), "dp").astype(jnp.float32),
        lax.psum(grad_proj_query.astype(jnp.bfloat16), "dp").astype(jnp.float32),
        lax.psum(grad_proj_key.astype(jnp.bfloat16), "dp").astype(jnp.float32),
        lax.psum(grad_proj_value.astype(jnp.bfloat16), "dp").astype(jnp.float32),
        lax.psum(grad_conv_weight.astype(jnp.bfloat16), "dp").astype(jnp.float32),
        lax.psum(grad_conv_bias.astype(jnp.bfloat16), "dp").astype(jnp.float32),
        lax.psum(grad_shared_conv.astype(jnp.bfloat16), "dp").astype(jnp.float32),
        lax.psum(grad_shared_bias.astype(jnp.bfloat16), "dp").astype(jnp.float32),
        lax.psum(grad_step_bias.astype(jnp.bfloat16), "dp").astype(jnp.float32),
        lax.psum(grad_decay_log.astype(jnp.bfloat16), "dp").astype(jnp.float32),
        lax.psum(grad_skip_gain.astype(jnp.bfloat16), "dp").astype(jnp.float32),
        lax.psum(grad_mamba_proj.astype(jnp.bfloat16), "dp").astype(jnp.float32),
        lax.psum(grad_attn_proj.astype(jnp.bfloat16), "dp").astype(jnp.float32),
        lax.psum(grad_ffn_gate.astype(jnp.bfloat16), "dp").astype(jnp.float32),
        lax.psum(grad_ffn_up.astype(jnp.bfloat16), "dp").astype(jnp.float32),
        lax.psum(grad_ffn_down.astype(jnp.bfloat16), "dp").astype(jnp.float32),
    )
    return (
        output,
        tokens_grad,
        grad_gain1,
        summed[0],
        summed[1],
        summed[2],
        summed[3],
        summed[4],
        summed[5],
        summed[6],
        summed[7],
        summed[8],
        summed[9],
        summed[10],
        summed[11],
        summed[12],
        summed[13],
        summed[14],
        summed[15],
        grad_gain2,
        summed[16],
        summed[17],
        summed[18],
    )


def solution(mesh):
    return jax.shard_map(
        on_device,
        mesh=mesh,
        in_specs=(
            P(("dp", "row"), "col"),
            P(("dp", "row"), "col"),
            P("dp", None),
            P("col"),
            P("col", "row"),
            P("col", "row"),
            P("col", "row"),
            P("col", "row"),
            P("col", "row"),
            P("col", "row"),
            P("col", "row"),
            P(None, ("row", "col")),
            P(("row", "col")),
            P(),
            P(),
            P(("row", "col")),
            P(("row", "col")),
            P(("row", "col")),
            P("row", "col"),
            P("row", "col"),
            P("col"),
            P("col", "row"),
            P("col", "row"),
            P("row", "col"),
        ),
        out_specs=(
            P(("dp", "row"), "col"),
            P(("dp", "row"), "col"),
            P("col"),
            P("col", "row"),
            P("col", "row"),
            P("col", "row"),
            P("col", "row"),
            P("col", "row"),
            P("col", "row"),
            P("col", "row"),
            P(None, ("row", "col")),
            P(("row", "col")),
            P(),
            P(),
            P(("row", "col")),
            P(("row", "col")),
            P(("row", "col")),
            P("row", "col"),
            P("row", "col"),
            P("col"),
            P("col", "row"),
            P("col", "row"),
            P("row", "col"),
        ),
        check_vma=False,
    )
```

profile of v0, /device:TPU:0, one launch (start us, length us, event | category | flops | bytes accessed | tf_op | source)
XLA Modules:
  0.0 2441.9 jit_solution(14392519076965539931)
XLA Ops:
  21.1 33.5 %all-gather.14.cloned.1.call-done = bf16[2048,512]{1,0:T(8,128)(2,1)} async-done(((bf16[1024,512]{1,0:T(8,128)(2,1)}), bf16[2048,512]{1,0:T(8,128)(2,1)}) %all-gather.14.cloned.1.call-update) | async-done | bytes 2097168 | tf_op jit(solution)/shard_map/all_gather | solution.py:40
  117.8 47.4 %fusion.204 = f32[2,8,128,6]{3,1,2,0:T(8,128)S(1)} fusion(f32[2,8,128,6]{3,1,2,0:T(8,128)S(1)} %multiply_select_fusion.10), kind=kOutput, calls=%fused_computation.344 | output fusion | flops 1560576 | bytes 98304 | tf_op jit(solution)/shard_map/jvp(jit(cumsum))/reduce_window_sum | solution.py:143
  217.2 84.6 %reduce-scatter.15.cloned.1.call-done = f32[2048,384]{1,0:T(8,128)} async-done(((f32[2048,1536]{1,0:T(8,128)}), f32[2048,384]{1,0:T(8,128)}) %reduce-scatter.15.cloned.1.call-update) | async-done | bytes 3145744 | tf_op jit(solution)/shard_map/reduce_scatter | solution.py:290
  336.6 62.4 %while.34 = (s32[]{:T(128)}, f32[2,6,256,64]{3,2,1,0:T(8,128)}, f32[8,2,6,256,64]{4,3,2,1,0:T(8,128)}, f32[8,2,6,1,1]{2,1,4,3,0:T(2,128)}, f32[8,2,6]{2,1,0:T(2,...) while((s32[]{:T(128)}, f32[2,6,256,64]{3,2,1,0:T(8,128)}, ...), condition=%wide.region_9.10_spmd.clone, body=%wide.region_8.9_spmd.clone.sunk | while | flops 786435 | bytes 18089356 | solution.py:156
  471.5 28.0 %all-gather.16.cloned.1.call-done = bf16[2048,1536]{1,0:T(8,128)(2,1)} async-done(((bf16[2048,384]{1,0:T(8,128)(2,1)}), bf16[2048,1536]{1,0:T(8,128)(2,1)}) %all-gather.16.cloned.1.call-update) | async-done | bytes 6291472 | tf_op jit(solution)/shard_map/all_gather | solution.py:56
  531.4 53.7 %reduce-scatter.21.cloned.1.call-done = f32[1024,512]{1,0:T(8,128)} async-done(((f32[2048,512]{1,0:T(8,128)}), f32[1024,512]{1,0:T(8,128)}) %reduce-scatter.21.cloned.1.call-update) | async-done | bytes 2097168 | tf_op jit(solution)/shard_map/reduce_scatter | solution.py:44
  598.2 21.7 all-gather.24.cloned.1.call-done
  630.4 24.6 %all-gather.20.cloned.1.call-done = bf16[2048,512]{1,0:T(8,128)(2,1)} async-done(((bf16[1024,512]{1,0:T(8,128)(2,1)}), bf16[2048,512]{1,0:T(8,128)(2,1)}) %all-gather.20.cloned.1.call-update) | async-done | bytes 2097168 | tf_op jit(solution)/shard_map/all_gather | solution.py:40
  681.2 48.3 %reduce-scatter.29.cloned.1.call-done = bf16[2048,512]{1,0:T(8,128)(2,1)} async-done(((bf16[2048,2048]{1,0:T(8,128)(2,1)}), bf16[2048,512]{1,0:T(8,128)(2,1)}) %reduce-scatter.29.cloned.1.call-update) | async-done | bytes 2097168 | tf_op jit(solution)/shard_map/reduce_scatter | solution.py:344
  729.6 128.6 %reduce-scatter.25.cloned.1.call-done = f32[2048,512]{1,0:T(8,128)} async-done(((f32[2048,2048]{1,0:T(8,128)}), f32[2048,512]{1,0:T(8,128)}) %reduce-scatter.25.cloned.1.call-update) | async-done | bytes 4194320 | tf_op jit(solution)/shard_map/reduce_scatter | solution.py:50
  858.2 129.0 %reduce-scatter.23.cloned.1.call-done = f32[2048,512]{1,0:T(8,128)} async-done(((f32[2048,2048]{1,0:T(8,128)}), f32[2048,512]{1,0:T(8,128)}) %reduce-scatter.23.cloned.1.call-update) | async-done | bytes 4194320 | tf_op jit(solution)/shard_map/reduce_scatter | solution.py:49
  995.3 57.6 %all-gather.26.cloned.1.call-done = bf16[2048,2048]{1,0:T(8,128)(2,1)} async-done(((bf16[2048,512]{1,0:T(8,128)(2,1)}), bf16[2048,2048]{1,0:T(8,128)(2,1)}) %all-gather.26.cloned.1.call-update) | async-done | bytes 8388624 | tf_op jit(solution)/shard_map/all_gather | solution.py:56
  1062.4 50.8 %all-gather.28.cloned.1.call-done = bf16[2048,2048]{1,0:T(8,128)(2,1)} async-done(((bf16[2048,512]{1,0:T(8,128)(2,1)}), bf16[2048,2048]{1,0:T(8,128)(2,1)}) %all-gather.28.cloned.1.call-update) | async-done | bytes 8388624 | tf_op jit(solution)/shard_map/all_gather | solution.py:57
  1125.1 54.4 %reduce-scatter.31.cloned.1.call-done = f32[1024,512]{1,0:T(8,128)} async-done(((f32[2048,512]{1,0:T(8,128)}), f32[1024,512]{1,0:T(8,128)}) %reduce-scatter.31.cloned.1.call-update) | async-done | bytes 2097168 | tf_op jit(solution)/shard_map/reduce_scatter | solution.py:44
  1192.8 32.3 %all-gather.30.cloned.1.call-done = bf16[2048,512]{1,0:T(8,128)(2,1)} async-done(((bf16[1024,512]{1,0:T(8,128)(2,1)}), bf16[2048,512]{1,0:T(8,128)(2,1)}) %all-gather.30.cloned.1.call-update) | async-done | bytes 2097168 | tf_op jit(solution)/shard_map/all_gather | solution.py:40
  1241.0 33.8 %reduce-scatter.35.cloned.1.call-done = f32[2048,128]{1,0:T(8,128)} async-done(((f32[2048,512]{1,0:T(8,128)}), f32[2048,128]{1,0:T(8,128)}) %reduce-scatter.35.cloned.1.call-update) | async-done | bytes 1048592 | tf_op jit(solution)/shard_map/reduce_scatter | solution.py:50
  1295.6 80.9 %reduce-scatter.33.cloned.1.call-done = f32[2048,384]{1,0:T(8,128)} async-done(((f32[2048,1536]{1,0:T(8,128)}), f32[2048,384]{1,0:T(8,128)}) %reduce-scatter.33.cloned.1.call-update) | async-done | bytes 3145744 | tf_op jit(solution)/shard_map/reduce_scatter | solution.py:49
  1404.0 59.1 %while.35 = (s32[]{:T(128)}, f32[2,6,256,64]{3,2,1,0:T(8,128)S(1)}, f32[8,2,6]{2,1,0:T(2,128)S(1)}, f32[8,2,6,256,64]{4,3,2,1,0:T(8,128)}, f32[8,2,6,256,64]{3,4...) while((s32[]{:T(128)}, f32[2,6,256,64]{3,2,1,0:T(8,128)S(1)}, ...), condition=%wide.region_30.31_spmd.clone, body=%wide.region_28.30_spmd.clone.sunk | while | flops 1179640 | bytes 11798900 | solution.py:156
  1463.8 19.6 multiply_reduce_fusion.1
  1525.6 23.6 fusion.6
  1595.6 139.1 %all-reduce.44 = bf16[2048,2,256]{2,0,1:T(8,128)(2,1)S(1)} all-reduce(f32[2048,2,256]{2,0,1:T(8,128)} %broadcast_multiply_fusion), channel_id=1, replica_groups=mesh['dp'=4,'row'=2,'col'=4] {'row','col'}, use_global_device_ids=true, to_apply=%region_39.40 | all-reduce | flops 1048576 | bytes 6291456 | tf_op jit(solution)/shard_map/psum | solution.py:62
  1763.8 35.9 %fusion.14 = f32[2,8,6,128,128]{4,1,2,3,0:T(8,128)S(1)} fusion(f32[2,8,6,128,128]{4,3,2,1,0:T(8,128)} %get-tuple-element.410), kind=kOutput, calls=%fused_computation.32 | output fusion | flops 199753728 | bytes 12582912 | tf_op jit(solution)/shard_map/transpose(jvp(jit(cumsum)))/reduce_window_sum | solution.py:137
  1922.6 19.6 all-reduce.32
  1978.8 433.4 %all-reduce.43.cloned.1.call-done = (bf16[512,1536]{1,0:T(8,128)(2,1)}, bf16[512,1536]{1,0:T(8,128)(2,1)}, bf16[512,256]{1,0:T(8,128)(2,1)}, bf16[512,512]{1,0:T...) async-done(((bf16[512,1536]{1,0:T(8,128)(2,1)}, ...) | async-done | bytes 12582928 | tf_op jit(solution)/shard_map/psum | solution.py:435
  (819 shorter events, 843.1 us)
Async XLA Ops:
  21.0 178.7 %all-reduce.41.cloned.1.call-start = ((), (), s32[]{:S(2)}) async-start(), calls=%async_computation.37 | async-start | bytes 16777216 | tf_op jit(solution)/shard_map/psum | solution.py:62
  70.7 231.1 %reduce-scatter.15.cloned.1.call-start = ((), (), s32[]{:S(2)}) async-start(), calls=%async_computation.13 | async-start | bytes 15728640 | tf_op jit(solution)/shard_map/reduce_scatter | solution.py:290
  80.8 362.8 %reduce-scatter.17.cloned.1.call-start = ((), (), s32[]{:S(2)}) async-start(), calls=%async_computation.14 | async-start | bytes 15728640 | tf_op jit(solution)/shard_map/reduce_scatter | solution.py:289
  91.1 363.6 %reduce-scatter.19.cloned.1.call-start = ((), (), s32[]{:S(2)}) async-start(), calls=%async_computation.16 | async-start | bytes 5242880 | tf_op jit(solution)/shard_map/reduce_scatter | solution.py:292
  115.4 384.1 %all-gather.16.cloned.1.call-start = ((), (), s32[]{:S(2)}) async-start(), calls=%async_computation.15 | async-start | bytes 7864320 | tf_op jit(solution)/shard_map/all_gather | solution.py:56
  471.0 114.1 %reduce-scatter.21.cloned.1.call-start = ((), (), s32[]{:S(2)}) async-start(), calls=%async_computation.18 | async-start | bytes 6291456 | tf_op jit(solution)/shard_map/reduce_scatter | solution.py:44
  530.6 89.2 %all-gather.24.cloned.1.call-start = ((), (), s32[]{:S(2)}) async-start(), calls=%async_computation.24 | async-start | bytes 3145728 | tf_op jit(solution)/shard_map/all_gather | solution.py:40
  531.4 123.7 %all-gather.20.cloned.1.call-start = ((), (), s32[]{:S(2)}) async-start(), calls=%async_computation.19 | async-start | bytes 3145728 | tf_op jit(solution)/shard_map/all_gather | solution.py:40
  598.1 131.4 %reduce-scatter.29.cloned.1.call-start = ((), (), s32[]{:S(2)}) async-start(), calls=%async_computation.25 | async-start | bytes 10485760 | tf_op jit(solution)/shard_map/reduce_scatter | solution.py:344
  630.2 228.0 %reduce-scatter.25.cloned.1.call-start = ((), (), s32[]{:S(2)}) async-start(), calls=%async_computation.21 | async-start | bytes 20971520 | tf_op jit(solution)/shard_map/reduce_scatter | solution.py:50
  670.8 316.4 %reduce-scatter.23.cloned.1.call-start = ((), (), s32[]{:S(2)}) async-start(), calls=%async_computation.20 | async-start | bytes 20971520 | tf_op jit(solution)/shard_map/reduce_scatter | solution.py:49
  681.2 371.7 %all-gather.26.cloned.1.call-start = ((), (), s32[]{:S(2)}) async-start(), calls=%async_computation.26 | async-start | bytes 10485760 | tf_op jit(solution)/shard_map/all_gather | solution.py:56
  994.4 118.8 %all-gather.28.cloned.1.call-start = ((), (), s32[]{:S(2)}) async-start(), calls=%async_computation.27 | async-start | bytes 10485760 | tf_op jit(solution)/shard_map/all_gather | solution.py:57
  995.0 184.5 %reduce-scatter.31.cloned.1.call-start = ((), (), s32[]{:S(2)}) async-start(), calls=%async_computation.28 | async-start | bytes 6291456 | tf_op jit(solution)/shard_map/reduce_scatter | solution.py:44
  1125.0 100.1 %all-gather.30.cloned.1.call-start = ((), (), s32[]{:S(2)}) async-start(), calls=%async_computation.29 | async-start | bytes 3145728 | tf_op jit(solution)/shard_map/all_gather | solution.py:40
  1230.1 146.4 %reduce-scatter.33.cloned.1.call-start = ((), (), s32[]{:S(2)}) async-start(), calls=%async_computation.30 | async-start | bytes 15728640 | tf_op jit(solution)/shard_map/reduce_scatter | solution.py:49
  1240.7 499.7 %all-gather.36.cloned.1.call-start = ((), (), s32[]{:S(2)}) async-start(), calls=%async_computation.34 | async-start | bytes 2621440 | tf_op jit(solution)/shard_map/all_gather | solution.py:409
  1295.1 525.9 %all-reduce.39.cloned.1.call-start = ((), (), s32[]{:S(2)}) async-start(), calls=%async_computation.35 | async-start | bytes 8388608 | tf_op jit(solution)/shard_map/psum | solution.py:62
  1520.8 318.7 %all-gather.32.cloned.1.call-start = ((), (), s32[]{:S(2)}) async-start(), calls=%async_computation.31 | async-start | bytes 7864320 | tf_op jit(solution)/shard_map/all_gather | solution.py:406
  1521.5 326.6 %all-gather.34.cloned.1.call-start = ((), (), s32[]{:S(2)}) async-start(), calls=%async_computation.32 | async-start | bytes 7864320 | tf_op jit(solution)/shard_map/all_gather | solution.py:407
  1587.0 274.1 %all-gather.22.cloned.1.call-start = ((), (), s32[]{:S(2)}) async-start(), calls=%async_computation.22 | async-start | bytes 10485760 | tf_op jit(solution)/shard_map/all_gather | solution.py:340
  1587.6 359.1 %reduce-scatter.37.cloned.1.call-start = ((), (), s32[]{:S(2)}) async-start(), calls=%async_computation.36 | async-start | bytes 6291456 | tf_op jit(solution)/shard_map/reduce_scatter | solution.py:44
  1861.0 113.1 %reduce-scatter.27.cloned.1.call-start = ((), (), s32[]{:S(2)}) async-start(), calls=%async_computation.23 | async-start | bytes 6291456 | tf_op jit(solution)/shard_map/reduce_scatter | solution.py:44
  1872.1 540.2 %all-reduce.43.cloned.1.call-start = ((), (), s32[]{:S(2)}) async-start(), calls=%async_computation.38 | async-start | bytes 25165824 | tf_op jit(solution)/shard_map/psum | solution.py:435
  (221 other events, 6653.8 us)
Sparse Core Ops, SparseCore 0:
  21.1 33.4 all-gather.13
  70.8 128.8 all-reduce.40
  202.5 99.2 reduce-scatter.14
  304.4 99.0 reduce-scatter.16
  406.7 44.4 reduce-scatter.18
  453.2 46.2 all-gather.15
  530.7 54.3 reduce-scatter.20
  586.7 33.0 all-gather.23
  621.9 33.1 all-gather.19
  657.8 71.7 reduce-scatter.28
  732.0 126.1 reduce-scatter.24
  860.9 126.1 reduce-scatter.22
  994.6 58.2 all-gather.25
  1054.9 58.2 all-gather.27
  1125.1 54.3 reduce-scatter.30
  1230.2 44.5 reduce-scatter.34
  1277.4 99.0 reduce-scatter.32
  1520.9 81.0 all-reduce.38
  1603.6 78.7 all-gather.31
  1684.6 64.7 all-gather.33
  1751.0 58.2 all-gather.21
  1861.2 53.9 reduce-scatter.36
  1917.9 54.8 reduce-scatter.26
  1979.0 433.2 all-reduce.42
  (3 shorter events, 77.7 us)
where the time goes:
time: 2450 us; the launch traced here: 2440 us
  waiting for transfers between devices  1320 us (54%)
  matrix products  353 us (14%)
  other arithmetic  328 us (13%)
  blocking collectives  224 us (9%)
  local copies, waits for them, and re-layouts  192 us (8%)
    psum x1, waiting for transfers between devices, on_device(): lax.psum(grad_proj_gate.astype(jnp.bfloat16), 'dp').astype(jnp.float32)  433 us
    reduce_scatter x2, waiting for transfers between devices, sum_pair(): lax.psum_scatter(former, 'col', scatter_dimension=1, tiled=True)  210 us
    reduce_scatter x2, waiting for transfers between devices, sum_pair(): lax.psum_scatter(latter, 'col', scatter_dimension=1, tiled=True)  162 us
    psum x1, blocking collectives, shared_total(): return lax.psum((former, latter), ('row', 'col'))  139 us
    all_gather x4, waiting for transfers between devices, gather_rows(): return lax.all_gather(values, 'row', axis=0, tiled=True)  112 us
    reduce_scatter x4, waiting for transfers between devices, sum_rows(): return lax.psum_scatter(values, 'row', scatter_dimension=0, tiled=True)  108 us
    all_gather x2, waiting for transfers between devices, gather_pair(): lax.all_gather(former, 'col', axis=1, tiled=True)  85.6 us
    reduce_scatter x1, waiting for transfers between devices, on_device(): lax.psum_scatter(matmul(mixer_rows, proj_conv), 'col', scatter_dimension=...  84.6 us
  transfers between devices with their start and end apart: 28, of which 18 were waited for; matrix products, arithmetic and copies ran while one was open for 32% of the time, Pallas kernels for 0%

commit v1 on v0

v1 whole, which is shorter than its diff:
```python
from functools import partial
import math

import jax
import jax.numpy as jnp
from jax import lax
from jax.experimental import pallas as pl
from jax.experimental.pallas import tpu as pltpu
from jax.sharding import PartitionSpec as P

EPS = 1e-05
ROPE_BASE = 100000000000.0
MASKED = -1e30
HIGHEST = lax.Precision.HIGHEST
DISTANCES = (0, 2, 1, 3)
LANES = 128
CHUNK = 128
TAIL = 8


def dot_any(former, latter, dims, precision=None):
    return lax.dot_general(
        former, latter, (dims, ((), ())), precision=precision, preferred_element_type=jnp.float32
    )


def nn(former, latter):
    return dot_any(former, latter, ((1,), (0,)))


def nt(former, latter):
    return dot_any(former, latter, ((1,), (1,)))


def tn(former, latter):
    return dot_any(former, latter, ((0,), (0,)))


def exact(former, latter):
    return dot_any(former, latter, ((1,), (0,)), HIGHEST)


def sigmoid_of(values):
    return 1.0 / (1.0 + jnp.exp(-values))


def softplus_of(values):
    return jnp.maximum(values, 0.0) + jnp.log1p(jnp.exp(-jnp.abs(values)))


def head_spread(head_width, width):
    heads = lax.broadcasted_iota(jnp.int32, (LANES, width), 0)
    columns = lax.broadcasted_iota(jnp.int32, (LANES, width), 1)
    return (columns // head_width == heads).astype(jnp.float32)


def head_gather(head_width, width):
    columns = lax.broadcasted_iota(jnp.int32, (width, LANES), 0)
    heads = lax.broadcasted_iota(jnp.int32, (width, LANES), 1)
    return (columns // head_width == heads).astype(jnp.float32)


def causal_conv(ext_ref, columns, weight_ref, bias_ref, position, taps):
    length = ext_ref.shape[0] - TAIL
    running = bias_ref[...] + weight_ref[taps - 1 : taps, :] * ext_ref[TAIL:, columns]
    for offset in range(1, taps):
        earlier = ext_ref[TAIL - offset : TAIL - offset + length, columns]
        running = running + weight_ref[taps - 1 - offset : taps - offset, :] * jnp.where(
            position >= offset, earlier, 0.0
        )
    return running


def chunk_decay(step_in, position, decay_rate):
    length = step_in.shape[0]
    step_size = softplus_of(step_in)
    log_decay = jnp.where(position == 0.0, 0.0, -step_size * decay_rate)
    rows = lax.broadcasted_iota(jnp.int32, (length, length), 0)
    columns = lax.broadcasted_iota(jnp.int32, (length, length), 1)
    causal = rows >= columns
    running = exact(causal.astype(jnp.float32), log_decay)
    return step_size, log_decay, running, jnp.transpose(running), causal


def split_pair(values, head_width):
    lane = lax.broadcasted_iota(jnp.int32, values.shape, 1)
    zero = jnp.zeros_like(values)
    return jnp.concatenate(
        [jnp.where(lane < head_width, values, zero), jnp.where(lane < head_width, zero, values)],
        axis=0,
    )


def mamba_forward_kernel(
    shared_ref, gate_ref, conv_ref, step_ref, info_ref, row_ref, weight_ref, bias_ref,
    shared_weight_ref, shared_bias_ref, head_ref, skip_ref, attended_ref,
    mixed_ref, combined_ref, states_ref,
    state, ext, *, head_width
):
    chunk = pl.program_id(0)
    length, width = conv_ref.shape
    states = shared_ref.shape[1] // 2
    taps = weight_ref.shape[0]
    low = jnp.bfloat16

    @pl.when(chunk == 0)
    def _():
        state[...] = jnp.zeros_like(state)
        ext[...] = jnp.zeros_like(ext)

    ext[:TAIL, :] = ext[length : length + TAIL, :]
    ext[TAIL:, :width] = conv_ref[...].astype(jnp.float32)
    ext[TAIL:, width:] = shared_ref[...].astype(jnp.float32)
    segment = info_ref[:, 0:1]
    position = info_ref[:, 1:2]
    pre = causal_conv(ext, slice(0, width), weight_ref, bias_ref, position, taps)
    conv_out = pre * sigmoid_of(pre)
    pre = causal_conv(
        ext, slice(width, None), shared_weight_ref, shared_bias_ref, position, taps
    )
    shared = (pre * sigmoid_of(pre)).astype(low)
    b_map = shared[:, :states]
    c_map = shared[:, states:]
    step_size, _, running, running_t, causal = chunk_decay(
        step_ref[...] + head_ref[0:1, :], position, head_ref[1:2, :]
    )
    segment_row = row_ref[0:1, :]
    allowed = causal & (segment == segment_row)
    local = lax.broadcasted_iota(jnp.int32, (length, 1), 0).astype(jnp.float32)
    enters = jnp.where(position > local, jnp.exp(running), 0.0)
    last = running[length - 1 : length, :]
    leaves = jnp.where(segment == segment_row[:, length - 1 :], jnp.exp(last - running), 0.0)
    spread = head_spread(head_width, width)
    wide = exact(jnp.concatenate([step_size, enters, leaves], axis=0), spread)
    weighted = conv_out * wide[:length]
    gram = nt(c_map, b_map)
    weighted_low = weighted.astype(low)
    parts = []
    for pair in range(width // (2 * head_width)):
        weights = []
        for head in (2 * pair, 2 * pair + 1):
            gap = jnp.where(allowed, running[:, head : head + 1] - running_t[head : head + 1, :], MASKED)
            weights.append((gram * jnp.exp(gap)).astype(low))
        columns = slice(2 * pair * head_width, 2 * (pair + 1) * head_width)
        parts.append(
            nn(jnp.concatenate(weights, axis=1), split_pair(weighted_low[:, columns], head_width))
        )
    held = state[...]
    held_low = held.astype(low)
    states_ref[...] = held_low
    scanned = jnp.concatenate(parts, axis=1) + nn(c_map, held_low) * wide[length : 2 * length]
    fade = wide[2 * length - 1 : 2 * length]
    state[...] = held * fade + tn(b_map, (weighted * wide[2 * length :]).astype(low))
    combined = scanned + skip_ref[...] * conv_out
    combined_ref[...] = combined.astype(low)
    gate = gate_ref[...].astype(jnp.float32)
    mixed_ref[:, :width] = (combined * (gate * sigmoid_of(gate))).astype(low)
    mixed_ref[:, width:] = attended_ref[...]


def mamba_backward_kernel(
    raw_ref, tail_ref, step_ref, info_ref, row_ref, weight_ref, bias_ref,
    shared_weight_ref, shared_bias_ref, head_ref, skip_ref, combined_ref, states_ref, grad_ref,
    query_ref, key_ref, value_ref,
    out_ref, inner_ref, sums_ref,
    grad_state, ext, ext_grad, *, head_width, places
):
    count = pl.num_programs(0)
    step = pl.program_id(0)
    length = grad_ref.shape[0]
    at_shared, at_query, at_key, at_gate, at_conv, at_value, at_step = places
    width = at_conv - at_gate
    states = (at_query - at_shared) // 2
    taps = weight_ref.shape[0]
    low = jnp.bfloat16
    f32 = jnp.float32
    gate_columns = slice(at_gate, at_gate + width)
    conv_columns = slice(at_conv, at_conv + width)
    shared_columns = slice(at_shared, at_shared + 2 * states)

    @pl.when(step == 0)
    def _():
        grad_state[...] = jnp.zeros_like(grad_state)
        ext_grad[...] = jnp.zeros_like(ext_grad)
        sums_ref[...] = jnp.zeros_like(sums_ref)

    ext[:TAIL, :width] = tail_ref[tail_ref.shape[0] - TAIL :, conv_columns].astype(f32)
    ext[:TAIL, width:] = tail_ref[tail_ref.shape[0] - TAIL :, shared_columns].astype(f32)
    ext[TAIL:, :width] = raw_ref[:, conv_columns].astype(f32)
    ext[TAIL:, width:] = raw_ref[:, shared_columns].astype(f32)
    segment = info_ref[:, 0:1]
    position = info_ref[:, 1:2]
    remaining = info_ref[:, 2:3]
    pre = causal_conv(ext, slice(0, width), weight_ref, bias_ref, position, taps)
    sig = sigmoid_of(pre)
    conv_out = pre * sig
    conv_slope = sig * (1.0 + pre * (1.0 - sig))
    pre = causal_conv(
        ext, slice(width, None), shared_weight_ref, shared_bias_ref, position, taps
    )
    sig = sigmoid_of(pre)
    shared = (pre * sig).astype(low)
    shared_slope = sig * (1.0 + pre * (1.0 - sig))
    b_map = shared[:, :states]
    c_map = shared[:, states:]
    step_in = step_ref[...] + head_ref[0:1, :]
    rate = head_ref[1:2, :]
    step_size, log_decay, running, running_t, causal = chunk_decay(step_in, position, rate)
    segment_row = row_ref[0:1, :]
    allowed = causal & (segment == segment_row)
    local = lax.broadcasted_iota(jnp.int32, (length, 1), 0).astype(f32)
    enters = jnp.where(position > local, jnp.exp(running), 0.0)
    last = running[length - 1 : length, :]
    leaves = jnp.where(segment == segment_row[:, length - 1 :], jnp.exp(last - running), 0.0)
    spread = head_spread(head_width, width)
    wide = exact(jnp.concatenate([step_size, enters, leaves], axis=0), spread)
    step_wide = wide[:length]
    enters_wide = wide[length : 2 * length]
    leaves_wide = wide[2 * length :]
    fade = wide[2 * length - 1 : 2 * length]
    weighted = conv_out * step_wide

    gate = raw_ref[:, gate_columns].astype(f32)
    sig = sigmoid_of(gate)
    grad_out = grad_ref[:, :width].astype(f32)
    grad_gate = grad_out * combined_ref[...].astype(f32) * (sig * (1.0 + gate * (1.0 - sig)))
    grad_scan = grad_out * (gate * sig)

    gram = nt(c_map, b_map)
    weighted_low = weighted.astype(low)
    grad_low = grad_scan.astype(low)
    lane = lax.broadcasted_iota(jnp.int32, (length, LANES), 1)
    sub = lax.broadcasted_iota(jnp.int32, (LANES, length), 0)
    grad_gram = jnp.zeros((length, length), f32)
    by_row = jnp.zeros((length, LANES), f32)
    by_column = jnp.zeros((LANES, length), f32)
    parts = []
    for pair in range(width // (2 * head_width)):
        columns = slice(2 * pair * head_width, 2 * (pair + 1) * head_width)
        split_grad = split_pair(grad_low[:, columns], head_width)
        products = nt(split_grad, weighted_low[:, columns])
        weights = []
        for place, head in enumerate((2 * pair, 2 * pair + 1)):
            gap = jnp.where(allowed, running[:, head : head + 1] - running_t[head : head + 1, :], MASKED)
            fading = jnp.exp(gap)
            weight = gram * fading
            product = products[place * length : (place + 1) * length]
            grad_gram = grad_gram + fading * product
            meeting = weight * product
            by_row = jnp.where(lane == head, jnp.sum(meeting, axis=1, keepdims=True), by_row)
            by_column = jnp.where(sub == head, jnp.sum(meeting, axis=0, keepdims=True), by_column)
            weights.append(weight.astype(low))
        parts.append(tn(jnp.concatenate(weights, axis=0), split_grad))
    held = states_ref[...]
    entering = (grad_scan * enters_wide).astype(low)
    leaving = (weighted * leaves_wide).astype(low)
    grad_held = grad_state[...]
    grad_held_low = grad_held.astype(low)
    from_state = nn(b_map, grad_held_low) * leaves_wide
    grad_weighted = jnp.concatenate(parts, axis=1) + from_state
    grad_gram_low = grad_gram.astype(low)
    grad_c = nn(grad_gram_low, b_map) + nt(entering, held)
    grad_b = tn(grad_gram_low, c_map) + nt(leaving, grad_held_low)
    met_in = grad_scan * enters_wide * nn(c_map, held)
    met_out = weighted * from_state
    met_state = fade * jnp.sum(held.astype(f32) * grad_held, axis=0, keepdims=True)
    grad_state[...] = grad_held * fade + tn(c_map, entering)
    grad_conv_out = grad_weighted * step_wide + skip_ref[...] * grad_scan
    gathered = exact(
        jnp.concatenate(
            [met_in, met_out, conv_out * grad_weighted, jnp.broadcast_to(met_state, (TAIL, width))],
            axis=0,
        ),
        head_gather(head_width, width),
    )
    out_rows = gathered[length : 2 * length]
    at_last = jnp.sum(out_rows, axis=0, keepdims=True) + gathered[3 * length : 3 * length + 1]
    grad_running = by_row - jnp.transpose(by_column) + gathered[:length] - out_rows
    grad_running = grad_running + jnp.where(local == length - 1.0, at_last, 0.0)
    rows = lax.broadcasted_iota(jnp.int32, (length, length), 0)
    later = lax.broadcasted_iota(jnp.int32, (length, length), 1) >= rows
    grad_decay = jnp.where(position == 0.0, 0.0, exact(later.astype(f32), grad_running))
    grad_step = (gathered[2 * length : 3 * length] - grad_decay * rate) * sigmoid_of(step_in)

    ext_grad[length : length + TAIL, :] = ext_grad[:TAIL, :]
    ext_grad[:length, :width] = grad_conv_out * conv_slope
    ext_grad[:length, width : width + states] = grad_b * shared_slope[:, :states]
    ext_grad[:length, width + states :] = grad_c * shared_slope[:, states:]

    def conv_back(columns, weights, row_at):
        now = ext_grad[:length, columns]
        running = weights[taps - 1 : taps, :] * now
        wide_columns = slice(0, now.shape[1])
        sums_ref[row_at + taps : row_at + taps + 1, wide_columns] += jnp.sum(now, axis=0, keepdims=True)
        sums_ref[row_at + taps - 1 : row_at + taps, wide_columns] += jnp.sum(
            now * ext[TAIL:, columns], axis=0, keepdims=True
        )
        for offset in range(1, taps):
            at = taps - 1 - offset
            running = running + weights[at : at + 1, :] * jnp.where(
                remaining >= offset, ext_grad[offset : offset + length, columns], 0.0
            )
            earlier = jnp.where(
                position >= offset, ext[TAIL - offset : TAIL - offset + length, columns], 0.0
            )
            sums_ref[row_at + at : row_at + at + 1, wide_columns] += jnp.sum(
                now * earlier, axis=0, keepdims=True
            )
        return running

    grad_conv = conv_back(slice(0, width), weight_ref, 0).astype(low)
    grad_shared = conv_back(slice(width, None), shared_weight_ref, taps + 1).astype(low)
    row_at = 2 * (taps + 1)
    sums_ref[row_at : row_at + 1, :width] += jnp.sum(grad_scan * conv_out, axis=0, keepdims=True)
    sums_ref[row_at + 1 : row_at + 2, :LANES] += jnp.sum(grad_step, axis=0, keepdims=True)
    sums_ref[row_at + 2 : row_at + 3, :LANES] += jnp.sum(
        grad_decay * log_decay, axis=0, keepdims=True
    )
    grad_step = grad_step.astype(low)
    out_ref[:, shared_columns] = grad_shared
    out_ref[:, at_query:at_key] = query_ref[...]
    out_ref[:, at_key:at_gate] = key_ref[...]
    out_ref[:, gate_columns] = grad_gate.astype(low)
    out_ref[:, conv_columns] = grad_conv
    out_ref[:, at_value:at_step] = value_ref[...]
    out_ref[:, at_step:] = grad_step
    inner = grad_step.astype(f32) * step_ref[...]
    for at in range(0, at_step, LANES):
        inner = inner + out_ref[:, at : at + LANES].astype(f32) * raw_ref[:, at : at + LANES].astype(f32)
    inner_ref[...] = inner


def rope(values, cosine, sine):
    return values * cosine + pltpu.roll(values, values.shape[1] // 2, 1) * sine


def attention_rows(query, key, begin, size, info_ref, row_ref, factor):
    seen = begin + size
    scores = nt(query, key) * factor
    rows = begin + lax.broadcasted_iota(jnp.int32, (size, seen), 0)
    columns = lax.broadcasted_iota(jnp.int32, (size, seen), 1)
    allowed = (rows >= columns) & (info_ref[begin:seen, 0:1] == row_ref[0:1, :seen])
    scores = jnp.where(allowed, scores, MASKED)
    raised = jnp.exp(scores - jnp.max(scores, axis=1, keepdims=True))
    return raised * (1.0 / jnp.sum(raised, axis=1, keepdims=True))


def attention_forward_kernel(
    query_ref, key_ref, value_ref, cosine_ref, sine_ref, info_ref, row_ref, out_ref, *, block
):
    low = jnp.bfloat16
    length, head_dim = query_ref.shape
    factor = 1.0 / math.sqrt(head_dim)
    cosine, sine = cosine_ref[...], sine_ref[...]
    query = rope(query_ref[...].astype(jnp.float32), cosine, sine).astype(low)
    key = rope(key_ref[...].astype(jnp.float32), cosine, sine).astype(low)
    value = value_ref[...]
    for begin in range(0, length, block):
        seen = begin + block
        probs = attention_rows(
            query[begin:seen], key[:seen], begin, block, info_ref, row_ref, factor
        )
        out_ref[begin:seen, :] = nn(probs.astype(low), value[:seen]).astype(low)


def attention_backward_kernel(
    query_ref, key_ref, value_ref, cosine_ref, sine_ref, info_ref, row_ref, grad_ref,
    grad_query_ref, grad_key_ref, grad_value_ref, key_total, value_total, *, block
):
    low = jnp.bfloat16
    length, head_dim = query_ref.shape
    factor = 1.0 / math.sqrt(head_dim)
    cosine, sine = cosine_ref[...], sine_ref[...]
    query = rope(query_ref[...].astype(jnp.float32), cosine, sine).astype(low)
    key = rope(key_ref[...].astype(jnp.float32), cosine, sine).astype(low)
    value = value_ref[...]
    key_total[...] = jnp.zeros_like(key_total)
    value_total[...] = jnp.zeros_like(value_total)
    for begin in range(0, length, block):
        seen = begin + block
        probs = attention_rows(
            query[begin:seen], key[:seen], begin, block, info_ref, row_ref, factor
        )
        grad_out = grad_ref[begin:seen, :]
        grad_probs = nt(grad_out, value[:seen])
        inner = jnp.sum(probs * grad_probs, axis=1, keepdims=True)
        grad_scores = (probs * (grad_probs - inner)).astype(low)
        grad_query = nn(grad_scores, key[:seen]) * factor
        grad_query_ref[begin:seen, :] = rope(
            grad_query, cosine[begin:seen], -sine[begin:seen]
        ).astype(low)
        key_total[:seen, :] += tn(grad_scores, query[begin:seen])
        value_total[:seen, :] += tn(probs.astype(low), grad_out)
    grad_key_ref[...] = rope(key_total[...] * factor, cosine, -sine).astype(low)
    grad_value_ref[...] = value_total[...].astype(low)


def whole(shape):
    return pl.BlockSpec(shape, lambda i: (0,) * len(shape))


def limits(megabytes):
    return pltpu.CompilerParams(vmem_limit_bytes=megabytes * 1024 * 1024)


def column_block(rows, width, at):
    return pl.BlockSpec((rows, width), lambda i: (0, at // width))


def attention_forward(raw, places, cosine, sine, info, row):
    length = raw.shape[0]
    _, at_query, at_key, _, _, at_value, _ = places
    width = cosine.shape[1]
    return pl.pallas_call(
        partial(attention_forward_kernel, block=256),
        grid=(1,),
        in_specs=[
            column_block(length, width, at_query),
            column_block(length, width, at_key),
            column_block(length, width, at_value),
            whole(cosine.shape), whole(sine.shape), whole(info.shape), whole(row.shape),
        ],
        out_specs=whole((length, width)),
        out_shape=jax.ShapeDtypeStruct((length, width), jnp.bfloat16),
        compiler_params=limits(48),
        name="attention_forward",
    )(raw, raw, raw, cosine, sine, info, row)


def attention_backward(raw, places, cosine, sine, info, row, grad_mixed):
    length = raw.shape[0]
    _, at_query, at_key, at_gate, at_conv, at_value, _ = places
    width = cosine.shape[1]
    out = jax.ShapeDtypeStruct((length, width), jnp.bfloat16)
    return pl.pallas_call(
        partial(attention_backward_kernel, block=256),
        grid=(1,),
        in_specs=[
            column_block(length, width, at_query),
            column_block(length, width, at_key),
            column_block(length, width, at_value),
            whole(cosine.shape), whole(sine.shape), whole(info.shape), whole(row.shape),
            column_block(length, width, at_conv - at_gate),
        ],
        out_specs=[whole((length, width))] * 3,
        out_shape=[out] * 3,
        scratch_shapes=[pltpu.VMEM((length, width), jnp.float32)] * 2,
        compiler_params=limits(48),
        name="attention_backward",
    )(raw, raw, raw, cosine, sine, info, row, grad_mixed)


def mamba_forward(raw, places, step_raw, info, row, params, attended, head_width):
    length = raw.shape[0]
    at_shared, at_query, at_key, at_gate, at_conv, at_value, at_step = places
    width = at_conv - at_gate
    shared = at_query - at_shared
    head_dim = attended.shape[1]
    chunks = length // CHUNK

    def block(columns, at=0):
        return pl.BlockSpec((CHUNK, columns), lambda i: (i, at // columns))

    return pl.pallas_call(
        partial(mamba_forward_kernel, head_width=head_width),
        grid=(chunks,),
        in_specs=[
            block(shared, at_shared), block(width, at_gate), block(width, at_conv),
            block(LANES), block(LANES), pl.BlockSpec((8, CHUNK), lambda i: (0, i)),
            *[whole(p.shape) for p in params],
            block(head_dim),
        ],
        out_specs=[
            block(width + head_dim), block(width),
            pl.BlockSpec((None, shared // 2, width), lambda i: (i, 0, 0)),
        ],
        out_shape=[
            jax.ShapeDtypeStruct((length, width + head_dim), jnp.bfloat16),
            jax.ShapeDtypeStruct((length, width), jnp.bfloat16),
            jax.ShapeDtypeStruct((chunks, shared // 2, width), jnp.bfloat16),
        ],
        scratch_shapes=[
            pltpu.VMEM((shared // 2, width), jnp.float32),
            pltpu.VMEM((TAIL + CHUNK, width + shared), jnp.float32),
        ],
        compiler_params=limits(48),
        name="mamba_forward",
    )(raw, raw, raw, step_raw, info, row, *params, attended)


def mamba_backward(
    raw, places, step_raw, info, row, params, combined, states, grad_mixed, grads, head_width
):
    length = raw.shape[0]
    at_shared, at_query, at_key, at_gate, at_conv, at_value, at_step = places
    width = at_conv - at_gate
    shared = at_query - at_shared
    head_dim = grads[0].shape[1]
    chunks = length // CHUNK
    total = at_step + LANES
    tail = 16

    def block(columns, at=0):
        return pl.BlockSpec((CHUNK, columns), lambda i: (chunks - 1 - i, at // columns))

    return pl.pallas_call(
        partial(mamba_backward_kernel, head_width=head_width, places=places),
        grid=(chunks,),
        in_specs=[
            block(at_step),
            pl.BlockSpec(
                (tail, at_step),
                lambda i: (jnp.maximum((chunks - 1 - i) * (CHUNK // tail) - 1, 0), 0),
            ),
            block(LANES), block(LANES),
            pl.BlockSpec((8, CHUNK), lambda i: (0, chunks - 1 - i)),
            *[whole(p.shape) for p in params],
            block(width),
            pl.BlockSpec((None, shared // 2, width), lambda i: (chunks - 1 - i, 0, 0)),
            block(grad_mixed.shape[1]),
            block(head_dim), block(head_dim), block(head_dim),
        ],
        out_specs=[block(total), block(LANES), whole((16, shared))],
        out_shape=[
            jax.ShapeDtypeStruct((length, total), jnp.bfloat16),
            jax.ShapeDtypeStruct((length, LANES), jnp.float32),
            jax.ShapeDtypeStruct((16, shared), jnp.float32),
        ],
        scratch_shapes=[
            pltpu.VMEM((shared // 2, width), jnp.float32),
            pltpu.VMEM((TAIL + CHUNK, width + shared), jnp.float32),
            pltpu.VMEM((TAIL + CHUNK, width + shared), jnp.float32),
        ],
        compiler_params=limits(48),
        name="mamba_backward",
    )(raw, raw, step_raw, info, row, *params, combined, states, grad_mixed, *grads)


def matmul(former, latter):
    return jnp.dot(former, latter, preferred_element_type=jnp.float32)


def matmul_left(former, latter):
    return lax.dot_general(
        former, latter, (((0,), (0,)), ((), ())), preferred_element_type=jnp.float32
    )


def matmul_right(former, latter):
    return lax.dot_general(
        former, latter, (((1,), (1,)), ((), ())), preferred_element_type=jnp.float32
    )


def col_swap(values, distance):
    count = lax.axis_size("col")
    return lax.ppermute(values, "col", [(i, i ^ distance) for i in range(count)])


def row_swap(values):
    return lax.ppermute(values, "row", [(0, 1), (1, 0)])


def gather_pieces(block):
    half = block.shape[0] // 2
    along_x = col_swap(block, 2)
    along_y = row_swap(block)
    core = col_swap(block, 1)
    top = col_swap(along_y[:half], 2)
    low = row_swap(along_x[half:])
    own = [block, along_x, core, col_swap(along_x, 1)]
    other = [along_y, (top, low), col_swap(along_y, 1), (col_swap(top, 1), col_swap(low, 1))]
    return own, other


def add_low(former, latter):
    return (former.astype(jnp.float32) + latter.astype(jnp.float32)).astype(jnp.bfloat16)


def scatter_sum(shares):
    (own, own_far), (other, other_far) = shares
    tokens = own.shape[0]
    half = tokens // 2
    width = own.shape[1] // 2
    other = add_low(other, col_swap(other_far, 1))
    own = add_low(own, col_swap(own_far, 1))
    top_got = col_swap(jnp.concatenate([own[:half, width:], other[:half, width:]], axis=0), 2)
    low_got = row_swap(other[half:])
    top_last = row_swap(add_low(other[:half, :width], top_got[half:]))
    low_last = col_swap(add_low(own[half:, width:], low_got[:, width:]), 2)
    wide = jnp.float32
    top = own[:half, :width].astype(wide) + top_got[:half].astype(wide) + top_last.astype(wide)
    low = own[half:, :width].astype(wide) + low_got[:, :width].astype(wide) + low_last.astype(wide)
    return jnp.concatenate([top, low], axis=0)


def token_total(own, other):
    total = own + row_swap(other)
    total = total + col_swap(total, 1)
    return total + col_swap(total, 2)


def dp_sum(values):
    if lax.axis_size("dp") != 4:
        return lax.psum(values, "dp")
    place = lax.axis_index("dp")
    pair = add_low(values, lax.ppermute(values, "dp", [(0, 1), (3, 2)]))
    total = add_low(pair, lax.ppermute(pair, "dp", [(1, 2), (2, 1)]))
    final = lax.ppermute(total, "dp", [(1, 0), (2, 3)])
    return jnp.where((place == 1) | (place == 2), total, final)


def dp_total(values):
    count = lax.axis_size("dp")
    if count & (count - 1):
        return lax.psum(values, "dp")
    distance = 1
    while distance < count:
        values = values + lax.ppermute(values, "dp", [(i, i ^ distance) for i in range(count)])
        distance *= 2
    return values


def exchange_blocks(blocks):
    return [col_swap(block, d) if d else block for block, d in zip(blocks, DISTANCES)]


def in_order(pieces, index, axis):
    stacked = jnp.stack([pieces[DISTANCES.index(d)] for d in range(len(DISTANCES))])
    return jnp.concatenate(
        [lax.dynamic_index_in_dim(stacked, index ^ b, 0, keepdims=False) for b in range(len(pieces))],
        axis=axis,
    )


def own_first(values, row_index):
    return jnp.where(row_index == 0, values, jnp.flip(values, 0))


def assemble_kernel(*refs, split, normed):
    tile = pl.program_id(0)
    tiles = pl.num_programs(0)
    count = len(split) + sum(split)
    pieces = list(refs[:count])
    rest = refs[count:]
    columns = []
    for halves in split:
        if halves:
            top, low = pieces.pop(0), pieces.pop(0)
            columns.append(jnp.where(tile < tiles // 2, top[...], low[...]))
        else:
            columns.append(pieces.pop(0)[...])
    width = columns[0].shape[1]
    if not normed:
        for at, piece in enumerate(columns):
            rest[0][:, at * width : (at + 1) * width] = piece
        return
    gain_ref, out_ref, factor_ref = rest
    total = jnp.zeros((columns[0].shape[0], 1), jnp.float32)
    for piece in columns:
        values = piece.astype(jnp.float32)
        total = total + jnp.sum(values * values, axis=1, keepdims=True)
    factor = lax.rsqrt(total * (1.0 / (width * len(columns))) + EPS)
    for at, piece in enumerate(columns):
        span = slice(at * width, (at + 1) * width)
        out_ref[:, span] = (piece.astype(jnp.float32) * factor * gain_ref[:, span]).astype(jnp.bfloat16)
    factor_ref[...] = jnp.broadcast_to(factor, factor_ref.shape)


def assemble(pieces, gain=None):
    tokens, width = pieces[0].shape
    tiles = 4
    size = tokens // tiles
    total = width * len(pieces)
    split = [isinstance(piece, tuple) for piece in pieces]
    specs, operands = [], []
    for piece, halves in zip(pieces, split):
        if halves:
            specs.append(pl.BlockSpec((size, width), lambda i: (jnp.minimum(i, tiles // 2 - 1), 0)))
            specs.append(pl.BlockSpec((size, width), lambda i: (jnp.maximum(i - tiles // 2, 0), 0)))
            operands.extend(piece)
        else:
            specs.append(pl.BlockSpec((size, width), lambda i: (i, 0)))
            operands.append(piece)
    out_specs = [pl.BlockSpec((size, total), lambda i: (i, 0))]
    out_shape = [jax.ShapeDtypeStruct((tokens, total), jnp.bfloat16)]
    if gain is not None:
        specs.append(whole((1, total)))
        operands.append(gain)
        out_specs.append(pl.BlockSpec((size, LANES), lambda i: (i, 0)))
        out_shape.append(jax.ShapeDtypeStruct((tokens, LANES), jnp.float32))
    out = pl.pallas_call(
        partial(assemble_kernel, split=split, normed=gain is not None),
        grid=(tiles,),
        in_specs=specs,
        out_specs=out_specs,
        out_shape=out_shape,
        compiler_params=limits(32),
        name="assemble",
    )(*operands)
    return out if gain is not None else out[0]


def on_device(
    tokens,
    cotangent,
    segment_ids,
    norm1_gain,
    proj_gate,
    proj_conv,
    proj_step,
    proj_shared,
    proj_query,
    proj_key,
    proj_value,
    conv_weight,
    conv_bias,
    shared_conv,
    shared_bias,
    step_bias,
    decay_log,
    skip_gain,
    mamba_out_proj,
    attn_out_proj,
    norm2_gain,
    ffn_gate,
    ffn_up,
    ffn_down,
):
    low = jnp.bfloat16
    wide = jnp.float32
    me = lax.axis_index("col")
    row_index = lax.axis_index("row")
    length = segment_ids.shape[1]
    width = tokens.shape[1]
    model = width * len(DISTANCES)
    head_dim = proj_key.shape[1]
    channels = proj_gate.shape[1] // 4
    steps = proj_step.shape[1] // 4
    head_width = channels // steps
    units = ffn_gate.shape[1] // 4
    query_width = proj_query.shape[1] // 4
    part = proj_shared.shape[1]
    at_query = 2 * part
    at_key = at_query + query_width
    at_gate = at_key + head_dim
    at_conv = at_gate + channels
    at_value = at_conv + channels
    at_step = at_value + head_dim
    places = (0, at_query, at_key, at_gate, at_conv, at_value, at_step)

    def cols(weight, place, count):
        return lax.dynamic_slice_in_dim(weight, place * count, count, 1)

    def rows(weight, place, count):
        return lax.dynamic_slice_in_dim(weight, place * count, count, 0)

    def first_block(place):
        step = jnp.pad(cols(proj_step, place, steps), ((0, 0), (0, LANES - steps)))
        return jnp.concatenate(
            [
                proj_shared,
                cols(proj_query, place, query_width),
                proj_key,
                cols(proj_gate, place, channels),
                cols(proj_conv, place, channels),
                proj_value,
                step,
            ],
            axis=1,
        )

    token_own, token_other = gather_pieces(tokens)
    blocks = exchange_blocks([first_block(me ^ d) for d in DISTANCES])
    shared_own = jnp.concatenate([b[:, :part] for b in blocks], axis=0)
    shared_other = row_swap(shared_own)
    weight_first = jnp.concatenate(
        [
            jnp.where(row_index == 0, shared_own, shared_other),
            jnp.where(row_index == 0, shared_other, shared_own),
            jnp.concatenate([b[:, part:] for b in blocks], axis=0),
        ],
        axis=1,
    )
    gains = jnp.stack([norm1_gain, norm2_gain])
    gains = jnp.concatenate(exchange_blocks([gains] * 4), axis=1)
    gain1, gain2 = gains[0:1], gains[1:2]
    weight_out = jnp.concatenate(
        exchange_blocks(
            [
                jnp.concatenate(
                    [rows(mamba_out_proj, me ^ d, channels), rows(attn_out_proj, me ^ d, query_width)],
                    axis=0,
                )
                for d in DISTANCES
            ]
        ),
        axis=1,
    )
    weight_in = jnp.concatenate(
        exchange_blocks(
            [
                jnp.concatenate([cols(ffn_gate, me ^ d, units), cols(ffn_up, me ^ d, units)], axis=1)
                for d in DISTANCES
            ]
        ),
        axis=0,
    )
    weight_down = jnp.concatenate(
        exchange_blocks([rows(ffn_down, me ^ d, units) for d in DISTANCES]), axis=1
    )

    segments = own_first(segment_ids, row_index)
    indices = jnp.arange(length, dtype=jnp.int32)
    same = segments[:, :, None] == segments[:, None, :]
    position = jnp.sum(same & (indices[:, None] > indices[None, :]), axis=2).astype(wide)
    remaining = jnp.sum(same & (indices[:, None] < indices[None, :]), axis=2).astype(wide)
    lane = jnp.arange(LANES)
    info = jnp.where(
        lane == 0,
        segments.astype(wide)[..., None],
        jnp.where(lane == 1, position[..., None], remaining[..., None]),
    )
    row_info = jnp.broadcast_to(segments.astype(wide)[:, None, :], (2, 8, length))
    half_dim = head_dim // 2
    frequency = ROPE_BASE ** (-2.0 * jnp.arange(half_dim, dtype=wide) / head_dim)
    angles = position[..., None] * frequency
    cosine, sine = jnp.cos(angles), jnp.sin(angles)
    cosine = jnp.concatenate([cosine, cosine], axis=2)
    sine = jnp.concatenate([-sine, sine], axis=2)
    head_rows = jnp.pad(
        jnp.stack([step_bias, jnp.exp(decay_log)]), ((0, 6), (0, LANES - steps))
    )
    params = (
        conv_weight, conv_bias[None], shared_conv, shared_bias[None], head_rows,
        jnp.repeat(skip_gain, head_width)[None],
    )

    both = (0, 1)
    normed1, factor1, raw, step_raw, mixed, combined, states = [], [], [], [], [], [], []
    for s, pieces in enumerate((token_own, token_other)):
        normed, factor = assemble(pieces, gain1)
        normed1.append(normed)
        factor1.append(factor)
        raw.append(matmul(normed, weight_first[:, :at_step]).astype(low))
        step_raw.append(matmul(normed, weight_first[:, at_step:]))
        attended = attention_forward(raw[s], places, cosine[s], sine[s], info[s], row_info[s])
        got = mamba_forward(
            raw[s], places, step_raw[s], info[s], row_info[s], params, attended, head_width
        )
        mixed.append(got[0])
        combined.append(got[1])
        states.append(got[2])

    def spread_out(values, weight):
        return (
            matmul(values, weight[:, : model // 2]).astype(low),
            matmul(values, weight[:, model // 2 :]).astype(low),
        )

    def spread_back(values, weight):
        return (
            matmul_right(values, weight[: model // 2]).astype(low),
            matmul_right(values, weight[model // 2 :]).astype(low),
        )

    hidden1 = tokens.astype(wide) + scatter_sum([spread_out(mixed[s], weight_out) for s in both])
    normed2, factor2, gate_pre, up_pre, hidden = [], [], [], [], []
    for pieces in gather_pieces(hidden1.astype(low)):
        normed, factor = assemble(pieces, gain2)
        normed2.append(normed)
        factor2.append(factor)
        gate_pre.append(matmul(normed, weight_in[:, :units]).astype(low))
        up_pre.append(matmul(normed, weight_in[:, units:]).astype(low))
        gate = gate_pre[-1].astype(wide)
        hidden.append((gate * jax.nn.sigmoid(gate) * up_pre[-1].astype(wide)).astype(low))
    cot = [assemble(pieces) for pieces in gather_pieces(cotangent)]
    grad_in, inner = [], []
    for s in both:
        grad_hidden = matmul_right(cot[s], weight_down)
        gate, up = gate_pre[s].astype(wide), up_pre[s].astype(wide)
        sigmoid = jax.nn.sigmoid(gate)
        grad_gate = (grad_hidden * up * sigmoid * (1.0 + gate * (1.0 - sigmoid))).astype(low)
        grad_up = (grad_hidden * gate * sigmoid).astype(low)
        inner.append(
            jnp.sum(grad_gate.astype(wide) * gate + grad_up.astype(wide) * up, axis=1)
            .reshape(length // LANES, LANES)
        )
        grad_in.append(jnp.concatenate([grad_gate, grad_up], axis=1))
    inner2 = token_total(*inner).reshape(length, 1)
    grad_normed2 = scatter_sum([spread_back(grad_in[s], weight_in) for s in both])
    output = (hidden1 + scatter_sum([spread_out(hidden[s], weight_down) for s in both])).astype(low)

    def token_grad(former, latter):
        return (matmul_left(former[0], latter[0]) + matmul_left(former[1], latter[1])).astype(low)

    grad_down = token_grad(hidden, cot)
    grad_weight_in = token_grad(normed2, grad_in)
    own_factor = factor2[0][:, :1]
    back2 = (
        own_factor * norm2_gain * grad_normed2
        - hidden1 * (own_factor * own_factor * inner2 / model)
    )
    grad_gain2 = jnp.sum(grad_normed2 * hidden1 * own_factor, axis=0)
    grad_hidden1 = cotangent.astype(wide) + back2
    mix_grad = [assemble(pieces) for pieces in gather_pieces(grad_hidden1.astype(low))]
    grad_weight_out = token_grad(mixed, mix_grad)
    grad_first, inner, sums = [], [], []
    for s in both:
        grad_mixed = matmul_right(mix_grad[s], weight_out).astype(low)
        grads = attention_backward(
            raw[s], places, cosine[s], sine[s], info[s], row_info[s], grad_mixed
        )
        got = mamba_backward(
            raw[s], places, step_raw[s], info[s], row_info[s], params, combined[s], states[s],
            grad_mixed, grads, head_width,
        )
        grad_first.append(got[0])
        inner.append(jnp.sum(got[1], axis=1).reshape(length // LANES, LANES))
        sums.append(got[2])
    inner1 = token_total(*inner).reshape(length, 1)
    grad_normed1 = scatter_sum([spread_back(grad_first[s], weight_first) for s in both])
    grad_weight_first = token_grad(normed1, grad_first)
    own_factor = factor1[0][:, :1]
    own_tokens = tokens.astype(wide)
    back1 = (
        own_factor * norm1_gain * grad_normed1
        - own_tokens * (own_factor * own_factor * inner1 / model)
    )
    grad_gain1 = jnp.sum(grad_normed1 * own_tokens * own_factor, axis=0)
    tokens_grad = (grad_hidden1 + back1).astype(low)

    four = range(4)
    down = exchange_blocks([grad_down[:, p * width : (p + 1) * width] for p in four])
    down = dp_sum(jnp.stack(down))
    d_ffn_down = in_order([down[p] for p in four], me, 0).astype(wide)
    into = exchange_blocks([grad_weight_in[p * width : (p + 1) * width] for p in four])
    into = dp_sum(jnp.stack(into))
    d_ffn_gate = in_order([into[p, :, :units] for p in four], me, 1).astype(wide)
    d_ffn_up = in_order([into[p, :, units:] for p in four], me, 1).astype(wide)
    outs = exchange_blocks([grad_weight_out[:, p * width : (p + 1) * width] for p in four])
    outs = dp_sum(jnp.stack(outs))
    d_mamba_out = in_order([outs[p, :channels] for p in four], me, 0).astype(wide)
    d_attn_out = in_order([outs[p, channels:] for p in four], me, 0).astype(wide)
    first = exchange_blocks([grad_weight_first[p * width : (p + 1) * width] for p in four])
    lone = dp_sum(jnp.stack([f[:, at_gate:at_value] for f in first]))
    d_gate = in_order([lone[p, :, :channels] for p in four], me, 1).astype(wide)
    d_conv = in_order([lone[p, :, channels:] for p in four], me, 1).astype(wide)

    def over_devices(begin, end):
        return sum(f[:, begin:end].astype(wide) for f in first).astype(low)

    shared_sum = over_devices(0, at_query)
    shared_keep = jnp.where(row_index == 0, shared_sum[:, :part], shared_sum[:, part:])
    shared_send = jnp.where(row_index == 0, shared_sum[:, part:], shared_sum[:, :part])
    shared_total = add_low(shared_keep, row_swap(shared_send))
    step_all = in_order([f[:, at_step : at_step + steps] for f in first], me, 1)
    query_all = in_order([f[:, at_query:at_key] for f in first], me, 1)
    common = dp_sum(
        jnp.concatenate(
            [
                query_all, over_devices(at_key, at_gate), over_devices(at_value, at_step),
                shared_total, jnp.pad(step_all, ((0, 0), (0, LANES - 4 * steps))),
            ],
            axis=1,
        )
    ).astype(wide)
    d_query = common[:, : 4 * query_width]
    at = 4 * query_width
    d_key = common[:, at : at + head_dim]
    d_value = common[:, at + head_dim : at + 2 * head_dim]
    at = at + 2 * head_dim
    d_shared = common[:, at : at + part]
    d_step = common[:, at + part : at + part + 4 * steps]

    sums = sums[0] + sums[1]
    sums = jnp.concatenate(
        [sums[:13], jnp.stack([grad_gain1, grad_gain2]), jnp.zeros((1, width), wide)], axis=0
    )
    line = jnp.arange(16)[:, None]
    taps = conv_weight.shape[0]
    is_shared = (line > taps) & (line < 2 * taps + 2)
    sums = sums + jnp.where(is_shared | (line >= 13), row_swap(sums), 0.0)
    sums = sums + jnp.where(is_shared, col_swap(sums, 1), 0.0)
    sums = sums + jnp.where(is_shared, col_swap(sums, 2), 0.0)
    sums = dp_total(sums)
    return (
        output, tokens_grad, sums[13], d_gate, d_conv, d_step, d_shared, d_query, d_key, d_value,
        sums[:taps, :channels], sums[taps, :channels], sums[taps + 1 : 2 * taps + 1],
        sums[2 * taps + 1],
        sums[11, :steps], sums[12, :steps],
        jnp.sum(sums[10, :channels].reshape(steps, head_width), axis=1),
        d_mamba_out, d_attn_out, sums[14], d_ffn_gate, d_ffn_up, d_ffn_down,
    )


def solution(mesh):
    return jax.shard_map(
        on_device,
        mesh=mesh,
        in_specs=(
            P(("dp", "row"), "col"),
            P(("dp", "row"), "col"),
            P("dp", None),
            P("col"),
            P("col", "row"),
            P("col", "row"),
            P("col", "row"),
            P("col", "row"),
            P("col", "row"),
            P("col", "row"),
            P("col", "row"),
            P(None, ("row", "col")),
            P(("row", "col")),
            P(),
            P(),
            P(("row", "col")),
            P(("row", "col")),
            P(("row", "col")),
            P("row", "col"),
            P("row", "col"),
            P("col"),
            P("col", "row"),
            P("col", "row"),
            P("row", "col"),
        ),
        out_specs=(
            P(("dp", "row"), "col"),
            P(("dp", "row"), "col"),
            P("col"),
            P("col", "row"),
            P("col", "row"),
            P("col", "row"),
            P("col", "row"),
            P("col", "row"),
            P("col", "row"),
            P("col", "row"),
            P(None, ("row", "col")),
            P(("row", "col")),
            P(),
            P(),
            P(("row", "col")),
            P(("row", "col")),
            P(("row", "col")),
            P("row", "col"),
            P("row", "col"),
            P("col"),
            P("col", "row"),
            P("col", "row"),
            P("row", "col"),
        ),
        check_vma=False,
    )
```

time: 2450 us -> 1410 us (0.58)
  waiting for transfers between devices: 1320 us -> 676 us
  blocking collectives: 224 us -> 0 us
  matrix products: 353 us -> 174 us
  other arithmetic: 328 us -> 166 us
  starting transfers between devices: 4.12 us -> 131 us
  Pallas kernels: 0 us -> 126 us
  local copies, waits for them, and re-layouts: 192 us -> 120 us
    ppermute x0 -> x115, waiting for transfers between devices: none -> 676 us  [the longest x77 405 us: col_swap(): lax.ppermute(values, 'col', [(i, i ^ distance) for i in range(count)])]
    reduce_scatter x12 -> x0, waiting for transfers between devices: 613 us -> none  [the longest x2 210 us: sum_pair(): lax.psum_scatter(former, 'col', scatter_dimension=1, tiled=True)]
    psum x3 -> x0, waiting for transfers between devices: 441 us -> none  [the longest x1 433 us: on_device(): lax.psum(grad_proj_gate.astype(jnp.bfloat16), 'dp').astype(jnp.float32)]
    all_gather x12 -> x0, waiting for transfers between devices: 265 us -> none  [the longest x4 112 us: gather_rows(): return lax.all_gather(values, 'row', axis=0, tiled=True)]
    psum x7 -> x0, blocking collectives: 206 us -> none  [the longest x1 139 us: shared_total(): return lax.psum((former, latter), ('row', 'col'))]
    dot_general x17 -> x0, matrix products: 138 us -> none  [the longest x3 46.9 us: state_scan(): jnp.einsum('abjn,abjh,abjhp->abhnp', b_map, jnp.exp(suffix) * step_size,...]
    ppermute x0 -> x115, starting transfers between devices: none -> 131 us  [the longest x77 42.4 us: col_swap(): lax.ppermute(values, 'col', [(i, i ^ distance) for i in range(count)])]
    pallas_call x0 -> x16, Pallas kernels: none -> 126 us  [the longest x2 63.1 us: mamba_backward(): pl.pallas_call(partial(mamba_backward_kernel, head_width=head_width, plac...]
  transfers between devices with their start and end apart: 28 -> 115, of which waited for: 18 -> 42; matrix products, arithmetic and copies ran while one was open for 32% -> 27% of each run, Pallas kernels for 0% -> 8%
where the time goes in v1:
time: 1410 us; the launch traced here: 1400 us
  waiting for transfers between devices  676 us (48%)
  matrix products  174 us (12%)
  other arithmetic  166 us (12%)
  starting transfers between devices  131 us (9%)
  Pallas kernels  126 us (9%)
  local copies, waits for them, and re-layouts  120 us (9%)
    ppermute x77, waiting for transfers between devices, col_swap(): lax.ppermute(values, 'col', [(i, i ^ distance) for i in range(count)])  405 us
    ppermute x5, waiting for transfers between devices, dp_sum(): final = lax.ppermute(total, 'dp', [(1, 0), (2, 3)])  89.6 us
    ppermute x21, waiting for transfers between devices, row_swap(): return lax.ppermute(values, 'row', [(0, 1), (1, 0)])  65.9 us
    pallas_call x2, Pallas kernels, mamba_backward(): pl.pallas_call(partial(mamba_backward_kernel, head_width=head_width, plac...  63.1 us
    dot_general x12, matrix products, matmul_right(): lax.dot_general(former, latter, (((1,), (1,)), ((), ())), preferred_eleme...  59.4 us
    dot_general x8, matrix products, matmul_left(): lax.dot_general(former, latter, (((0,), (0,)), ((), ())), preferred_eleme...  59.2 us
    ppermute x2, waiting for transfers between devices, dp_total(): lax.ppermute(values, 'dp', [(i, i ^ distance) for i in range(count)])  58.9 us
    ppermute x5, waiting for transfers between devices, dp_sum(): pair = add_low(values, lax.ppermute(values, 'dp', [(0, 1), (3, 2)]))  56.9 us
  transfers between devices with their start and end apart: 115, of which 42 were waited for; matrix products, arithmetic and copies ran while one was open for 27% of the time, Pallas kernels for 8%

profile of v1, /device:TPU:0, one launch (start us, length us, event | category | flops | bytes accessed | tf_op | source)
XLA Modules:
  0.0 1398.5 jit_solution(6895460865967023866)
XLA Ops:
  48.4 21.3 %collective-permute-done.14.refs_0_ = bf16[1024,512]{1,0:T(8,128)(2,1)} collective-permute-done((bf16[1024,512]{1,0:T(8,128)(2,1)S(1)}, bf16[1024,512]{1,0:T(8,128)(2,1)}, u32[]{:S(2)}, u32[]{:S(2)}) %collective-permute-start.14) | collective-permute-done | bytes 1048608 | tf_op jit(solution)/shard_map/ppermute | solution.py:561
  72.6 49.6 %collective-permute-done.12 = bf16[512,512]{1,0:T(8,128)(2,1)} collective-permute-done((bf16[512,512]{1,0:T(8,128)(2,1)}, bf16[512,512]{1,0:T(8,128)(2,1)}, u32[]{:S(2)}, u32[]{:S(2)}) %collective-permute-start.12) | collective-permute-done | bytes 524320 | tf_op jit(solution)/shard_map/ppermute | solution.py:557
  162.6 35.9 %maximum_maximum_fusion = bf16[2048,1792]{1,0:T(8,128)(2,1)S(1)} fusion(bf16[512,1280]{1,0:T(8,128)(2,1)S(1)} %slice.698, bf16[512,1280]{1,0:T(8,128)(2,1)S(1)} %slice.697, bf16[512,1280]{1,0:T(8,128)(2,1)S(1)} %slice.696, bf16[512,1280]{1,0:T(8,128)(2,1)S(1)} %copy-done.87, bf16[2048,256]{1,0:T(8,128)(2,1)S(1)} %get-tuple-element.265, ...), kind=kLoop, calls=%fused_computation.8 | loop fusion | flops 44040192 | bytes 14680064 | tf_op jit(solution)/shard_map/concatenate | solution.py:777
  198.5 17.8 %fusion.4.query_ref.key_ref.value_ref.shared_ref.gate_ref.conv_ref.raw_ref.tail_ref = bf16[1024,1664]{1,0:T(8,128)(2,1)S(1)} fusion(bf16[1024,2048]{1,0:T(8,128)(2,1)S(1)} %get-tuple-element.47, bf16[2048,1792]{1,0:T(8,128)(2,1)S(1)} %maximum_maximum_fusion), kind=kOutput, calls=%fused_computation.44 | convolution fusion | flops 6981025792 | bytes 14417920 | tf_op jit(solution)/shard_map/dot_general | solution.py:540
  289.1 21.3 %collective-permute-done.21 = bf16[1024,512]{1,0:T(8,128)(2,1)S(1)} collective-permute-done((bf16[1024,512]{1,0:T(8,128)(2,1)S(1)}, bf16[1024,512]{1,0:T(8,128)(2,1)S(1)}, u32[]{:S(2)}, u32[]{:S(2)}) %collective-permute-start.21) | collective-permute-done | bytes 1048608 | tf_op jit(solution)/shard_map/ppermute | solution.py:557
  331.8 15.3 %collective-permute-done.50.refs_0_ = bf16[1024,512]{1,0:T(8,128)(2,1)} collective-permute-done((bf16[1024,512]{1,0:T(8,128)(2,1)}, bf16[1024,512]{1,0:T(8,128)(2,1)}, u32[]{:S(2)}, u32[]{:S(2)}) %collective-permute-start.50) | collective-permute-done | bytes 1048608 | tf_op jit(solution)/shard_map/ppermute | solution.py:561
  347.0 17.9 %collective-permute-done.24 = bf16[512,512]{1,0:T(8,128)(2,1)S(1)} collective-permute-done((bf16[512,512]{1,0:T(8,128)(2,1)S(1)}, bf16[512,512]{1,0:T(8,128)(2,1)S(1)}, u32[]{:S(2)}, u32[]{:S(2)}) %collective-permute-start.24) | collective-permute-done | bytes 524320 | tf_op jit(solution)/shard_map/ppermute | solution.py:557
  370.2 17.2 %collective-permute-done.46.refs_1_ = bf16[1024,512]{1,0:T(8,128)(2,1)S(1)} collective-permute-done((bf16[1024,512]{1,0:T(8,128)(2,1)}, bf16[1024,512]{1,0:T(8,128)(2,1)S(1)}, u32[]{:S(2)}, u32[]{:S(2)}) %collective-permute-start.46) | collective-permute-done | bytes 1048608 | tf_op jit(solution)/shard_map/ppermute | solution.py:557
  389.1 20.0 %collective-permute-done.30 = bf16[512,1024]{1,0:T(8,128)(2,1)S(1)} collective-permute-done((bf16[512,1024]{1,0:T(8,128)(2,1)S(1)}, bf16[512,1024]{1,0:T(8,128)(2,1)S(1)}, u32[]{:S(2)}, u32[]{:S(2)}) %collective-permute-start.30) | collective-permute-done | bytes 1048608 | tf_op jit(solution)/shard_map/ppermute | solution.py:557
  424.1 18.9 %collective-permute-done.25.refs_1_ = bf16[1024,512]{1,0:T(8,128)(2,1)S(1)} collective-permute-done((bf16[1024,512]{1,0:T(8,128)(2,1)S(1)}, bf16[1024,512]{1,0:T(8,128)(2,1)S(1)}, u32[]{:S(2)}, u32[]{:S(2)}) %collective-permute-start.25) | collective-permute-done | bytes 1048608 | tf_op jit(solution)/shard_map/ppermute | solution.py:557
  555.2 17.0 %collective-permute-done.103 = bf16[512,1024]{0,1:T(8,128)(2,1)S(1)} collective-permute-done((bf16[512,1024]{0,1:T(8,128)(2,1)S(1)}, bf16[512,1024]{0,1:T(8,128)(2,1)S(1)}, u32[]{:S(2)}, u32[]{:S(2)}) %collective-permute-start.103) | collective-permute-done | bytes 1048608 | tf_op jit(solution)/shard_map/ppermute | solution.py:557
  579.1 14.6 %collective-permute-done.105 = bf16[512,1024]{0,1:T(8,128)(2,1)S(1)} collective-permute-done((bf16[512,1024]{0,1:T(8,128)(2,1)S(1)}, bf16[512,1024]{0,1:T(8,128)(2,1)S(1)}, u32[]{:S(2)}, u32[]{:S(2)}) %collective-permute-start.105) | collective-permute-done | bytes 1048608 | tf_op jit(solution)/shard_map/ppermute | solution.py:557
  599.9 16.8 %collective-permute-done.57 = bf16[1024,512]{1,0:T(8,128)(2,1)S(1)} collective-permute-done((bf16[1024,512]{1,0:T(8,128)(2,1)S(1)}, bf16[1024,512]{1,0:T(8,128)(2,1)S(1)}, u32[]{:S(2)}, u32[]{:S(2)}) %collective-permute-start.57) | collective-permute-done | bytes 1048608 | tf_op jit(solution)/shard_map/ppermute | solution.py:557
  675.8 27.6 %collective-permute-done.45 = bf16[512,512]{1,0:T(8,128)(2,1)} collective-permute-done((bf16[512,512]{1,0:T(8,128)(2,1)}, bf16[512,512]{1,0:T(8,128)(2,1)}, u32[]{:S(2)}, u32[]{:S(2)}) %collective-permute-start.45) | collective-permute-done | bytes 524320 | tf_op jit(solution)/shard_map/ppermute | solution.py:557
  739.6 31.5 %mamba_backward.2 = (bf16[1024,1792]{1,0:T(8,128)(2,1)}, f32[1024,128]{1,0:T(8,128)S(1)}, f32[16,512]{1,0:T(8,128)S(1)}) custom-call(bf16[1024,1664]{1,0:T(8,128)(2,1)} %copy-done.1, bf16[1024,1664]{1,0:T(8,128)(2,1)} %copy-done.1, f32[1024,128]{1,0:T(8,128)S(1)} %copy-done.15, f32[1024,128]{1,0:T(8,128)S(1)} %copy-done.7, f32[8,1024]{1,0:T(8,128)S(1)} %copy-done.27, ...), custom_call_target="tpu_custom_call" | custom-call | tf_op jit(solution)/shard_map/mamba_backward/pallas_call | solution.py:506
  803.4 31.7 %mamba_backward.3 = (bf16[1024,1792]{1,0:T(8,128)(2,1)}, f32[1024,128]{1,0:T(8,128)S(1)}, f32[16,512]{1,0:T(8,128)S(1)}) custom-call(bf16[1024,1664]{1,0:T(8,128)(2,1)} %copy-done, bf16[1024,1664]{1,0:T(8,128)(2,1)} %copy-done, f32[1024,128]{1,0:T(8,128)S(1)} %copy-done.13, f32[1024,128]{1,0:T(8,128)S(1)} %copy-done.5, f32[8,1024]{1,0:T(8,128)S(1)} %copy-done.25, ...), custom_call_target="tpu_custom_call" | custom-call | tf_op jit(solution)/shard_map/mamba_backward/pallas_call | solution.py:506
  893.1 78.6 %collective-permute-done.81 = f32[8,128]{1,0:T(8,128)S(1)} collective-permute-done((f32[8,128]{1,0:T(8,128)S(1)}, f32[8,128]{1,0:T(8,128)S(1)}, u32[]{:S(2)}, u32[]{:S(2)}) %collective-permute-start.81) | collective-permute-done | bytes 4128 | tf_op jit(solution)/shard_map/ppermute | solution.py:557
  1028.6 18.5 %collective-permute-done.75 = bf16[1024,512]{1,0:T(8,128)(2,1)S(1)} collective-permute-done((bf16[1024,512]{1,0:T(8,128)(2,1)S(1)}, bf16[1024,512]{1,0:T(8,128)(2,1)S(1)}, u32[]{:S(2)}, u32[]{:S(2)}) %collective-permute-start.75) | collective-permute-done | bytes 1048608 | tf_op jit(solution)/shard_map/ppermute | solution.py:557
  1064.7 14.5 %collective-permute-done.94 = bf16[512,1152]{0,1:T(8,128)(2,1)S(1)} collective-permute-done((bf16[512,1152]{0,1:T(8,128)(2,1)S(1)}, bf16[512,1152]{0,1:T(8,128)(2,1)S(1)}, u32[]{:S(2)}, u32[]{:S(2)}) %collective-permute-start.94) | collective-permute-done | bytes 1179680 | tf_op jit(solution)/shard_map/ppermute | solution.py:607
  1107.3 38.8 %collective-permute-done.90 = bf16[4,512,768]{1,2,0:T(8,128)(2,1)S(1)} collective-permute-done((bf16[4,512,768]{1,2,0:T(8,128)(2,1)}, bf16[4,512,768]{1,2,0:T(8,128)(2,1)S(1)}, u32[]{:S(2)}, u32[]{:S(2)}) %collective-permute-start.90) | collective-permute-done | bytes 3145760 | tf_op jit(solution)/shard_map/ppermute | solution.py:607
  1157.5 25.9 %collective-permute-start.86 = (f32[16,512]{1,0:T(8,128)S(1)}, f32[16,512]{1,0:T(8,128)S(1)}, u32[]{:S(2)}, u32[]{:S(2)}) collective-permute-start(f32[16,512]{1,0:T(8,128)S(1)} %add.434), channel_id=1, source_target_pairs={{0,16},{8,24},{16,0},{24,8},{1,17},{9,25},{17,1},{25,9},{2,18},{10... | collective-permute-start | bytes 98312 | tf_op jit(solution)/shard_map/ppermute | solution.py:619
  1186.0 58.9 %collective-permute-done.86 = f32[16,512]{1,0:T(8,128)S(1)} collective-permute-done((f32[16,512]{1,0:T(8,128)S(1)}, f32[16,512]{1,0:T(8,128)S(1)}, u32[]{:S(2)}, u32[]{:S(2)}) %collective-permute-start.86) | collective-permute-done | bytes 32800 | tf_op jit(solution)/shard_map/ppermute | solution.py:619
  1269.3 54.8 %collective-permute-done.108 = bf16[4,512,1024]{1,2,0:T(8,128)(2,1)} collective-permute-done((bf16[4,512,1024]{1,2,0:T(8,128)(2,1)}, bf16[4,512,1024]{1,2,0:T(8,128)(2,1)}, u32[]{:S(2)}, u32[]{:S(2)}) %collective-permute-start.108) | collective-permute-done | bytes 4194336 | tf_op jit(solution)/shard_map/ppermute | solution.py:609
  1356.4 34.8 %collective-permute-done.92 = bf16[4,512,768]{1,2,0:T(8,128)(2,1)S(1)} collective-permute-done((bf16[4,512,768]{1,2,0:T(8,128)(2,1)}, bf16[4,512,768]{1,2,0:T(8,128)(2,1)S(1)}, u32[]{:S(2)}, u32[]{:S(2)}) %collective-permute-start.92) | collective-permute-done | bytes 3145760 | tf_op jit(solution)/shard_map/ppermute | solution.py:609
  (890 shorter events, 695.3 us)
Async XLA Ops:
  40.5 82.2 %collective-permute-start.6 = (bf16[512,1536]{1,0:T(8,128)(2,1)}, bf16[512,1536]{1,0:T(8,128)(2,1)}, u32[]{:S(2)}, u32[]{:S(2)}) collective-permute-start(bf16[512,1536]{1,0:T(8,128)(2,1)} %pad_dynamic-update-slice_fusion.3), channel_id=1, source_target_pairs={{0,2},{1,3},{2,0},{3,1},{4,6},{5,7},{6,4},{7,5},{8,10},{9,11},{10,... | collective-permute-start | bytes 4718600 | tf_op jit(solution)/shard_map/ppermute | solution.py:557
  40.8 82.8 %collective-permute-start.7 = (bf16[512,1536]{1,0:T(8,128)(2,1)}, bf16[512,1536]{1,0:T(8,128)(2,1)}, u32[]{:S(2)}, u32[]{:S(2)}) collective-permute-start(bf16[512,1536]{1,0:T(8,128)(2,1)} %pad_dynamic-update-slice_fusion.2), channel_id=1, source_target_pairs={{0,1},{1,0},{2,3},{3,2},{4,5},{5,4},{6,7},{7,6},{8,9},{9,8},{10,11... | collective-permute-start | bytes 4718600 | tf_op jit(solution)/shard_map/ppermute | solution.py:557
  41.2 82.3 %collective-permute-start.8 = (bf16[512,1536]{1,0:T(8,128)(2,1)}, bf16[512,1536]{1,0:T(8,128)(2,1)}, u32[]{:S(2)}, u32[]{:S(2)}) collective-permute-start(bf16[512,1536]{1,0:T(8,128)(2,1)} %pad_dynamic-update-slice_fusion.1), channel_id=1, source_target_pairs={{0,3},{1,2},{2,1},{3,0},{4,7},{5,6},{6,5},{7,4},{8,11},{9,10},{10,... | collective-permute-start | bytes 4718600 | tf_op jit(solution)/shard_map/ppermute | solution.py:557
  46.8 75.4 %collective-permute-start.12 = (bf16[512,512]{1,0:T(8,128)(2,1)}, bf16[512,512]{1,0:T(8,128)(2,1)}, u32[]{:S(2)}, u32[]{:S(2)}) collective-permute-start(bf16[512,512]{1,0:T(8,128)(2,1)} %pad_maximum_fusion.45), channel_id=1, source_target_pairs={{0,3},{1,2},{2,1},{3,0},{4,7},{5,6},{6,5},{7,4},{8,11},{9,10},{10,... | collective-permute-start | bytes 1572872 | tf_op jit(solution)/shard_map/ppermute | solution.py:557
  69.7 67.2 %collective-permute-start.1 = (bf16[1024,512]{1,0:T(8,128)(2,1)S(1)}, bf16[1024,512]{1,0:T(8,128)(2,1)S(1)}, u32[]{:S(2)}, u32[]{:S(2)}) collective-permute-start(bf16[1024,512]{1,0:T(8,128)(2,1)S(1)} %copy-done.2), channel_id=1, source_target_pairs={{0,1},{1,0},{2,3},{3,2},{4,5},{5,4},{6,7},{7,6},{8,9},{9,8},{10,11... | collective-permute-start | bytes 3145736 | tf_op jit(solution)/shard_map/ppermute | solution.py:557
  480.0 69.6 %collective-permute-start.49 = (bf16[1024,1024]{1,0:T(8,128)(2,1)}, bf16[1024,1024]{1,0:T(8,128)(2,1)}, u32[]{:S(2)}, u32[]{:S(2)}) collective-permute-start(bf16[1024,1024]{1,0:T(8,128)(2,1)} %convolution_convert_fusion.1), channel_id=1, source_target_pairs={{0,1},{1,0},{2,3},{3,2},{4,5},{5,4},{6,7},{7,6},{8,9},{9,8},{10,11... | collective-permute-start | bytes 6291464 | tf_op jit(solution)/shard_map/ppermute | solution.py:557
  549.8 73.5 %collective-permute-start.41 = (bf16[1024,1024]{1,0:T(8,128)(2,1)S(1)}, bf16[1024,1024]{1,0:T(8,128)(2,1)S(1)}, u32[]{:S(2)}, u32[]{:S(2)}) collective-permute-start(bf16[1024,1024]{1,0:T(8,128)(2,1)S(1)} %convolution_convert_fusion.2), channel_id=1, source_target_pairs={{0,1},{1,0},{2,3},{3,2},{4,5},{5,4},{6,7},{7,6},{8,9},{9,8},{10,11... | collective-permute-start | bytes 6291464 | tf_op jit(solution)/shard_map/ppermute | solution.py:557
  574.3 66.5 %collective-permute-start.112 = (bf16[4,512,512]{2,1,0:T(8,128)(2,1)}, bf16[4,512,512]{2,1,0:T(8,128)(2,1)}, u32[]{:S(2)}, u32[]{:S(2)}) collective-permute-start(bf16[4,512,512]{2,1,0:T(8,128)(2,1)} %pad_maximum_fusion.13), channel_id=1, source_target_pairs={{0,8},{24,16},{1,9},{25,17},{2,10},{26,18},{3,11},{27,19},{4,12},{... | collective-permute-start | bytes 6291464 | tf_op jit(solution)/shard_map/ppermute | solution.py:607
  616.7 97.7 %collective-permute-start.106 = (bf16[4,512,1024]{1,2,0:T(8,128)(2,1)}, bf16[4,512,1024]{1,2,0:T(8,128)(2,1)}, u32[]{:S(2)}, u32[]{:S(2)}) collective-permute-start(bf16[4,512,1024]{1,2,0:T(8,128)(2,1)} %pad_maximum_fusion.1), channel_id=1, source_target_pairs={{0,8},{24,16},{1,9},{25,17},{2,10},{26,18},{3,11},{27,19},{4,12},{... | collective-permute-start | bytes 12582920 | tf_op jit(solution)/shard_map/ppermute | solution.py:607
  710.2 266.8 %collective-permute-start.114 = (bf16[4,512,512]{2,1,0:T(8,128)(2,1)}, bf16[4,512,512]{2,1,0:T(8,128)(2,1)}, u32[]{:S(2)}, u32[]{:S(2)}) collective-permute-start(bf16[4,512,512]{2,1,0:T(8,128)(2,1)} %add_convert_fusion.6), channel_id=1, source_target_pairs={{8,0},{16,24},{9,1},{17,25},{10,2},{18,26},{11,3},{19,27},{12,4},{... | collective-permute-start | bytes 6291464 | tf_op jit(solution)/shard_map/ppermute | solution.py:609
  719.8 67.1 %collective-permute-start.71 = (bf16[1024,512]{1,0:T(8,128)(2,1)}, bf16[1024,512]{1,0:T(8,128)(2,1)}, u32[]{:S(2)}, u32[]{:S(2)}) collective-permute-start(bf16[1024,512]{1,0:T(8,128)(2,1)} %collective-permute-done.68.refs_0_), channel_id=1, source_target_pairs={{0,1},{1,0},{2,3},{3,2},{4,5},{5,4},{6,7},{7,6},{8,9},{9,8},{10,11... | collective-permute-start | bytes 3145736 | tf_op jit(solution)/shard_map/ppermute | solution.py:557
  889.7 111.9 %collective-permute-start.89 = (bf16[512,1792]{0,1:T(8,128)(2,1)}, bf16[512,1792]{0,1:T(8,128)(2,1)}, u32[]{:S(2)}, u32[]{:S(2)}) collective-permute-start(bf16[512,1792]{0,1:T(8,128)(2,1)} %get-tuple-element.184), channel_id=1, source_target_pairs={{0,3},{1,2},{2,1},{3,0},{4,7},{5,6},{6,5},{7,4},{8,11},{9,10},{10,... | collective-permute-start | bytes 5505032 | tf_op jit(solution)/shard_map/ppermute | solution.py:557
  891.0 111.3 %collective-permute-start.87 = (bf16[512,1792]{0,1:T(8,128)(2,1)}, bf16[512,1792]{0,1:T(8,128)(2,1)}, u32[]{:S(2)}, u32[]{:S(2)}) collective-permute-start(bf16[512,1792]{0,1:T(8,128)(2,1)} %get-tuple-element.183), channel_id=1, source_target_pairs={{0,2},{1,3},{2,0},{3,1},{4,6},{5,7},{6,4},{7,5},{8,10},{9,11},{10,... | collective-permute-start | bytes 5505032 | tf_op jit(solution)/shard_map/ppermute | solution.py:557
  891.6 116.6 %collective-permute-start.88 = (bf16[512,1792]{0,1:T(8,128)(2,1)}, bf16[512,1792]{0,1:T(8,128)(2,1)}, u32[]{:S(2)}, u32[]{:S(2)}) collective-permute-start(bf16[512,1792]{0,1:T(8,128)(2,1)} %get-tuple-element.185), channel_id=1, source_target_pairs={{0,1},{1,0},{2,3},{3,2},{4,5},{5,4},{6,7},{7,6},{8,9},{9,8},{10,11... | collective-permute-start | bytes 5505032 | tf_op jit(solution)/shard_map/ppermute | solution.py:557
  891.6 80.1 %collective-permute-start.81 = (f32[8,128]{1,0:T(8,128)S(1)}, f32[8,128]{1,0:T(8,128)S(1)}, u32[]{:S(2)}, u32[]{:S(2)}) collective-permute-start(f32[8,128]{1,0:T(8,128)S(1)} %fusion.185), channel_id=1, source_target_pairs={{0,2},{1,3},{2,0},{3,1},{4,6},{5,7},{6,4},{7,5},{8,10},{9,11},{10,... | collective-permute-start | bytes 12296 | tf_op jit(solution)/shard_map/ppermute | solution.py:557
  990.0 161.2 %collective-permute-start.107 = (bf16[4,512,1024]{1,2,0:T(8,128)(2,1)S(1)}, bf16[4,512,1024]{1,2,0:T(8,128)(2,1)S(1)}, u32[]{:S(2)}, u32[]{:S(2)}) collective-permute-start(bf16[4,512,1024]{1,2,0:T(8,128)(2,1)S(1)} %copy-done.97), channel_id=1, source_target_pairs={{8,16},{16,8},{9,17},{17,9},{10,18},{18,10},{11,19},{19,11},{12,20... | collective-permute-start | bytes 12582920 | tf_op jit(solution)/shard_map/ppermute | solution.py:608
  1053.9 92.3 %collective-permute-start.90 = (bf16[4,512,768]{1,2,0:T(8,128)(2,1)}, bf16[4,512,768]{1,2,0:T(8,128)(2,1)S(1)}, u32[]{:S(2)}, u32[]{:S(2)}) collective-permute-start(bf16[4,512,768]{1,2,0:T(8,128)(2,1)} %pad_maximum_fusion.2), channel_id=1, source_target_pairs={{0,8},{24,16},{1,9},{25,17},{2,10},{26,18},{3,11},{27,19},{4,12},{... | collective-permute-start | bytes 9437192 | tf_op jit(solution)/shard_map/ppermute | solution.py:607
  1095.3 62.2 %collective-permute-start.85 = (f32[16,512]{1,0:T(8,128)S(1)}, f32[16,512]{1,0:T(8,128)S(1)}, u32[]{:S(2)}, u32[]{:S(2)}) collective-permute-start(f32[16,512]{1,0:T(8,128)S(1)} %select_add_fusion), channel_id=1, source_target_pairs={{0,8},{8,0},{16,24},{24,16},{1,9},{9,1},{17,25},{25,17},{2,10},{10... | collective-permute-start | bytes 98312 | tf_op jit(solution)/shard_map/ppermute | solution.py:619
  1101.3 147.3 %collective-permute-start.96 = (bf16[512,1152]{0,1:T(8,128)(2,1)S(1)}, bf16[512,1152]{0,1:T(8,128)(2,1)}, u32[]{:S(2)}, u32[]{:S(2)}) collective-permute-start(bf16[512,1152]{0,1:T(8,128)(2,1)S(1)} %add_convert_fusion.20), channel_id=1, source_target_pairs={{8,0},{16,24},{9,1},{17,25},{10,2},{18,26},{11,3},{19,27},{12,4},{... | collective-permute-start | bytes 3538952 | tf_op jit(solution)/shard_map/ppermute | solution.py:609
  1105.8 151.3 %collective-permute-start.102 = (bf16[4,512,512]{2,1,0:T(8,128)(2,1)}, bf16[4,512,512]{2,1,0:T(8,128)(2,1)}, u32[]{:S(2)}, u32[]{:S(2)}) collective-permute-start(bf16[4,512,512]{2,1,0:T(8,128)(2,1)} %add_convert_fusion.9), channel_id=1, source_target_pairs={{8,0},{16,24},{9,1},{17,25},{10,2},{18,26},{11,3},{19,27},{12,4},{... | collective-permute-start | bytes 6291464 | tf_op jit(solution)/shard_map/ppermute | solution.py:609
  1148.8 111.4 %collective-permute-start.91 = (bf16[4,512,768]{1,2,0:T(8,128)(2,1)}, bf16[4,512,768]{1,2,0:T(8,128)(2,1)}, u32[]{:S(2)}, u32[]{:S(2)}) collective-permute-start(bf16[4,512,768]{1,2,0:T(8,128)(2,1)} %add_convert_fusion.5), channel_id=1, source_target_pairs={{8,16},{16,8},{9,17},{17,9},{10,18},{18,10},{11,19},{19,11},{12,20... | collective-permute-start | bytes 9437192 | tf_op jit(solution)/shard_map/ppermute | solution.py:608
  1156.0 168.1 %collective-permute-start.108 = (bf16[4,512,1024]{1,2,0:T(8,128)(2,1)}, bf16[4,512,1024]{1,2,0:T(8,128)(2,1)}, u32[]{:S(2)}, u32[]{:S(2)}) collective-permute-start(bf16[4,512,1024]{1,2,0:T(8,128)(2,1)} %add_convert_fusion.1), channel_id=1, source_target_pairs={{8,0},{16,24},{9,1},{17,25},{10,2},{18,26},{11,3},{19,27},{12,4},{... | collective-permute-start | bytes 12582920 | tf_op jit(solution)/shard_map/ppermute | solution.py:609
  1157.5 87.4 %collective-permute-start.86 = (f32[16,512]{1,0:T(8,128)S(1)}, f32[16,512]{1,0:T(8,128)S(1)}, u32[]{:S(2)}, u32[]{:S(2)}) collective-permute-start(f32[16,512]{1,0:T(8,128)S(1)} %add.434), channel_id=1, source_target_pairs={{0,16},{8,24},{16,0},{24,8},{1,17},{9,25},{17,1},{25,9},{2,18},{10... | collective-permute-start | bytes 98312 | tf_op jit(solution)/shard_map/ppermute | solution.py:619
  1265.5 125.7 %collective-permute-start.92 = (bf16[4,512,768]{1,2,0:T(8,128)(2,1)}, bf16[4,512,768]{1,2,0:T(8,128)(2,1)S(1)}, u32[]{:S(2)}, u32[]{:S(2)}) collective-permute-start(bf16[4,512,768]{1,2,0:T(8,128)(2,1)} %add_convert_fusion.4), channel_id=1, source_target_pairs={{8,0},{16,24},{9,1},{17,25},{10,2},{18,26},{11,3},{19,27},{12,4},{... | collective-permute-start | bytes 9437192 | tf_op jit(solution)/shard_map/ppermute | solution.py:609
  (285 other events, 6066.1 us)

commit v2 on v1

v2 whole, which is shorter than its diff:
```python
from functools import partial
import math
from typing import NamedTuple

import jax
import jax.numpy as jnp
from jax import lax
from jax.experimental import pallas as pl
from jax.experimental.pallas import tpu as pltpu
from jax.sharding import PartitionSpec as P

EPS = 1e-05
ROPE_BASE = 100000000000.0
MASKED = -1e30
HIGHEST = lax.Precision.HIGHEST
DISTANCES = (0, 2, 1, 3)
LANES = 128
CHUNK = 128
TAIL = 8


class Places(NamedTuple):
    query: int
    key: int
    gate: int
    value: int
    shared: int
    conv: int
    step: int


def dot_any(former, latter, dims, precision=None):
    return lax.dot_general(
        former, latter, (dims, ((), ())), precision=precision, preferred_element_type=jnp.float32
    )


def nn(former, latter):
    return dot_any(former, latter, ((1,), (0,)))


def nt(former, latter):
    return dot_any(former, latter, ((1,), (1,)))


def tn(former, latter):
    return dot_any(former, latter, ((0,), (0,)))


def exact(former, latter):
    return dot_any(former, latter, ((1,), (0,)), HIGHEST)


def sigmoid_of(values):
    return 1.0 / (1.0 + jnp.exp(-values))


def softplus_of(values):
    return jnp.maximum(values, 0.0) + jnp.log1p(jnp.exp(-jnp.abs(values)))


def head_spread(head_width, width):
    heads = lax.broadcasted_iota(jnp.int32, (LANES, width), 0)
    columns = lax.broadcasted_iota(jnp.int32, (LANES, width), 1)
    return (columns // head_width == heads).astype(jnp.float32)


def head_gather(head_width, width):
    columns = lax.broadcasted_iota(jnp.int32, (width, LANES), 0)
    heads = lax.broadcasted_iota(jnp.int32, (width, LANES), 1)
    return (columns // head_width == heads).astype(jnp.float32)


def causal_conv(ext_ref, columns, weight_ref, bias_ref, position, taps):
    length = ext_ref.shape[0] - TAIL
    running = bias_ref[...] + weight_ref[taps - 1 : taps, :] * ext_ref[TAIL:, columns]
    for offset in range(1, taps):
        earlier = ext_ref[TAIL - offset : TAIL - offset + length, columns]
        running = running + weight_ref[taps - 1 - offset : taps - offset, :] * jnp.where(
            position >= offset, earlier, 0.0
        )
    return running


def chunk_decay(step_in, position, decay_rate):
    length = step_in.shape[0]
    step_size = softplus_of(step_in)
    log_decay = jnp.where(position == 0.0, 0.0, -step_size * decay_rate)
    rows = lax.broadcasted_iota(jnp.int32, (length, length), 0)
    columns = lax.broadcasted_iota(jnp.int32, (length, length), 1)
    causal = rows >= columns
    running = exact(causal.astype(jnp.float32), log_decay)
    return step_size, log_decay, running, jnp.transpose(running), causal


def split_pair(values, head_width):
    lane = lax.broadcasted_iota(jnp.int32, values.shape, 1)
    zero = jnp.zeros_like(values)
    return jnp.concatenate(
        [jnp.where(lane < head_width, values, zero), jnp.where(lane < head_width, zero, values)],
        axis=0,
    )


def mamba_forward_kernel(
    raw_ref, step_ref, info_ref, row_ref, weight_ref, bias_ref,
    shared_weight_ref, shared_bias_ref, head_ref, skip_ref, attended_ref,
    mixed_ref, combined_ref, states_ref,
    state, ext, *, head_width, places
):
    chunk = pl.program_id(0)
    length, width = combined_ref.shape
    gate_columns = slice(places.gate, places.value)
    conv_columns = slice(places.conv, places.step)
    shared_columns = slice(places.shared, places.conv)
    states = (places.conv - places.shared) // 2
    taps = weight_ref.shape[0]
    low = jnp.bfloat16

    @pl.when(chunk == 0)
    def _():
        state[...] = jnp.zeros_like(state)
        ext[...] = jnp.zeros_like(ext)

    ext[:TAIL, :] = ext[length : length + TAIL, :]
    ext[TAIL:, :width] = raw_ref[:, conv_columns].astype(jnp.float32)
    ext[TAIL:, width:] = raw_ref[:, shared_columns].astype(jnp.float32)
    segment = info_ref[:, 0:1]
    position = info_ref[:, 1:2]
    pre = causal_conv(ext, slice(0, width), weight_ref, bias_ref, position, taps)
    conv_out = pre * sigmoid_of(pre)
    pre = causal_conv(
        ext, slice(width, None), shared_weight_ref, shared_bias_ref, position, taps
    )
    shared = (pre * sigmoid_of(pre)).astype(low)
    b_map = shared[:, :states]
    c_map = shared[:, states:]
    step_size, _, running, running_t, causal = chunk_decay(
        step_ref[...] + head_ref[0:1, :], position, head_ref[1:2, :]
    )
    segment_row = row_ref[0:1, :]
    allowed = causal & (segment == segment_row)
    local = lax.broadcasted_iota(jnp.int32, (length, 1), 0).astype(jnp.float32)
    enters = jnp.where(position > local, jnp.exp(running), 0.0)
    last = running[length - 1 : length, :]
    leaves = jnp.where(segment == segment_row[:, length - 1 :], jnp.exp(last - running), 0.0)
    spread = head_spread(head_width, width)
    wide = exact(jnp.concatenate([step_size, enters, leaves], axis=0), spread)
    weighted = conv_out * wide[:length]
    gram = nt(c_map, b_map)
    weighted_low = weighted.astype(low)
    parts = []
    for pair in range(width // (2 * head_width)):
        weights = []
        for head in (2 * pair, 2 * pair + 1):
            gap = jnp.where(allowed, running[:, head : head + 1] - running_t[head : head + 1, :], MASKED)
            weights.append((gram * jnp.exp(gap)).astype(low))
        columns = slice(2 * pair * head_width, 2 * (pair + 1) * head_width)
        parts.append(
            nn(jnp.concatenate(weights, axis=1), split_pair(weighted_low[:, columns], head_width))
        )
    held = state[...]
    held_low = held.astype(low)
    states_ref[...] = held_low
    scanned = jnp.concatenate(parts, axis=1) + nn(c_map, held_low) * wide[length : 2 * length]
    fade = wide[2 * length - 1 : 2 * length]
    state[...] = held * fade + tn(b_map, (weighted * wide[2 * length :]).astype(low))
    combined = scanned + skip_ref[...] * conv_out
    combined_ref[...] = combined.astype(low)
    gate = raw_ref[:, gate_columns].astype(jnp.float32)
    mixed_ref[:, :width] = (combined * (gate * sigmoid_of(gate))).astype(low)
    mixed_ref[:, width:] = attended_ref[...]


def mamba_backward_kernel(
    raw_ref, tail_ref, step_ref, info_ref, row_ref, weight_ref, bias_ref,
    shared_weight_ref, shared_bias_ref, head_ref, skip_ref, states_ref, grad_ref,
    out_ref, inner_ref, sums_ref,
    grad_state, ext, ext_grad, *, head_width, places
):
    count = pl.num_programs(0)
    step = pl.program_id(0)
    length = grad_ref.shape[0]
    width = places.step - places.conv
    states = (places.conv - places.shared) // 2
    taps = weight_ref.shape[0]
    low = jnp.bfloat16
    f32 = jnp.float32
    gate_columns = slice(places.gate, places.value)
    conv_columns = slice(places.conv, places.step)
    shared_columns = slice(places.shared, places.conv)

    @pl.when(step == 0)
    def _():
        grad_state[...] = jnp.zeros_like(grad_state)
        ext_grad[...] = jnp.zeros_like(ext_grad)
        sums_ref[...] = jnp.zeros_like(sums_ref)

    tail_at = tail_ref.shape[0] - TAIL
    ext[:TAIL, :width] = tail_ref[:, conv_columns].astype(f32)[tail_at:]
    ext[:TAIL, width:] = tail_ref[:, shared_columns].astype(f32)[tail_at:]
    ext[TAIL:, :width] = raw_ref[:, conv_columns].astype(f32)
    ext[TAIL:, width:] = raw_ref[:, shared_columns].astype(f32)
    segment = info_ref[:, 0:1]
    position = info_ref[:, 1:2]
    remaining = info_ref[:, 2:3]
    pre = causal_conv(ext, slice(0, width), weight_ref, bias_ref, position, taps)
    sig = sigmoid_of(pre)
    conv_out = pre * sig
    conv_slope = sig * (1.0 + pre * (1.0 - sig))
    pre = causal_conv(
        ext, slice(width, None), shared_weight_ref, shared_bias_ref, position, taps
    )
    sig = sigmoid_of(pre)
    shared = (pre * sig).astype(low)
    shared_slope = sig * (1.0 + pre * (1.0 - sig))
    b_map = shared[:, :states]
    c_map = shared[:, states:]
    step_in = step_ref[...] + head_ref[0:1, :]
    rate = head_ref[1:2, :]
    step_size, log_decay, running, running_t, causal = chunk_decay(step_in, position, rate)
    segment_row = row_ref[0:1, :]
    allowed = causal & (segment == segment_row)
    local = lax.broadcasted_iota(jnp.int32, (length, 1), 0).astype(f32)
    enters = jnp.where(position > local, jnp.exp(running), 0.0)
    last = running[length - 1 : length, :]
    leaves = jnp.where(segment == segment_row[:, length - 1 :], jnp.exp(last - running), 0.0)
    spread = head_spread(head_width, width)
    wide = exact(jnp.concatenate([step_size, enters, leaves], axis=0), spread)
    step_wide = wide[:length]
    enters_wide = wide[length : 2 * length]
    leaves_wide = wide[2 * length :]
    fade = wide[2 * length - 1 : 2 * length]
    weighted = conv_out * step_wide

    gate = raw_ref[:, gate_columns].astype(f32)
    sig = sigmoid_of(gate)
    grad_scan = grad_ref[:, :width].astype(f32) * (gate * sig)

    gram = nt(c_map, b_map)
    weighted_low = weighted.astype(low)
    grad_low = grad_scan.astype(low)
    lane = lax.broadcasted_iota(jnp.int32, (length, LANES), 1)
    sub = lax.broadcasted_iota(jnp.int32, (LANES, length), 0)
    grad_gram = jnp.zeros((length, length), f32)
    by_row = jnp.zeros((length, LANES), f32)
    by_column = jnp.zeros((LANES, length), f32)
    parts = []
    for pair in range(width // (2 * head_width)):
        columns = slice(2 * pair * head_width, 2 * (pair + 1) * head_width)
        split_grad = split_pair(grad_low[:, columns], head_width)
        products = nt(split_grad, weighted_low[:, columns])
        weights = []
        for place, head in enumerate((2 * pair, 2 * pair + 1)):
            gap = jnp.where(allowed, running[:, head : head + 1] - running_t[head : head + 1, :], MASKED)
            fading = jnp.exp(gap)
            weight = gram * fading
            product = products[place * length : (place + 1) * length]
            grad_gram = grad_gram + fading * product
            meeting = weight * product
            by_row = jnp.where(lane == head, jnp.sum(meeting, axis=1, keepdims=True), by_row)
            by_column = jnp.where(sub == head, jnp.sum(meeting, axis=0, keepdims=True), by_column)
            weights.append(weight.astype(low))
        parts.append(tn(jnp.concatenate(weights, axis=0), split_grad))
    held = states_ref[...]
    entering = (grad_scan * enters_wide).astype(low)
    leaving = (weighted * leaves_wide).astype(low)
    grad_held = grad_state[...]
    grad_held_low = grad_held.astype(low)
    from_state = nn(b_map, grad_held_low) * leaves_wide
    grad_weighted = jnp.concatenate(parts, axis=1) + from_state
    grad_gram_low = grad_gram.astype(low)
    grad_c = nn(grad_gram_low, b_map) + nt(entering, held)
    grad_b = tn(grad_gram_low, c_map) + nt(leaving, grad_held_low)
    met_in = grad_scan * enters_wide * nn(c_map, held)
    met_out = weighted * from_state
    met_state = fade * jnp.sum(held.astype(f32) * grad_held, axis=0, keepdims=True)
    grad_state[...] = grad_held * fade + tn(c_map, entering)
    grad_conv_out = grad_weighted * step_wide + skip_ref[...] * grad_scan
    gathered = exact(
        jnp.concatenate(
            [met_in, met_out, conv_out * grad_weighted, jnp.broadcast_to(met_state, (TAIL, width))],
            axis=0,
        ),
        head_gather(head_width, width),
    )
    out_rows = gathered[length : 2 * length]
    at_last = jnp.sum(out_rows, axis=0, keepdims=True) + gathered[3 * length : 3 * length + 1]
    grad_running = by_row - jnp.transpose(by_column) + gathered[:length] - out_rows
    grad_running = grad_running + jnp.where(local == length - 1.0, at_last, 0.0)
    rows = lax.broadcasted_iota(jnp.int32, (length, length), 0)
    later = lax.broadcasted_iota(jnp.int32, (length, length), 1) >= rows
    grad_decay = jnp.where(position == 0.0, 0.0, exact(later.astype(f32), grad_running))
    grad_step = (gathered[2 * length : 3 * length] - grad_decay * rate) * sigmoid_of(step_in)

    ext_grad[length : length + TAIL, :] = ext_grad[:TAIL, :]
    ext_grad[:length, :width] = grad_conv_out * conv_slope
    ext_grad[:length, width : width + states] = grad_b * shared_slope[:, :states]
    ext_grad[:length, width + states :] = grad_c * shared_slope[:, states:]

    def conv_back(columns, weights, row_at):
        now = ext_grad[:length, columns]
        running = weights[taps - 1 : taps, :] * now
        wide_columns = slice(0, now.shape[1])
        sums_ref[row_at + taps : row_at + taps + 1, wide_columns] += jnp.sum(now, axis=0, keepdims=True)
        sums_ref[row_at + taps - 1 : row_at + taps, wide_columns] += jnp.sum(
            now * ext[TAIL:, columns], axis=0, keepdims=True
        )
        for offset in range(1, taps):
            at = taps - 1 - offset
            running = running + weights[at : at + 1, :] * jnp.where(
                remaining >= offset, ext_grad[offset : offset + length, columns], 0.0
            )
            earlier = jnp.where(
                position >= offset, ext[TAIL - offset : TAIL - offset + length, columns], 0.0
            )
            sums_ref[row_at + at : row_at + at + 1, wide_columns] += jnp.sum(
                now * earlier, axis=0, keepdims=True
            )
        return running

    grad_conv = conv_back(slice(0, width), weight_ref, 0).astype(low)
    grad_shared = conv_back(slice(width, None), shared_weight_ref, taps + 1).astype(low)
    row_at = 2 * (taps + 1)
    sums_ref[row_at : row_at + 1, :width] += jnp.sum(grad_scan * conv_out, axis=0, keepdims=True)
    sums_ref[row_at + 1 : row_at + 2, :LANES] += jnp.sum(grad_step, axis=0, keepdims=True)
    sums_ref[row_at + 2 : row_at + 3, :LANES] += jnp.sum(
        grad_decay * log_decay, axis=0, keepdims=True
    )
    grad_step = grad_step.astype(low)
    out_ref[:, : 2 * states] = grad_shared
    out_ref[:, 2 * states : 2 * states + width] = grad_conv
    out_ref[:, 2 * states + width :] = grad_step
    inner = grad_step.astype(f32) * step_ref[...]
    for at in range(0, places.step - places.shared, LANES):
        raw = raw_ref[:, places.shared + at : places.shared + at + LANES]
        inner = inner + out_ref[:, at : at + LANES].astype(f32) * raw.astype(f32)
    inner_ref[...] = inner


def rope(values, cosine, sine):
    return values * cosine + pltpu.roll(values, values.shape[1] // 2, 1) * sine


def attention_rows(query, key, begin, size, info_ref, row_ref, factor):
    seen = begin + size
    scores = nt(query, key) * factor
    rows = begin + lax.broadcasted_iota(jnp.int32, (size, seen), 0)
    columns = lax.broadcasted_iota(jnp.int32, (size, seen), 1)
    allowed = (rows >= columns) & (info_ref[begin:seen, 0:1] == row_ref[0:1, :seen])
    scores = jnp.where(allowed, scores, MASKED)
    raised = jnp.exp(scores - jnp.max(scores, axis=1, keepdims=True))
    return raised * (1.0 / jnp.sum(raised, axis=1, keepdims=True))


def attention_forward_kernel(
    query_ref, key_ref, value_ref, cosine_ref, sine_ref, info_ref, row_ref, out_ref, *, block
):
    low = jnp.bfloat16
    length, head_dim = query_ref.shape
    factor = 1.0 / math.sqrt(head_dim)
    cosine, sine = cosine_ref[...], sine_ref[...]
    query = rope(query_ref[...].astype(jnp.float32), cosine, sine).astype(low)
    key = rope(key_ref[...].astype(jnp.float32), cosine, sine).astype(low)
    value = value_ref[...]
    for begin in range(0, length, block):
        seen = begin + block
        probs = attention_rows(
            query[begin:seen], key[:seen], begin, block, info_ref, row_ref, factor
        )
        out_ref[begin:seen, :] = nn(probs.astype(low), value[:seen]).astype(low)


def attention_backward_kernel(
    raw_ref, cosine_ref, sine_ref, info_ref, row_ref, combined_ref, grad_ref,
    out_ref, inner_ref, key_total, value_total, *, block, places
):
    low = jnp.bfloat16
    length, head_dim = cosine_ref.shape
    channels = combined_ref.shape[1]
    factor = 1.0 / math.sqrt(head_dim)
    cosine, sine = cosine_ref[...], sine_ref[...]
    query = rope(raw_ref[:, : places.key].astype(jnp.float32), cosine, sine).astype(low)
    key = rope(raw_ref[:, places.key : places.gate].astype(jnp.float32), cosine, sine).astype(low)
    value = raw_ref[:, places.value : places.shared]
    key_total[...] = jnp.zeros_like(key_total)
    value_total[...] = jnp.zeros_like(value_total)
    for begin in range(0, length, block):
        seen = begin + block
        probs = attention_rows(
            query[begin:seen], key[:seen], begin, block, info_ref, row_ref, factor
        )
        grad_out = grad_ref[begin:seen, channels:]
        gate = raw_ref[begin:seen, places.gate : places.value].astype(jnp.float32)
        sig = sigmoid_of(gate)
        out_ref[begin:seen, places.gate : places.value] = (
            grad_ref[begin:seen, :channels].astype(jnp.float32)
            * combined_ref[begin:seen, :].astype(jnp.float32)
            * (sig * (1.0 + gate * (1.0 - sig)))
        ).astype(low)
        grad_probs = nt(grad_out, value[:seen])
        inner = jnp.sum(probs * grad_probs, axis=1, keepdims=True)
        grad_scores = (probs * (grad_probs - inner)).astype(low)
        grad_query = nn(grad_scores, key[:seen]) * factor
        out_ref[begin:seen, : places.key] = rope(
            grad_query, cosine[begin:seen], -sine[begin:seen]
        ).astype(low)
        key_total[:seen, :] += tn(grad_scores, query[begin:seen])
        value_total[:seen, :] += tn(probs.astype(low), grad_out)
    out_ref[:, places.key : places.gate] = rope(key_total[...] * factor, cosine, -sine).astype(low)
    out_ref[:, places.value :] = value_total[...].astype(low)
    inner = jnp.zeros(inner_ref.shape, jnp.float32)
    for at in range(0, places.shared, LANES):
        span = slice(at, at + LANES)
        inner = inner + out_ref[:, span].astype(jnp.float32) * raw_ref[:, span].astype(jnp.float32)
    inner_ref[...] = inner


BRIEF = pl.CostEstimate(flops=1, bytes_accessed=1, transcendentals=0)


def whole(shape):
    return pl.BlockSpec(shape, lambda i: (0,) * len(shape))


def limits(megabytes):
    return pltpu.CompilerParams(vmem_limit_bytes=megabytes * 1024 * 1024)


def column_block(rows, width, at):
    return pl.BlockSpec((rows, width), lambda i: (0, at // width))


def attention_forward(raw, places, cosine, sine, info, row):
    length, width = cosine.shape
    return pl.pallas_call(
        partial(attention_forward_kernel, block=256),
        grid=(1,),
        in_specs=[
            column_block(length, width, places.query),
            column_block(length, width, places.key),
            column_block(length, width, places.value),
            whole(cosine.shape), whole(sine.shape), whole(info.shape), whole(row.shape),
        ],
        out_specs=whole((length, width)),
        out_shape=jax.ShapeDtypeStruct((length, width), jnp.bfloat16),
        compiler_params=limits(48),
        cost_estimate=BRIEF,
        name="attention_forward",
    )(raw, raw, raw, cosine, sine, info, row)


def attention_backward(raw, places, cosine, sine, info, row, combined, grad_mixed):
    length, width = cosine.shape
    return pl.pallas_call(
        partial(attention_backward_kernel, block=256, places=places),
        grid=(1,),
        in_specs=[
            column_block(length, places.shared, 0),
            whole(cosine.shape), whole(sine.shape), whole(info.shape), whole(row.shape),
            whole(combined.shape), whole(grad_mixed.shape),
        ],
        out_specs=[whole((length, places.shared)), whole((length, LANES))],
        out_shape=[
            jax.ShapeDtypeStruct((length, places.shared), jnp.bfloat16),
            jax.ShapeDtypeStruct((length, LANES), jnp.float32),
        ],
        scratch_shapes=[pltpu.VMEM((length, width), jnp.float32)] * 2,
        compiler_params=limits(48),
        cost_estimate=BRIEF,
        name="attention_backward",
    )(raw, cosine, sine, info, row, combined, grad_mixed)


def mamba_forward(raw, places, step_raw, info, row, params, attended, head_width):
    length = raw.shape[0]
    width = places.step - places.conv
    states = (places.conv - places.shared) // 2
    head_dim = attended.shape[1]
    chunks = length // CHUNK

    def block(columns):
        return pl.BlockSpec((CHUNK, columns), lambda i: (i, 0))

    return pl.pallas_call(
        partial(mamba_forward_kernel, head_width=head_width, places=places),
        grid=(chunks,),
        in_specs=[
            block(places.step),
            block(LANES), block(LANES), pl.BlockSpec((8, CHUNK), lambda i: (0, i)),
            *[whole(p.shape) for p in params],
            block(head_dim),
        ],
        out_specs=[
            block(width + head_dim), block(width),
            pl.BlockSpec((None, states, width), lambda i: (i, 0, 0)),
        ],
        out_shape=[
            jax.ShapeDtypeStruct((length, width + head_dim), jnp.bfloat16),
            jax.ShapeDtypeStruct((length, width), jnp.bfloat16),
            jax.ShapeDtypeStruct((chunks, states, width), jnp.bfloat16),
        ],
        scratch_shapes=[
            pltpu.VMEM((states, width), jnp.float32),
            pltpu.VMEM((TAIL + CHUNK, width + 2 * states), jnp.float32),
        ],
        compiler_params=limits(48),
        cost_estimate=BRIEF,
        name="mamba_forward",
    )(raw, step_raw, info, row, *params, attended)


def mamba_backward(raw, places, step_raw, info, row, params, states, grad_mixed, head_width):
    length = raw.shape[0]
    width = places.step - places.conv
    shared = places.conv - places.shared
    chunks = length // CHUNK
    total = places.step + LANES - places.shared
    tail = 16

    def block(columns):
        return pl.BlockSpec((CHUNK, columns), lambda i: (chunks - 1 - i, 0))

    return pl.pallas_call(
        partial(mamba_backward_kernel, head_width=head_width, places=places),
        grid=(chunks,),
        in_specs=[
            block(places.step),
            pl.BlockSpec(
                (tail, places.step),
                lambda i: (jnp.maximum((chunks - 1 - i) * (CHUNK // tail) - 1, 0), 0),
            ),
            block(LANES), block(LANES),
            pl.BlockSpec((8, CHUNK), lambda i: (0, chunks - 1 - i)),
            *[whole(p.shape) for p in params],
            pl.BlockSpec((None, shared // 2, width), lambda i: (chunks - 1 - i, 0, 0)),
            block(grad_mixed.shape[1]),
        ],
        out_specs=[block(total), block(LANES), whole((16, shared))],
        out_shape=[
            jax.ShapeDtypeStruct((length, total), jnp.bfloat16),
            jax.ShapeDtypeStruct((length, LANES), jnp.float32),
            jax.ShapeDtypeStruct((16, shared), jnp.float32),
        ],
        scratch_shapes=[
            pltpu.VMEM((shared // 2, width), jnp.float32),
            pltpu.VMEM((TAIL + CHUNK, width + shared), jnp.float32),
            pltpu.VMEM((TAIL + CHUNK, width + shared), jnp.float32),
        ],
        compiler_params=limits(48),
        cost_estimate=BRIEF,
        name="mamba_backward",
    )(raw, raw, step_raw, info, row, *params, states, grad_mixed)


def matmul(former, latter):
    return jnp.dot(former, latter, preferred_element_type=jnp.float32)


def matmul_left(former, latter):
    return lax.dot_general(
        former, latter, (((0,), (0,)), ((), ())), preferred_element_type=jnp.float32
    )


def matmul_right(former, latter):
    return lax.dot_general(
        former, latter, (((1,), (1,)), ((), ())), preferred_element_type=jnp.float32
    )


def col_swap(values, distance):
    count = lax.axis_size("col")
    return lax.ppermute(values, "col", [(i, i ^ distance) for i in range(count)])


def row_swap(values):
    return lax.ppermute(values, "row", [(0, 1), (1, 0)])


def together(*values):
    return lax.optimization_barrier(values)


def after(value, *earlier):
    return lax.optimization_barrier((value, earlier))[0]


def gather_start(block):
    return col_swap(block, 2), row_swap(block), col_swap(block, 1)


def gather_middle(block, first):
    along_x, along_y, _ = first
    half = block.shape[0] // 2
    return col_swap(along_y[:half], 2), row_swap(along_x[half:]), col_swap(along_x, 1), col_swap(along_y, 1)


def gather_end(block, first, middle):
    along_x, along_y, core = first
    top, low, core_x, core_y = middle
    own = [block, along_x, core, core_x]
    other = [along_y, (top, low), core_y, (col_swap(top, 1), col_swap(low, 1))]
    return own, other


def gather_slow_second(first):
    along_x, along_y, _ = first
    return row_swap(along_x), col_swap(along_x, 1), col_swap(along_y, 1)


def gather_slow_end(block, first, second):
    along_x, along_y, core = first
    diagonal, core_x, core_y = second
    return [block, along_x, core, core_x], [along_y, diagonal, core_y, col_swap(diagonal, 1)]


def add_low(former, latter):
    return (former.astype(jnp.float32) + latter.astype(jnp.float32)).astype(jnp.bfloat16)


def other_first(near, far_core):
    other = add_low(near, far_core)
    half = other.shape[1] // 2
    return other, row_swap(other[:, half:]), col_swap(other[1, :half], 2)


def other_second(other, other_got):
    half = other.shape[1] // 2
    return row_swap(add_low(other[0, :half], other_got))


def own_second(near, far_core, low_got):
    own = add_low(near, far_core)
    half = own.shape[1] // 2
    return own, col_swap(own[1, :half], 2), col_swap(add_low(own[1, half:], low_got[1]), 2)


def own_sum(own, low_got, own_got, top_last, low_last):
    half = own.shape[1] // 2
    wide = jnp.float32
    top = own[0, :half].astype(wide) + own_got.astype(wide) + top_last.astype(wide)
    low = own[0, half:].astype(wide) + low_got[0].astype(wide) + low_last.astype(wide)
    return jnp.concatenate([top, low], axis=0)


def scatter_sum_slow(shares):
    (own, own_far), (other, other_far) = shares
    wide = jnp.float32
    other = add_low(other, col_swap(other_far, 1))
    got, near = lax.optimization_barrier((row_swap(other), col_swap(own_far, 1)))
    total = own.astype(wide) + near.astype(wide) + got.astype(wide)
    last = col_swap(total[1].astype(jnp.bfloat16), 2)
    return total[0] + last.astype(wide)


def token_total(own, other):
    total = own + row_swap(other)
    total = total + col_swap(total, 1)
    return total + col_swap(total, 2)


def line_update_kernel(flags_ref, now_ref, got_ref, pair_ref, crossed_ref, later_ref, out_ref, sent_ref):
    @pl.when(flags_ref[1] == 1)
    def _():
        wide = jnp.float32
        out_ref[...] = (now_ref[...].astype(wide) + got_ref[...].astype(wide)).astype(out_ref.dtype)
        sent_ref[...] = (pair_ref[...].astype(wide) + crossed_ref[...].astype(wide)).astype(sent_ref.dtype)

    @pl.when(flags_ref[1] == 0)
    def _():
        sent_ref[...] = later_ref[...]


def line_update(flags, now, got, pair, crossed, later):
    rows, columns = now.shape[1:]

    def middle_block(i, f):
        return (i * f[1], 0, 0)

    def end_block(i, f):
        return (i * (1 - f[1]), 0, 0)

    def every_block(i, f):
        return (i, 0, 0)

    block = (None, rows, columns)
    return pl.pallas_call(
        line_update_kernel,
        grid_spec=pltpu.PrefetchScalarGridSpec(
            num_scalar_prefetch=1,
            grid=(4,),
            in_specs=[pl.BlockSpec(block, middle_block)] * 4 + [pl.BlockSpec(block, end_block)],
            out_specs=[pl.BlockSpec(block, middle_block), pl.BlockSpec(block, every_block)],
        ),
        out_shape=[jax.ShapeDtypeStruct(now.shape, now.dtype)] * 2,
        compiler_params=limits(32),
        cost_estimate=BRIEF,
        name="line_update",
    )(flags, now, got, pair, crossed, later)


class LineSums:
    def __init__(self, flags):
        self.flags = flags
        self.step = 0
        self.now = self.sent = self.pair = None
        self.outward = False
        self.flying = ()
        self.done = []

    def advance(self, later=None):
        if lax.axis_size("dp") != 4:
            if later is not None:
                total = lax.psum(later, "dp")
                self.sent = later
                self.done.append((total, total))
            return
        if self.outward:
            self.done.append((self.sent, self.flying[0]))
        self.outward = self.pair is not None
        sent = self.now if later is None else later
        if self.step == 0:
            self.sent = later
        elif self.now is None:
            self.sent = add_low(self.pair, self.flying[1])
            self.pair = None
            if later is not None:
                self.sent = jnp.where(self.flags[1] == 1, self.sent, later)
        elif self.pair is None:
            self.pair = add_low(self.now, self.flying[0])
            self.sent = sent
        else:
            self.pair, self.sent = line_update(
                self.flags, self.now, self.flying[0], self.pair, self.flying[1], sent
            )
        self.now = later
        self.step += 1
        self._start()

    def finish(self):
        if lax.axis_size("dp") == 4:
            self.done.append((self.sent, self.flying[0]))

    def _start(self):
        move = lax.ppermute(self.sent, "dp", [(0, 1), (3, 2), (1, 0), (2, 3)])
        if self.pair is None:
            self.flying = (move,)
        else:
            self.flying = (move, lax.ppermute(self.pair, "dp", [(1, 2), (2, 1)]))


def chosen(flags, pair):
    return jnp.where(flags[1] == 1, pair[0], pair[1])


def dp_total(values):
    count = lax.axis_size("dp")
    if count & (count - 1):
        return lax.psum(values, "dp")
    distance = 1
    while distance < count:
        values = values + lax.ppermute(values, "dp", [(i, i ^ distance) for i in range(count)])
        distance *= 2
    return values


def far_pair(blocks):
    return col_swap(jnp.stack([blocks[1], blocks[3]]), 2)


def near_pair(blocks, fetched):
    return col_swap(jnp.stack([blocks[2], fetched[1]]), 1)


def block_specs(size, count):
    return [
        pl.BlockSpec((None, size, count), lambda i, *_, at=at: (at, i, 0)) for at in (0, 0, 0, 1)
    ]


def block_values(blocks, fetched, passed):
    return blocks, fetched, passed, passed


def own_first(values, row_index):
    return jnp.where(row_index == 0, values, jnp.flip(values, 0))


def tile_blocks(refs, split):
    tile = pl.program_id(0)
    tiles = pl.num_programs(0)
    refs = list(refs)
    blocks = []
    for halves in split:
        if halves:
            top, low = refs.pop(0), refs.pop(0)
            blocks.append(jnp.where(tile < tiles // 2, top[...], low[...]))
        else:
            blocks.append(refs.pop(0)[...])
    return blocks, refs


def write_normed(blocks, gain_ref, out_ref, factor_ref):
    width = blocks[0].shape[1]
    total = jnp.zeros((blocks[0].shape[0], 1), jnp.float32)
    for block in blocks:
        values = block.astype(jnp.float32)
        total = total + jnp.sum(values * values, axis=1, keepdims=True)
    factor = lax.rsqrt(total * (1.0 / (width * len(blocks))) + EPS)
    for at, block in enumerate(blocks):
        span = slice(at * width, (at + 1) * width)
        out_ref[:, span] = (block.astype(jnp.float32) * factor * gain_ref[:, span]).astype(jnp.bfloat16)
    factor_ref[...] = jnp.broadcast_to(factor, factor_ref.shape)


def project_kernel(*refs, split):
    blocks, refs = tile_blocks(refs, split)
    gain_ref, weight_ref, normed_ref, factor_ref, raw_ref, step_ref = refs
    write_normed(blocks, gain_ref, normed_ref, factor_ref)
    raw = nn(normed_ref[...], weight_ref[...])
    main = raw_ref.shape[1]
    raw_ref[...] = raw[:, :main].astype(jnp.bfloat16)
    step_ref[...] = raw[:, main:]


def ffn_kernel(*refs, split):
    blocks, refs = tile_blocks(refs, split)
    gain_ref, weight_ref, grad_hidden_ref, normed_ref, factor_ref, hidden_ref, grad_ref, inner_ref = refs
    write_normed(blocks, gain_ref, normed_ref, factor_ref)
    low, wide = jnp.bfloat16, jnp.float32
    units = hidden_ref.shape[1]
    gate_up = nn(normed_ref[...], weight_ref[...])
    gate, up = gate_up[:, :units], gate_up[:, units:]
    sig = sigmoid_of(gate)
    silu = gate * sig
    hidden_ref[...] = (silu * up).astype(low)
    grad_hidden = grad_hidden_ref[...]
    grad_gate = (grad_hidden * up * sig * (1.0 + gate * (1.0 - sig))).astype(low)
    grad_up = (grad_hidden * silu).astype(low)
    grad_ref[:, :units] = grad_gate
    grad_ref[:, units:] = grad_up
    products = grad_gate.astype(wide) * gate + grad_up.astype(wide) * up
    inner = products[:, :LANES]
    for at in range(LANES, units, LANES):
        inner = inner + products[:, at : at + LANES]
    inner_ref[...] = inner


def meet_kernel(*refs, split):
    blocks, refs = tile_blocks(refs, split)
    weight_ref, out_ref, product_ref = refs
    width = blocks[0].shape[1]
    for at, block in enumerate(blocks):
        out_ref[:, at * width : (at + 1) * width] = block
    product_ref[...] = nt(out_ref[...], weight_ref[...]).astype(product_ref.dtype)


def tiled_call(kernel, name, pieces, operands, outs, tiles=4):
    tokens, width = pieces[0].shape
    size = tokens // tiles
    split = [isinstance(piece, tuple) for piece in pieces]
    specs, values = [], []
    for piece, halves in zip(pieces, split):
        if halves:
            specs.append(pl.BlockSpec((size, width), lambda i: (jnp.minimum(i, tiles // 2 - 1), 0)))
            specs.append(pl.BlockSpec((size, width), lambda i: (jnp.maximum(i - tiles // 2, 0), 0)))
            values.extend(piece)
        else:
            specs.append(pl.BlockSpec((size, width), lambda i: (i, 0)))
            values.append(piece)
    for value, is_whole in operands:
        specs.append(whole(value.shape) if is_whole else pl.BlockSpec((size, value.shape[1]), lambda i: (i, 0)))
        values.append(value)
    return pl.pallas_call(
        partial(kernel, split=split),
        grid=(tiles,),
        in_specs=specs,
        out_specs=[pl.BlockSpec((size, columns), lambda i: (i, 0)) for columns, _ in outs],
        out_shape=[jax.ShapeDtypeStruct((tokens, columns), dtype) for columns, dtype in outs],
        compiler_params=limits(56),
        cost_estimate=BRIEF,
        name=name,
    )(*values)


def weight_grad_kernel(former_0, former_1, latter_0, latter_1, out_ref):
    total = tn(former_0[...], latter_0[...]) + tn(former_1[...], latter_1[...])
    out_ref[...] = total.astype(out_ref.dtype)


def weight_grad(former, latter, width, at=0, count=None):
    length, depth = former[0].shape
    if count is None:
        left = pl.BlockSpec((length, depth), lambda i: (0, 0))
        right = pl.BlockSpec((length, width), lambda i: (0, i))
        shape = (4, depth, width)
    else:
        left = pl.BlockSpec((length, width), lambda i: (0, i))
        right = pl.BlockSpec((length, count), lambda i: (0, at))
        shape = (4, width, count)
    return pl.pallas_call(
        weight_grad_kernel,
        grid=(4,),
        in_specs=[left, left, right, right],
        out_specs=pl.BlockSpec((None, *shape[1:]), lambda i: (i, 0, 0)),
        out_shape=jax.ShapeDtypeStruct(shape, jnp.bfloat16),
        compiler_params=limits(56),
        cost_estimate=BRIEF,
        name="weight_grad",
    )(*former, *latter)


def spread_kernel(*refs, transposed):
    values, (weight_ref, far_ref, near_ref) = refs[:-3], refs[-3:]
    step = pl.program_id(0)
    total = None
    at = 0
    for ref in values:
        if transposed:
            part = nt(ref[...], weight_ref[:, at : at + ref.shape[1]])
            at += ref.shape[1]
        else:
            part = nn(ref[...], weight_ref[...])
        total = part if total is None else total + part
    total = total.astype(far_ref.dtype)

    @pl.when(step < 2)
    def _():
        far_ref[...] = total

    @pl.when(step >= 2)
    def _():
        near_ref[...] = total


def spread(values, weight, width, transposed):
    tokens = values[0].shape[0]

    def block_of(i):
        return (i + 2) % 4

    if transposed:
        weight_spec = pl.BlockSpec((width, weight.shape[1]), lambda i: (block_of(i), 0))
    else:
        weight_spec = pl.BlockSpec((weight.shape[0], width), lambda i: (0, block_of(i)))
    shape = jax.ShapeDtypeStruct((2, tokens, width), jnp.bfloat16)
    far, near = pl.pallas_call(
        partial(spread_kernel, transposed=transposed),
        grid=(4,),
        in_specs=[whole(v.shape) for v in values] + [weight_spec],
        out_specs=[
            pl.BlockSpec((None, tokens, width), lambda i: (jnp.minimum(i, 1), 0, 0)),
            pl.BlockSpec((None, tokens, width), lambda i: (jnp.maximum(i - 2, 0), 0, 0)),
        ],
        out_shape=[shape, shape],
        compiler_params=limits(56),
        cost_estimate=BRIEF,
        name="spread",
    )(*values, weight)
    return near, far


def cut_first_kernel(flags_ref, query_ref, gate_ref, conv_ref, step_ref, out_ref, *, distances, steps):
    at = 0
    for ref in (query_ref, gate_ref, conv_ref):
        out_ref[:, at : at + ref.shape[1]] = ref[...]
        at += ref.shape[1]
    place = jnp.bitwise_xor(flags_ref[0], distance_at(pl.program_id(0), distances))
    step = pltpu.roll(step_ref[...].astype(jnp.float32), (LANES - place * steps) % LANES, 1)
    lane = lax.broadcasted_iota(jnp.int32, step.shape, 1)
    out_ref[:, at:] = jnp.where(lane < steps, step, 0.0).astype(out_ref.dtype)


def distance_at(i, distances):
    value = distances[0]
    for at, distance in enumerate(distances[1:], 1):
        value = jnp.where(i == at, distance, value)
    return value


def cut_first(flags, query, gate, conv, step, distances, size, at_share):
    depth = gate.shape[0]
    widths = [array.shape[1] // 4 for array in (query, gate, conv)]
    steps = step.shape[1] // 4
    total = sum(widths) + LANES
    step = jnp.pad(step, ((0, 0), (0, LANES - step.shape[1])))

    def row(f):
        return f[3] if at_share else 0

    def column_index(i, f):
        return (row(f), jnp.bitwise_xor(f[0], distance_at(i, distances)))

    return pl.pallas_call(
        partial(cut_first_kernel, distances=distances, steps=steps),
        grid_spec=pltpu.PrefetchScalarGridSpec(
            num_scalar_prefetch=1,
            grid=(len(distances),),
            in_specs=[pl.BlockSpec((size, w), column_index) for w in widths]
            + [pl.BlockSpec((size, LANES), lambda i, f: (row(f), 0))],
            out_specs=pl.BlockSpec((None, size, total), lambda i, f: (i, 0, 0)),
        ),
        out_shape=jax.ShapeDtypeStruct((len(distances), size, total), gate.dtype),
        compiler_params=limits(32),
        cost_estimate=BRIEF,
        name="cut_first",
    )(flags, query, gate, conv, step)


def cut_rest_kernel(flags_ref, gate_ref, up_ref, down_ref, out_ref):
    at = 0
    for ref in (gate_ref, up_ref, down_ref):
        out_ref[:, at : at + ref.shape[1]] = ref[...]
        at += ref.shape[1]


def cut_rest(flags, gate, up, down, distances, size, at_share):
    units = gate.shape[1] // 4
    width = down.shape[1]
    total = 2 * units + width
    parts = units // size

    def column_index(i, f):
        return (f[3] if at_share else 0, jnp.bitwise_xor(f[0], distance_at(i, distances)))

    def row_index(i, f):
        place = jnp.bitwise_xor(f[0], distance_at(i, distances))
        return (place * parts + (f[3] if at_share else 0), 0)

    return pl.pallas_call(
        cut_rest_kernel,
        grid_spec=pltpu.PrefetchScalarGridSpec(
            num_scalar_prefetch=1,
            grid=(len(distances),),
            in_specs=[
                pl.BlockSpec((size, units), column_index),
                pl.BlockSpec((size, units), column_index),
                pl.BlockSpec((size, width), row_index),
            ],
            out_specs=pl.BlockSpec((None, size, total), lambda i, f: (i, 0, 0)),
        ),
        out_shape=jax.ShapeDtypeStruct((len(distances), size, total), gate.dtype),
        compiler_params=limits(32),
        cost_estimate=BRIEF,
        name="cut_rest",
    )(flags, gate, up, down)


def cut_out_kernel(flags_ref, mamba_ref, attn_ref, out_ref):
    out_ref[: mamba_ref.shape[0], :] = mamba_ref[...]
    out_ref[mamba_ref.shape[0] :, :] = attn_ref[...]


def cut_out(flags, mamba, attn):
    channels, query = mamba.shape[0] // 4, attn.shape[0] // 4
    width = mamba.shape[1]

    def row_index(i, f):
        return (jnp.bitwise_xor(f[0], distance_at(i, DISTANCES)), 0)

    return pl.pallas_call(
        cut_out_kernel,
        grid_spec=pltpu.PrefetchScalarGridSpec(
            num_scalar_prefetch=1,
            grid=(4,),
            in_specs=[pl.BlockSpec((channels, width), row_index), pl.BlockSpec((query, width), row_index)],
            out_specs=pl.BlockSpec((None, channels + query, width), lambda i, f: (i, 0, 0)),
        ),
        out_shape=jax.ShapeDtypeStruct((4, channels + query, width), mamba.dtype),
        compiler_params=limits(32),
        cost_estimate=BRIEF,
        name="cut_out",
    )(flags, mamba, attn)


def pack_first_kernel(*refs, places):
    pieces, out_ref = refs[:-1], refs[-1]
    query = places.key - places.query
    channels = places.value - places.gate
    head = places.gate - places.key
    total = out_ref.shape[2]

    def place(at, ref, begin, count, to):
        out_ref[at, :, to : to + count] = ref[:, begin : begin + count]

    for at in range(4):
        alone, common = pieces[2 * at], pieces[2 * at + 1]
        place(at, alone, 0, query, places.query)
        place(at, alone, query, channels, places.gate)
        place(at, alone, query + channels, channels, places.conv)
        place(at, alone, query + 2 * channels, total - places.step, places.step)
        place(at, common, 0, head, places.key)
        place(at, common, head, head, places.value)
        place(at, common, 2 * head, places.conv - places.shared, places.shared)


def pack_first(sources, places, total):
    depth, dtype = sources[0][0].shape[1], sources[0][0].dtype
    tiles = 4
    size = depth // tiles
    out = pl.pallas_call(
        partial(pack_first_kernel, places=places),
        grid=(tiles,),
        in_specs=[
            pl.BlockSpec((None, size, v.shape[2]), lambda i, at=at: (at, i, 0)) for v, at in sources
        ],
        out_specs=pl.BlockSpec((4, size, total), lambda i: (0, i, 0)),
        out_shape=jax.ShapeDtypeStruct((4, depth, total), dtype),
        compiler_params=limits(32),
        cost_estimate=BRIEF,
        name="pack_first",
    )(*[v for v, _ in sources])
    return out.reshape(4 * depth, total)


def pack_rest_kernel(mine_ref, far_ref, near_ref, both_ref, in_ref, down_ref):
    width = down_ref.shape[1] // 4
    inner = in_ref.shape[2]
    for at, ref in enumerate((mine_ref, far_ref, near_ref, both_ref)):
        in_ref[at] = ref[:, :inner]
        down_ref[:, at * width : (at + 1) * width] = ref[:, inner : inner + width]


def pack_rest(sources, width):
    _, depth, total = sources[0][0].shape
    dtype = sources[0][0].dtype
    inner = total - width
    tiles = 4
    size = depth // tiles
    into, down = pl.pallas_call(
        pack_rest_kernel,
        grid=(tiles,),
        in_specs=[
            pl.BlockSpec((None, size, total), lambda i, at=at: (at, i, 0)) for _, at in sources
        ],
        out_specs=[
            pl.BlockSpec((4, size, inner), lambda i: (0, i, 0)),
            pl.BlockSpec((size, 4 * width), lambda i: (i, 0)),
        ],
        out_shape=[
            jax.ShapeDtypeStruct((4, depth, inner), dtype),
            jax.ShapeDtypeStruct((depth, 4 * width), dtype),
        ],
        compiler_params=limits(32),
        cost_estimate=BRIEF,
        name="pack_rest",
    )(*[v for v, _ in sources])
    return into.reshape(4 * depth, inner), down


def collect_early_kernel(*refs, places):
    pieces, (out_ref, common_ref) = refs[:4], refs[4:]
    query = places.key - places.query
    key = jnp.zeros((out_ref.shape[1], places.gate - places.key), jnp.float32)
    value = jnp.zeros((out_ref.shape[1], places.shared - places.value), jnp.float32)
    for at, piece in enumerate(pieces):
        out_ref[at, :, :query] = piece[:, : places.key]
        out_ref[at, :, query:] = piece[:, places.gate : places.value]
        key = key + piece[:, places.key : places.gate].astype(jnp.float32)
        value = value + piece[:, places.value :].astype(jnp.float32)
    common_ref[:, : key.shape[1]] = key.astype(common_ref.dtype)
    common_ref[:, key.shape[1] :] = value.astype(common_ref.dtype)


def collect_early(blocks, fetched, passed, places):
    _, depth, count = blocks.shape
    alone = places.key - places.query + places.value - places.gate
    tiles = 2
    size = depth // tiles
    return pl.pallas_call(
        partial(collect_early_kernel, places=places),
        grid=(tiles,),
        in_specs=block_specs(size, count),
        out_specs=[
            pl.BlockSpec((4, size, alone), lambda i: (0, i, 0)),
            pl.BlockSpec((size, count - alone), lambda i: (i, 0)),
        ],
        out_shape=[
            jax.ShapeDtypeStruct((4, depth, alone), blocks.dtype),
            jax.ShapeDtypeStruct((depth, count - alone), blocks.dtype),
        ],
        compiler_params=limits(32),
        cost_estimate=BRIEF,
        name="collect_early",
    )(*block_values(blocks, fetched, passed))


def collect_late_kernel(*refs, shared, channels):
    pieces, (out_ref, step_ref) = refs[:4], refs[4:]
    quarter = shared // 4
    steps = jnp.zeros(step_ref.shape, jnp.float32)
    for at, piece in enumerate(pieces):
        out_ref[at, :, :channels] = piece[:, shared : shared + channels]
        span = slice(at * quarter, (at + 1) * quarter)
        total = jnp.zeros((out_ref.shape[1], quarter), jnp.float32)
        for other in pieces:
            total = total + other[:, span].astype(jnp.float32)
        out_ref[at, :, channels:] = total.astype(out_ref.dtype)
        step = piece[:, shared + channels :].astype(jnp.float32)
        steps = steps + (pltpu.roll(step, at * 8, 1) if at else step)
    step_ref[...] = steps


def collect_late(blocks, fetched, passed, shared, channels):
    _, depth, count = blocks.shape
    tiles = 2
    size = depth // tiles
    return pl.pallas_call(
        partial(collect_late_kernel, shared=shared, channels=channels),
        grid=(tiles,),
        in_specs=block_specs(size, count),
        out_specs=[
            pl.BlockSpec((4, size, channels + shared // 4), lambda i: (0, i, 0)),
            pl.BlockSpec((size, LANES), lambda i: (i, 0)),
        ],
        out_shape=[
            jax.ShapeDtypeStruct((4, depth, channels + shared // 4), blocks.dtype),
            jax.ShapeDtypeStruct((depth, LANES), jnp.float32),
        ],
        compiler_params=limits(32),
        cost_estimate=BRIEF,
        name="collect_late",
    )(*block_values(blocks, fetched, passed))


def slot_of(flags, place):
    distance = jnp.bitwise_xor(flags[0], place)
    return 2 * jnp.bitwise_and(distance, 1) + distance // 2


def finalize_kernel(flags_ref, total_ref, last_ref, *out_refs, cuts):
    values = jnp.where(flags_ref[1] == 1, total_ref[...], last_ref[...])
    for (span, columns), out_ref in zip(cuts, out_refs):
        out_ref[...] = values[span, columns].astype(jnp.float32)


def finalize(flags, total, last, block, index, outs):
    return pl.pallas_call(
        partial(finalize_kernel, cuts=[(rows, columns) for _, _, _, rows, columns in outs]),
        grid_spec=pltpu.PrefetchScalarGridSpec(
            num_scalar_prefetch=1,
            grid=(4,),
            in_specs=[pl.BlockSpec(block, index)] * 2,
            out_specs=[pl.BlockSpec(out_block, out_index) for _, out_block, out_index, _, _ in outs],
        ),
        out_shape=[jax.ShapeDtypeStruct(shape, jnp.float32) for shape, _, _, _, _ in outs],
        compiler_params=limits(32),
        cost_estimate=BRIEF,
        name="finalize",
    )(flags, total, last)


def finalize_blocks_kernel(flags_ref, *refs, cuts):
    pieces, out_refs = refs[:4], refs[4:]
    slot = slot_of(flags_ref, pl.program_id(0))
    for at, piece in enumerate(pieces):

        @pl.when(slot == at)
        def _():
            for (rows, columns), out_ref in zip(cuts, out_refs):
                out_ref[...] = piece[rows, columns].astype(jnp.float32)


def finalize_blocks(flags, blocks, fetched, passed, outs):
    _, rows, columns = blocks.shape
    return pl.pallas_call(
        partial(finalize_blocks_kernel, cuts=[(rows, columns) for _, _, _, rows, columns in outs]),
        grid_spec=pltpu.PrefetchScalarGridSpec(
            num_scalar_prefetch=1,
            grid=(4,),
            in_specs=[
                pl.BlockSpec((None, rows, columns), lambda i, f, at=at: (at, 0, 0)) for at in (0, 0, 0, 1)
            ],
            out_specs=[pl.BlockSpec(out_block, out_index) for _, out_block, out_index, _, _ in outs],
        ),
        out_shape=[jax.ShapeDtypeStruct(shape, jnp.float32) for shape, _, _, _, _ in outs],
        compiler_params=limits(32),
        cost_estimate=BRIEF,
        name="finalize_blocks",
    )(flags, *block_values(blocks, fetched, passed))


def meet_gathered_kernel(flags_ref, *refs):
    meet_kernel(*refs, split=[False] * 4)


def meet_gathered(flags, gathered, weight, other, tiles=4):
    _, tokens, width = gathered.shape
    size = tokens // tiles

    def block_at(distance):
        def index(i, f):
            row = jnp.bitwise_xor(f[2], other)
            return (4 * row + jnp.bitwise_xor(f[0], distance), i, 0)

        return pl.BlockSpec((None, size, width), index)

    model, units = weight.shape[1], weight.shape[0]
    return pl.pallas_call(
        meet_gathered_kernel,
        grid_spec=pltpu.PrefetchScalarGridSpec(
            num_scalar_prefetch=1,
            grid=(tiles,),
            in_specs=[block_at(d) for d in DISTANCES] + [pl.BlockSpec(weight.shape, lambda i, f: (0, 0))],
            out_specs=[
                pl.BlockSpec((size, model), lambda i, f: (i, 0)),
                pl.BlockSpec((size, units), lambda i, f: (i, 0)),
            ],
        ),
        out_shape=[
            jax.ShapeDtypeStruct((tokens, model), jnp.bfloat16),
            jax.ShapeDtypeStruct((tokens, units), jnp.float32),
        ],
        compiler_params=limits(56),
        cost_estimate=BRIEF,
        name="meet_gathered",
    )(flags, *[gathered] * 4, weight)


def on_device(
    tokens,
    cotangent,
    segment_ids,
    norm1_gain,
    proj_gate,
    proj_conv,
    proj_step,
    proj_shared,
    proj_query,
    proj_key,
    proj_value,
    conv_weight,
    conv_bias,
    shared_conv,
    shared_bias,
    step_bias,
    decay_log,
    skip_gain,
    mamba_out_proj,
    attn_out_proj,
    norm2_gain,
    ffn_gate,
    ffn_up,
    ffn_down,
):
    low = jnp.bfloat16
    wide = jnp.float32
    me = lax.axis_index("col")
    row_index = lax.axis_index("row")
    length = segment_ids.shape[1]
    width = tokens.shape[1]
    model = width * len(DISTANCES)
    head_dim = proj_key.shape[1]
    channels = proj_gate.shape[1] // 4
    steps = proj_step.shape[1] // 4
    head_width = channels // steps
    units = ffn_gate.shape[1] // 4
    query_width = proj_query.shape[1] // 4
    part = proj_shared.shape[1]
    at_gate = query_width + head_dim
    at_value = at_gate + channels
    at_shared = at_value + head_dim
    at_conv = at_shared + 2 * part
    at_step = at_conv + channels
    places = Places(0, query_width, at_gate, at_value, at_shared, at_conv, at_step)
    line_place = lax.axis_index("dp")
    share = width // lax.axis_size("dp")
    flags = jnp.stack(
        [me, ((line_place == 1) | (line_place == 2)).astype(me.dtype), row_index, line_place]
    ).astype(jnp.int32)
    firsts = (proj_query, proj_gate, proj_conv, proj_step)
    rests = (ffn_gate, ffn_up, ffn_down)

    def along_line(values):
        return lax.all_gather(values, "dp", axis=1, tiled=True)

    shared_twin = row_swap(proj_shared)
    fetched = col_swap(cut_first(flags, *firsts, DISTANCES[1::2], share, True), 2)
    gains = jnp.stack([norm1_gain, norm2_gain])
    gains_far = col_swap(gains, 2)
    block, shared_twin, fetched, gains_far = together(tokens, shared_twin, fetched, gains_far)
    first = gather_start(block)
    far = along_line(fetched)
    common = jnp.concatenate(
        [
            proj_key, proj_value,
            jnp.where(row_index == 0, proj_shared, shared_twin),
            jnp.where(row_index == 0, shared_twin, proj_shared),
        ],
        axis=1,
    )[None]
    common_far = col_swap(common, 2)
    alone = cut_first(flags, *firsts, DISTANCES[::2], width, False)
    segments = own_first(segment_ids, row_index)
    indices = jnp.arange(length, dtype=jnp.int32)
    same = segments[:, :, None] == segments[:, None, :]
    position = jnp.sum(same & (indices[:, None] > indices[None, :]), axis=2).astype(wide)
    remaining = jnp.sum(same & (indices[:, None] < indices[None, :]), axis=2).astype(wide)
    lane = jnp.arange(LANES)
    info = jnp.where(
        lane == 0,
        segments.astype(wide)[..., None],
        jnp.where(lane == 1, position[..., None], remaining[..., None]),
    )
    row_info = jnp.broadcast_to(segments.astype(wide)[:, None, :], (2, 8, length))
    half_dim = head_dim // 2
    frequency = ROPE_BASE ** (-2.0 * jnp.arange(half_dim, dtype=wide) / head_dim)
    angles = position[..., None] * frequency
    cosine, sine = jnp.cos(angles), jnp.sin(angles)
    cosine = jnp.concatenate([cosine, cosine], axis=2)
    sine = jnp.concatenate([-sine, sine], axis=2)
    head_rows = jnp.pad(
        jnp.stack([step_bias, jnp.exp(decay_log)]), ((0, 6), (0, LANES - steps))
    )
    gain1, gain2 = gains[0:1], gains[1:2]
    params = (
        conv_weight, conv_bias[None], shared_conv, shared_bias[None], head_rows,
        jnp.repeat(skip_gain, head_width)[None],
    )

    both = (0, 1)


    first, common_far, alone, info, row_info, cosine, sine, params = together(
        first, common_far, alone, info, row_info, cosine, sine, params
    )
    middle = gather_middle(block, first)
    gains = jnp.concatenate([gains, gains_far], axis=1)
    gains = jnp.concatenate([gains, col_swap(gains, 1)], axis=1)
    out_blocks = cut_out(flags, mamba_out_proj, attn_out_proj)
    middle, gains, out_blocks = together(middle, gains, out_blocks)
    gain1, gain2 = gains[0:1], gains[1:2]
    out_fetched = far_pair(out_blocks)
    near_common = col_swap(jnp.concatenate([common, common_far], axis=0), 1)
    near = col_swap(alone[1:], 1)
    cot_gathered = lax.all_gather(after(cotangent, middle), ("row", "col"), axis=0)
    token_own, token_other = gather_end(block, first, middle)
    rest_sent = cut_rest(flags, *rests, DISTANCES[1::2], share, True)
    rest_kept = cut_rest(flags, *rests, DISTANCES[::2], width, False)
    far, out_fetched, near_common, near, token_other, rest_sent, rest_kept = together(
        far, out_fetched, near_common, near, token_other, rest_sent, rest_kept
    )
    both_far = col_swap(far[1:], 1)
    out_passed = near_pair(out_blocks, out_fetched)
    both_far, out_passed = together(both_far, out_passed)
    weight_first = pack_first(
        [
            (alone, 0), (common, 0), (far, 0), (common_far, 0),
            (near, 0), (near_common, 0), (both_far, 0), (near_common, 1),
        ],
        places, at_step + LANES,
    )
    rest_sent, rest_kept = after((rest_sent, rest_kept), both_far)
    fetched = col_swap(rest_sent, 2)
    rest_near = col_swap(rest_kept[1:], 1)
    weight_out = jnp.concatenate(
        [out_blocks[0], out_fetched[0], out_passed[0], out_passed[1]], axis=1
    )

    both = (0, 1)
    normed1, factor1, raw, step_raw, mixed, combined, states = [[None, None] for _ in range(7)]

    def project(s, pieces):
        normed1[s], factor1[s], raw[s], step_raw[s] = tiled_call(
            project_kernel, "project", pieces, [(gain1, True), (weight_first, True)],
            [(model, low), (LANES, wide), (at_step, low), (LANES, wide)],
        )
        return attention_forward(raw[s], places, cosine[s], sine[s], info[s], row_info[s])

    def mamba(s, attended):
        mixed[s], combined[s], states[s] = mamba_forward(
            raw[s], places, step_raw[s], info[s], row_info[s], params, attended, head_width
        )

    attended = project(1, token_other)
    attended, fetched, rest_near = together(attended, fetched, rest_near)
    rest_far = along_line(fetched)
    mamba(1, attended)
    near, far = spread([mixed[1]], weight_out, width, False)
    far = col_swap(far, 1)
    near, far, token_own = together(near, far, token_own)
    other, low_got, other_got = other_first(near, far)
    attended = project(0, after(token_own, other))
    attended, low_got, other_got = together(attended, low_got, other_got)
    top_last = other_second(other, other_got)
    mamba(0, attended)
    near, far = spread([mixed[0]], weight_out, width, False)
    far = col_swap(far, 1)
    near, far, top_last = together(near, far, top_last)
    own, own_got, low_last = own_second(near, far, low_got)
    own_got, low_last, rest_far = together(own_got, low_last, rest_far)
    hidden1 = tokens.astype(wide) + own_sum(own, low_got, own_got, top_last, low_last)
    block, hidden1, rest_far = together(hidden1.astype(low), hidden1, rest_far)
    first = gather_start(block)
    rest_both = col_swap(rest_far[1:], 1)
    weight_in, weight_down = pack_rest(
        [(rest_kept, 0), (rest_far, 0), (rest_near, 0), (rest_both, 0)], width
    )
    first, weight_in, weight_down, cot_gathered = together(first, weight_in, weight_down, cot_gathered)
    middle = gather_middle(block, first)
    cot, grad_hidden = [None, None], [None, None]
    for s in both:
        cot[s], grad_hidden[s] = meet_gathered(flags, cot_gathered, weight_down, s)
    middle, cot, grad_hidden = together(middle, cot, grad_hidden)
    pieces = gather_end(block, first, middle)
    normed2, factor2, hidden, grad_in, inner = [[None, None] for _ in range(5)]

    def feed_forward(s, pieces):
        normed2[s], factor2[s], hidden[s], grad_in[s], products = tiled_call(
            ffn_kernel, "ffn", pieces, [(gain2, True), (weight_in, True), (grad_hidden[s], False)],
            [(model, low), (LANES, wide), (units, low), (2 * units, low), (LANES, wide)],
        )
        inner[s] = jnp.sum(products, axis=1).reshape(length // LANES, LANES)

    def piece_index(i, f):
        return (slot_of(f, i), 0, 0)

    def row_index_map(i, f):
        return (i, 0)

    def column_index_map(i, f):
        return (0, i)

    every = slice(None)
    line = LineSums(flags)
    feed_forward(1, pieces[1])
    near, far = spread([grad_in[1]], weight_in, width, True)
    far = col_swap(far, 1)
    feed_forward(0, after(pieces[0], near))
    near, far, hidden, inner, grad_in = together(near, far, hidden, inner, grad_in)
    other, low_got, other_got = other_first(near, far)
    inner_row = row_swap(inner[1])
    near, far = spread([after(grad_in[0], other)], weight_in, width, True)
    far = col_swap(far, 1)
    near, far = together(near, far)
    own = add_low(near, far)
    own_got = col_swap(own[1, : length // 2], 2)
    down = weight_grad(after(hidden, own), cot, width)
    line.advance(down)
    gate = weight_grad(after(normed2, down), grad_in, width, 0, units)
    low_got, other_got, own_got, inner_row, gate = together(low_got, other_got, own_got, inner_row, gate)
    top_last = other_second(other, other_got)
    low_last = col_swap(add_low(own[1, length // 2 :], low_got[1]), 2)
    inner = inner[0] + inner_row
    inner = inner + col_swap(inner, 1)
    up = weight_grad(after(normed2, own_got), grad_in, width, 1, units)
    top_last, low_last, inner, up, line.flying = together(top_last, low_last, inner, up, line.flying)
    line.advance(gate)
    inner = inner + col_swap(inner, 2)
    inner2 = inner.reshape(length, 1)
    grad_normed2 = own_sum(own, low_got, own_got, top_last, low_last)
    own_factor = factor2[0][:, :1]
    back2 = (
        own_factor * norm2_gain * grad_normed2
        - hidden1 * (own_factor * own_factor * inner2 / model)
    )
    grad_gain2 = jnp.sum(grad_normed2 * hidden1 * own_factor, axis=0)
    grad_hidden1 = cotangent.astype(wide) + back2
    block, grad_hidden1, grad_gain2 = together(grad_hidden1.astype(low), grad_hidden1, grad_gain2)
    first = together(*gather_start(block))
    middle = gather_middle(block, first)
    middle, line.flying = together(middle, line.flying)
    line.advance(up)
    pieces = gather_end(block, first, middle)
    mix_grad, grad_mixed = [None, None], [None, None]
    for s in both:
        mix_grad[s], grad_mixed[s] = tiled_call(
            meet_kernel, "meet_mixed", pieces[s], [(weight_out, True)],
            [(model, low), (channels + query_width, low)],
        )
    mix_grad, grad_mixed = together(mix_grad, grad_mixed)
    early, late, sums, products = [[None, None] for _ in range(4)]
    for s in both:
        early[s], products[s] = attention_backward(
            raw[s], places, cosine[s], sine[s], info[s], row_info[s], combined[s], grad_mixed[s]
        )
    first = weight_grad(normed1, after(early, line.sent), width, 0, at_shared)
    out = weight_grad(mixed, after(mix_grad, first), width)
    out, first, early, mix_grad, grad_mixed, line.flying = together(
        out, first, early, mix_grad, grad_mixed, line.flying
    )
    line.advance(out)
    first_far = far_pair(first)

    def mamba_step(s, *earlier):
        late[s], more, sums[s] = mamba_backward(
            raw[s], places, step_raw[s], info[s], row_info[s], params, states[s],
            after(grad_mixed[s], *earlier), head_width,
        )
        inner[s] = jnp.sum(products[s] + more, axis=1).reshape(length // LANES, LANES)

    inner = [None, None]
    mamba_step(1, line.sent)
    late[1], inner[1], first_far, line.flying = together(late[1], inner[1], first_far, line.flying)
    first_near = together(near_pair(first, first_far))[0]
    first, common_sum = collect_early(first, first_far, first_near, places)
    line.advance(first)
    down = chosen(flags, line.done[0])
    down_far = far_pair(down)
    mamba_step(0, late[1], line.sent)
    last = weight_grad(normed1, late, width, 0, late[0].shape[1])
    sums = sums[0] + sums[1]
    sums = jnp.concatenate([sums[:13], grad_gain2[None], jnp.zeros((2, width), wide)], axis=0)
    late, last, inner, sums, down_far, common_sum, line.flying = together(
        late, last, inner, sums, down_far, common_sum, line.flying
    )
    last_far = far_pair(last)
    line.advance()
    rank = jnp.arange(16)[:, None]
    taps = conv_weight.shape[0]
    is_shared = (rank > taps) & (rank < 2 * taps + 2)
    near, far = spread([early[1], after(late[1], line.sent)], weight_first, width, True)
    own_near, own_far = spread([early[0], after(late[0], near)], weight_first, width, True)
    near, far, own_near, own_far, last_far, line.flying = together(
        near, far, own_near, own_far, last_far, line.flying
    )
    last_near, far, own_far = together(near_pair(last, last_far), col_swap(far, 1), col_swap(own_far, 1))
    last, step_sum = collect_late(last, last_far, last_near, 2 * part, channels)
    line.advance(last)
    other, low_got, other_got = other_first(near, far)
    own = add_low(own_near, own_far)
    own_got = col_swap(own[1, : length // 2], 2)
    inner_row, sums_row = row_swap(inner[1]), row_swap(sums)
    low_got, other_got, own_got, inner_row, sums_row = together(low_got, other_got, own_got, inner_row, sums_row)
    top_last = other_second(other, other_got)
    low_last = col_swap(add_low(own[1, length // 2 :], low_got[1]), 2)
    inner = inner[0] + inner_row
    sums = sums + jnp.where(is_shared | (rank >= 13), sums_row, 0.0)
    inner_core, sums_core = col_swap(inner, 1), col_swap(sums, 1)
    output_shares = [spread([after(hidden[s], low_got)], weight_down, width, False) for s in both]
    top_last, low_last, inner_core, sums_core, line.flying, output_shares = together(
        top_last, low_last, inner_core, sums_core, line.flying, output_shares
    )
    line.advance()
    inner = inner + inner_core
    sums = sums + jnp.where(is_shared, sums_core, 0.0)
    inner_far, sums_far = col_swap(inner, 2), col_swap(sums, 2)
    down_near = near_pair(down, down_far)
    gate = chosen(flags, line.done[1])
    gate_far = far_pair(gate)
    inner_far, sums_far, down_near, gate_far = together(inner_far, sums_far, down_near, gate_far)
    inner1 = (inner + inner_far).reshape(length, 1)
    sums = sums + jnp.where(is_shared, sums_far, 0.0)
    grad_normed1 = own_sum(own, low_got, own_got, top_last, low_last)
    own_factor = factor1[0][:, :1]
    own_tokens = tokens.astype(wide)
    back1 = (
        own_factor * norm1_gain * grad_normed1
        - own_tokens * (own_factor * own_factor * inner1 / model)
    )
    grad_gain1 = jnp.sum(grad_normed1 * own_tokens * own_factor, axis=0)
    tokens_grad = (grad_hidden1 + back1).astype(low)
    gate_near = near_pair(gate, gate_far)
    up = chosen(flags, line.done[2])
    up_far = far_pair(up)
    gain_row = row_swap(grad_gain1[None])
    (d_ffn_down,) = finalize_blocks(
        flags, down, down_far, down_near, [(ffn_down.shape, (units, width), row_index_map, every, every)]
    )
    tokens_grad, gate_near, up_far, gain_row, d_ffn_down, line.flying = together(
        tokens_grad, gate_near, up_far, gain_row, d_ffn_down, line.flying
    )
    line.advance()
    up_near = near_pair(up, up_far)
    out = chosen(flags, line.done[3])
    out_far = far_pair(out)
    sums = jnp.concatenate(
        [
            jnp.where(rank == 14, grad_gain1[None] + gain_row, sums),
            jnp.transpose(step_sum)[: 4 * 8],
        ],
        axis=0,
    )
    (d_ffn_gate,) = finalize_blocks(
        flags, gate, gate_far, gate_near,
        [(ffn_gate.shape, (width, units), column_index_map, every, every)],
    )
    total, final = line.done[4]
    alone = query_width + channels
    d_query, d_gate = finalize(
        flags, total, final, (None, width, alone), piece_index,
        [
            (proj_query.shape, (width, query_width), column_index_map, every, slice(0, query_width)),
            (proj_gate.shape, (width, channels), column_index_map, every, slice(query_width, None)),
        ],
    )
    sums = dp_total(sums)
    common_sum = dp_total(common_sum)
    up_near, out_far, sums, common_sum, d_ffn_gate, d_query, d_gate = together(
        up_near, out_far, sums, common_sum, d_ffn_gate, d_query, d_gate
    )
    out_near = near_pair(out, out_far)
    (d_ffn_up,) = finalize_blocks(
        flags, up, up_far, up_near,
        [(ffn_up.shape, (width, units), column_index_map, every, every)],
    )
    d_mamba_out, d_attn_out = finalize_blocks(
        flags, out, out_far, out_near,
        [
            (mamba_out_proj.shape, (channels, width), row_index_map, slice(0, channels), every),
            (attn_out_proj.shape, (query_width, width), row_index_map, slice(channels, None), every),
        ],
    )
    output = (hidden1 + scatter_sum_slow(output_shares)).astype(low)
    line.finish()
    total, final = line.done[5]
    (d_conv,) = finalize(
        flags, total, final, (None, width, channels + part // 2), piece_index,
        [(proj_conv.shape, (width, channels), column_index_map, every, slice(0, channels))],
    )
    shared_sum = jnp.where(flags[1] == 1, total[:, :, channels:], final[:, :, channels:])
    halves = [jnp.concatenate([shared_sum[p], shared_sum[p + 1]], axis=1) for p in (0, 2)]
    kept = jnp.where(row_index == 0, halves[0], halves[1]).astype(wide)
    d_shared = kept + row_swap(jnp.where(row_index == 0, halves[1], halves[0])).astype(wide)
    step_sum = jnp.stack([sums[16 + p * 8 : 16 + p * 8 + steps] for p in (0, 2, 1, 3)])
    d_step = jnp.transpose(
        jnp.concatenate([lax.dynamic_index_in_dim(step_sum, me ^ d, 0, keepdims=False) for d in range(4)])
    )
    d_key = common_sum[:, :head_dim].astype(wide)
    d_value = common_sum[:, head_dim:].astype(wide)
    return (
        output, tokens_grad, sums[14], d_gate, d_conv, d_step, d_shared, d_query, d_key, d_value,
        sums[:taps, :channels], sums[taps, :channels], sums[taps + 1 : 2 * taps + 1],
        sums[2 * taps + 1],
        sums[11, :steps], sums[12, :steps],
        jnp.sum(sums[10, :channels].reshape(steps, head_width), axis=1),
        d_mamba_out, d_attn_out, sums[13], d_ffn_gate, d_ffn_up, d_ffn_down,
    )


def solution(mesh):
    return jax.shard_map(
        on_device,
        mesh=mesh,
        in_specs=(
            P(("dp", "row"), "col"),
            P(("dp", "row"), "col"),
            P("dp", None),
            P("col"),
            P("col", "row"),
            P("col", "row"),
            P("col", "row"),
            P("col", "row"),
            P("col", "row"),
            P("col", "row"),
            P("col", "row"),
            P(None, ("row", "col")),
            P(("row", "col")),
            P(),
            P(),
            P(("row", "col")),
            P(("row", "col")),
            P(("row", "col")),
            P("row", "col"),
            P("row", "col"),
            P("col"),
            P("col", "row"),
            P("col", "row"),
            P("row", "col"),
        ),
        out_specs=(
            P(("dp", "row"), "col"),
            P(("dp", "row"), "col"),
            P("col"),
            P("col", "row"),
            P("col", "row"),
            P("col", "row"),
            P("col", "row"),
            P("col", "row"),
            P("col", "row"),
            P("col", "row"),
            P(None, ("row", "col")),
            P(("row", "col")),
            P(),
            P(),
            P(("row", "col")),
            P(("row", "col")),
            P(("row", "col")),
            P("row", "col"),
            P("row", "col"),
            P("col"),
            P("col", "row"),
            P("col", "row"),
            P("row", "col"),
        ),
        check_vma=False,
    )
```

time: 1410 us -> 1010 us (0.72)
  waiting for transfers between devices: 676 us -> 319 us
  Pallas kernels: 126 us -> 368 us
  matrix products: 174 us -> 0 us
  other arithmetic: 166 us -> 116 us
  local copies, waits for them, and re-layouts: 120 us -> 84.8 us
  starting transfers between devices: 131 us -> 98.7 us
    ppermute x77 -> x69, waiting for transfers between devices: 405 us -> 152 us  [col_swap(): lax.ppermute(values, 'col', [(i, i ^ distance) for i in range(count)])]
    pallas_call x12 -> x45, Pallas kernels: 58.3 us -> 302 us  [the longest x8 71.7 us: spread(): pl.pallas_call(partial(spread_kernel, transposed=transposed), grid=(4,),...]
    dot_general x36 -> x0, matrix products: 174 us -> none  [the longest x12 59.4 us: matmul_right(): lax.dot_general(former, latter, (((1,), (1,)), ((), ())), preferred_eleme...]
    ppermute x15 -> x14, waiting for transfers between devices: 146 us -> 59.3 us  [the longest x8 59.2 us: _start(): move = lax.ppermute(self.sent, 'dp', [(0, 1), (3, 2), (1, 0), (2, 3)])]
    ppermute x2 -> x4, waiting for transfers between devices: 58.9 us -> 16.4 us  [dp_total(): lax.ppermute(values, 'dp', [(i, i ^ distance) for i in range(count)])]
    concatenate x17 -> x8, other arithmetic: 44.2 us -> 7.33 us  [the longest x1 3 us: on_device(): cosine = jnp.concatenate([cosine, cosine], axis=2)]
    dynamic_slice x25 -> x0, local copies, waits for them, and re-layouts: 27.7 us -> none  [the longest x20 21.2 us: in_order(): lax.dynamic_index_in_dim(stacked, index ^ b, 0, keepdims=False)]
    ppermute x2 -> x4, starting transfers between devices: 30.3 us -> 4.59 us  [dp_total(): lax.ppermute(values, 'dp', [(i, i ^ distance) for i in range(count)])]
  transfers between devices with their start and end apart: 115 -> 109, of which waited for: 42 -> 46; matrix products, arithmetic and copies ran while one was open for 27% -> 14% of each run, Pallas kernels for 8% -> 32%
where the time goes in v2:
time: 1010 us; the launch traced here: 1000 us
  Pallas kernels  368 us (36%)
  waiting for transfers between devices  319 us (32%)
  other arithmetic  116 us (11%)
  starting transfers between devices  98.7 us (10%)
  local copies, waits for them, and re-layouts  84.8 us (8%)
  between operations  16.2 us (2%)
    ppermute x69, waiting for transfers between devices, col_swap(): lax.ppermute(values, 'col', [(i, i ^ distance) for i in range(count)])  152 us
    ppermute x19, waiting for transfers between devices, row_swap(): return lax.ppermute(values, 'row', [(0, 1), (1, 0)])  90.6 us
    pallas_call x8, Pallas kernels, spread(): pl.pallas_call(partial(spread_kernel, transposed=transposed), grid=(4,),...  71.7 us
    pallas_call x6, Pallas kernels, tiled_call(): pl.pallas_call(partial(kernel, split=split), grid=(tiles,), in_specs=spec...  64.9 us
    pallas_call x2, Pallas kernels, mamba_backward(): pl.pallas_call(partial(mamba_backward_kernel, head_width=head_width, plac...  61.3 us
    pallas_call x6, Pallas kernels, weight_grad(): pl.pallas_call(weight_grad_kernel, grid=(4,), in_specs=[left, left, right...  59.6 us
    ppermute x8, waiting for transfers between devices, _start(): move = lax.ppermute(self.sent, 'dp', [(0, 1), (3, 2), (1, 0), (2, 3)])  59.2 us
    unnamed x365, local copies, waits for them, and re-layouts  46.1 us
  transfers between devices with their start and end apart: 109, of which 46 were waited for; matrix products, arithmetic and copies ran while one was open for 14% of the time, Pallas kernels for 32%

profile of v2, /device:TPU:0, one launch (start us, length us, event | category | flops | bytes accessed | tf_op | source)
XLA Modules:
  0.0 1002.8 jit_solution(13415968978136818223)
XLA Ops:
  48.3 26.6 %collective-permute-done.6.refs_3_ = bf16[1,512,768]{2,1,0:T(8,128)(2,1)} collective-permute-done((bf16[1,512,768]{2,1,0:T(8,128)(2,1)S(1)}, bf16[1,512,768]{2,1,0:T(8,128)(2,1)}, u32[]{:S(2)}, u32[]{:S(2)}) %collective-permute-start.6) | collective-permute-done | bytes 786464 | tf_op jit(solution)/shard_map/ppermute | solution.py:574
  103.9 17.0 %collective-permute-done.12 = bf16[2,512,512]{2,1,0:T(8,128)(2,1)} collective-permute-done((bf16[2,512,512]{2,1,0:T(8,128)(2,1)}, bf16[2,512,512]{2,1,0:T(8,128)(2,1)}, u32[]{:S(2)}, u32[]{:S(2)}) %collective-permute-start.12) | collective-permute-done | bytes 1048608 | tf_op jit(solution)/shard_map/ppermute | solution.py:574
  139.9 14.3 %project.2 = (bf16[1024,2048]{1,0:T(8,128)(2,1)}, f32[1024,128]{1,0:T(8,128)}, bf16[1024,1664]{1,0:T(8,128)(2,1)}, f32[1024,128]{1,0:T(8,128)}) custom-call(bf16[1024,512]{1,0:T(8,128)(2,1)} %collective-permute-done.4.refs_0_, bf16[512,512]{1,0:T(8,128)(2,1)} %copy-done.147, bf16[512,512]{1,0:T(8,128)(2,1)} %copy-done.146, bf16[1024,512]{1,0:T(8,128)(2,1)} %copy-done.135, ...), custom_call_target="tpu_custom_call" | custom-call | flops 1 | bytes 1 | tf_op jit(solution)/shard_map/project/pallas_call | solution.py:875
  163.7 12.9 %mamba_forward.2 = (bf16[1024,512]{1,0:T(8,128)(2,1)S(1)}, bf16[1024,384]{1,0:T(8,128)(2,1)S(1)}, bf16[8,256,384]{2,1,0:T(8,128)(2,1)S(1)}) custom-call(bf16[1024,1664]{1,0:T(8,128)(2,1)} %get-tuple-element.325.query_ref.key_ref.value_ref.raw_ref.tail_ref, f32[1024,128]{1,0:T(8,128)S(1)} %copy-done.74, f32[1024,128]{1,0:T(8,128)S(1)} %copy-done.21, ...), custom_call_target="tpu_custom_call" | custom-call | flops 1 | bytes 1 | tf_op jit(solution)/shard_map/mamba_forward/pallas_call | solution.py:485
  197.0 13.9 %project.3 = (bf16[1024,2048]{1,0:T(8,128)(2,1)}, f32[1024,128]{1,0:T(8,128)}, bf16[1024,1664]{1,0:T(8,128)(2,1)}, f32[1024,128]{1,0:T(8,128)}) custom-call(bf16[1024,512]{1,0:T(8,128)(2,1)} %refs_0_, bf16[1024,512]{1,0:T(8,128)(2,1)} %collective-permute-done.3.refs_1_, bf16[1024,512]{1,0:T(8,128)(2,1)} %collective-permute-done.5.refs_2_, ...), custom_call_target="tpu_custom_call" | custom-call | flops 1 | bytes 1 | tf_op jit(solution)/shard_map/project/pallas_call | solution.py:875
  219.4 12.4 %mamba_forward.3 = (bf16[1024,512]{1,0:T(8,128)(2,1)S(1)}, bf16[1024,384]{1,0:T(8,128)(2,1)S(1)}, bf16[8,256,384]{2,1,0:T(8,128)(2,1)S(1)}) custom-call(bf16[1024,1664]{1,0:T(8,128)(2,1)} %get-tuple-element.358.query_ref.key_ref.value_ref.raw_ref.tail_ref, f32[1024,128]{1,0:T(8,128)S(1)} %copy-done.72, f32[1024,128]{1,0:T(8,128)S(1)} %copy-done.18, ...), custom_call_target="tpu_custom_call" | custom-call | flops 1 | bytes 1 | tf_op jit(solution)/shard_map/mamba_forward/pallas_call | solution.py:485
  242.7 17.2 %collective-permute-done.25 = bf16[512,512]{1,0:T(8,128)(2,1)S(1)} collective-permute-done((bf16[512,512]{1,0:T(8,128)(2,1)S(1)}, bf16[512,512]{1,0:T(8,128)(2,1)S(1)}, u32[]{:S(2)}, u32[]{:S(2)}) %collective-permute-start.25) | collective-permute-done | bytes 524320 | tf_op jit(solution)/shard_map/ppermute | solution.py:578
  267.8 22.6 %collective-permute-done.26 = bf16[512,512]{1,0:T(8,128)(2,1)} collective-permute-done((bf16[512,512]{1,0:T(8,128)(2,1)}, bf16[512,512]{1,0:T(8,128)(2,1)}, u32[]{:S(2)}, u32[]{:S(2)}) %collective-permute-start.26) | collective-permute-done | bytes 524320 | tf_op jit(solution)/shard_map/ppermute | solution.py:574
  316.3 16.1 %collective-permute-done.29.refs_0_ = bf16[1024,512]{1,0:T(8,128)(2,1)S(1)} collective-permute-done((bf16[1024,512]{1,0:T(8,128)(2,1)S(1)}, bf16[1024,512]{1,0:T(8,128)(2,1)S(1)}, u32[]{:S(2)}, u32[]{:S(2)}) %collective-permute-start.29) | collective-permute-done | bytes 1048608 | tf_op jit(solution)/shard_map/ppermute | solution.py:578
  357.1 11.5 %ffn.2 = (bf16[1024,2048]{1,0:T(8,128)(2,1)}, f32[1024,128]{1,0:T(8,128)}, bf16[1024,512]{1,0:T(8,128)(2,1)}, bf16[1024,1024]{1,0:T(8,128)(2,1)}, f32[1024,128]{1,0:T(8,128)}) custom-call(bf16[1024,512]{1,0:T(8,128)(2,1)} %copy-done.114, bf16[512,512]{1,0:T(8,128)(2,1)} %copy-done.151, bf16[512,512]{1,0:T(8,128)(2,1)} %copy-done.152, ...), custom_call_target="tpu_custom_call" | custom-call | flops 1 | bytes 1 | tf_op jit(solution)/shard_map/ffn/pallas_call | solution.py:875
  377.9 11.2 %ffn.3 = (bf16[1024,2048]{1,0:T(8,128)(2,1)}, f32[1024,128]{1,0:T(8,128)}, bf16[1024,512]{1,0:T(8,128)(2,1)}, bf16[1024,1024]{1,0:T(8,128)(2,1)}, f32[1024,128]{1,0:T(8,128)}) custom-call(bf16[1024,512]{1,0:T(8,128)(2,1)} %copy-done.111, bf16[1024,512]{1,0:T(8,128)(2,1)} %collective-permute-done.28.refs_1_, bf16[1024,512]{1,0:T(8,128)(2,1)} %copy-done.136, ...), custom_call_target="tpu_custom_call" | custom-call | flops 1 | bytes 1 | tf_op jit(solution)/shard_map/ffn/pallas_call | solution.py:875
  480.6 20.3 %collective-permute-done.50.refs_0_ = bf16[1024,512]{1,0:T(8,128)(2,1)S(1)} collective-permute-done((bf16[1024,512]{1,0:T(8,128)(2,1)S(1)}, bf16[1024,512]{1,0:T(8,128)(2,1)S(1)}, u32[]{:S(2)}, u32[]{:S(2)}) %collective-permute-start.50) | collective-permute-done | bytes 1048608 | tf_op jit(solution)/shard_map/ppermute | solution.py:578
  528.9 11.3 %collective-permute-start.60 = (bf16[4,512,512]{2,1,0:T(8,128)(2,1)}, bf16[4,512,512]{2,1,0:T(8,128)(2,1)S(1)}, u32[]{:S(2)}, u32[]{:S(2)}) collective-permute-start(bf16[4,512,512]{2,1,0:T(8,128)(2,1)} %get-tuple-element.466), channel_id=1, source_target_pairs={{0,8},{24,16},{8,0},{16,24},{1,9},{25,17},{9,1},{17,25},{2,10},{26... | collective-permute-start | bytes 6291464 | tf_op jit(solution)/shard_map/ppermute | solution.py:746
  573.1 11.0 %weight_grad.9.refs_0_ = bf16[4,512,768]{2,1,0:T(8,128)(2,1)} custom-call(bf16[1024,2048]{1,0:T(8,128)(2,1)} %get-tuple-element.455.former_0, bf16[1024,2048]{1,0:T(8,128)(2,1)} %get-tuple-element.456.former_1, bf16[1024,768]{1,0:T(8,128)(2,1)} %copy-done.43, bf16[1024,768]{1,0:T(8,128)(2,1)} %copy-done.44), custom_call_target="tpu_custom_call" | custom-call | flops 1 | bytes 1 | tf_op jit(solution)/shard_map/weight_grad/pallas_call | solution.py:902
  605.0 30.7 %mamba_backward.2 = (bf16[1024,1024]{1,0:T(8,128)(2,1)}, f32[1024,128]{1,0:T(8,128)S(1)}, f32[16,512]{1,0:T(8,128)S(1)}) custom-call(bf16[1024,1664]{1,0:T(8,128)(2,1)} %get-tuple-element.325.query_ref.key_ref.value_ref.raw_ref.tail_ref, bf16[1024,1664]{1,0:T(8,128)(2,1)} %get-tuple-element.325.query_ref.key_ref.value_ref.raw_ref.tail_ref, ...), custom_call_target="tpu_custom_call" | custom-call | flops 1 | bytes 1 | tf_op jit(solution)/shard_map/mamba_backward/pallas_call | solution.py:524
  667.7 30.6 %mamba_backward.3 = (bf16[1024,1024]{1,0:T(8,128)(2,1)}, f32[1024,128]{1,0:T(8,128)S(1)}, f32[16,512]{1,0:T(8,128)S(1)}) custom-call(bf16[1024,1664]{1,0:T(8,128)(2,1)} %get-tuple-element.358.query_ref.key_ref.value_ref.raw_ref.tail_ref, bf16[1024,1664]{1,0:T(8,128)(2,1)} %get-tuple-element.358.query_ref.key_ref.value_ref.raw_ref.tail_ref, ...), custom_call_target="tpu_custom_call" | custom-call | flops 1 | bytes 1 | tf_op jit(solution)/shard_map/mamba_backward/pallas_call | solution.py:524
  698.3 13.4 %weight_grad.11.refs_0_ = bf16[4,512,1024]{2,1,0:T(8,128)(2,1)} custom-call(bf16[1024,2048]{1,0:T(8,128)(2,1)} %get-tuple-element.455.former_0, bf16[1024,2048]{1,0:T(8,128)(2,1)} %get-tuple-element.456.former_1, bf16[1024,1024]{1,0:T(8,128)(2,1)} %get-tuple-element.512.latter_0.refs_1_, bf16[1024,1024]{1,0:T(8,128)(2,1)} %get-tuple-element.507.latter_1.refs_1_), custom_call_target="tpu_custom_call" | custom-call | flops 1 | bytes 1 | tf_op jit(solution)/shard_map/weight_grad/pallas_call | solution.py:902
  725.5 13.1 %spread.12 = (bf16[2,1024,512]{2,1,0:T(8,128)(2,1)}, bf16[2,1024,512]{2,1,0:T(8,128)(2,1)}) custom-call(bf16[1024,768]{1,0:T(8,128)(2,1)} %copy-done.44, bf16[1024,1024]{1,0:T(8,128)(2,1)} %get-tuple-element.507.latter_1.refs_1_, bf16[2048,1792]{1,0:T(8,128)(2,1)} %bitcast.149), custom_call_target="tpu_custom_call" | custom-call | flops 1 | bytes 1 | tf_op jit(solution)/shard_map/spread/pallas_call | solution.py:948
  738.6 12.9 %spread.13 = (bf16[2,1024,512]{2,1,0:T(8,128)(2,1)}, bf16[2,1024,512]{2,1,0:T(8,128)(2,1)}) custom-call(bf16[1024,768]{1,0:T(8,128)(2,1)} %copy-done.43, bf16[1024,1024]{1,0:T(8,128)(2,1)} %get-tuple-element.512.latter_0.refs_1_, bf16[2048,1792]{1,0:T(8,128)(2,1)} %bitcast.150), custom_call_target="tpu_custom_call" | custom-call | flops 1 | bytes 1 | tf_op jit(solution)/shard_map/spread/pallas_call | solution.py:948
  751.5 16.1 %collective-permute-done.70 = bf16[4,512,512]{2,1,0:T(8,128)(2,1)} collective-permute-done((bf16[4,512,512]{2,1,0:T(8,128)(2,1)}, bf16[4,512,512]{2,1,0:T(8,128)(2,1)}, u32[]{:S(2)}, u32[]{:S(2)}) %collective-permute-start.70) | collective-permute-done | bytes 2097184 | tf_op jit(solution)/shard_map/ppermute | solution.py:746
  796.3 16.0 %collective-permute-done.78 = f32[8,128]{1,0:T(8,128)S(1)} collective-permute-done((f32[8,128]{1,0:T(8,128)S(1)}, f32[8,128]{1,0:T(8,128)S(1)}, u32[]{:S(2)}, u32[]{:S(2)}) %collective-permute-start.78) | collective-permute-done | bytes 4128 | tf_op jit(solution)/shard_map/ppermute | solution.py:578
  848.3 14.6 %collective-permute-done.92.refs_1_ = bf16[2,512,512]{2,1,0:T(8,128)(2,1)S(1)} collective-permute-done((bf16[2,512,512]{2,1,0:T(8,128)(2,1)}, bf16[2,512,512]{2,1,0:T(8,128)(2,1)S(1)}, u32[]{:S(2)}, u32[]{:S(2)}) %collective-permute-start.92) | collective-permute-done | bytes 1048608 | tf_op jit(solution)/shard_map/ppermute | solution.py:574
  902.6 11.8 %collective-permute-done.102 = bf16[512,256]{1,0:T(8,128)(2,1)S(1)} collective-permute-done((bf16[512,256]{1,0:T(8,128)(2,1)S(1)}, bf16[512,256]{1,0:T(8,128)(2,1)S(1)}, u32[]{:S(2)}, u32[]{:S(2)}) %collective-permute-start.102) | collective-permute-done | bytes 262176 | tf_op jit(solution)/shard_map/ppermute | solution.py:763
  945.4 23.8 %collective-permute-done.103.last_ref = bf16[4,512,512]{2,1,0:T(8,128)(2,1)} collective-permute-done((bf16[4,512,512]{2,1,0:T(8,128)(2,1)}, bf16[4,512,512]{2,1,0:T(8,128)(2,1)}, u32[]{:S(2)}, u32[]{:S(2)}) %collective-permute-start.103) | collective-permute-done | bytes 2097184 | tf_op jit(solution)/shard_map/ppermute | solution.py:746
  (768 shorter events, 585.3 us)
Async XLA Ops:
  7.2 96.7 %all-gather.5.cloned.1.call-start = ((), (), s32[]{:S(2)}) async-start(), calls=%async_computation | async-start | bytes 2621440 | tf_op jit(solution)/shard_map/all_gather | solution.py:1376
  32.0 43.0 %collective-permute-start.5 = (bf16[1024,512]{1,0:T(8,128)(2,1)}, bf16[1024,512]{1,0:T(8,128)(2,1)}, u32[]{:S(2)}, u32[]{:S(2)}) collective-permute-start(bf16[1024,512]{1,0:T(8,128)(2,1)} %refs_0_), channel_id=1, source_target_pairs={{0,1},{1,0},{2,3},{3,2},{4,5},{5,4},{6,7},{7,6},{8,9},{9,8},{10,11... | collective-permute-start | bytes 3145736 | tf_op jit(solution)/shard_map/ppermute | solution.py:574
  32.0 43.0 %collective-permute-start.4 = (bf16[1024,512]{1,0:T(8,128)(2,1)}, bf16[1024,512]{1,0:T(8,128)(2,1)}, u32[]{:S(2)}, u32[]{:S(2)}) collective-permute-start(bf16[1024,512]{1,0:T(8,128)(2,1)} %refs_0_), channel_id=1, source_target_pairs={{0,4},{4,0},{1,5},{5,1},{2,6},{6,2},{3,7},{7,3},{8,12},{12,8},{9,1... | collective-permute-start | bytes 3145736 | tf_op jit(solution)/shard_map/ppermute | solution.py:578
  35.3 232.5 %all-gather.7.cloned.1.call-start = ((), (), s32[]{:S(2)}) async-start(), calls=%async_computation.1 | async-start | bytes 3932160 | tf_op jit(solution)/shard_map/all_gather | solution.py:1376
  159.7 174.0 %all-gather.9.cloned.1.call-start = ((), (), s32[]{:S(2)}) async-start(), calls=%async_computation.2 | async-start | bytes 9437184 | tf_op jit(solution)/shard_map/all_gather | solution.py:1437
  415.6 48.8 %collective-permute-start.47 = (bf16[4,512,512]{2,1,0:T(8,128)(2,1)}, bf16[4,512,512]{2,1,0:T(8,128)(2,1)}, u32[]{:S(2)}, u32[]{:S(2)}) collective-permute-start(bf16[4,512,512]{2,1,0:T(8,128)(2,1)} %weight_grad.6), channel_id=1, source_target_pairs={{0,8},{24,16},{8,0},{16,24},{1,9},{25,17},{9,1},{17,25},{2,10},{26... | collective-permute-start | bytes 6291464 | tf_op jit(solution)/shard_map/ppermute | solution.py:746
  447.9 60.9 %collective-permute-start.56 = (bf16[4,512,512]{2,1,0:T(8,128)(2,1)S(1)}, bf16[4,512,512]{2,1,0:T(8,128)(2,1)}, u32[]{:S(2)}, u32[]{:S(2)}) collective-permute-start(bf16[4,512,512]{2,1,0:T(8,128)(2,1)S(1)} %copy-done.30), channel_id=1, source_target_pairs={{0,8},{24,16},{8,0},{16,24},{1,9},{25,17},{9,1},{17,25},{2,10},{26... | collective-permute-start | bytes 6291464 | tf_op jit(solution)/shard_map/ppermute | solution.py:746
  526.9 65.8 %collective-permute-start.61 = (bf16[4,512,512]{2,1,0:T(8,128)(2,1)}, bf16[4,512,512]{2,1,0:T(8,128)(2,1)}, u32[]{:S(2)}, u32[]{:S(2)}) collective-permute-start(bf16[4,512,512]{2,1,0:T(8,128)(2,1)} %get-tuple-element.471.pair_ref), channel_id=1, source_target_pairs={{8,16},{16,8},{9,17},{17,9},{10,18},{18,10},{11,19},{19,11},{12,20... | collective-permute-start | bytes 6291464 | tf_op jit(solution)/shard_map/ppermute | solution.py:750
  528.9 63.8 %collective-permute-start.60 = (bf16[4,512,512]{2,1,0:T(8,128)(2,1)}, bf16[4,512,512]{2,1,0:T(8,128)(2,1)S(1)}, u32[]{:S(2)}, u32[]{:S(2)}) collective-permute-start(bf16[4,512,512]{2,1,0:T(8,128)(2,1)} %get-tuple-element.466), channel_id=1, source_target_pairs={{0,8},{24,16},{8,0},{16,24},{1,9},{25,17},{9,1},{17,25},{2,10},{26... | collective-permute-start | bytes 6291464 | tf_op jit(solution)/shard_map/ppermute | solution.py:746
  599.6 48.4 %collective-permute-start.63 = (bf16[4,512,512]{2,1,0:T(8,128)(2,1)S(1)}, bf16[4,512,512]{2,1,0:T(8,128)(2,1)S(1)}, u32[]{:S(2)}, u32[]{:S(2)}) collective-permute-start(bf16[4,512,512]{2,1,0:T(8,128)(2,1)S(1)} %get-tuple-element.480), channel_id=1, source_target_pairs={{0,8},{24,16},{8,0},{16,24},{1,9},{25,17},{9,1},{17,25},{2,10},{26... | collective-permute-start | bytes 6291464 | tf_op jit(solution)/shard_map/ppermute | solution.py:746
  656.0 56.0 %collective-permute-start.68 = (bf16[4,512,512]{2,1,0:T(8,128)(2,1)}, bf16[4,512,512]{2,1,0:T(8,128)(2,1)}, u32[]{:S(2)}, u32[]{:S(2)}) collective-permute-start(bf16[4,512,512]{2,1,0:T(8,128)(2,1)} %get-tuple-element.502.pair_ref), channel_id=1, source_target_pairs={{8,16},{16,8},{9,17},{17,9},{10,18},{18,10},{11,19},{19,11},{12,20... | collective-permute-start | bytes 6291464 | tf_op jit(solution)/shard_map/ppermute | solution.py:750
  658.0 54.0 %collective-permute-start.67 = (bf16[4,512,512]{2,1,0:T(8,128)(2,1)}, bf16[4,512,512]{2,1,0:T(8,128)(2,1)}, u32[]{:S(2)}, u32[]{:S(2)}) collective-permute-start(bf16[4,512,512]{2,1,0:T(8,128)(2,1)} %get-tuple-element.492), channel_id=1, source_target_pairs={{0,8},{24,16},{8,0},{16,24},{1,9},{25,17},{9,1},{17,25},{2,10},{26... | collective-permute-start | bytes 6291464 | tf_op jit(solution)/shard_map/ppermute | solution.py:746
  666.4 45.6 %collective-permute-start.66 = (bf16[2,512,512]{2,1,0:T(8,128)(2,1)S(1)}, bf16[2,512,512]{2,1,0:T(8,128)(2,1)S(1)}, u32[]{:S(2)}, u32[]{:S(2)}) collective-permute-start(bf16[2,512,512]{2,1,0:T(8,128)(2,1)S(1)} %pad_maximum_fusion.12), channel_id=1, source_target_pairs={{0,2},{1,3},{2,0},{3,1},{4,6},{5,7},{6,4},{7,5},{8,10},{9,11},{10,... | collective-permute-start | bytes 3145736 | tf_op jit(solution)/shard_map/ppermute | solution.py:574
  719.3 48.3 %collective-permute-start.70 = (bf16[4,512,512]{2,1,0:T(8,128)(2,1)}, bf16[4,512,512]{2,1,0:T(8,128)(2,1)}, u32[]{:S(2)}, u32[]{:S(2)}) collective-permute-start(bf16[4,512,512]{2,1,0:T(8,128)(2,1)} %get-tuple-element.506), channel_id=1, source_target_pairs={{0,8},{24,16},{8,0},{16,24},{1,9},{25,17},{9,1},{17,25},{2,10},{26... | collective-permute-start | bytes 6291464 | tf_op jit(solution)/shard_map/ppermute | solution.py:746
  724.6 47.0 %collective-permute-start.69 = (bf16[2,512,1024]{2,1,0:T(8,128)(2,1)}, bf16[2,512,1024]{2,1,0:T(8,128)(2,1)S(1)}, u32[]{:S(2)}, u32[]{:S(2)}) collective-permute-start(bf16[2,512,1024]{2,1,0:T(8,128)(2,1)} %pad_maximum_fusion.2), channel_id=1, source_target_pairs={{0,2},{1,3},{2,0},{3,1},{4,6},{5,7},{6,4},{7,5},{8,10},{9,11},{10,... | collective-permute-start | bytes 6291464 | tf_op jit(solution)/shard_map/ppermute | solution.py:574
  793.2 47.0 %collective-permute-start.84 = (bf16[4,512,512]{2,1,0:T(8,128)(2,1)}, bf16[4,512,512]{2,1,0:T(8,128)(2,1)S(1)}, u32[]{:S(2)}, u32[]{:S(2)}) collective-permute-start(bf16[4,512,512]{2,1,0:T(8,128)(2,1)} %fusion.5.total_ref), channel_id=1, source_target_pairs={{0,8},{24,16},{8,0},{16,24},{1,9},{25,17},{9,1},{17,25},{2,10},{26... | collective-permute-start | bytes 6291464 | tf_op jit(solution)/shard_map/ppermute | solution.py:746
  840.2 43.8 %collective-permute-start.85 = (bf16[2,1024,512]{2,1,0:T(8,128)(2,1)}, bf16[2,1024,512]{2,1,0:T(8,128)(2,1)}, u32[]{:S(2)}, u32[]{:S(2)}) collective-permute-start(bf16[2,1024,512]{2,1,0:T(8,128)(2,1)} %get-tuple-element.542), channel_id=1, source_target_pairs={{0,1},{1,0},{2,3},{3,2},{4,5},{5,4},{6,7},{7,6},{8,9},{9,8},{10,11... | collective-permute-start | bytes 6291464 | tf_op jit(solution)/shard_map/ppermute | solution.py:574
  842.3 50.2 %collective-permute-start.96 = (bf16[4,512,512]{2,1,0:T(8,128)(2,1)}, bf16[4,512,512]{2,1,0:T(8,128)(2,1)}, u32[]{:S(2)}, u32[]{:S(2)}) collective-permute-start(bf16[4,512,512]{2,1,0:T(8,128)(2,1)} %add_convert_fusion.1), channel_id=1, source_target_pairs={{8,16},{16,8},{9,17},{17,9},{10,18},{18,10},{11,19},{19,11},{12,20... | collective-permute-start | bytes 6291464 | tf_op jit(solution)/shard_map/ppermute | solution.py:750
  890.7 43.6 %collective-permute-start.98 = (bf16[2,512,512]{2,1,0:T(8,128)(2,1)}, bf16[2,512,512]{2,1,0:T(8,128)(2,1)}, u32[]{:S(2)}, u32[]{:S(2)}) collective-permute-start(bf16[2,512,512]{2,1,0:T(8,128)(2,1)} %pad_maximum_fusion.18), channel_id=1, source_target_pairs={{0,2},{1,3},{2,0},{3,1},{4,6},{5,7},{6,4},{7,5},{8,10},{9,11},{10,... | collective-permute-start | bytes 3145736 | tf_op jit(solution)/shard_map/ppermute | solution.py:574
  891.5 46.9 %collective-permute-start.87 = (bf16[2,1024,512]{2,1,0:T(8,128)(2,1)}, bf16[2,1024,512]{2,1,0:T(8,128)(2,1)}, u32[]{:S(2)}, u32[]{:S(2)}) collective-permute-start(bf16[2,1024,512]{2,1,0:T(8,128)(2,1)} %get-tuple-element.543), channel_id=1, source_target_pairs={{0,1},{1,0},{2,3},{3,2},{4,5},{5,4},{6,7},{7,6},{8,9},{9,8},{10,11... | collective-permute-start | bytes 6291464 | tf_op jit(solution)/shard_map/ppermute | solution.py:574
  891.5 48.4 %collective-permute-start.86 = (bf16[2,1024,512]{2,1,0:T(8,128)(2,1)}, bf16[2,1024,512]{2,1,0:T(8,128)(2,1)}, u32[]{:S(2)}, u32[]{:S(2)}) collective-permute-start(bf16[2,1024,512]{2,1,0:T(8,128)(2,1)} %add_convert_fusion.2), channel_id=1, source_target_pairs={{0,4},{4,0},{1,5},{5,1},{2,6},{6,2},{3,7},{7,3},{8,12},{12,8},{9,1... | collective-permute-start | bytes 6291464 | tf_op jit(solution)/shard_map/ppermute | solution.py:578
  922.1 47.1 %collective-permute-start.103 = (bf16[4,512,512]{2,1,0:T(8,128)(2,1)}, bf16[4,512,512]{2,1,0:T(8,128)(2,1)}, u32[]{:S(2)}, u32[]{:S(2)}) collective-permute-start(bf16[4,512,512]{2,1,0:T(8,128)(2,1)} %add_convert_fusion.total_ref), channel_id=1, source_target_pairs={{0,8},{24,16},{8,0},{16,24},{1,9},{25,17},{9,1},{17,25},{2,10},{26... | collective-permute-start | bytes 6291464 | tf_op jit(solution)/shard_map/ppermute | solution.py:746
  936.6 49.9 %collective-permute-start.105 = (bf16[2,512,512]{2,1,0:T(8,128)(2,1)}, bf16[2,512,512]{2,1,0:T(8,128)(2,1)}, u32[]{:S(2)}, u32[]{:S(2)}) collective-permute-start(bf16[2,512,512]{2,1,0:T(8,128)(2,1)} %pad_maximum_fusion.19), channel_id=1, source_target_pairs={{0,1},{1,0},{2,3},{3,2},{4,5},{5,4},{6,7},{7,6},{8,9},{9,8},{10,11... | collective-permute-start | bytes 3145736 | tf_op jit(solution)/shard_map/ppermute | solution.py:574
  944.2 48.9 %collective-permute-start.88 = (bf16[1024,512]{1,0:T(8,128)(2,1)}, bf16[1024,512]{1,0:T(8,128)(2,1)}, u32[]{:S(2)}, u32[]{:S(2)}) collective-permute-start(bf16[1024,512]{1,0:T(8,128)(2,1)} %fusion.9), channel_id=1, source_target_pairs={{0,2},{1,3},{2,0},{3,1},{4,6},{5,7},{6,4},{7,5},{8,10},{9,11},{10,... | collective-permute-start | bytes 3145736 | tf_op jit(solution)/shard_map/ppermute | solution.py:574
  (268 other events, 2971.5 us)
Sparse Core Ops, SparseCore 0:
  35.4 46.2 all-gather.4
  159.9 63.9 all-gather.6
  225.8 64.5 all-gather.8

commit v3 on v2

--- a/solution.py
+++ b/solution.py
@@ -615,43 +615,150 @@
     return [block, along_x, core, core_x], [along_y, diagonal, core_y, col_swap(diagonal, 1)]
 
 
+def add_kernel(former_ref, latter_ref, out_ref):
+    total = former_ref[...].astype(jnp.float32) + latter_ref[...].astype(jnp.float32)
+    out_ref[...] = total.astype(out_ref.dtype)
+
+
 def add_low(former, latter):
-    return (former.astype(jnp.float32) + latter.astype(jnp.float32)).astype(jnp.bfloat16)
-
-
-def other_first(near, far_core):
-    other = add_low(near, far_core)
-    half = other.shape[1] // 2
-    return other, row_swap(other[:, half:]), col_swap(other[1, :half], 2)
-
-
-def other_second(other, other_got):
-    half = other.shape[1] // 2
-    return row_swap(add_low(other[0, :half], other_got))
-
-
-def own_second(near, far_core, low_got):
-    own = add_low(near, far_core)
-    half = own.shape[1] // 2
-    return own, col_swap(own[1, :half], 2), col_swap(add_low(own[1, half:], low_got[1]), 2)
+    shape = former.shape
+    tiles = shape[0] if len(shape) == 3 else 2
+    block = (1, *shape[1:]) if len(shape) == 3 else (shape[0] // tiles, shape[1])
+    spec = pl.BlockSpec(block, lambda i: (i,) + (0,) * (len(shape) - 1))
+    return pl.pallas_call(
+        add_kernel,
+        grid=(tiles,),
+        in_specs=[spec, spec],
+        out_specs=spec,
+        out_shape=jax.ShapeDtypeStruct(shape, jnp.bfloat16),
+        compiler_params=limits(32),
+        cost_estimate=BRIEF,
+        name="add",
+    )(former, latter)
+
+
+def add_three_kernel(first_ref, second_ref, third_ref, out_ref):
+    wide = jnp.float32
+    total = first_ref[...].astype(wide) + second_ref[...].astype(wide) + third_ref[...].astype(wide)
+    out_ref[...] = total.astype(out_ref.dtype)
+
+
+def add_three(first, second, third, at):
+    _, rows, columns = first.shape
+    tiles = 2
+    spec = pl.BlockSpec((None, rows // tiles, columns), lambda i: (at, i, 0))
+    return pl.pallas_call(
+        add_three_kernel,
+        grid=(tiles,),
+        in_specs=[spec] * 3,
+        out_specs=pl.BlockSpec((rows // tiles, columns), lambda i: (i, 0)),
+        out_shape=jax.ShapeDtypeStruct((rows, columns), jnp.bfloat16),
+        compiler_params=limits(32),
+        cost_estimate=BRIEF,
+        name="add_three",
+    )(first, second, third)
+
+
+def sum_quarters_kernel(base_ref, *refs):
+    (*parts, out_ref, low_ref) = refs
+    tops, lows = parts[:3], parts[3:]
+    wide = jnp.float32
+
+    def write(pieces):
+        total = base_ref[...].astype(wide)
+        for piece in pieces:
+            total = total + piece[...].astype(wide)
+        out_ref[...] = total
+        low_ref[...] = total.astype(low_ref.dtype)
+
+    @pl.when(pl.program_id(0) == 0)
+    def _():
+        write(tops)
+
+    @pl.when(pl.program_id(0) == 1)
+    def _():
+        write(lows)
+
+
+def sum_quarters(base, own, low_got, own_got, top_last, low_last):
+    tokens, width = base.shape
+    half = tokens // 2
+    row = pl.BlockSpec((half, width), lambda i: (i, 0))
+    part = pl.BlockSpec((half, width), lambda i: (0, 0))
+    first = pl.BlockSpec((None, half, width), lambda i: (0, 0, 0))
+    return pl.pallas_call(
+        sum_quarters_kernel,
+        grid=(2,),
+        in_specs=[row, part, part, part, part, first, part],
+        out_specs=[row, row],
+        out_shape=[
+            jax.ShapeDtypeStruct((tokens, width), jnp.float32),
+            jax.ShapeDtypeStruct((tokens, width), jnp.bfloat16),
+        ],
+        compiler_params=limits(32),
+        cost_estimate=BRIEF,
+        name="sum_quarters",
+    )(base, own[0], own_got, top_last, own[2], low_got, low_last)
+
+
+def fold_other_kernel(near_ref, far_ref, top_near_ref, top_far_ref, low_ref):
+    half = low_ref.shape[0]
+    total = (near_ref[...].astype(jnp.float32) + far_ref[...].astype(jnp.float32)).astype(low_ref.dtype)
+    low_ref[...] = total[half:]
+
+    @pl.when(pl.program_id(0) == 0)
+    def _():
+        top_near_ref[...] = total[:half]
+
+    @pl.when(pl.program_id(0) == 1)
+    def _():
+        top_far_ref[...] = total[:half]
+
+
+def fold_own_kernel(near_ref, far_ref, top_near_ref, top_far_ref, low_near_ref, low_far_ref):
+    half = top_near_ref.shape[0]
+    total = (near_ref[...].astype(jnp.float32) + far_ref[...].astype(jnp.float32)).astype(top_near_ref.dtype)
+
+    @pl.when(pl.program_id(0) == 0)
+    def _():
+        top_near_ref[...] = total[:half]
+        low_near_ref[...] = total[half:]
+
+    @pl.when(pl.program_id(0) == 1)
+    def _():
+        top_far_ref[...] = total[:half]
+        low_far_ref[...] = total[half:]
+
+
+def fold(near, far, is_own):
+    _, tokens, width = near.shape
+    half = tokens // 2
+    share = pl.BlockSpec((None, tokens, width), lambda i: (i, 0, 0))
+    quarter = pl.BlockSpec((half, width), lambda i: (0, 0))
+    shape = jax.ShapeDtypeStruct((half, width), near.dtype)
+    if is_own:
+        specs, shapes = [quarter] * 4, [shape] * 4
+    else:
+        specs = [quarter, quarter, pl.BlockSpec((None, half, width), lambda i: (i, 0, 0))]
+        shapes = [shape, shape, jax.ShapeDtypeStruct((2, half, width), near.dtype)]
+    return pl.pallas_call(
+        fold_own_kernel if is_own else fold_other_kernel,
+        grid=(2,),
+        in_specs=[share, share],
+        out_specs=specs,
+        out_shape=shapes,
+        compiler_params=limits(32),
+        cost_estimate=BRIEF,
+        name="fold",
+    )(near, far)
 
 
 def own_sum(own, low_got, own_got, top_last, low_last):
-    half = own.shape[1] // 2
+    top_near, _, low_near, _ = own
     wide = jnp.float32
-    top = own[0, :half].astype(wide) + own_got.astype(wide) + top_last.astype(wide)
-    low = own[0, half:].astype(wide) + low_got[0].astype(wide) + low_last.astype(wide)
+    top = top_near.astype(wide) + own_got.astype(wide) + top_last.astype(wide)
+    low = low_near.astype(wide) + low_got[0].astype(wide) + low_last.astype(wide)
     return jnp.concatenate([top, low], axis=0)
-
-
-def scatter_sum_slow(shares):
-    (own, own_far), (other, other_far) = shares
-    wide = jnp.float32
-    other = add_low(other, col_swap(other_far, 1))
-    got, near = lax.optimization_barrier((row_swap(other), col_swap(own_far, 1)))
-    total = own.astype(wide) + near.astype(wide) + got.astype(wide)
-    last = col_swap(total[1].astype(jnp.bfloat16), 2)
-    return total[0] + last.astype(wide)
 
 
 def token_total(own, other):
@@ -750,27 +857,186 @@
             self.flying = (move, lax.ppermute(self.pair, "dp", [(1, 2), (2, 1)]))
 
 
-def chosen(flags, pair):
-    return jnp.where(flags[1] == 1, pair[0], pair[1])
-
-
-def dp_total(values):
+def dp_part(values, distance):
     count = lax.axis_size("dp")
-    if count & (count - 1):
-        return lax.psum(values, "dp")
-    distance = 1
-    while distance < count:
-        values = values + lax.ppermute(values, "dp", [(i, i ^ distance) for i in range(count)])
+    return lax.ppermute(values, "dp", [(i, i ^ distance) for i in range(count)])
+
+
+def dp_rest(values):
+    distance = 2
+    while distance < lax.axis_size("dp"):
+        values = values + dp_part(values, distance)
         distance *= 2
     return values
 
 
+def pick_kernel(*refs, count):
+    out_ref = refs[-1]
+    for at in range(count):
+
+        @pl.when(pl.program_id(0) == at)
+        def _():
+            out_ref[...] = refs[at][...]
+
+
+def pick(sources):
+    rows, columns = sources[0][0].shape[1:]
+    return pl.pallas_call(
+        partial(pick_kernel, count=len(sources)),
+        grid=(len(sources),),
+        in_specs=[pl.BlockSpec((None, rows, columns), lambda i, at=at: (at, 0, 0)) for _, at in sources],
+        out_specs=pl.BlockSpec((None, rows, columns), lambda i: (i, 0, 0)),
+        out_shape=jax.ShapeDtypeStruct((len(sources), rows, columns), sources[0][0].dtype),
+        compiler_params=limits(32),
+        cost_estimate=BRIEF,
+        name="pick",
+    )(*[array for array, _ in sources])
+
+
+def pick_at_kernel(flags_ref, in_ref, out_ref):
+    out_ref[...] = in_ref[...]
+
+
+def pick_at(flags, values, distance, tiles=2):
+    _, rows, columns = values.shape
+    size = rows // tiles
+    return pl.pallas_call(
+        pick_at_kernel,
+        grid_spec=pltpu.PrefetchScalarGridSpec(
+            num_scalar_prefetch=1,
+            grid=(tiles,),
+            in_specs=[
+                pl.BlockSpec((None, size, columns), lambda i, f: (jnp.bitwise_xor(f[0], distance), i, 0))
+            ],
+            out_specs=pl.BlockSpec((size, columns), lambda i, f: (i, 0)),
+        ),
+        out_shape=jax.ShapeDtypeStruct((rows, columns), values.dtype),
+        compiler_params=limits(32),
+        cost_estimate=BRIEF,
+        name="pick_at",
+    )(flags, values)
+
+
+def choose_kernel(flags_ref, middle_ref, end_ref, out_ref):
+    @pl.when(flags_ref[1] == 1)
+    def _():
+        out_ref[...] = middle_ref[...]
+
+    @pl.when(flags_ref[1] == 0)
+    def _():
+        out_ref[...] = end_ref[...]
+
+
+def chosen(flags, pair):
+    middle, end = pair
+    block = (None, *middle.shape[1:])
+    return pl.pallas_call(
+        choose_kernel,
+        grid_spec=pltpu.PrefetchScalarGridSpec(
+            num_scalar_prefetch=1,
+            grid=(middle.shape[0],),
+            in_specs=[
+                pl.BlockSpec(block, lambda i, f: (i * f[1], 0, 0)),
+                pl.BlockSpec(block, lambda i, f: (i * (1 - f[1]), 0, 0)),
+            ],
+            out_specs=pl.BlockSpec(block, lambda i, f: (i, 0, 0)),
+        ),
+        out_shape=jax.ShapeDtypeStruct(middle.shape, middle.dtype),
+        compiler_params=limits(32),
+        cost_estimate=BRIEF,
+        name="choose",
+    )(flags, middle, end)
+
+
+def pick_chosen_kernel(flags_ref, middle_ref, end_ref, out_ref):
+    choose_kernel(flags_ref, middle_ref, end_ref, out_ref)
+
+
+def pick_chosen(flags, pair, places):
+    middle, end = pair
+    block = (None, *middle.shape[1:])
+    return pl.pallas_call(
+        pick_chosen_kernel,
+        grid_spec=pltpu.PrefetchScalarGridSpec(
+            num_scalar_prefetch=1,
+            grid=(len(places),),
+            in_specs=[
+                pl.BlockSpec(block, lambda i, f: (distance_at(i, places) * f[1], 0, 0)),
+                pl.BlockSpec(block, lambda i, f: (distance_at(i, places) * (1 - f[1]), 0, 0)),
+            ],
+            out_specs=pl.BlockSpec(block, lambda i, f: (i, 0, 0)),
+        ),
+        out_shape=jax.ShapeDtypeStruct((len(places), *middle.shape[1:]), middle.dtype),
+        compiler_params=limits(32),
+        cost_estimate=BRIEF,
+        name="pick_chosen",
+    )(flags, middle, end)
+
+
+def near_of_sum(flags, pair, fetched):
+    kept = pick_chosen(flags, pair, (2,))
+    return col_swap(pick([(kept, 0), (fetched, 1)]), 1)
+
+
 def far_pair(blocks):
-    return col_swap(jnp.stack([blocks[1], blocks[3]]), 2)
+    return col_swap(pick([(blocks, 1), (blocks, 3)]), 2)
 
 
 def near_pair(blocks, fetched):
-    return col_swap(jnp.stack([blocks[2], fetched[1]]), 1)
+    return col_swap(pick([(blocks, 2), (fetched, 1)]), 1)
+
+
+def halves_kernel(flags_ref, in_ref, keep_ref, send_ref):
+    part = keep_ref.shape[1]
+
+    @pl.when(flags_ref[2] == 0)
+    def _():
+        keep_ref[...] = in_ref[:, :part]
+        send_ref[...] = in_ref[:, part:]
+
+    @pl.when(flags_ref[2] == 1)
+    def _():
+        keep_ref[...] = in_ref[:, part:]
+        send_ref[...] = in_ref[:, :part]
+
+
+def row_halves(flags, blocks):
+    count, rows, columns = blocks.shape
+    half = pl.BlockSpec((None, rows, columns // 2), lambda i, f: (i, 0, 0))
+    return pl.pallas_call(
+        halves_kernel,
+        grid_spec=pltpu.PrefetchScalarGridSpec(
+            num_scalar_prefetch=1,
+            grid=(count,),
+            in_specs=[pl.BlockSpec((None, rows, columns), lambda i, f: (i, 0, 0))],
+            out_specs=[half, half],
+        ),
+        out_shape=[jax.ShapeDtypeStruct((count, rows, columns // 2), blocks.dtype)] * 2,
+        compiler_params=limits(32),
+        cost_estimate=BRIEF,
+        name="row_halves",
+    )(flags, blocks)
+
+
+def pack_out_kernel(mine_ref, far_ref, near_ref, both_ref, out_ref):
+    width = mine_ref.shape[1]
+    for at, ref in enumerate((mine_ref, far_ref, near_ref, both_ref)):
+        out_ref[:, at * width : (at + 1) * width] = ref[...]
+
+
+def pack_out(blocks, fetched, passed):
+    _, depth, width = blocks.shape
+    tiles = 2
+    return pl.pallas_call(
+        pack_out_kernel,
+        grid=(tiles,),
+        in_specs=block_specs(depth // tiles, width),
+        out_specs=pl.BlockSpec((depth // tiles, 4 * width), lambda i: (i, 0)),
+        out_shape=jax.ShapeDtypeStruct((depth, 4 * width), blocks.dtype),
+        compiler_params=limits(32),
+        cost_estimate=BRIEF,
+        name="pack_out",
+    )(*block_values(blocks, fetched, passed))
 
 
 def block_specs(size, count):
@@ -884,31 +1150,35 @@
     )(*values)
 
 
-def weight_grad_kernel(former_0, former_1, latter_0, latter_1, out_ref):
+def weight_grad_kernel(former_0, former_1, latter_0, latter_1, *out_refs):
     total = tn(former_0[...], latter_0[...]) + tn(former_1[...], latter_1[...])
-    out_ref[...] = total.astype(out_ref.dtype)
-
-
-def weight_grad(former, latter, width, at=0, count=None):
+    at = 0
+    for out_ref in out_refs:
+        out_ref[...] = total[:, at : at + out_ref.shape[1]].astype(out_ref.dtype)
+        at += out_ref.shape[1]
+
+
+def weight_grad(former, latter, width, at=0, counts=None):
     length, depth = former[0].shape
-    if count is None:
+    if counts is None:
         left = pl.BlockSpec((length, depth), lambda i: (0, 0))
         right = pl.BlockSpec((length, width), lambda i: (0, i))
-        shape = (4, depth, width)
+        shapes = [(4, depth, width)]
     else:
         left = pl.BlockSpec((length, width), lambda i: (0, i))
-        right = pl.BlockSpec((length, count), lambda i: (0, at))
-        shape = (4, width, count)
-    return pl.pallas_call(
+        right = pl.BlockSpec((length, sum(counts)), lambda i: (0, at))
+        shapes = [(4, width, count) for count in counts]
+    out = pl.pallas_call(
         weight_grad_kernel,
         grid=(4,),
         in_specs=[left, left, right, right],
-        out_specs=pl.BlockSpec((None, *shape[1:]), lambda i: (i, 0, 0)),
-        out_shape=jax.ShapeDtypeStruct(shape, jnp.bfloat16),
+        out_specs=[pl.BlockSpec((None, *shape[1:]), lambda i: (i, 0, 0)) for shape in shapes],
+        out_shape=[jax.ShapeDtypeStruct(shape, jnp.bfloat16) for shape in shapes],
         compiler_params=limits(56),
         cost_estimate=BRIEF,
         name="weight_grad",
     )(*former, *latter)
+    return out[0] if len(out) == 1 else out
 
 
 def spread_kernel(*refs, transposed):
@@ -1074,7 +1344,7 @@
     )(flags, mamba, attn)
 
 
-def pack_first_kernel(*refs, places):
+def pack_first_kernel(*refs, places, begins):
     pieces, out_ref = refs[:-1], refs[-1]
     query = places.key - places.query
     channels = places.value - places.gate
@@ -1086,13 +1356,14 @@
 
     for at in range(4):
         alone, common = pieces[2 * at], pieces[2 * at + 1]
+        begin = begins[2 * at + 1]
         place(at, alone, 0, query, places.query)
         place(at, alone, query, channels, places.gate)
         place(at, alone, query + channels, channels, places.conv)
         place(at, alone, query + 2 * channels, total - places.step, places.step)
-        place(at, common, 0, head, places.key)
-        place(at, common, head, head, places.value)
-        place(at, common, 2 * head, places.conv - places.shared, places.shared)
+        place(at, common, begin, head, places.key)
+        place(at, common, begin + head, head, places.value)
+        place(at, common, begin + 2 * head, places.conv - places.shared, places.shared)
 
 
 def pack_first(sources, places, total):
@@ -1100,17 +1371,17 @@
     tiles = 4
     size = depth // tiles
     out = pl.pallas_call(
-        partial(pack_first_kernel, places=places),
+        partial(pack_first_kernel, places=places, begins=[begin for _, _, begin in sources]),
         grid=(tiles,),
         in_specs=[
-            pl.BlockSpec((None, size, v.shape[2]), lambda i, at=at: (at, i, 0)) for v, at in sources
+            pl.BlockSpec((None, size, v.shape[2]), lambda i, at=at: (at, i, 0)) for v, at, _ in sources
         ],
         out_specs=pl.BlockSpec((4, size, total), lambda i: (0, i, 0)),
         out_shape=jax.ShapeDtypeStruct((4, depth, total), dtype),
-        compiler_params=limits(32),
+        compiler_params=limits(48),
         cost_estimate=BRIEF,
         name="pack_first",
-    )(*[v for v, _ in sources])
+    )(*[v for v, _, _ in sources])
     return out.reshape(4 * depth, total)
 
 
@@ -1186,42 +1457,48 @@
     )(*block_values(blocks, fetched, passed))
 
 
-def collect_late_kernel(*refs, shared, channels):
-    pieces, (out_ref, step_ref) = refs[:4], refs[4:]
-    quarter = shared // 4
-    steps = jnp.zeros(step_ref.shape, jnp.float32)
-    for at, piece in enumerate(pieces):
-        out_ref[at, :, :channels] = piece[:, shared : shared + channels]
+def collect_late_kernel(*refs, channels):
+    alone, shared, (common_ref, out_ref, step_ref) = refs[:4], refs[4:8], refs[8:]
+    quarter = out_ref.shape[2] - channels
+    wide = jnp.float32
+    steps = jnp.zeros(step_ref.shape, wide)
+    total = jnp.zeros((out_ref.shape[1], shared[0].shape[1]), wide)
+    for at, piece in enumerate(alone):
+        out_ref[at, :, :channels] = piece[:, :channels]
+        step = piece[:, channels:].astype(wide)
+        steps = steps + (pltpu.roll(step, at * 8, 1) if at else step)
+        total = total + shared[at][...].astype(wide)
+    step_ref[...] = steps
+    for at in range(2):
         span = slice(at * quarter, (at + 1) * quarter)
-        total = jnp.zeros((out_ref.shape[1], quarter), jnp.float32)
-        for other in pieces:
-            total = total + other[:, span].astype(jnp.float32)
-        out_ref[at, :, channels:] = total.astype(out_ref.dtype)
-        step = piece[:, shared + channels :].astype(jnp.float32)
-        steps = steps + (pltpu.roll(step, at * 8, 1) if at else step)
-    step_ref[...] = steps
-
-
-def collect_late(blocks, fetched, passed, shared, channels):
-    _, depth, count = blocks.shape
+        out_ref[at, :, channels:] = total[:, span].astype(out_ref.dtype)
+        out_ref[at + 2, :, channels:] = common_ref[:, span]
+
+
+def collect_late(alone, shared, common, channels):
+    _, depth, count = alone[0].shape
+    part = shared[0].shape[2]
     tiles = 2
     size = depth // tiles
     return pl.pallas_call(
-        partial(collect_late_kernel, shared=shared, channels=channels),
+        partial(collect_late_kernel, channels=channels),
         grid=(tiles,),
-        in_specs=block_specs(size, count),
+        in_specs=[
+            *block_specs(size, count), *block_specs(size, part),
+            pl.BlockSpec((size, common.shape[1]), lambda i: (i, 0)),
+        ],
         out_specs=[
-            pl.BlockSpec((4, size, channels + shared // 4), lambda i: (0, i, 0)),
+            pl.BlockSpec((4, size, channels + part // 2), lambda i: (0, i, 0)),
             pl.BlockSpec((size, LANES), lambda i: (i, 0)),
         ],
         out_shape=[
-            jax.ShapeDtypeStruct((4, depth, channels + shared // 4), blocks.dtype),
+            jax.ShapeDtypeStruct((4, depth, channels + part // 2), alone[0].dtype),
             jax.ShapeDtypeStruct((depth, LANES), jnp.float32),
         ],
         compiler_params=limits(32),
         cost_estimate=BRIEF,
         name="collect_late",
-    )(*block_values(blocks, fetched, passed))
+    )(*block_values(*alone), *block_values(*shared), common)
 
 
 def slot_of(flags, place):
@@ -1285,16 +1562,12 @@
     meet_kernel(*refs, split=[False] * 4)
 
 
-def meet_gathered(flags, gathered, weight, other, tiles=4):
+def meet_gathered(flags, gathered, weight, tiles=4):
     _, tokens, width = gathered.shape
     size = tokens // tiles
 
     def block_at(distance):
-        def index(i, f):
-            row = jnp.bitwise_xor(f[2], other)
-            return (4 * row + jnp.bitwise_xor(f[0], distance), i, 0)
-
-        return pl.BlockSpec((None, size, width), index)
+        return pl.BlockSpec((None, size, width), lambda i, f: (jnp.bitwise_xor(f[0], distance), i, 0))
 
     model, units = weight.shape[1], weight.shape[0]
     return pl.pallas_call(
@@ -1390,8 +1663,10 @@
         ],
         axis=1,
     )[None]
+    alone = cut_first(flags, *firsts, DISTANCES[::2], width, False)
+    lone = alone.shape[2]
+    near = col_swap(jnp.concatenate([alone[1:], common], axis=2), 1)
     common_far = col_swap(common, 2)
-    alone = cut_first(flags, *firsts, DISTANCES[::2], width, False)
     segments = own_first(segment_ids, row_index)
     indices = jnp.arange(length, dtype=jnp.int32)
     same = segments[:, :, None] == segments[:, None, :]
@@ -1422,40 +1697,29 @@
     both = (0, 1)
 
 
-    first, common_far, alone, info, row_info, cosine, sine, params = together(
-        first, common_far, alone, info, row_info, cosine, sine, params
+    first, near, alone, info, row_info, cosine, sine, params = together(
+        first, near, alone, info, row_info, cosine, sine, params
     )
     middle = gather_middle(block, first)
     gains = jnp.concatenate([gains, gains_far], axis=1)
-    gains = jnp.concatenate([gains, col_swap(gains, 1)], axis=1)
     out_blocks = cut_out(flags, mamba_out_proj, attn_out_proj)
-    middle, gains, out_blocks = together(middle, gains, out_blocks)
-    gain1, gain2 = gains[0:1], gains[1:2]
-    out_fetched = far_pair(out_blocks)
-    near_common = col_swap(jnp.concatenate([common, common_far], axis=0), 1)
-    near = col_swap(alone[1:], 1)
-    cot_gathered = lax.all_gather(after(cotangent, middle), ("row", "col"), axis=0)
-    token_own, token_other = gather_end(block, first, middle)
     rest_sent = cut_rest(flags, *rests, DISTANCES[1::2], share, True)
     rest_kept = cut_rest(flags, *rests, DISTANCES[::2], width, False)
-    far, out_fetched, near_common, near, token_other, rest_sent, rest_kept = together(
-        far, out_fetched, near_common, near, token_other, rest_sent, rest_kept
-    )
-    both_far = col_swap(far[1:], 1)
-    out_passed = near_pair(out_blocks, out_fetched)
-    both_far, out_passed = together(both_far, out_passed)
+    middle, far, common_far, out_blocks, rest_sent, rest_kept = together(
+        middle, far, common_far, out_blocks, rest_sent, rest_kept
+    )
+    both_far = col_swap(jnp.concatenate([far[1:], common_far], axis=2), 1)
+    out_fetched = far_pair(out_blocks)
+    gains = jnp.concatenate([gains, col_swap(gains, 1)], axis=1)
+    gain1, gain2 = gains[0:1], gains[1:2]
+    token_own, token_other = gather_end(block, first, middle)
+    both_far, gain1, gain2, token_other = together(both_far, gain1, gain2, token_other)
     weight_first = pack_first(
         [
-            (alone, 0), (common, 0), (far, 0), (common_far, 0),
-            (near, 0), (near_common, 0), (both_far, 0), (near_common, 1),
+            (alone, 0, 0), (common, 0, 0), (far, 0, 0), (common_far, 0, 0),
+            (near, 0, 0), (near, 0, lone), (both_far, 0, 0), (both_far, 0, lone),
         ],
         places, at_step + LANES,
-    )
-    rest_sent, rest_kept = after((rest_sent, rest_kept), both_far)
-    fetched = col_swap(rest_sent, 2)
-    rest_near = col_swap(rest_kept[1:], 1)
-    weight_out = jnp.concatenate(
-        [out_blocks[0], out_fetched[0], out_passed[0], out_passed[1]], axis=1
     )
 
     both = (0, 1)
@@ -1473,35 +1737,51 @@
             raw[s], places, step_raw[s], info[s], row_info[s], params, attended, head_width
         )
 
+    cot_y = row_swap(after(cotangent, weight_first))
     attended = project(1, token_other)
-    attended, fetched, rest_near = together(attended, fetched, rest_near)
+    attended, out_fetched, cot_y = together(attended, out_fetched, cot_y)
+    out_passed = near_pair(out_blocks, out_fetched)
+    fetched = col_swap(after(rest_sent, out_fetched), 2)
+    mamba(1, attended)
+    mixed[1], out_passed, fetched = together(mixed[1], out_passed, fetched)
+    cot_col = lax.all_gather(after(cotangent, fetched), "col", axis=0)
     rest_far = along_line(fetched)
-    mamba(1, attended)
+    weight_out = pack_out(out_blocks, out_fetched, out_passed)
     near, far = spread([mixed[1]], weight_out, width, False)
     far = col_swap(far, 1)
     near, far, token_own = together(near, far, token_own)
-    other, low_got, other_got = other_first(near, far)
-    attended = project(0, after(token_own, other))
-    attended, low_got, other_got = together(attended, low_got, other_got)
-    top_last = other_second(other, other_got)
+    rest_near = col_swap(rest_kept[1:], 1)
+    top_near, top_far, low_send = fold(near, far, False)
+    low_got, other_got = row_swap(low_send), col_swap(top_far, 2)
+    attended = project(0, after(token_own, low_send))
+    attended, low_got, other_got, rest_near = together(attended, low_got, other_got, rest_near)
+    top_last = row_swap(add_low(top_near, other_got))
     mamba(0, attended)
+    mixed[0], top_last = together(mixed[0], top_last)
     near, far = spread([mixed[0]], weight_out, width, False)
     far = col_swap(far, 1)
-    near, far, top_last = together(near, far, top_last)
-    own, own_got, low_last = own_second(near, far, low_got)
-    own_got, low_last, rest_far = together(own_got, low_last, rest_far)
-    hidden1 = tokens.astype(wide) + own_sum(own, low_got, own_got, top_last, low_last)
-    block, hidden1, rest_far = together(hidden1.astype(low), hidden1, rest_far)
+    near, far, cot_col = together(near, far, cot_col)
+    own = fold(near, far, True)
+    low_sent = add_low(own[3], low_got[1])
+    own_got, low_last = col_swap(own[1], 2), col_swap(low_sent, 2)
+    cot_xy = row_swap(pick_at(flags, after(cot_col, low_sent), 2))
+    own_got, low_last, cot_xy = together(own_got, low_last, cot_xy)
+    hidden1, block = sum_quarters(tokens, own, low_got, own_got, top_last, low_last)
+    block, hidden1, rest_far = together(block, hidden1, rest_far)
     first = gather_start(block)
     rest_both = col_swap(rest_far[1:], 1)
+    cot_cores = [col_swap(cot_y, 1), col_swap(cot_xy, 1)]
     weight_in, weight_down = pack_rest(
         [(rest_kept, 0), (rest_far, 0), (rest_near, 0), (rest_both, 0)], width
     )
-    first, weight_in, weight_down, cot_gathered = together(first, weight_in, weight_down, cot_gathered)
+    first, weight_in, weight_down, cot_cores = together(first, weight_in, weight_down, cot_cores)
     middle = gather_middle(block, first)
     cot, grad_hidden = [None, None], [None, None]
-    for s in both:
-        cot[s], grad_hidden[s] = meet_gathered(flags, cot_gathered, weight_down, s)
+    cot[0], grad_hidden[0] = meet_gathered(flags, cot_col, weight_down)
+    cot[1], grad_hidden[1] = tiled_call(
+        meet_kernel, "meet_cotangent", [cot_y, cot_xy, *cot_cores], [(weight_down, True)],
+        [(model, low), (units, wide)],
+    )
     middle, cot, grad_hidden = together(middle, cot, grad_hidden)
     pieces = gather_end(block, first, middle)
     normed2, factor2, hidden, grad_in, inner = [[None, None] for _ in range(5)]
@@ -1529,24 +1809,27 @@
     far = col_swap(far, 1)
     feed_forward(0, after(pieces[0], near))
     near, far, hidden, inner, grad_in = together(near, far, hidden, inner, grad_in)
-    other, low_got, other_got = other_first(near, far)
+    top_near, top_far, low_send = fold(near, far, False)
+    low_got, other_got = row_swap(low_send), col_swap(top_far, 2)
     inner_row = row_swap(inner[1])
-    near, far = spread([after(grad_in[0], other)], weight_in, width, True)
+    near, far = spread([after(grad_in[0], low_send)], weight_in, width, True)
     far = col_swap(far, 1)
     near, far = together(near, far)
-    own = add_low(near, far)
-    own_got = col_swap(own[1, : length // 2], 2)
+    own = fold(near, far, True)
+    own_got = col_swap(own[1], 2)
     down = weight_grad(after(hidden, own), cot, width)
+    low_got, other_got, inner_row, down, own = together(low_got, other_got, inner_row, down, own)
+    top_last = row_swap(add_low(top_near, other_got))
+    low_last = col_swap(add_low(own[3], low_got[1]), 2)
+    inner = inner[0] + inner_row
+    inner_core = col_swap(inner, 1)
     line.advance(down)
-    gate = weight_grad(after(normed2, down), grad_in, width, 0, units)
-    low_got, other_got, own_got, inner_row, gate = together(low_got, other_got, own_got, inner_row, gate)
-    top_last = other_second(other, other_got)
-    low_last = col_swap(add_low(own[1, length // 2 :], low_got[1]), 2)
-    inner = inner[0] + inner_row
-    inner = inner + col_swap(inner, 1)
-    up = weight_grad(after(normed2, own_got), grad_in, width, 1, units)
-    top_last, low_last, inner, up, line.flying = together(top_last, low_last, inner, up, line.flying)
-    line.advance(gate)
+    gate = weight_grad(after(normed2, line.sent), grad_in, width, 0, [units])
+    up = weight_grad(after(normed2, gate), grad_in, width, 1, [units])
+    top_last, low_last, own_got, inner_core, up, gate = together(
+        top_last, low_last, own_got, inner_core, up, gate
+    )
+    inner = inner + inner_core
     inner = inner + col_swap(inner, 2)
     inner2 = inner.reshape(length, 1)
     grad_normed2 = own_sum(own, low_got, own_got, top_last, low_last)
@@ -1558,124 +1841,120 @@
     grad_gain2 = jnp.sum(grad_normed2 * hidden1 * own_factor, axis=0)
     grad_hidden1 = cotangent.astype(wide) + back2
     block, grad_hidden1, grad_gain2 = together(grad_hidden1.astype(low), grad_hidden1, grad_gain2)
-    first = together(*gather_start(block))
-    middle = gather_middle(block, first)
-    middle, line.flying = together(middle, line.flying)
-    line.advance(up)
+    first = gather_start(block)
+    output_shares = [spread([after(hidden[s], block)], weight_down, width, False) for s in both]
+    first, output_shares, line.flying = together(first, output_shares, line.flying)
+    line.advance(gate)
+    middle = together(*gather_middle(block, first))
     pieces = gather_end(block, first, middle)
+    output_far = [col_swap(output_shares[s][1], 1) for s in both]
     mix_grad, grad_mixed = [None, None], [None, None]
     for s in both:
         mix_grad[s], grad_mixed[s] = tiled_call(
             meet_kernel, "meet_mixed", pieces[s], [(weight_out, True)],
             [(model, low), (channels + query_width, low)],
         )
-    mix_grad, grad_mixed = together(mix_grad, grad_mixed)
-    early, late, sums, products = [[None, None] for _ in range(4)]
-    for s in both:
-        early[s], products[s] = attention_backward(
-            raw[s], places, cosine[s], sine[s], info[s], row_info[s], combined[s], grad_mixed[s]
-        )
-    first = weight_grad(normed1, after(early, line.sent), width, 0, at_shared)
-    out = weight_grad(mixed, after(mix_grad, first), width)
-    out, first, early, mix_grad, grad_mixed, line.flying = together(
-        out, first, early, mix_grad, grad_mixed, line.flying
-    )
-    line.advance(out)
-    first_far = far_pair(first)
+    out = weight_grad(mixed, mix_grad, width)
+    early, late, sums, products, inner = [[None, None] for _ in range(5)]
 
     def mamba_step(s, *earlier):
-        late[s], more, sums[s] = mamba_backward(
+        late[s], inner[s], sums[s] = mamba_backward(
             raw[s], places, step_raw[s], info[s], row_info[s], params, states[s],
             after(grad_mixed[s], *earlier), head_width,
         )
-        inner[s] = jnp.sum(products[s] + more, axis=1).reshape(length // LANES, LANES)
-
-    inner = [None, None]
-    mamba_step(1, line.sent)
-    late[1], inner[1], first_far, line.flying = together(late[1], inner[1], first_far, line.flying)
-    first_near = together(near_pair(first, first_far))[0]
+
+    for s in both:
+        early[s], products[s] = attention_backward(
+            raw[s], places, cosine[s], sine[s], info[s], row_info[s], combined[s],
+            after(grad_mixed[s], out),
+        )
+    out, grad_mixed, early, output_far, line.flying = together(out, grad_mixed, early, output_far, line.flying)
+    line.advance(up)
+    output_other = add_low(output_shares[1][0], output_far[1])
+    output_got = row_swap(output_other)
+    early = after(early, line.sent, output_other)
+    first = weight_grad(normed1, early, width, 0, [at_shared])
+    first_far = far_pair(first)
+    mamba_step(1, first)
+    late[1], output_got, output_near, first_far, line.flying = together(
+        late[1], output_got, output_far[0], first_far, line.flying
+    )
+    line.advance(out)
+    first_near = near_pair(first, first_far)
+    output_sent = add_three(output_shares[0][0], output_near, output_got, 1)
+    output_last = col_swap(output_sent, 2)
+    down = line.done[0]
+    down_sent = pick_chosen(flags, down, (1, 3))
+    down_far = col_swap(down_sent, 2)
+    mamba_step(0, line.sent, output_sent, down_sent)
+    shared, last = weight_grad(normed1, late, width, 0, [2 * part, channels + LANES])
+    shared, last, late, sums, inner, output_last, down_far, first_near, line.flying = together(
+        shared, last, late, sums, inner, output_last, down_far, first_near, line.flying
+    )
+    shared_keep, shared_send = row_halves(flags, shared)
+    shared_got = row_swap(shared_send)
+    last_far = far_pair(last)
+    down_near = near_of_sum(flags, down, down_far)
     first, common_sum = collect_early(first, first_far, first_near, places)
     line.advance(first)
-    down = chosen(flags, line.done[0])
-    down_far = far_pair(down)
-    mamba_step(0, late[1], line.sent)
-    last = weight_grad(normed1, late, width, 0, late[0].shape[1])
-    sums = sums[0] + sums[1]
-    sums = jnp.concatenate([sums[:13], grad_gain2[None], jnp.zeros((2, width), wide)], axis=0)
-    late, last, inner, sums, down_far, common_sum, line.flying = together(
-        late, last, inner, sums, down_far, common_sum, line.flying
-    )
-    last_far = far_pair(last)
-    line.advance()
-    rank = jnp.arange(16)[:, None]
+    small_rows = length // width
+    inner = [
+        jnp.sum(inner[s] + products[s], axis=1).reshape(small_rows, width) for s in both
+    ]
+    small = jnp.concatenate(
+        [(sums[0] + sums[1])[:13], grad_gain2[None], inner[0], inner[1], jnp.zeros((14, width), wide)],
+        axis=0,
+    )[:24]
+    rank = jnp.arange(24)[:, None]
     taps = conv_weight.shape[0]
     is_shared = (rank > taps) & (rank < 2 * taps + 2)
-    near, far = spread([early[1], after(late[1], line.sent)], weight_first, width, True)
+    is_inner = (rank >= 14) & (rank < 14 + small_rows)
+    is_gain = rank == 13
+    last_far, shared_got, small, down_near = together(last_far, shared_got, small, down_near)
+    shared = add_low(shared_keep, shared_got)
+    shared_far = far_pair(shared)
+    small_got = row_swap(small)
+    last_near = near_pair(last, last_far)
+    shared_far, last_near, small_got, line.flying = together(shared_far, last_near, small_got, line.flying)
+    shared_near = together(near_pair(shared, shared_far))[0]
+    last, step_sum = collect_late(
+        (last, last_far, last_near), (shared, shared_far, shared_near), common_sum, channels
+    )
+    line.advance(last)
+    small_other = jnp.concatenate(
+        [small_got[:14], small_got[14 + small_rows : 14 + 2 * small_rows], small_got[14 + small_rows :]], axis=0
+    )[:24]
+    late, small, small_other = after((late, small, small_other), line.sent)
+    gate, up = line.done[1], line.done[2]
+    gate_far = col_swap(pick_chosen(flags, gate, (1, 3)), 2)
+    up_far = col_swap(pick_chosen(flags, up, (1, 3)), 2)
+    near, far = spread([early[1], late[1]], weight_first, width, True)
     own_near, own_far = spread([early[0], after(late[0], near)], weight_first, width, True)
-    near, far, own_near, own_far, last_far, line.flying = together(
-        near, far, own_near, own_far, last_far, line.flying
-    )
-    last_near, far, own_far = together(near_pair(last, last_far), col_swap(far, 1), col_swap(own_far, 1))
-    last, step_sum = collect_late(last, last_far, last_near, 2 * part, channels)
-    line.advance(last)
-    other, low_got, other_got = other_first(near, far)
-    own = add_low(own_near, own_far)
-    own_got = col_swap(own[1, : length // 2], 2)
-    inner_row, sums_row = row_swap(inner[1]), row_swap(sums)
-    low_got, other_got, own_got, inner_row, sums_row = together(low_got, other_got, own_got, inner_row, sums_row)
-    top_last = other_second(other, other_got)
-    low_last = col_swap(add_low(own[1, length // 2 :], low_got[1]), 2)
-    inner = inner[0] + inner_row
-    sums = sums + jnp.where(is_shared | (rank >= 13), sums_row, 0.0)
-    inner_core, sums_core = col_swap(inner, 1), col_swap(sums, 1)
-    output_shares = [spread([after(hidden[s], low_got)], weight_down, width, False) for s in both]
-    top_last, low_last, inner_core, sums_core, line.flying, output_shares = together(
-        top_last, low_last, inner_core, sums_core, line.flying, output_shares
+    small = small + jnp.where(is_shared | is_gain | is_inner, small_other, 0.0)
+    near, far, own_near, own_far, small, gate_far, up_far, line.flying = together(
+        near, far, own_near, own_far, small, gate_far, up_far, line.flying
     )
     line.advance()
-    inner = inner + inner_core
-    sums = sums + jnp.where(is_shared, sums_core, 0.0)
-    inner_far, sums_far = col_swap(inner, 2), col_swap(sums, 2)
-    down_near = near_pair(down, down_far)
-    gate = chosen(flags, line.done[1])
-    gate_far = far_pair(gate)
-    inner_far, sums_far, down_near, gate_far = together(inner_far, sums_far, down_near, gate_far)
-    inner1 = (inner + inner_far).reshape(length, 1)
-    sums = sums + jnp.where(is_shared, sums_far, 0.0)
-    grad_normed1 = own_sum(own, low_got, own_got, top_last, low_last)
-    own_factor = factor1[0][:, :1]
-    own_tokens = tokens.astype(wide)
-    back1 = (
-        own_factor * norm1_gain * grad_normed1
-        - own_tokens * (own_factor * own_factor * inner1 / model)
-    )
-    grad_gain1 = jnp.sum(grad_normed1 * own_tokens * own_factor, axis=0)
-    tokens_grad = (grad_hidden1 + back1).astype(low)
-    gate_near = near_pair(gate, gate_far)
-    up = chosen(flags, line.done[2])
-    up_far = far_pair(up)
-    gain_row = row_swap(grad_gain1[None])
-    (d_ffn_down,) = finalize_blocks(
-        flags, down, down_far, down_near, [(ffn_down.shape, (units, width), row_index_map, every, every)]
-    )
-    tokens_grad, gate_near, up_far, gain_row, d_ffn_down, line.flying = together(
-        tokens_grad, gate_near, up_far, gain_row, d_ffn_down, line.flying
+    far, own_far, small = after((far, own_far, small), line.sent)
+    far, own_far, small_got = together(col_swap(far, 1), col_swap(own_far, 1), col_swap(small, 1))
+    top_near, top_far, low_send = fold(near, far, False)
+    low_got, other_got = row_swap(low_send), col_swap(top_far, 2)
+    own = fold(own_near, own_far, True)
+    own_got = col_swap(own[1], 2)
+    small = small + jnp.where(is_shared | is_inner, small_got, 0.0)
+    small_got = col_swap(small, 2)
+    gate_near = near_of_sum(flags, gate, gate_far)
+    up_near = near_of_sum(flags, up, up_far)
+    low_got, other_got, own_got, small_got, gate_near, up_near, line.flying = together(
+        low_got, other_got, own_got, small_got, gate_near, up_near, line.flying
     )
     line.advance()
-    up_near = near_pair(up, up_far)
-    out = chosen(flags, line.done[3])
-    out_far = far_pair(out)
-    sums = jnp.concatenate(
-        [
-            jnp.where(rank == 14, grad_gain1[None] + gain_row, sums),
-            jnp.transpose(step_sum)[: 4 * 8],
-        ],
-        axis=0,
-    )
-    (d_ffn_gate,) = finalize_blocks(
-        flags, gate, gate_far, gate_near,
-        [(ffn_gate.shape, (width, units), column_index_map, every, every)],
-    )
+    low_got, other_got, small, small_got = after((low_got, other_got, small, small_got), line.sent)
+    top_last = row_swap(add_low(top_near, other_got))
+    low_last = col_swap(add_low(own[3], low_got[1]), 2)
+    out = line.done[3]
+    out_far = col_swap(pick_chosen(flags, out, (1, 3)), 2)
+    small = small + jnp.where(is_shared | is_inner, small_got, 0.0)
     total, final = line.done[4]
     alone = query_width + channels
     d_query, d_gate = finalize(
@@ -1685,40 +1964,68 @@
             (proj_gate.shape, (width, channels), column_index_map, every, slice(query_width, None)),
         ],
     )
-    sums = dp_total(sums)
-    common_sum = dp_total(common_sum)
-    up_near, out_far, sums, common_sum, d_ffn_gate, d_query, d_gate = together(
-        up_near, out_far, sums, common_sum, d_ffn_gate, d_query, d_gate
-    )
-    out_near = near_pair(out, out_far)
+    (d_ffn_down,) = finalize_blocks(
+        flags, pick_chosen(flags, down, (0,)), down_far, down_near,
+        [(ffn_down.shape, (units, width), row_index_map, every, every)],
+    )
+    (d_ffn_gate,) = finalize_blocks(
+        flags, pick_chosen(flags, gate, (0,)), gate_far, gate_near,
+        [(ffn_gate.shape, (width, units), column_index_map, every, every)],
+    )
     (d_ffn_up,) = finalize_blocks(
-        flags, up, up_far, up_near,
+        flags, pick_chosen(flags, up, (0,)), up_far, up_near,
         [(ffn_up.shape, (width, units), column_index_map, every, every)],
     )
-    d_mamba_out, d_attn_out = finalize_blocks(
-        flags, out, out_far, out_near,
+    output = (
+        hidden1 + output_shares[0][0][0].astype(wide) + output_near[0].astype(wide)
+        + output_got[0].astype(wide) + output_last.astype(wide)
+    ).astype(low)
+    top_last, low_last, out_far, d_query, d_gate, d_ffn_down, d_ffn_gate, d_ffn_up, output = together(
+        top_last, low_last, out_far, d_query, d_gate, d_ffn_down, d_ffn_gate, d_ffn_up, output
+    )
+    out_near = near_of_sum(flags, out, out_far)
+    inner1 = small[14 : 14 + small_rows].reshape(length, 1)
+    grad_normed1 = own_sum(own, low_got, own_got, top_last, low_last)
+    own_factor = factor1[0][:, :1]
+    own_tokens = tokens.astype(wide)
+    back1 = (
+        own_factor * norm1_gain * grad_normed1
+        - own_tokens * (own_factor * own_factor * inner1 / model)
+    )
+    grad_gain1 = jnp.sum(grad_normed1 * own_tokens * own_factor, axis=0)
+    tokens_grad = (grad_hidden1 + back1).astype(low)
+    gain_got = row_swap(grad_gain1[None])
+    tokens_grad, gain_got, out_near, line.flying = together(tokens_grad, gain_got, out_near, line.flying)
+    small = jnp.concatenate(
         [
-            (mamba_out_proj.shape, (channels, width), row_index_map, slice(0, channels), every),
-            (attn_out_proj.shape, (query_width, width), row_index_map, slice(channels, None), every),
-        ],
-    )
-    output = (hidden1 + scatter_sum_slow(output_shares)).astype(low)
+            small[:14], grad_gain1[None] + gain_got, jnp.zeros((1, width), wide),
+            jnp.transpose(step_sum)[: 4 * 8],
+        ],
+        axis=0,
+    )
+    small_got = dp_part(small, 1)
     line.finish()
     total, final = line.done[5]
     (d_conv,) = finalize(
         flags, total, final, (None, width, channels + part // 2), piece_index,
         [(proj_conv.shape, (width, channels), column_index_map, every, slice(0, channels))],
     )
-    shared_sum = jnp.where(flags[1] == 1, total[:, :, channels:], final[:, :, channels:])
-    halves = [jnp.concatenate([shared_sum[p], shared_sum[p + 1]], axis=1) for p in (0, 2)]
-    kept = jnp.where(row_index == 0, halves[0], halves[1]).astype(wide)
-    d_shared = kept + row_swap(jnp.where(row_index == 0, halves[1], halves[0])).astype(wide)
+    small_got, d_conv = together(small_got, d_conv)
+    sums = dp_rest(small + small_got)
+    d_mamba_out, d_attn_out = finalize_blocks(
+        flags, pick_chosen(flags, out, (0,)), out_far, out_near,
+        [
+            (mamba_out_proj.shape, (channels, width), row_index_map, slice(0, channels), every),
+            (attn_out_proj.shape, (query_width, width), row_index_map, slice(channels, None), every),
+        ],
+    )
+    extra = jnp.where(flags[1] == 1, total[:, :, channels:], final[:, :, channels:]).astype(wide)
+    d_shared = jnp.concatenate([extra[0], extra[1]], axis=1)
+    d_key, d_value = extra[2], extra[3]
     step_sum = jnp.stack([sums[16 + p * 8 : 16 + p * 8 + steps] for p in (0, 2, 1, 3)])
     d_step = jnp.transpose(
         jnp.concatenate([lax.dynamic_index_in_dim(step_sum, me ^ d, 0, keepdims=False) for d in range(4)])
     )
-    d_key = common_sum[:, :head_dim].astype(wide)
-    d_value = common_sum[:, head_dim:].astype(wide)
     return (
         output, tokens_grad, sums[14], d_gate, d_conv, d_step, d_shared, d_query, d_key, d_value,
         sums[:taps, :channels], sums[taps, :channels], sums[taps + 1 : 2 * taps + 1],

time: 1010 us -> 932 us (0.923)
  waiting for transfers between devices: 319 us -> 236 us
  other arithmetic: 116 us -> 40.5 us
  Pallas kernels: 368 us -> 442 us
    pallas_call x2 -> x47, Pallas kernels: 3.76 us -> 64.7 us  [the longest x12 17.8 us: pick_chosen(): pl.pallas_call(pick_chosen_kernel, grid_spec=pltpu.PrefetchScalarGridSpec...]
    ppermute x19 -> x20, waiting for transfers between devices: 90.6 us -> 58.3 us  [row_swap(): return lax.ppermute(values, 'row', [(0, 1), (1, 0)])]
    convert_element_type x19 -> x2, other arithmetic: 35.9 us -> 4.82 us  [the longest x1 3.53 us: on_device(): output = (hidden1 + output_shares[0][0][0].astype(wide) + output_near[0]....]
    ppermute x69 -> x70, waiting for transfers between devices: 152 us -> 127 us  [col_swap(): lax.ppermute(values, 'col', [(i, i ^ distance) for i in range(count)])]
    pallas_call x6 -> x7, Pallas kernels: 64.9 us -> 83.3 us  [tiled_call(): pl.pallas_call(partial(kernel, split=split), grid=(tiles,), in_specs=spec...]
    unnamed x365 -> x380, local copies, waits for them, and re-layouts: 46.1 us -> 64.2 us
    another operation x14 -> x0, other arithmetic: 13 us -> none  [the longest x7 7.2 us: far_pair(): return col_swap(jnp.stack([blocks[1], blocks[3]]), 2)]
    select_n x8 -> x0, other arithmetic: 12.2 us -> none  [the longest x4 5.66 us: chosen(): return jnp.where(flags[1] == 1, pair[0], pair[1])]
  transfers between devices with their start and end apart: 109 -> 109, of which waited for: 46 -> 40; matrix products, arithmetic and copies ran while one was open for 14% -> 5% of each run, Pallas kernels for 32% -> 42%
where the time goes in v3:
time: 932 us; the launch traced here: 923 us
  Pallas kernels  442 us (47%)
  waiting for transfers between devices  236 us (25%)
  starting transfers between devices  108 us (12%)
  local copies, waits for them, and re-layouts  80.7 us (9%)
  other arithmetic  40.5 us (4%)
  between operations  16.1 us (2%)
    ppermute x70, waiting for transfers between devices, col_swap(): lax.ppermute(values, 'col', [(i, i ^ distance) for i in range(count)])  127 us
    pallas_call x7, Pallas kernels, tiled_call(): pl.pallas_call(partial(kernel, split=split), grid=(tiles,), in_specs=spec...  83.3 us
    pallas_call x8, Pallas kernels, spread(): pl.pallas_call(partial(spread_kernel, transposed=transposed), grid=(4,),...  70.8 us
    unnamed x380, local copies, waits for them, and re-layouts  64.2 us
    pallas_call x2, Pallas kernels, mamba_backward(): pl.pallas_call(partial(mamba_backward_kernel, head_width=head_width, plac...  61.8 us
    pallas_call x6, Pallas kernels, weight_grad(): pl.pallas_call(weight_grad_kernel, grid=(4,), in_specs=[left, left, right...  59.1 us
    ppermute x20, waiting for transfers between devices, row_swap(): return lax.ppermute(values, 'row', [(0, 1), (1, 0)])  58.3 us
    ppermute x8, waiting for transfers between devices, _start(): move = lax.ppermute(self.sent, 'dp', [(0, 1), (3, 2), (1, 0), (2, 3)])  47 us
  transfers between devices with their start and end apart: 109, of which 40 were waited for; matrix products, arithmetic and copies ran while one was open for 5% of the time, Pallas kernels for 42%

profile of v3, /device:TPU:0, one launch (start us, length us, event | category | flops | bytes accessed | tf_op | source)
XLA Modules:
  0.0 923.0 jit_solution(8924833369508742906)
XLA Ops:
  47.4 16.5 %collective-permute-done.4.refs_0_ = bf16[1024,512]{1,0:T(8,128)(2,1)S(1)} collective-permute-done((bf16[1024,512]{1,0:T(8,128)(2,1)S(1)}, bf16[1024,512]{1,0:T(8,128)(2,1)S(1)}, u32[]{:S(2)}, u32[]{:S(2)}) %collective-permute-start.4) | collective-permute-done | bytes 1048608 | tf_op jit(solution)/shard_map/ppermute | solution.py:578
  73.3 11.8 %collective-permute-done.11.refs_3_ = bf16[1,512,768]{2,1,0:T(8,128)(2,1)S(1)} collective-permute-done((bf16[1,512,768]{2,1,0:T(8,128)(2,1)S(1)}, bf16[1,512,768]{2,1,0:T(8,128)(2,1)S(1)}, u32[]{:S(2)}, u32[]{:S(2)}) %collective-permute-start.11) | collective-permute-done | bytes 786464 | tf_op jit(solution)/shard_map/ppermute | solution.py:574
  86.0 9.5 %collective-permute-done.7.refs_1_ = bf16[512,512]{1,0:T(8,128)(2,1)S(1)} collective-permute-done((bf16[512,512]{1,0:T(8,128)(2,1)S(1)}, bf16[512,512]{1,0:T(8,128)(2,1)S(1)}, u32[]{:S(2)}, u32[]{:S(2)}) %collective-permute-start.7) | collective-permute-done | bytes 524320 | tf_op jit(solution)/shard_map/ppermute | solution.py:574
  114.7 25.2 %project.2 = (bf16[1024,2048]{1,0:T(8,128)(2,1)}, f32[1024,128]{1,0:T(8,128)}, bf16[1024,1664]{1,0:T(8,128)(2,1)}, f32[1024,128]{1,0:T(8,128)}) custom-call(bf16[1024,512]{1,0:T(8,128)(2,1)} %copy-done.145, bf16[512,512]{1,0:T(8,128)(2,1)} %copy-done.165, bf16[512,512]{1,0:T(8,128)(2,1)} %copy-done.163, bf16[1024,512]{1,0:T(8,128)(2,1)} %copy-done.152, ...), custom_call_target="tpu_custom_call" | custom-call | flops 1 | bytes 1 | tf_op jit(solution)/shard_map/project/pallas_call | solution.py:1141
  147.5 12.5 %mamba_forward.2 = (bf16[1024,512]{1,0:T(8,128)(2,1)S(1)}, bf16[1024,384]{1,0:T(8,128)(2,1)S(1)}, bf16[8,256,384]{2,1,0:T(8,128)(2,1)S(1)}) custom-call(bf16[1024,1664]{1,0:T(8,128)(2,1)} %get-tuple-element.375.query_ref.key_ref.value_ref.raw_ref.tail_ref, f32[1024,128]{1,0:T(8,128)S(1)} %copy-done.94, f32[1024,128]{1,0:T(8,128)S(1)} %get-tuple-element.755.info_ref, ...), custom_call_target="tpu_custom_call" | custom-call | flops 1 | bytes 1 | tf_op jit(solution)/shard_map/mamba_forward/pallas_call | solution.py:485
  188.7 13.9 %project.3 = (bf16[1024,2048]{1,0:T(8,128)(2,1)}, f32[1024,128]{1,0:T(8,128)}, bf16[1024,1664]{1,0:T(8,128)(2,1)}, f32[1024,128]{1,0:T(8,128)}) custom-call(bf16[1024,512]{1,0:T(8,128)(2,1)} %base_ref.1, bf16[1024,512]{1,0:T(8,128)(2,1)} %copy-done.144, bf16[1024,512]{1,0:T(8,128)(2,1)} %copy-done.150, bf16[1024,512]{1,0:T(8,128)(2,1)} %collective-permute-done.9.refs_3_, ...), custom_call_target="tpu_custom_call" | custom-call | flops 1 | bytes 1 | tf_op jit(solution)/shard_map/project/pallas_call | solution.py:1141
  212.4 12.5 %mamba_forward.3 = (bf16[1024,512]{1,0:T(8,128)(2,1)S(1)}, bf16[1024,384]{1,0:T(8,128)(2,1)S(1)}, bf16[8,256,384]{2,1,0:T(8,128)(2,1)S(1)}) custom-call(bf16[1024,1664]{1,0:T(8,128)(2,1)} %get-tuple-element.411.query_ref.key_ref.value_ref.raw_ref.tail_ref, f32[1024,128]{1,0:T(8,128)S(1)} %copy-done.96, f32[1024,128]{1,0:T(8,128)S(1)} %copy-done.30, ...), custom_call_target="tpu_custom_call" | custom-call | flops 1 | bytes 1 | tf_op jit(solution)/shard_map/mamba_forward/pallas_call | solution.py:485
  249.9 12.8 %collective-permute-done.26.refs_1_ = bf16[512,512]{1,0:T(8,128)(2,1)S(1)} collective-permute-done((bf16[512,512]{1,0:T(8,128)(2,1)S(1)}, bf16[512,512]{1,0:T(8,128)(2,1)S(1)}, u32[]{:S(2)}, u32[]{:S(2)}) %collective-permute-start.26) | collective-permute-done | bytes 524320 | tf_op jit(solution)/shard_map/ppermute | solution.py:574
  262.7 10.2 %collective-permute-done.27.refs_5_ = bf16[512,512]{1,0:T(8,128)(2,1)S(1)} collective-permute-done((bf16[512,512]{1,0:T(8,128)(2,1)S(1)}, bf16[512,512]{1,0:T(8,128)(2,1)S(1)}, u32[]{:S(2)}, u32[]{:S(2)}) %collective-permute-start.27) | collective-permute-done | bytes 524320 | tf_op jit(solution)/shard_map/ppermute | solution.py:574
  290.5 15.4 %collective-permute-done.30.refs_0_ = bf16[1024,512]{1,0:T(8,128)(2,1)S(1)} collective-permute-done((bf16[1024,512]{1,0:T(8,128)(2,1)}, bf16[1024,512]{1,0:T(8,128)(2,1)S(1)}, u32[]{:S(2)}, u32[]{:S(2)}) %collective-permute-start.30) | collective-permute-done | bytes 1048608 | tf_op jit(solution)/shard_map/ppermute | solution.py:578
  329.5 11.6 %ffn.2 = (bf16[1024,2048]{1,0:T(8,128)(2,1)}, f32[1024,128]{1,0:T(8,128)}, bf16[1024,512]{1,0:T(8,128)(2,1)}, bf16[1024,1024]{1,0:T(8,128)(2,1)}, f32[1024,128]{1,0:T(8,128)}) custom-call(bf16[1024,512]{1,0:T(8,128)(2,1)} %copy-done.147, bf16[512,512]{1,0:T(8,128)(2,1)} %copy-done.170, bf16[512,512]{1,0:T(8,128)(2,1)} %copy-done.171, ...), custom_call_target="tpu_custom_call" | custom-call | flops 1 | bytes 1 | tf_op jit(solution)/shard_map/ffn/pallas_call | solution.py:1141
  350.2 11.2 %ffn.3 = (bf16[1024,2048]{1,0:T(8,128)(2,1)}, f32[1024,128]{1,0:T(8,128)}, bf16[1024,512]{1,0:T(8,128)(2,1)}, bf16[1024,1024]{1,0:T(8,128)(2,1)}, f32[1024,128]{1,0:T(8,128)}) custom-call(bf16[1024,512]{1,0:T(8,128)(2,1)} %copy-done.103, bf16[1024,512]{1,0:T(8,128)(2,1)} %copy-done.146, bf16[1024,512]{1,0:T(8,128)(2,1)} %copy-done.151, ...), custom_call_target="tpu_custom_call" | custom-call | flops 1 | bytes 1 | tf_op jit(solution)/shard_map/ffn/pallas_call | solution.py:1141
  365.0 9.1 spread.11
  390.0 9.8 %collective-permute-done.44 = f32[8,128]{1,0:T(8,128)S(1)} collective-permute-done((f32[8,128]{1,0:T(8,128)S(1)}, f32[8,128]{1,0:T(8,128)S(1)}, u32[]{:S(2)}, u32[]{:S(2)}) %collective-permute-start.44) | collective-permute-done | bytes 4128 | tf_op jit(solution)/shard_map/ppermute | solution.py:578
  450.1 9.7 %collective-permute-done.52.refs_0_ = bf16[1024,512]{1,0:T(8,128)(2,1)S(1)} collective-permute-done((bf16[1024,512]{1,0:T(8,128)(2,1)S(1)}, bf16[1024,512]{1,0:T(8,128)(2,1)S(1)}, u32[]{:S(2)}, u32[]{:S(2)}) %collective-permute-start.52) | collective-permute-done | bytes 1048608 | tf_op jit(solution)/shard_map/ppermute | solution.py:578
  540.1 10.8 %weight_grad.10.refs_0_.refs_1_ = bf16[4,512,768]{2,1,0:T(8,128)(2,1)} custom-call(bf16[1024,2048]{1,0:T(8,128)(2,1)} %get-tuple-element.555.former_0, bf16[1024,2048]{1,0:T(8,128)(2,1)} %get-tuple-element.556.former_1, bf16[1024,768]{1,0:T(8,128)(2,1)} %copy-done.55, bf16[1024,768]{1,0:T(8,128)(2,1)} %copy-done.56), custom_call_target="tpu_custom_call" | custom-call | flops 1 | bytes 1 | tf_op jit(solution)/shard_map/weight_grad/pallas_call | solution.py:1171
  555.3 30.8 %mamba_backward.2 = (bf16[1024,1024]{1,0:T(8,128)(2,1)}, f32[1024,128]{1,0:T(8,128)S(1)}, f32[16,512]{1,0:T(8,128)S(1)}) custom-call(bf16[1024,1664]{1,0:T(8,128)(2,1)} %get-tuple-element.375.query_ref.key_ref.value_ref.raw_ref.tail_ref, bf16[1024,1664]{1,0:T(8,128)(2,1)} %get-tuple-element.375.query_ref.key_ref.value_ref.raw_ref.tail_ref, ...), custom_call_target="tpu_custom_call" | custom-call | flops 1 | bytes 1 | tf_op jit(solution)/shard_map/mamba_backward/pallas_call | solution.py:524
  608.1 31.0 %mamba_backward.3 = (bf16[1024,1024]{1,0:T(8,128)(2,1)}, f32[1024,128]{1,0:T(8,128)S(1)}, f32[16,512]{1,0:T(8,128)S(1)}) custom-call(bf16[1024,1664]{1,0:T(8,128)(2,1)} %get-tuple-element.411.query_ref.key_ref.value_ref.raw_ref.tail_ref, bf16[1024,1664]{1,0:T(8,128)(2,1)} %get-tuple-element.411.query_ref.key_ref.value_ref.raw_ref.tail_ref, ...), custom_call_target="tpu_custom_call" | custom-call | flops 1 | bytes 1 | tf_op jit(solution)/shard_map/mamba_backward/pallas_call | solution.py:524
  639.9 13.3 %weight_grad.11 = (bf16[4,512,512]{2,1,0:T(8,128)(2,1)}, bf16[4,512,512]{2,1,0:T(8,128)(2,1)}) custom-call(bf16[1024,2048]{1,0:T(8,128)(2,1)} %get-tuple-element.555.former_0, bf16[1024,2048]{1,0:T(8,128)(2,1)} %get-tuple-element.556.former_1, bf16[1024,1024]{1,0:T(8,128)(2,1)} %get-tuple-element.619.latter_0.refs_1_, ...), custom_call_target="tpu_custom_call" | custom-call | flops 1 | bytes 1 | tf_op jit(solution)/shard_map/weight_grad/pallas_call | solution.py:1171
  707.8 12.3 %collective-permute-done.80.got_ref.end_ref = bf16[4,512,512]{2,1,0:T(8,128)(2,1)} collective-permute-done((bf16[4,512,512]{2,1,0:T(8,128)(2,1)}, bf16[4,512,512]{2,1,0:T(8,128)(2,1)}, u32[]{:S(2)}, u32[]{:S(2)}) %collective-permute-start.80) | collective-permute-done | bytes 2097184 | tf_op jit(solution)/shard_map/ppermute | solution.py:853
  741.7 12.9 %spread.14 = (bf16[2,1024,512]{2,1,0:T(8,128)(2,1)}, bf16[2,1024,512]{2,1,0:T(8,128)(2,1)}) custom-call(bf16[1024,768]{1,0:T(8,128)(2,1)} %copy-done.56, bf16[1024,1024]{1,0:T(8,128)(2,1)} %get-tuple-element.615.latter_1.refs_1_, bf16[2048,1792]{1,0:T(8,128)(2,1)} %bitcast.119), custom_call_target="tpu_custom_call" | custom-call | flops 1 | bytes 1 | tf_op jit(solution)/shard_map/spread/pallas_call | solution.py:1218
  754.6 12.9 %spread.15 = (bf16[2,1024,512]{2,1,0:T(8,128)(2,1)}, bf16[2,1024,512]{2,1,0:T(8,128)(2,1)}) custom-call(bf16[1024,768]{1,0:T(8,128)(2,1)} %copy-done.55, bf16[1024,1024]{1,0:T(8,128)(2,1)} %get-tuple-element.619.latter_0.refs_1_, bf16[2048,1792]{1,0:T(8,128)(2,1)} %bitcast.120), custom_call_target="tpu_custom_call" | custom-call | flops 1 | bytes 1 | tf_op jit(solution)/shard_map/spread/pallas_call | solution.py:1218
  767.5 16.7 %collective-permute-done.84.refs_1_ = bf16[2,512,512]{2,1,0:T(8,128)(2,1)} collective-permute-done((bf16[2,512,512]{2,1,0:T(8,128)(2,1)}, bf16[2,512,512]{2,1,0:T(8,128)(2,1)}, u32[]{:S(2)}, u32[]{:S(2)}) %collective-permute-start.84) | collective-permute-done | bytes 1048608 | tf_op jit(solution)/shard_map/ppermute | solution.py:574
  810.4 30.0 %collective-permute-done.96.last_ref = bf16[4,512,512]{2,1,0:T(8,128)(2,1)S(1)} collective-permute-done((bf16[4,512,512]{2,1,0:T(8,128)(2,1)S(1)}, bf16[4,512,512]{2,1,0:T(8,128)(2,1)S(1)}, u32[]{:S(2)}, u32[]{:S(2)}) %collective-permute-start.96) | collective-permute-done | bytes 2097184 | tf_op jit(solution)/shard_map/ppermute | solution.py:853
  (771 shorter events, 544.4 us)
Async XLA Ops:
  7.2 90.1 %all-gather.5.cloned.1.call-start = ((), (), s32[]{:S(2)}) async-start(), calls=%async_computation | async-start | bytes 2621440 | tf_op jit(solution)/shard_map/all_gather | solution.py:1649
  32.0 208.9 %all-gather.9.cloned.1.call-start = ((), (), s32[]{:S(2)}) async-start(), calls=%async_computation.2 | async-start | bytes 5242880 | tf_op jit(solution)/shard_map/all_gather | solution.py:1747
  103.5 41.0 %collective-permute-start.16 = (bf16[2,512,512]{2,1,0:T(8,128)(2,1)S(1)}, bf16[2,512,512]{2,1,0:T(8,128)(2,1)S(1)}, u32[]{:S(2)}, u32[]{:S(2)}) collective-permute-start(bf16[2,512,512]{2,1,0:T(8,128)(2,1)S(1)} %pick.12), channel_id=1, source_target_pairs={{0,2},{1,3},{2,0},{3,1},{4,6},{5,7},{6,4},{7,5},{8,10},{9,11},{10,... | collective-permute-start | bytes 3145736 | tf_op jit(solution)/shard_map/ppermute | solution.py:574
  165.9 111.9 %all-gather.7.cloned.1.call-start = ((), (), s32[]{:S(2)}) async-start(), calls=%async_computation.1 | async-start | bytes 3932160 | tf_op jit(solution)/shard_map/all_gather | solution.py:1649
  403.9 57.2 %collective-permute-start.54 = (bf16[4,512,512]{2,1,0:T(8,128)(2,1)}, bf16[4,512,512]{2,1,0:T(8,128)(2,1)}, u32[]{:S(2)}, u32[]{:S(2)}) collective-permute-start(bf16[4,512,512]{2,1,0:T(8,128)(2,1)} %weight_grad.6.former_ref), channel_id=1, source_target_pairs={{0,8},{24,16},{8,0},{16,24},{1,9},{25,17},{9,1},{17,25},{2,10},{26... | collective-permute-start | bytes 6291464 | tf_op jit(solution)/shard_map/ppermute | solution.py:853
  462.5 61.3 %collective-permute-start.63 = (bf16[4,512,512]{2,1,0:T(8,128)(2,1)S(1)}, bf16[4,512,512]{2,1,0:T(8,128)(2,1)}, u32[]{:S(2)}, u32[]{:S(2)}) collective-permute-start(bf16[4,512,512]{2,1,0:T(8,128)(2,1)S(1)} %copy-done.43), channel_id=1, source_target_pairs={{0,8},{24,16},{8,0},{16,24},{1,9},{25,17},{9,1},{17,25},{2,10},{26... | collective-permute-start | bytes 6291464 | tf_op jit(solution)/shard_map/ppermute | solution.py:853
  475.6 48.2 %collective-permute-start.61 = (bf16[2,1024,512]{2,1,0:T(8,128)(2,1)}, bf16[2,1024,512]{2,1,0:T(8,128)(2,1)}, u32[]{:S(2)}, u32[]{:S(2)}) collective-permute-start(bf16[2,1024,512]{2,1,0:T(8,128)(2,1)} %get-tuple-element.542), channel_id=1, source_target_pairs={{0,1},{1,0},{2,3},{3,2},{4,5},{5,4},{6,7},{7,6},{8,9},{9,8},{10,11... | collective-permute-start | bytes 6291464 | tf_op jit(solution)/shard_map/ppermute | solution.py:574
  476.3 47.6 %collective-permute-start.62 = (bf16[2,1024,512]{2,1,0:T(8,128)(2,1)}, bf16[2,1024,512]{2,1,0:T(8,128)(2,1)}, u32[]{:S(2)}, u32[]{:S(2)}) collective-permute-start(bf16[2,1024,512]{2,1,0:T(8,128)(2,1)} %get-tuple-element.543), channel_id=1, source_target_pairs={{0,1},{1,0},{2,3},{3,2},{4,5},{5,4},{6,7},{7,6},{8,9},{9,8},{10,11... | collective-permute-start | bytes 6291464 | tf_op jit(solution)/shard_map/ppermute | solution.py:574
  476.3 47.6 %collective-permute-start.64 = (bf16[4,512,512]{2,1,0:T(8,128)(2,1)S(1)}, bf16[4,512,512]{2,1,0:T(8,128)(2,1)}, u32[]{:S(2)}, u32[]{:S(2)}) collective-permute-start(bf16[4,512,512]{2,1,0:T(8,128)(2,1)S(1)} %add.188.pair_ref), channel_id=1, source_target_pairs={{8,16},{16,8},{9,17},{17,9},{10,18},{18,10},{11,19},{19,11},{12,20... | collective-permute-start | bytes 6291464 | tf_op jit(solution)/shard_map/ppermute | solution.py:857
  527.5 61.9 %collective-permute-start.68 = (bf16[4,512,512]{2,1,0:T(8,128)(2,1)}, bf16[4,512,512]{2,1,0:T(8,128)(2,1)}, u32[]{:S(2)}, u32[]{:S(2)}) collective-permute-start(bf16[4,512,512]{2,1,0:T(8,128)(2,1)} %get-tuple-element.565.pair_ref), channel_id=1, source_target_pairs={{8,16},{16,8},{9,17},{17,9},{10,18},{18,10},{11,19},{19,11},{12,20... | collective-permute-start | bytes 6291464 | tf_op jit(solution)/shard_map/ppermute | solution.py:857
  529.5 59.9 %collective-permute-start.67 = (bf16[4,512,512]{2,1,0:T(8,128)(2,1)S(1)}, bf16[4,512,512]{2,1,0:T(8,128)(2,1)S(1)}, u32[]{:S(2)}, u32[]{:S(2)}) collective-permute-start(bf16[4,512,512]{2,1,0:T(8,128)(2,1)S(1)} %get-tuple-element.551.middle_ref), channel_id=1, source_target_pairs={{0,8},{24,16},{8,0},{16,24},{1,9},{25,17},{9,1},{17,25},{2,10},{26... | collective-permute-start | bytes 6291464 | tf_op jit(solution)/shard_map/ppermute | solution.py:853
  539.6 49.8 %collective-permute-start.65 = (bf16[2,1024,512]{2,1,0:T(8,128)(2,1)}, bf16[2,1024,512]{2,1,0:T(8,128)(2,1)}, u32[]{:S(2)}, u32[]{:S(2)}) collective-permute-start(bf16[2,1024,512]{2,1,0:T(8,128)(2,1)} %add.189), channel_id=1, source_target_pairs={{0,4},{4,0},{1,5},{5,1},{2,6},{6,2},{3,7},{7,3},{8,12},{12,8},{9,1... | collective-permute-start | bytes 6291464 | tf_op jit(solution)/shard_map/ppermute | solution.py:578
  594.9 58.3 %collective-permute-start.73 = (bf16[4,512,512]{2,1,0:T(8,128)(2,1)}, bf16[4,512,512]{2,1,0:T(8,128)(2,1)}, u32[]{:S(2)}, u32[]{:S(2)}) collective-permute-start(bf16[4,512,512]{2,1,0:T(8,128)(2,1)} %get-tuple-element.583.pair_ref), channel_id=1, source_target_pairs={{8,16},{16,8},{9,17},{17,9},{10,18},{18,10},{11,19},{19,11},{12,20... | collective-permute-start | bytes 6291464 | tf_op jit(solution)/shard_map/ppermute | solution.py:857
  596.9 56.4 %collective-permute-start.72 = (bf16[4,512,512]{2,1,0:T(8,128)(2,1)}, bf16[4,512,512]{2,1,0:T(8,128)(2,1)S(1)}, u32[]{:S(2)}, u32[]{:S(2)}) collective-permute-start(bf16[4,512,512]{2,1,0:T(8,128)(2,1)} %get-tuple-element.569.middle_ref), channel_id=1, source_target_pairs={{0,8},{24,16},{8,0},{16,24},{1,9},{25,17},{9,1},{17,25},{2,10},{26... | collective-permute-start | bytes 6291464 | tf_op jit(solution)/shard_map/ppermute | solution.py:853
  600.7 52.6 %collective-permute-start.71 = (bf16[2,512,768]{2,1,0:T(8,128)(2,1)}, bf16[2,512,768]{2,1,0:T(8,128)(2,1)}, u32[]{:S(2)}, u32[]{:S(2)}) collective-permute-start(bf16[2,512,768]{2,1,0:T(8,128)(2,1)} %pick.15), channel_id=1, source_target_pairs={{0,1},{1,0},{2,3},{3,2},{4,5},{5,4},{6,7},{7,6},{8,9},{9,8},{10,11... | collective-permute-start | bytes 4718600 | tf_op jit(solution)/shard_map/ppermute | solution.py:574
  603.3 49.9 %collective-permute-start.69 = (bf16[1024,512]{1,0:T(8,128)(2,1)}, bf16[1024,512]{1,0:T(8,128)(2,1)}, u32[]{:S(2)}, u32[]{:S(2)}) collective-permute-start(bf16[1024,512]{1,0:T(8,128)(2,1)} %add_three.1), channel_id=1, source_target_pairs={{0,2},{1,3},{2,0},{3,1},{4,6},{5,7},{6,4},{7,5},{8,10},{9,11},{10,... | collective-permute-start | bytes 3145736 | tf_op jit(solution)/shard_map/ppermute | solution.py:574
  606.2 47.0 %collective-permute-start.70 = (bf16[2,512,512]{2,1,0:T(8,128)(2,1)}, bf16[2,512,512]{2,1,0:T(8,128)(2,1)}, u32[]{:S(2)}, u32[]{:S(2)}) collective-permute-start(bf16[2,512,512]{2,1,0:T(8,128)(2,1)} %pick_chosen.12), channel_id=1, source_target_pairs={{0,2},{1,3},{2,0},{3,1},{4,6},{5,7},{6,4},{7,5},{8,10},{9,11},{10,... | collective-permute-start | bytes 3145736 | tf_op jit(solution)/shard_map/ppermute | solution.py:574
  667.9 39.9 %collective-permute-start.81 = (bf16[4,512,512]{2,1,0:T(8,128)(2,1)}, bf16[4,512,512]{2,1,0:T(8,128)(2,1)}, u32[]{:S(2)}, u32[]{:S(2)}) collective-permute-start(bf16[4,512,512]{2,1,0:T(8,128)(2,1)} %get-tuple-element.606.pair_ref), channel_id=1, source_target_pairs={{8,16},{16,8},{9,17},{17,9},{10,18},{18,10},{11,19},{19,11},{12,20... | collective-permute-start | bytes 6291464 | tf_op jit(solution)/shard_map/ppermute | solution.py:857
  669.9 50.2 %collective-permute-start.80 = (bf16[4,512,512]{2,1,0:T(8,128)(2,1)}, bf16[4,512,512]{2,1,0:T(8,128)(2,1)}, u32[]{:S(2)}, u32[]{:S(2)}) collective-permute-start(bf16[4,512,512]{2,1,0:T(8,128)(2,1)} %get-tuple-element.605.middle_ref), channel_id=1, source_target_pairs={{0,8},{24,16},{8,0},{16,24},{1,9},{25,17},{9,1},{17,25},{2,10},{26... | collective-permute-start | bytes 6291464 | tf_op jit(solution)/shard_map/ppermute | solution.py:853
  727.3 57.0 %collective-permute-start.86 = (bf16[4,512,512]{2,1,0:T(8,128)(2,1)}, bf16[4,512,512]{2,1,0:T(8,128)(2,1)}, u32[]{:S(2)}, u32[]{:S(2)}) collective-permute-start(bf16[4,512,512]{2,1,0:T(8,128)(2,1)} %get-tuple-element.624.pair_ref), channel_id=1, source_target_pairs={{8,16},{16,8},{9,17},{17,9},{10,18},{18,10},{11,19},{19,11},{12,20... | collective-permute-start | bytes 6291464 | tf_op jit(solution)/shard_map/ppermute | solution.py:857
  729.3 55.0 %collective-permute-start.85 = (bf16[4,512,512]{2,1,0:T(8,128)(2,1)S(1)}, bf16[4,512,512]{2,1,0:T(8,128)(2,1)S(1)}, u32[]{:S(2)}, u32[]{:S(2)}) collective-permute-start(bf16[4,512,512]{2,1,0:T(8,128)(2,1)S(1)} %get-tuple-element.614.middle_ref), channel_id=1, source_target_pairs={{0,8},{24,16},{8,0},{16,24},{1,9},{25,17},{9,1},{17,25},{2,10},{26... | collective-permute-start | bytes 6291464 | tf_op jit(solution)/shard_map/ppermute | solution.py:853
  740.8 43.5 %collective-permute-start.84 = (bf16[2,512,512]{2,1,0:T(8,128)(2,1)}, bf16[2,512,512]{2,1,0:T(8,128)(2,1)}, u32[]{:S(2)}, u32[]{:S(2)}) collective-permute-start(bf16[2,512,512]{2,1,0:T(8,128)(2,1)} %pick_chosen.15), channel_id=1, source_target_pairs={{0,2},{1,3},{2,0},{3,1},{4,6},{5,7},{6,4},{7,5},{8,10},{9,11},{10,... | collective-permute-start | bytes 3145736 | tf_op jit(solution)/shard_map/ppermute | solution.py:574
  790.0 50.4 %collective-permute-start.96 = (bf16[4,512,512]{2,1,0:T(8,128)(2,1)S(1)}, bf16[4,512,512]{2,1,0:T(8,128)(2,1)S(1)}, u32[]{:S(2)}, u32[]{:S(2)}) collective-permute-start(bf16[4,512,512]{2,1,0:T(8,128)(2,1)S(1)} %get-tuple-element.631.total_ref), channel_id=1, source_target_pairs={{0,8},{24,16},{8,0},{16,24},{1,9},{25,17},{9,1},{17,25},{2,10},{26... | collective-permute-start | bytes 6291464 | tf_op jit(solution)/shard_map/ppermute | solution.py:853
  844.4 48.3 %collective-permute-start.103 = (bf16[4,512,512]{2,1,0:T(8,128)(2,1)}, bf16[4,512,512]{2,1,0:T(8,128)(2,1)}, u32[]{:S(2)}, u32[]{:S(2)}) collective-permute-start(bf16[4,512,512]{2,1,0:T(8,128)(2,1)} %add.191.total_ref), channel_id=1, source_target_pairs={{0,8},{24,16},{8,0},{16,24},{1,9},{25,17},{9,1},{17,25},{2,10},{26... | collective-permute-start | bytes 6291464 | tf_op jit(solution)/shard_map/ppermute | solution.py:853
  (274 other events, 2973.5 us)
Sparse Core Ops, SparseCore 0:
  32.2 45.2 all-gather.4
  166.1 44.4 all-gather.8
  212.1 64.1 all-gather.6

commit v4 on v3

--- a/solution.py
+++ b/solution.py
@@ -47,8 +47,21 @@
     return dot_any(former, latter, ((0,), (0,)))
 
 
-def exact(former, latter):
-    return dot_any(former, latter, ((1,), (0,)), HIGHEST)
+def low_terms(values, count):
+    terms = []
+    for _ in range(count):
+        term = values.astype(jnp.bfloat16)
+        values = values - term.astype(jnp.float32)
+        terms.append(term)
+    return terms
+
+
+def times_marks(values, marks, count):
+    return sum(nn(term, marks) for term in low_terms(values, count))
+
+
+def marks_times(marks, values, count):
+    return sum(nn(marks, term) for term in low_terms(values, count))
 
 
 def sigmoid_of(values):
@@ -62,13 +75,13 @@
 def head_spread(head_width, width):
     heads = lax.broadcasted_iota(jnp.int32, (LANES, width), 0)
     columns = lax.broadcasted_iota(jnp.int32, (LANES, width), 1)
-    return (columns // head_width == heads).astype(jnp.float32)
+    return (columns // head_width == heads).astype(jnp.bfloat16)
 
 
 def head_gather(head_width, width):
     columns = lax.broadcasted_iota(jnp.int32, (width, LANES), 0)
     heads = lax.broadcasted_iota(jnp.int32, (width, LANES), 1)
-    return (columns // head_width == heads).astype(jnp.float32)
+    return (columns // head_width == heads).astype(jnp.bfloat16)
 
 
 def causal_conv(ext_ref, columns, weight_ref, bias_ref, position, taps):
@@ -89,7 +102,7 @@
     rows = lax.broadcasted_iota(jnp.int32, (length, length), 0)
     columns = lax.broadcasted_iota(jnp.int32, (length, length), 1)
     causal = rows >= columns
-    running = exact(causal.astype(jnp.float32), log_decay)
+    running = marks_times(causal.astype(jnp.bfloat16), log_decay, 3)
     return step_size, log_decay, running, jnp.transpose(running), causal
 
 
@@ -145,7 +158,7 @@
     last = running[length - 1 : length, :]
     leaves = jnp.where(segment == segment_row[:, length - 1 :], jnp.exp(last - running), 0.0)
     spread = head_spread(head_width, width)
-    wide = exact(jnp.concatenate([step_size, enters, leaves], axis=0), spread)
+    wide = times_marks(jnp.concatenate([step_size, enters, leaves], axis=0), spread, 2)
     weighted = conv_out * wide[:length]
     gram = nt(c_map, b_map)
     weighted_low = weighted.astype(low)
@@ -226,7 +239,7 @@
     last = running[length - 1 : length, :]
     leaves = jnp.where(segment == segment_row[:, length - 1 :], jnp.exp(last - running), 0.0)
     spread = head_spread(head_width, width)
-    wide = exact(jnp.concatenate([step_size, enters, leaves], axis=0), spread)
+    wide = times_marks(jnp.concatenate([step_size, enters, leaves], axis=0), spread, 2)
     step_wide = wide[:length]
     enters_wide = wide[length : 2 * length]
     leaves_wide = wide[2 * length :]
@@ -277,12 +290,13 @@
     met_state = fade * jnp.sum(held.astype(f32) * grad_held, axis=0, keepdims=True)
     grad_state[...] = grad_held * fade + tn(c_map, entering)
     grad_conv_out = grad_weighted * step_wide + skip_ref[...] * grad_scan
-    gathered = exact(
+    gathered = times_marks(
         jnp.concatenate(
             [met_in, met_out, conv_out * grad_weighted, jnp.broadcast_to(met_state, (TAIL, width))],
             axis=0,
         ),
         head_gather(head_width, width),
+        2,
     )
     out_rows = gathered[length : 2 * length]
     at_last = jnp.sum(out_rows, axis=0, keepdims=True) + gathered[3 * length : 3 * length + 1]
@@ -290,7 +304,7 @@
     grad_running = grad_running + jnp.where(local == length - 1.0, at_last, 0.0)
     rows = lax.broadcasted_iota(jnp.int32, (length, length), 0)
     later = lax.broadcasted_iota(jnp.int32, (length, length), 1) >= rows
-    grad_decay = jnp.where(position == 0.0, 0.0, exact(later.astype(f32), grad_running))
+    grad_decay = jnp.where(position == 0.0, 0.0, marks_times(later.astype(low), grad_running, 3))
     grad_step = (gathered[2 * length : 3 * length] - grad_decay * rate) * sigmoid_of(step_in)
 
     ext_grad[length : length + TAIL, :] = ext_grad[:TAIL, :]
@@ -1774,10 +1788,12 @@
     weight_in, weight_down = pack_rest(
         [(rest_kept, 0), (rest_far, 0), (rest_near, 0), (rest_both, 0)], width
     )
-    first, weight_in, weight_down, cot_cores = together(first, weight_in, weight_down, cot_cores)
-    middle = gather_middle(block, first)
     cot, grad_hidden = [None, None], [None, None]
     cot[0], grad_hidden[0] = meet_gathered(flags, cot_col, weight_down)
+    first, weight_in, weight_down, cot_cores, cot[0], grad_hidden[0] = together(
+        first, weight_in, weight_down, cot_cores, cot[0], grad_hidden[0]
+    )
+    middle = gather_middle(block, first)
     cot[1], grad_hidden[1] = tiled_call(
         meet_kernel, "meet_cotangent", [cot_y, cot_xy, *cot_cores], [(weight_down, True)],
         [(model, low), (units, wide)],
@@ -1995,7 +2011,17 @@
     grad_gain1 = jnp.sum(grad_normed1 * own_tokens * own_factor, axis=0)
     tokens_grad = (grad_hidden1 + back1).astype(low)
     gain_got = row_swap(grad_gain1[None])
-    tokens_grad, gain_got, out_near, line.flying = together(tokens_grad, gain_got, out_near, line.flying)
+    out_near, tokens_grad = together(out_near, tokens_grad)
+    d_mamba_out, d_attn_out = finalize_blocks(
+        flags, pick_chosen(flags, out, (0,)), out_far, out_near,
+        [
+            (mamba_out_proj.shape, (channels, width), row_index_map, slice(0, channels), every),
+            (attn_out_proj.shape, (query_width, width), row_index_map, slice(channels, None), every),
+        ],
+    )
+    tokens_grad, gain_got, d_mamba_out, d_attn_out, line.flying = together(
+        tokens_grad, gain_got, d_mamba_out, d_attn_out, line.flying
+    )
     small = jnp.concatenate(
         [
             small[:14], grad_gain1[None] + gain_got, jnp.zeros((1, width), wide),
@@ -2012,13 +2038,6 @@
     )
     small_got, d_conv = together(small_got, d_conv)
     sums = dp_rest(small + small_got)
-    d_mamba_out, d_attn_out = finalize_blocks(
-        flags, pick_chosen(flags, out, (0,)), out_far, out_near,
-        [
-            (mamba_out_proj.shape, (channels, width), row_index_map, slice(0, channels), every),
-            (attn_out_proj.shape, (query_width, width), row_index_map, slice(channels, None), every),
-        ],
-    )
     extra = jnp.where(flags[1] == 1, total[:, :, channels:], final[:, :, channels:]).astype(wide)
     d_shared = jnp.concatenate([extra[0], extra[1]], axis=1)
     d_key, d_value = extra[2], extra[3]

time: 932 us -> 918 us (0.985)
  Pallas kernels: 442 us -> 412 us
  waiting for transfers between devices: 236 us -> 253 us
    ppermute x70, waiting for transfers between devices: 127 us -> 149 us  [col_swap(): lax.ppermute(values, 'col', [(i, i ^ distance) for i in range(count)])]
    pallas_call x2, Pallas kernels: 61.8 us -> 49.1 us  [mamba_backward(): pl.pallas_call(partial(mamba_backward_kernel, head_width=head_width, plac...]
    pallas_call x7, Pallas kernels: 83.3 us -> 72.4 us  [tiled_call(): pl.pallas_call(partial(kernel, split=split), grid=(tiles,), in_specs=spec...]
  transfers between devices with their start and end apart: 109 -> 109, of which waited for: 40 -> 45; matrix products, arithmetic and copies ran while one was open for 5% -> 6% of each run, Pallas kernels for 42% -> 40%
where the time goes in v4:
time: 918 us; the launch traced here: 905 us
  Pallas kernels  412 us (45%)
  waiting for transfers between devices  253 us (28%)
  starting transfers between devices  102 us (11%)
  local copies, waits for them, and re-layouts  80.6 us (9%)
  other arithmetic  40.5 us (4%)
  between operations  16.3 us (2%)
    ppermute x70, waiting for transfers between devices, col_swap(): lax.ppermute(values, 'col', [(i, i ^ distance) for i in range(count)])  149 us
    pallas_call x7, Pallas kernels, tiled_call(): pl.pallas_call(partial(kernel, split=split), grid=(tiles,), in_specs=spec...  72.4 us
    pallas_call x8, Pallas kernels, spread(): pl.pallas_call(partial(spread_kernel, transposed=transposed), grid=(4,),...  70.8 us
    unnamed x380, local copies, waits for them, and re-layouts  64.1 us
    pallas_call x6, Pallas kernels, weight_grad(): pl.pallas_call(weight_grad_kernel, grid=(4,), in_specs=[left, left, right...  59.5 us
    ppermute x20, waiting for transfers between devices, row_swap(): return lax.ppermute(values, 'row', [(0, 1), (1, 0)])  56.5 us
    pallas_call x2, Pallas kernels, mamba_backward(): pl.pallas_call(partial(mamba_backward_kernel, head_width=head_width, plac...  49.1 us
    ppermute x8, waiting for transfers between devices, _start(): move = lax.ppermute(self.sent, 'dp', [(0, 1), (3, 2), (1, 0), (2, 3)])  41.5 us
  transfers between devices with their start and end apart: 109, of which 45 were waited for; matrix products, arithmetic and copies ran while one was open for 6% of the time, Pallas kernels for 40%

profile of v4, /device:TPU:0, one launch (start us, length us, event | category | flops | bytes accessed | tf_op | source)
XLA Modules:
  0.0 904.7 jit_solution(7463850041980503479)
XLA Ops:
  47.4 16.5 %collective-permute-done.4.refs_0_ = bf16[1024,512]{1,0:T(8,128)(2,1)S(1)} collective-permute-done((bf16[1024,512]{1,0:T(8,128)(2,1)S(1)}, bf16[1024,512]{1,0:T(8,128)(2,1)S(1)}, u32[]{:S(2)}, u32[]{:S(2)}) %collective-permute-start.4) | collective-permute-done | bytes 1048608 | tf_op jit(solution)/shard_map/ppermute | solution.py:592
  73.3 11.9 %collective-permute-done.11.refs_3_ = bf16[1,512,768]{2,1,0:T(8,128)(2,1)S(1)} collective-permute-done((bf16[1,512,768]{2,1,0:T(8,128)(2,1)S(1)}, bf16[1,512,768]{2,1,0:T(8,128)(2,1)S(1)}, u32[]{:S(2)}, u32[]{:S(2)}) %collective-permute-start.11) | collective-permute-done | bytes 786464 | tf_op jit(solution)/shard_map/ppermute | solution.py:588
  86.0 9.5 %collective-permute-done.7.refs_1_ = bf16[512,512]{1,0:T(8,128)(2,1)S(1)} collective-permute-done((bf16[512,512]{1,0:T(8,128)(2,1)S(1)}, bf16[512,512]{1,0:T(8,128)(2,1)S(1)}, u32[]{:S(2)}, u32[]{:S(2)}) %collective-permute-start.7) | collective-permute-done | bytes 524320 | tf_op jit(solution)/shard_map/ppermute | solution.py:588
  114.7 14.7 %project.2 = (bf16[1024,2048]{1,0:T(8,128)(2,1)}, f32[1024,128]{1,0:T(8,128)}, bf16[1024,1664]{1,0:T(8,128)(2,1)}, f32[1024,128]{1,0:T(8,128)}) custom-call(bf16[1024,512]{1,0:T(8,128)(2,1)} %copy-done.145, bf16[512,512]{1,0:T(8,128)(2,1)} %copy-done.164, bf16[512,512]{1,0:T(8,128)(2,1)} %copy-done.162, bf16[1024,512]{1,0:T(8,128)(2,1)} %copy-done.152, ...), custom_call_target="tpu_custom_call" | custom-call | flops 1 | bytes 1 | tf_op jit(solution)/shard_map/project/pallas_call | solution.py:1155
  180.6 13.9 %project.3 = (bf16[1024,2048]{1,0:T(8,128)(2,1)}, f32[1024,128]{1,0:T(8,128)}, bf16[1024,1664]{1,0:T(8,128)(2,1)}, f32[1024,128]{1,0:T(8,128)}) custom-call(bf16[1024,512]{1,0:T(8,128)(2,1)} %base_ref.1, bf16[1024,512]{1,0:T(8,128)(2,1)} %copy-done.144, bf16[1024,512]{1,0:T(8,128)(2,1)} %copy-done.150, bf16[1024,512]{1,0:T(8,128)(2,1)} %collective-permute-done.9.refs_3_, ...), custom_call_target="tpu_custom_call" | custom-call | flops 1 | bytes 1 | tf_op jit(solution)/shard_map/project/pallas_call | solution.py:1155
  239.4 12.8 %collective-permute-done.26.refs_1_ = bf16[512,512]{1,0:T(8,128)(2,1)S(1)} collective-permute-done((bf16[512,512]{1,0:T(8,128)(2,1)S(1)}, bf16[512,512]{1,0:T(8,128)(2,1)S(1)}, u32[]{:S(2)}, u32[]{:S(2)}) %collective-permute-start.26) | collective-permute-done | bytes 524320 | tf_op jit(solution)/shard_map/ppermute | solution.py:588
  252.2 10.1 %collective-permute-done.27.refs_5_ = bf16[512,512]{1,0:T(8,128)(2,1)S(1)} collective-permute-done((bf16[512,512]{1,0:T(8,128)(2,1)S(1)}, bf16[512,512]{1,0:T(8,128)(2,1)S(1)}, u32[]{:S(2)}, u32[]{:S(2)}) %collective-permute-start.27) | collective-permute-done | bytes 524320 | tf_op jit(solution)/shard_map/ppermute | solution.py:588
  317.2 11.6 %ffn.2 = (bf16[1024,2048]{1,0:T(8,128)(2,1)}, f32[1024,128]{1,0:T(8,128)}, bf16[1024,512]{1,0:T(8,128)(2,1)}, bf16[1024,1024]{1,0:T(8,128)(2,1)}, f32[1024,128]{1,0:T(8,128)}) custom-call(bf16[1024,512]{1,0:T(8,128)(2,1)} %copy-done.147, bf16[512,512]{1,0:T(8,128)(2,1)} %copy-done.169, bf16[512,512]{1,0:T(8,128)(2,1)} %copy-done.170, ...), custom_call_target="tpu_custom_call" | custom-call | flops 1 | bytes 1 | tf_op jit(solution)/shard_map/ffn/pallas_call | solution.py:1155
  338.0 11.3 %ffn.3 = (bf16[1024,2048]{1,0:T(8,128)(2,1)}, f32[1024,128]{1,0:T(8,128)}, bf16[1024,512]{1,0:T(8,128)(2,1)}, bf16[1024,1024]{1,0:T(8,128)(2,1)}, f32[1024,128]{1,0:T(8,128)}) custom-call(bf16[1024,512]{1,0:T(8,128)(2,1)} %copy-done.103, bf16[1024,512]{1,0:T(8,128)(2,1)} %copy-done.146, bf16[1024,512]{1,0:T(8,128)(2,1)} %copy-done.151, ...), custom_call_target="tpu_custom_call" | custom-call | flops 1 | bytes 1 | tf_op jit(solution)/shard_map/ffn/pallas_call | solution.py:1155
  352.8 9.1 %spread.11 = (bf16[2,1024,512]{2,1,0:T(8,128)(2,1)}, bf16[2,1024,512]{2,1,0:T(8,128)(2,1)}) custom-call(bf16[1024,1024]{1,0:T(8,128)(2,1)} %get-tuple-element.491.refs_0_.latter_0, bf16[2048,1024]{1,0:T(8,128)(2,1)} %bitcast.111), custom_call_target="tpu_custom_call" | custom-call | flops 1 | bytes 1 | tf_op jit(solution)/shard_map/spread/pallas_call | solution.py:1232
  377.8 9.8 %collective-permute-done.44 = f32[8,128]{1,0:T(8,128)S(1)} collective-permute-done((f32[8,128]{1,0:T(8,128)S(1)}, f32[8,128]{1,0:T(8,128)S(1)}, u32[]{:S(2)}, u32[]{:S(2)}) %collective-permute-start.44) | collective-permute-done | bytes 4128 | tf_op jit(solution)/shard_map/ppermute | solution.py:592
  436.9 10.7 %collective-permute-done.52.refs_0_ = bf16[1024,512]{1,0:T(8,128)(2,1)S(1)} collective-permute-done((bf16[1024,512]{1,0:T(8,128)(2,1)S(1)}, bf16[1024,512]{1,0:T(8,128)(2,1)S(1)}, u32[]{:S(2)}, u32[]{:S(2)}) %collective-permute-start.52) | collective-permute-done | bytes 1048608 | tf_op jit(solution)/shard_map/ppermute | solution.py:592
  526.8 10.8 %weight_grad.10.refs_0_.refs_1_ = bf16[4,512,768]{2,1,0:T(8,128)(2,1)} custom-call(bf16[1024,2048]{1,0:T(8,128)(2,1)} %get-tuple-element.562.former_0, bf16[1024,2048]{1,0:T(8,128)(2,1)} %get-tuple-element.563.former_1, bf16[1024,768]{1,0:T(8,128)(2,1)} %copy-done.55, bf16[1024,768]{1,0:T(8,128)(2,1)} %copy-done.56), custom_call_target="tpu_custom_call" | custom-call | flops 1 | bytes 1 | tf_op jit(solution)/shard_map/weight_grad/pallas_call | solution.py:1185
  542.0 24.6 %mamba_backward.2 = (bf16[1024,1024]{1,0:T(8,128)(2,1)}, f32[1024,128]{1,0:T(8,128)S(1)}, f32[16,512]{1,0:T(8,128)S(1)}) custom-call(bf16[1024,1664]{1,0:T(8,128)(2,1)} %get-tuple-element.380.query_ref.key_ref.value_ref.raw_ref.tail_ref, bf16[1024,1664]{1,0:T(8,128)(2,1)} %get-tuple-element.380.query_ref.key_ref.value_ref.raw_ref.tail_ref, ...), custom_call_target="tpu_custom_call" | custom-call | flops 1 | bytes 1 | tf_op jit(solution)/shard_map/mamba_backward/pallas_call | solution.py:538
  566.6 9.5 %collective-permute-done.66.refs_1_ = bf16[2,512,768]{2,1,0:T(8,128)(2,1)S(1)} collective-permute-done((bf16[2,512,768]{2,1,0:T(8,128)(2,1)}, bf16[2,512,768]{2,1,0:T(8,128)(2,1)S(1)}, u32[]{:S(2)}, u32[]{:S(2)}) %collective-permute-start.66) | collective-permute-done | bytes 1572896 | tf_op jit(solution)/shard_map/ppermute | solution.py:588
  594.9 24.5 %mamba_backward.3 = (bf16[1024,1024]{1,0:T(8,128)(2,1)}, f32[1024,128]{1,0:T(8,128)S(1)}, f32[16,512]{1,0:T(8,128)S(1)}) custom-call(bf16[1024,1664]{1,0:T(8,128)(2,1)} %get-tuple-element.416.query_ref.key_ref.value_ref.raw_ref.tail_ref, bf16[1024,1664]{1,0:T(8,128)(2,1)} %get-tuple-element.416.query_ref.key_ref.value_ref.raw_ref.tail_ref, ...), custom_call_target="tpu_custom_call" | custom-call | flops 1 | bytes 1 | tf_op jit(solution)/shard_map/mamba_backward/pallas_call | solution.py:538
  620.2 13.3 %weight_grad.11 = (bf16[4,512,512]{2,1,0:T(8,128)(2,1)}, bf16[4,512,512]{2,1,0:T(8,128)(2,1)}) custom-call(bf16[1024,2048]{1,0:T(8,128)(2,1)} %get-tuple-element.562.former_0, bf16[1024,2048]{1,0:T(8,128)(2,1)} %get-tuple-element.563.former_1, bf16[1024,1024]{1,0:T(8,128)(2,1)} %get-tuple-element.626.latter_0.refs_1_, ...), custom_call_target="tpu_custom_call" | custom-call | flops 1 | bytes 1 | tf_op jit(solution)/shard_map/weight_grad/pallas_call | solution.py:1185
  659.9 9.6 %collective-permute-done.74.refs_1_ = bf16[2,512,512]{2,1,0:T(8,128)(2,1)} collective-permute-done((bf16[2,512,512]{2,1,0:T(8,128)(2,1)}, bf16[2,512,512]{2,1,0:T(8,128)(2,1)}, u32[]{:S(2)}, u32[]{:S(2)}) %collective-permute-start.74) | collective-permute-done | bytes 1048608 | tf_op jit(solution)/shard_map/ppermute | solution.py:588
  683.9 9.4 %collective-permute-done.77.refs_1_.refs_5_ = bf16[2,512,256]{2,1,0:T(8,128)(2,1)S(1)} collective-permute-done((bf16[2,512,256]{2,1,0:T(8,128)(2,1)S(1)}, bf16[2,512,256]{2,1,0:T(8,128)(2,1)S(1)}, u32[]{:S(2)}, u32[]{:S(2)}) %collective-permute-start.77) | collective-permute-done | bytes 524320 | tf_op jit(solution)/shard_map/ppermute | solution.py:588
  693.3 10.7 %collective-permute-done.80.got_ref.end_ref = bf16[4,512,512]{2,1,0:T(8,128)(2,1)} collective-permute-done((bf16[4,512,512]{2,1,0:T(8,128)(2,1)}, bf16[4,512,512]{2,1,0:T(8,128)(2,1)}, u32[]{:S(2)}, u32[]{:S(2)}) %collective-permute-start.80) | collective-permute-done | bytes 2097184 | tf_op jit(solution)/shard_map/ppermute | solution.py:867
  725.4 12.9 %spread.14 = (bf16[2,1024,512]{2,1,0:T(8,128)(2,1)}, bf16[2,1024,512]{2,1,0:T(8,128)(2,1)}) custom-call(bf16[1024,768]{1,0:T(8,128)(2,1)} %copy-done.56, bf16[1024,1024]{1,0:T(8,128)(2,1)} %get-tuple-element.622.latter_1.refs_1_, bf16[2048,1792]{1,0:T(8,128)(2,1)} %bitcast.119), custom_call_target="tpu_custom_call" | custom-call | flops 1 | bytes 1 | tf_op jit(solution)/shard_map/spread/pallas_call | solution.py:1232
  738.3 12.9 %spread.15 = (bf16[2,1024,512]{2,1,0:T(8,128)(2,1)}, bf16[2,1024,512]{2,1,0:T(8,128)(2,1)}) custom-call(bf16[1024,768]{1,0:T(8,128)(2,1)} %copy-done.55, bf16[1024,1024]{1,0:T(8,128)(2,1)} %get-tuple-element.626.latter_0.refs_1_, bf16[2048,1792]{1,0:T(8,128)(2,1)} %bitcast.120), custom_call_target="tpu_custom_call" | custom-call | flops 1 | bytes 1 | tf_op jit(solution)/shard_map/spread/pallas_call | solution.py:1232
  751.3 16.7 %collective-permute-done.84.refs_1_ = bf16[2,512,512]{2,1,0:T(8,128)(2,1)} collective-permute-done((bf16[2,512,512]{2,1,0:T(8,128)(2,1)}, bf16[2,512,512]{2,1,0:T(8,128)(2,1)}, u32[]{:S(2)}, u32[]{:S(2)}) %collective-permute-start.84) | collective-permute-done | bytes 1048608 | tf_op jit(solution)/shard_map/ppermute | solution.py:588
  794.3 29.9 %collective-permute-done.96.last_ref = bf16[4,512,512]{2,1,0:T(8,128)(2,1)S(1)} collective-permute-done((bf16[4,512,512]{2,1,0:T(8,128)(2,1)S(1)}, bf16[4,512,512]{2,1,0:T(8,128)(2,1)S(1)}, u32[]{:S(2)}, u32[]{:S(2)}) %collective-permute-start.96) | collective-permute-done | bytes 2097184 | tf_op jit(solution)/shard_map/ppermute | solution.py:867
  (772 shorter events, 561.6 us)
Async XLA Ops:
  7.2 90.1 %all-gather.5.cloned.1.call-start = ((), (), s32[]{:S(2)}) async-start(), calls=%async_computation | async-start | bytes 2621440 | tf_op jit(solution)/shard_map/all_gather | solution.py:1663
  32.0 197.9 %all-gather.9.cloned.1.call-start = ((), (), s32[]{:S(2)}) async-start(), calls=%async_computation.2 | async-start | bytes 5242880 | tf_op jit(solution)/shard_map/all_gather | solution.py:1761
  156.9 110.7 %all-gather.7.cloned.1.call-start = ((), (), s32[]{:S(2)}) async-start(), calls=%async_computation.1 | async-start | bytes 3932160 | tf_op jit(solution)/shard_map/all_gather | solution.py:1663
  390.8 57.2 %collective-permute-start.54 = (bf16[4,512,512]{2,1,0:T(8,128)(2,1)}, bf16[4,512,512]{2,1,0:T(8,128)(2,1)}, u32[]{:S(2)}, u32[]{:S(2)}) collective-permute-start(bf16[4,512,512]{2,1,0:T(8,128)(2,1)} %weight_grad.6.former_ref), channel_id=1, source_target_pairs={{0,8},{24,16},{8,0},{16,24},{1,9},{25,17},{9,1},{17,25},{2,10},{26... | collective-permute-start | bytes 6291464 | tf_op jit(solution)/shard_map/ppermute | solution.py:867
  450.4 60.2 %collective-permute-start.63 = (bf16[4,512,512]{2,1,0:T(8,128)(2,1)S(1)}, bf16[4,512,512]{2,1,0:T(8,128)(2,1)}, u32[]{:S(2)}, u32[]{:S(2)}) collective-permute-start(bf16[4,512,512]{2,1,0:T(8,128)(2,1)S(1)} %copy-done.43), channel_id=1, source_target_pairs={{0,8},{24,16},{8,0},{16,24},{1,9},{25,17},{9,1},{17,25},{2,10},{26... | collective-permute-start | bytes 6291464 | tf_op jit(solution)/shard_map/ppermute | solution.py:867
  462.4 48.1 %collective-permute-start.61 = (bf16[2,1024,512]{2,1,0:T(8,128)(2,1)}, bf16[2,1024,512]{2,1,0:T(8,128)(2,1)}, u32[]{:S(2)}, u32[]{:S(2)}) collective-permute-start(bf16[2,1024,512]{2,1,0:T(8,128)(2,1)} %get-tuple-element.549), channel_id=1, source_target_pairs={{0,1},{1,0},{2,3},{3,2},{4,5},{5,4},{6,7},{7,6},{8,9},{9,8},{10,11... | collective-permute-start | bytes 6291464 | tf_op jit(solution)/shard_map/ppermute | solution.py:588
  463.1 47.4 %collective-permute-start.62 = (bf16[2,1024,512]{2,1,0:T(8,128)(2,1)}, bf16[2,1024,512]{2,1,0:T(8,128)(2,1)}, u32[]{:S(2)}, u32[]{:S(2)}) collective-permute-start(bf16[2,1024,512]{2,1,0:T(8,128)(2,1)} %get-tuple-element.550), channel_id=1, source_target_pairs={{0,1},{1,0},{2,3},{3,2},{4,5},{5,4},{6,7},{7,6},{8,9},{9,8},{10,11... | collective-permute-start | bytes 6291464 | tf_op jit(solution)/shard_map/ppermute | solution.py:588
  463.1 47.4 %collective-permute-start.64 = (bf16[4,512,512]{2,1,0:T(8,128)(2,1)S(1)}, bf16[4,512,512]{2,1,0:T(8,128)(2,1)}, u32[]{:S(2)}, u32[]{:S(2)}) collective-permute-start(bf16[4,512,512]{2,1,0:T(8,128)(2,1)S(1)} %add.188.pair_ref), channel_id=1, source_target_pairs={{8,16},{16,8},{9,17},{17,9},{10,18},{18,10},{11,19},{19,11},{12,20... | collective-permute-start | bytes 6291464 | tf_op jit(solution)/shard_map/ppermute | solution.py:871
  514.2 61.9 %collective-permute-start.68 = (bf16[4,512,512]{2,1,0:T(8,128)(2,1)}, bf16[4,512,512]{2,1,0:T(8,128)(2,1)}, u32[]{:S(2)}, u32[]{:S(2)}) collective-permute-start(bf16[4,512,512]{2,1,0:T(8,128)(2,1)} %get-tuple-element.572.pair_ref), channel_id=1, source_target_pairs={{8,16},{16,8},{9,17},{17,9},{10,18},{18,10},{11,19},{19,11},{12,20... | collective-permute-start | bytes 6291464 | tf_op jit(solution)/shard_map/ppermute | solution.py:871
  516.2 59.9 %collective-permute-start.67 = (bf16[4,512,512]{2,1,0:T(8,128)(2,1)S(1)}, bf16[4,512,512]{2,1,0:T(8,128)(2,1)S(1)}, u32[]{:S(2)}, u32[]{:S(2)}) collective-permute-start(bf16[4,512,512]{2,1,0:T(8,128)(2,1)S(1)} %get-tuple-element.558.middle_ref), channel_id=1, source_target_pairs={{0,8},{24,16},{8,0},{16,24},{1,9},{25,17},{9,1},{17,25},{2,10},{26... | collective-permute-start | bytes 6291464 | tf_op jit(solution)/shard_map/ppermute | solution.py:867
  525.8 50.3 %collective-permute-start.65 = (bf16[2,1024,512]{2,1,0:T(8,128)(2,1)}, bf16[2,1024,512]{2,1,0:T(8,128)(2,1)}, u32[]{:S(2)}, u32[]{:S(2)}) collective-permute-start(bf16[2,1024,512]{2,1,0:T(8,128)(2,1)} %add.189), channel_id=1, source_target_pairs={{0,4},{4,0},{1,5},{5,1},{2,6},{6,2},{3,7},{7,3},{8,12},{12,8},{9,1... | collective-permute-start | bytes 6291464 | tf_op jit(solution)/shard_map/ppermute | solution.py:592
  581.5 56.8 %collective-permute-start.73 = (bf16[4,512,512]{2,1,0:T(8,128)(2,1)}, bf16[4,512,512]{2,1,0:T(8,128)(2,1)}, u32[]{:S(2)}, u32[]{:S(2)}) collective-permute-start(bf16[4,512,512]{2,1,0:T(8,128)(2,1)} %get-tuple-element.590.pair_ref), channel_id=1, source_target_pairs={{8,16},{16,8},{9,17},{17,9},{10,18},{18,10},{11,19},{19,11},{12,20... | collective-permute-start | bytes 6291464 | tf_op jit(solution)/shard_map/ppermute | solution.py:871
  583.5 54.9 %collective-permute-start.72 = (bf16[4,512,512]{2,1,0:T(8,128)(2,1)}, bf16[4,512,512]{2,1,0:T(8,128)(2,1)S(1)}, u32[]{:S(2)}, u32[]{:S(2)}) collective-permute-start(bf16[4,512,512]{2,1,0:T(8,128)(2,1)} %get-tuple-element.576.middle_ref), channel_id=1, source_target_pairs={{0,8},{24,16},{8,0},{16,24},{1,9},{25,17},{9,1},{17,25},{2,10},{26... | collective-permute-start | bytes 6291464 | tf_op jit(solution)/shard_map/ppermute | solution.py:867
  587.5 50.9 %collective-permute-start.71 = (bf16[2,512,768]{2,1,0:T(8,128)(2,1)}, bf16[2,512,768]{2,1,0:T(8,128)(2,1)}, u32[]{:S(2)}, u32[]{:S(2)}) collective-permute-start(bf16[2,512,768]{2,1,0:T(8,128)(2,1)} %pick.15), channel_id=1, source_target_pairs={{0,1},{1,0},{2,3},{3,2},{4,5},{5,4},{6,7},{7,6},{8,9},{9,8},{10,11... | collective-permute-start | bytes 4718600 | tf_op jit(solution)/shard_map/ppermute | solution.py:588
  590.2 43.4 %collective-permute-start.69 = (bf16[1024,512]{1,0:T(8,128)(2,1)}, bf16[1024,512]{1,0:T(8,128)(2,1)}, u32[]{:S(2)}, u32[]{:S(2)}) collective-permute-start(bf16[1024,512]{1,0:T(8,128)(2,1)} %add_three.1), channel_id=1, source_target_pairs={{0,2},{1,3},{2,0},{3,1},{4,6},{5,7},{6,4},{7,5},{8,10},{9,11},{10,... | collective-permute-start | bytes 3145736 | tf_op jit(solution)/shard_map/ppermute | solution.py:588
  593.0 45.3 %collective-permute-start.70 = (bf16[2,512,512]{2,1,0:T(8,128)(2,1)}, bf16[2,512,512]{2,1,0:T(8,128)(2,1)}, u32[]{:S(2)}, u32[]{:S(2)}) collective-permute-start(bf16[2,512,512]{2,1,0:T(8,128)(2,1)} %pick_chosen.12), channel_id=1, source_target_pairs={{0,2},{1,3},{2,0},{3,1},{4,6},{5,7},{6,4},{7,5},{8,10},{9,11},{10,... | collective-permute-start | bytes 3145736 | tf_op jit(solution)/shard_map/ppermute | solution.py:588
  652.8 40.6 %collective-permute-start.81 = (bf16[4,512,512]{2,1,0:T(8,128)(2,1)}, bf16[4,512,512]{2,1,0:T(8,128)(2,1)}, u32[]{:S(2)}, u32[]{:S(2)}) collective-permute-start(bf16[4,512,512]{2,1,0:T(8,128)(2,1)} %get-tuple-element.613.pair_ref), channel_id=1, source_target_pairs={{8,16},{16,8},{9,17},{17,9},{10,18},{18,10},{11,19},{19,11},{12,20... | collective-permute-start | bytes 6291464 | tf_op jit(solution)/shard_map/ppermute | solution.py:871
  654.9 49.1 %collective-permute-start.80 = (bf16[4,512,512]{2,1,0:T(8,128)(2,1)}, bf16[4,512,512]{2,1,0:T(8,128)(2,1)}, u32[]{:S(2)}, u32[]{:S(2)}) collective-permute-start(bf16[4,512,512]{2,1,0:T(8,128)(2,1)} %get-tuple-element.612.middle_ref), channel_id=1, source_target_pairs={{0,8},{24,16},{8,0},{16,24},{1,9},{25,17},{9,1},{17,25},{2,10},{26... | collective-permute-start | bytes 6291464 | tf_op jit(solution)/shard_map/ppermute | solution.py:867
  711.3 56.7 %collective-permute-start.86 = (bf16[4,512,512]{2,1,0:T(8,128)(2,1)}, bf16[4,512,512]{2,1,0:T(8,128)(2,1)}, u32[]{:S(2)}, u32[]{:S(2)}) collective-permute-start(bf16[4,512,512]{2,1,0:T(8,128)(2,1)} %get-tuple-element.631.pair_ref), channel_id=1, source_target_pairs={{8,16},{16,8},{9,17},{17,9},{10,18},{18,10},{11,19},{19,11},{12,20... | collective-permute-start | bytes 6291464 | tf_op jit(solution)/shard_map/ppermute | solution.py:871
  713.2 54.8 %collective-permute-start.85 = (bf16[4,512,512]{2,1,0:T(8,128)(2,1)S(1)}, bf16[4,512,512]{2,1,0:T(8,128)(2,1)S(1)}, u32[]{:S(2)}, u32[]{:S(2)}) collective-permute-start(bf16[4,512,512]{2,1,0:T(8,128)(2,1)S(1)} %get-tuple-element.621.middle_ref), channel_id=1, source_target_pairs={{0,8},{24,16},{8,0},{16,24},{1,9},{25,17},{9,1},{17,25},{2,10},{26... | collective-permute-start | bytes 6291464 | tf_op jit(solution)/shard_map/ppermute | solution.py:867
  724.1 43.9 %collective-permute-start.84 = (bf16[2,512,512]{2,1,0:T(8,128)(2,1)}, bf16[2,512,512]{2,1,0:T(8,128)(2,1)}, u32[]{:S(2)}, u32[]{:S(2)}) collective-permute-start(bf16[2,512,512]{2,1,0:T(8,128)(2,1)} %pick_chosen.15), channel_id=1, source_target_pairs={{0,2},{1,3},{2,0},{3,1},{4,6},{5,7},{6,4},{7,5},{8,10},{9,11},{10,... | collective-permute-start | bytes 3145736 | tf_op jit(solution)/shard_map/ppermute | solution.py:588
  773.8 50.4 %collective-permute-start.96 = (bf16[4,512,512]{2,1,0:T(8,128)(2,1)S(1)}, bf16[4,512,512]{2,1,0:T(8,128)(2,1)S(1)}, u32[]{:S(2)}, u32[]{:S(2)}) collective-permute-start(bf16[4,512,512]{2,1,0:T(8,128)(2,1)S(1)} %get-tuple-element.638.total_ref), channel_id=1, source_target_pairs={{0,8},{24,16},{8,0},{16,24},{1,9},{25,17},{9,1},{17,25},{2,10},{26... | collective-permute-start | bytes 6291464 | tf_op jit(solution)/shard_map/ppermute | solution.py:867
  786.0 38.9 %collective-permute-start.90 = (bf16[2,512,512]{2,1,0:T(8,128)(2,1)S(1)}, bf16[2,512,512]{2,1,0:T(8,128)(2,1)}, u32[]{:S(2)}, u32[]{:S(2)}) collective-permute-start(bf16[2,512,512]{2,1,0:T(8,128)(2,1)S(1)} %get-tuple-element.644), channel_id=1, source_target_pairs={{0,4},{4,0},{1,5},{5,1},{2,6},{6,2},{3,7},{7,3},{8,12},{12,8},{9,1... | collective-permute-start | bytes 3145736 | tf_op jit(solution)/shard_map/ppermute | solution.py:592
  827.9 48.7 %collective-permute-start.103 = (bf16[4,512,512]{2,1,0:T(8,128)(2,1)}, bf16[4,512,512]{2,1,0:T(8,128)(2,1)}, u32[]{:S(2)}, u32[]{:S(2)}) collective-permute-start(bf16[4,512,512]{2,1,0:T(8,128)(2,1)} %add.191.total_ref), channel_id=1, source_target_pairs={{0,8},{24,16},{8,0},{16,24},{1,9},{25,17},{9,1},{17,25},{2,10},{26... | collective-permute-start | bytes 6291464 | tf_op jit(solution)/shard_map/ppermute | solution.py:867
  (275 other events, 2919.5 us)
Sparse Core Ops, SparseCore 0:
  32.2 45.2 all-gather.4
  157.0 44.5 all-gather.8
  203.2 64.3 all-gather.6

commit v5 on v4

--- a/solution.py
+++ b/solution.py
@@ -1892,10 +1892,11 @@
     first = weight_grad(normed1, early, width, 0, [at_shared])
     first_far = far_pair(first)
     mamba_step(1, first)
-    late[1], output_got, output_near, first_far, line.flying = together(
-        late[1], output_got, output_far[0], first_far, line.flying
+    late[1], output_got, output_near, line.flying = together(
+        late[1], output_got, output_far[0], line.flying
     )
     line.advance(out)
+    first_far = after(first_far, line.sent)
     first_near = near_pair(first, first_far)
     output_sent = add_three(output_shares[0][0], output_near, output_got, 1)
     output_last = col_swap(output_sent, 2)
@@ -2019,9 +2020,7 @@
             (attn_out_proj.shape, (query_width, width), row_index_map, slice(channels, None), every),
         ],
     )
-    tokens_grad, gain_got, d_mamba_out, d_attn_out, line.flying = together(
-        tokens_grad, gain_got, d_mamba_out, d_attn_out, line.flying
-    )
+    gain_got, d_mamba_out, d_attn_out = together(gain_got, d_mamba_out, d_attn_out)
     small = jnp.concatenate(
         [
             small[:14], grad_gain1[None] + gain_got, jnp.zeros((1, width), wide),
@@ -2030,13 +2029,13 @@
         axis=0,
     )
     small_got = dp_part(small, 1)
+    tokens_grad, small, small_got, line.flying = together(tokens_grad, small, small_got, line.flying)
     line.finish()
     total, final = line.done[5]
     (d_conv,) = finalize(
         flags, total, final, (None, width, channels + part // 2), piece_index,
         [(proj_conv.shape, (width, channels), column_index_map, every, slice(0, channels))],
     )
-    small_got, d_conv = together(small_got, d_conv)
     sums = dp_rest(small + small_got)
     extra = jnp.where(flags[1] == 1, total[:, :, channels:], final[:, :, channels:]).astype(wide)
     d_shared = jnp.concatenate([extra[0], extra[1]], axis=1)

time: 918 us -> 913 us (level)
    ppermute x70, waiting for transfers between devices: 149 us -> 140 us  [col_swap(): lax.ppermute(values, 'col', [(i, i ^ distance) for i in range(count)])]
where the time goes in v5:
time: 913 us; the launch traced here: 900 us
  Pallas kernels  411 us (45%)
  waiting for transfers between devices  247 us (27%)
  starting transfers between devices  105 us (12%)
  local copies, waits for them, and re-layouts  81 us (9%)
  other arithmetic  40.5 us (4%)
  between operations  16.3 us (2%)
    ppermute x70, waiting for transfers between devices, col_swap(): lax.ppermute(values, 'col', [(i, i ^ distance) for i in range(count)])  140 us
    pallas_call x7, Pallas kernels, tiled_call(): pl.pallas_call(partial(kernel, split=split), grid=(tiles,), in_specs=spec...  72.4 us
    pallas_call x8, Pallas kernels, spread(): pl.pallas_call(partial(spread_kernel, transposed=transposed), grid=(4,),...  70.7 us
    unnamed x380, local copies, waits for them, and re-layouts  64.5 us
    ppermute x20, waiting for transfers between devices, row_swap(): return lax.ppermute(values, 'row', [(0, 1), (1, 0)])  61.1 us
    pallas_call x6, Pallas kernels, weight_grad(): pl.pallas_call(weight_grad_kernel, grid=(4,), in_specs=[left, left, right...  59.5 us
    pallas_call x2, Pallas kernels, mamba_backward(): pl.pallas_call(partial(mamba_backward_kernel, head_width=head_width, plac...  49.1 us
    ppermute x8, waiting for transfers between devices, _start(): move = lax.ppermute(self.sent, 'dp', [(0, 1), (3, 2), (1, 0), (2, 3)])  42.1 us
  transfers between devices with their start and end apart: 109, of which 45 were waited for; matrix products, arithmetic and copies ran while one was open for 6% of the time, Pallas kernels for 40%

profile of v5, /device:TPU:0, one launch (start us, length us, event | category | flops | bytes accessed | tf_op | source)
XLA Modules:
  0.0 899.6 jit_solution(8630153576606223422)
XLA Ops:
  47.4 16.5 %collective-permute-done.4.refs_0_ = bf16[1024,512]{1,0:T(8,128)(2,1)S(1)} collective-permute-done((bf16[1024,512]{1,0:T(8,128)(2,1)S(1)}, bf16[1024,512]{1,0:T(8,128)(2,1)S(1)}, u32[]{:S(2)}, u32[]{:S(2)}) %collective-permute-start.4) | collective-permute-done | bytes 1048608 | tf_op jit(solution)/shard_map/ppermute | solution.py:592
  73.3 11.9 %collective-permute-done.11.refs_3_ = bf16[1,512,768]{2,1,0:T(8,128)(2,1)S(1)} collective-permute-done((bf16[1,512,768]{2,1,0:T(8,128)(2,1)S(1)}, bf16[1,512,768]{2,1,0:T(8,128)(2,1)S(1)}, u32[]{:S(2)}, u32[]{:S(2)}) %collective-permute-start.11) | collective-permute-done | bytes 786464 | tf_op jit(solution)/shard_map/ppermute | solution.py:588
  86.0 9.5 %collective-permute-done.7.refs_1_ = bf16[512,512]{1,0:T(8,128)(2,1)S(1)} collective-permute-done((bf16[512,512]{1,0:T(8,128)(2,1)S(1)}, bf16[512,512]{1,0:T(8,128)(2,1)S(1)}, u32[]{:S(2)}, u32[]{:S(2)}) %collective-permute-start.7) | collective-permute-done | bytes 524320 | tf_op jit(solution)/shard_map/ppermute | solution.py:588
  114.7 14.7 %project.2 = (bf16[1024,2048]{1,0:T(8,128)(2,1)}, f32[1024,128]{1,0:T(8,128)}, bf16[1024,1664]{1,0:T(8,128)(2,1)}, f32[1024,128]{1,0:T(8,128)}) custom-call(bf16[1024,512]{1,0:T(8,128)(2,1)} %copy-done.145, bf16[512,512]{1,0:T(8,128)(2,1)} %copy-done.164, bf16[512,512]{1,0:T(8,128)(2,1)} %copy-done.162, bf16[1024,512]{1,0:T(8,128)(2,1)} %copy-done.152, ...), custom_call_target="tpu_custom_call" | custom-call | flops 1 | bytes 1 | tf_op jit(solution)/shard_map/project/pallas_call | solution.py:1155
  180.6 13.9 %project.3 = (bf16[1024,2048]{1,0:T(8,128)(2,1)}, f32[1024,128]{1,0:T(8,128)}, bf16[1024,1664]{1,0:T(8,128)(2,1)}, f32[1024,128]{1,0:T(8,128)}) custom-call(bf16[1024,512]{1,0:T(8,128)(2,1)} %base_ref.1, bf16[1024,512]{1,0:T(8,128)(2,1)} %copy-done.144, bf16[1024,512]{1,0:T(8,128)(2,1)} %copy-done.150, bf16[1024,512]{1,0:T(8,128)(2,1)} %collective-permute-done.9.refs_3_, ...), custom_call_target="tpu_custom_call" | custom-call | flops 1 | bytes 1 | tf_op jit(solution)/shard_map/project/pallas_call | solution.py:1155
  239.4 12.8 %collective-permute-done.26.refs_1_ = bf16[512,512]{1,0:T(8,128)(2,1)S(1)} collective-permute-done((bf16[512,512]{1,0:T(8,128)(2,1)S(1)}, bf16[512,512]{1,0:T(8,128)(2,1)S(1)}, u32[]{:S(2)}, u32[]{:S(2)}) %collective-permute-start.26) | collective-permute-done | bytes 524320 | tf_op jit(solution)/shard_map/ppermute | solution.py:588
  252.2 10.1 %collective-permute-done.27.refs_5_ = bf16[512,512]{1,0:T(8,128)(2,1)S(1)} collective-permute-done((bf16[512,512]{1,0:T(8,128)(2,1)S(1)}, bf16[512,512]{1,0:T(8,128)(2,1)S(1)}, u32[]{:S(2)}, u32[]{:S(2)}) %collective-permute-start.27) | collective-permute-done | bytes 524320 | tf_op jit(solution)/shard_map/ppermute | solution.py:588
  317.2 11.6 %ffn.2 = (bf16[1024,2048]{1,0:T(8,128)(2,1)}, f32[1024,128]{1,0:T(8,128)}, bf16[1024,512]{1,0:T(8,128)(2,1)}, bf16[1024,1024]{1,0:T(8,128)(2,1)}, f32[1024,128]{1,0:T(8,128)}) custom-call(bf16[1024,512]{1,0:T(8,128)(2,1)} %copy-done.147, bf16[512,512]{1,0:T(8,128)(2,1)} %copy-done.169, bf16[512,512]{1,0:T(8,128)(2,1)} %copy-done.170, ...), custom_call_target="tpu_custom_call" | custom-call | flops 1 | bytes 1 | tf_op jit(solution)/shard_map/ffn/pallas_call | solution.py:1155
  328.8 9.1 %spread.10 = (bf16[2,1024,512]{2,1,0:T(8,128)(2,1)}, bf16[2,1024,512]{2,1,0:T(8,128)(2,1)}) custom-call(bf16[1024,1024]{1,0:T(8,128)(2,1)} %get-tuple-element.516.refs_0_.latter_1, bf16[2048,1024]{1,0:T(8,128)(2,1)} %bitcast.109), custom_call_target="tpu_custom_call" | custom-call | flops 1 | bytes 1 | tf_op jit(solution)/shard_map/spread/pallas_call | solution.py:1232
  338.0 11.3 %ffn.3 = (bf16[1024,2048]{1,0:T(8,128)(2,1)}, f32[1024,128]{1,0:T(8,128)}, bf16[1024,512]{1,0:T(8,128)(2,1)}, bf16[1024,1024]{1,0:T(8,128)(2,1)}, f32[1024,128]{1,0:T(8,128)}) custom-call(bf16[1024,512]{1,0:T(8,128)(2,1)} %copy-done.103, bf16[1024,512]{1,0:T(8,128)(2,1)} %copy-done.146, bf16[1024,512]{1,0:T(8,128)(2,1)} %copy-done.151, ...), custom_call_target="tpu_custom_call" | custom-call | flops 1 | bytes 1 | tf_op jit(solution)/shard_map/ffn/pallas_call | solution.py:1155
  352.8 9.1 %spread.11 = (bf16[2,1024,512]{2,1,0:T(8,128)(2,1)}, bf16[2,1024,512]{2,1,0:T(8,128)(2,1)}) custom-call(bf16[1024,1024]{1,0:T(8,128)(2,1)} %get-tuple-element.491.refs_0_.latter_0, bf16[2048,1024]{1,0:T(8,128)(2,1)} %bitcast.111), custom_call_target="tpu_custom_call" | custom-call | flops 1 | bytes 1 | tf_op jit(solution)/shard_map/spread/pallas_call | solution.py:1232
  377.8 9.8 %collective-permute-done.44 = f32[8,128]{1,0:T(8,128)S(1)} collective-permute-done((f32[8,128]{1,0:T(8,128)S(1)}, f32[8,128]{1,0:T(8,128)S(1)}, u32[]{:S(2)}, u32[]{:S(2)}) %collective-permute-start.44) | collective-permute-done | bytes 4128 | tf_op jit(solution)/shard_map/ppermute | solution.py:592
  436.9 10.7 %collective-permute-done.52.refs_0_ = bf16[1024,512]{1,0:T(8,128)(2,1)S(1)} collective-permute-done((bf16[1024,512]{1,0:T(8,128)(2,1)S(1)}, bf16[1024,512]{1,0:T(8,128)(2,1)S(1)}, u32[]{:S(2)}, u32[]{:S(2)}) %collective-permute-start.52) | collective-permute-done | bytes 1048608 | tf_op jit(solution)/shard_map/ppermute | solution.py:592
  526.8 10.8 %weight_grad.10.refs_0_.refs_1_ = bf16[4,512,768]{2,1,0:T(8,128)(2,1)} custom-call(bf16[1024,2048]{1,0:T(8,128)(2,1)} %get-tuple-element.562.former_0, bf16[1024,2048]{1,0:T(8,128)(2,1)} %get-tuple-element.563.former_1, bf16[1024,768]{1,0:T(8,128)(2,1)} %copy-done.55, bf16[1024,768]{1,0:T(8,128)(2,1)} %copy-done.56), custom_call_target="tpu_custom_call" | custom-call | flops 1 | bytes 1 | tf_op jit(solution)/shard_map/weight_grad/pallas_call | solution.py:1185
  542.0 24.6 %mamba_backward.2 = (bf16[1024,1024]{1,0:T(8,128)(2,1)}, f32[1024,128]{1,0:T(8,128)S(1)}, f32[16,512]{1,0:T(8,128)S(1)}) custom-call(bf16[1024,1664]{1,0:T(8,128)(2,1)} %get-tuple-element.380.query_ref.key_ref.value_ref.raw_ref.tail_ref, bf16[1024,1664]{1,0:T(8,128)(2,1)} %get-tuple-element.380.query_ref.key_ref.value_ref.raw_ref.tail_ref, ...), custom_call_target="tpu_custom_call" | custom-call | flops 1 | bytes 1 | tf_op jit(solution)/shard_map/mamba_backward/pallas_call | solution.py:538
  590.6 24.5 %mamba_backward.3 = (bf16[1024,1024]{1,0:T(8,128)(2,1)}, f32[1024,128]{1,0:T(8,128)S(1)}, f32[16,512]{1,0:T(8,128)S(1)}) custom-call(bf16[1024,1664]{1,0:T(8,128)(2,1)} %get-tuple-element.416.query_ref.key_ref.value_ref.raw_ref.tail_ref, bf16[1024,1664]{1,0:T(8,128)(2,1)} %get-tuple-element.416.query_ref.key_ref.value_ref.raw_ref.tail_ref, ...), custom_call_target="tpu_custom_call" | custom-call | flops 1 | bytes 1 | tf_op jit(solution)/shard_map/mamba_backward/pallas_call | solution.py:538
  615.9 13.3 %weight_grad.11 = (bf16[4,512,512]{2,1,0:T(8,128)(2,1)}, bf16[4,512,512]{2,1,0:T(8,128)(2,1)}) custom-call(bf16[1024,2048]{1,0:T(8,128)(2,1)} %get-tuple-element.562.former_0, bf16[1024,2048]{1,0:T(8,128)(2,1)} %get-tuple-element.563.former_1, bf16[1024,1024]{1,0:T(8,128)(2,1)} %get-tuple-element.626.latter_0.refs_1_, ...), custom_call_target="tpu_custom_call" | custom-call | flops 1 | bytes 1 | tf_op jit(solution)/shard_map/weight_grad/pallas_call | solution.py:1185
  655.5 9.7 %collective-permute-done.74.refs_1_ = bf16[2,512,512]{2,1,0:T(8,128)(2,1)} collective-permute-done((bf16[2,512,512]{2,1,0:T(8,128)(2,1)}, bf16[2,512,512]{2,1,0:T(8,128)(2,1)}, u32[]{:S(2)}, u32[]{:S(2)}) %collective-permute-start.74) | collective-permute-done | bytes 1048608 | tf_op jit(solution)/shard_map/ppermute | solution.py:588
  679.7 9.4 %collective-permute-done.77.refs_1_.refs_5_ = bf16[2,512,256]{2,1,0:T(8,128)(2,1)S(1)} collective-permute-done((bf16[2,512,256]{2,1,0:T(8,128)(2,1)S(1)}, bf16[2,512,256]{2,1,0:T(8,128)(2,1)S(1)}, u32[]{:S(2)}, u32[]{:S(2)}) %collective-permute-start.77) | collective-permute-done | bytes 524320 | tf_op jit(solution)/shard_map/ppermute | solution.py:588
  689.1 10.6 %collective-permute-done.80.got_ref.end_ref = bf16[4,512,512]{2,1,0:T(8,128)(2,1)} collective-permute-done((bf16[4,512,512]{2,1,0:T(8,128)(2,1)}, bf16[4,512,512]{2,1,0:T(8,128)(2,1)}, u32[]{:S(2)}, u32[]{:S(2)}) %collective-permute-start.80) | collective-permute-done | bytes 2097184 | tf_op jit(solution)/shard_map/ppermute | solution.py:867
  721.1 12.9 %spread.14 = (bf16[2,1024,512]{2,1,0:T(8,128)(2,1)}, bf16[2,1024,512]{2,1,0:T(8,128)(2,1)}) custom-call(bf16[1024,768]{1,0:T(8,128)(2,1)} %copy-done.56, bf16[1024,1024]{1,0:T(8,128)(2,1)} %get-tuple-element.622.latter_1.refs_1_, bf16[2048,1792]{1,0:T(8,128)(2,1)} %bitcast.119), custom_call_target="tpu_custom_call" | custom-call | flops 1 | bytes 1 | tf_op jit(solution)/shard_map/spread/pallas_call | solution.py:1232
  734.0 12.9 %spread.15 = (bf16[2,1024,512]{2,1,0:T(8,128)(2,1)}, bf16[2,1024,512]{2,1,0:T(8,128)(2,1)}) custom-call(bf16[1024,768]{1,0:T(8,128)(2,1)} %copy-done.55, bf16[1024,1024]{1,0:T(8,128)(2,1)} %get-tuple-element.626.latter_0.refs_1_, bf16[2048,1792]{1,0:T(8,128)(2,1)} %bitcast.120), custom_call_target="tpu_custom_call" | custom-call | flops 1 | bytes 1 | tf_op jit(solution)/shard_map/spread/pallas_call | solution.py:1232
  746.9 16.7 %collective-permute-done.84.refs_1_ = bf16[2,512,512]{2,1,0:T(8,128)(2,1)} collective-permute-done((bf16[2,512,512]{2,1,0:T(8,128)(2,1)}, bf16[2,512,512]{2,1,0:T(8,128)(2,1)}, u32[]{:S(2)}, u32[]{:S(2)}) %collective-permute-start.84) | collective-permute-done | bytes 1048608 | tf_op jit(solution)/shard_map/ppermute | solution.py:588
  790.0 29.8 %collective-permute-done.96.last_ref = bf16[4,512,512]{2,1,0:T(8,128)(2,1)S(1)} collective-permute-done((bf16[4,512,512]{2,1,0:T(8,128)(2,1)S(1)}, bf16[4,512,512]{2,1,0:T(8,128)(2,1)S(1)}, u32[]{:S(2)}, u32[]{:S(2)}) %collective-permute-start.96) | collective-permute-done | bytes 2097184 | tf_op jit(solution)/shard_map/ppermute | solution.py:867
  (772 shorter events, 557.0 us)
Async XLA Ops:
  7.2 90.1 %all-gather.5.cloned.1.call-start = ((), (), s32[]{:S(2)}) async-start(), calls=%async_computation | async-start | bytes 2621440 | tf_op jit(solution)/shard_map/all_gather | solution.py:1663
  32.0 197.9 %all-gather.9.cloned.1.call-start = ((), (), s32[]{:S(2)}) async-start(), calls=%async_computation.2 | async-start | bytes 5242880 | tf_op jit(solution)/shard_map/all_gather | solution.py:1761
  156.9 110.7 %all-gather.7.cloned.1.call-start = ((), (), s32[]{:S(2)}) async-start(), calls=%async_computation.1 | async-start | bytes 3932160 | tf_op jit(solution)/shard_map/all_gather | solution.py:1663
  390.8 57.2 %collective-permute-start.54 = (bf16[4,512,512]{2,1,0:T(8,128)(2,1)}, bf16[4,512,512]{2,1,0:T(8,128)(2,1)}, u32[]{:S(2)}, u32[]{:S(2)}) collective-permute-start(bf16[4,512,512]{2,1,0:T(8,128)(2,1)} %weight_grad.6.former_ref), channel_id=1, source_target_pairs={{0,8},{24,16},{8,0},{16,24},{1,9},{25,17},{9,1},{17,25},{2,10},{26... | collective-permute-start | bytes 6291464 | tf_op jit(solution)/shard_map/ppermute | solution.py:867
  450.4 60.2 %collective-permute-start.63 = (bf16[4,512,512]{2,1,0:T(8,128)(2,1)S(1)}, bf16[4,512,512]{2,1,0:T(8,128)(2,1)}, u32[]{:S(2)}, u32[]{:S(2)}) collective-permute-start(bf16[4,512,512]{2,1,0:T(8,128)(2,1)S(1)} %copy-done.43), channel_id=1, source_target_pairs={{0,8},{24,16},{8,0},{16,24},{1,9},{25,17},{9,1},{17,25},{2,10},{26... | collective-permute-start | bytes 6291464 | tf_op jit(solution)/shard_map/ppermute | solution.py:867
  462.4 48.1 %collective-permute-start.61 = (bf16[2,1024,512]{2,1,0:T(8,128)(2,1)}, bf16[2,1024,512]{2,1,0:T(8,128)(2,1)}, u32[]{:S(2)}, u32[]{:S(2)}) collective-permute-start(bf16[2,1024,512]{2,1,0:T(8,128)(2,1)} %get-tuple-element.549), channel_id=1, source_target_pairs={{0,1},{1,0},{2,3},{3,2},{4,5},{5,4},{6,7},{7,6},{8,9},{9,8},{10,11... | collective-permute-start | bytes 6291464 | tf_op jit(solution)/shard_map/ppermute | solution.py:588
  463.1 47.4 %collective-permute-start.62 = (bf16[2,1024,512]{2,1,0:T(8,128)(2,1)}, bf16[2,1024,512]{2,1,0:T(8,128)(2,1)}, u32[]{:S(2)}, u32[]{:S(2)}) collective-permute-start(bf16[2,1024,512]{2,1,0:T(8,128)(2,1)} %get-tuple-element.550), channel_id=1, source_target_pairs={{0,1},{1,0},{2,3},{3,2},{4,5},{5,4},{6,7},{7,6},{8,9},{9,8},{10,11... | collective-permute-start | bytes 6291464 | tf_op jit(solution)/shard_map/ppermute | solution.py:588
  463.1 47.4 %collective-permute-start.64 = (bf16[4,512,512]{2,1,0:T(8,128)(2,1)S(1)}, bf16[4,512,512]{2,1,0:T(8,128)(2,1)}, u32[]{:S(2)}, u32[]{:S(2)}) collective-permute-start(bf16[4,512,512]{2,1,0:T(8,128)(2,1)S(1)} %add.188.pair_ref), channel_id=1, source_target_pairs={{8,16},{16,8},{9,17},{17,9},{10,18},{18,10},{11,19},{19,11},{12,20... | collective-permute-start | bytes 6291464 | tf_op jit(solution)/shard_map/ppermute | solution.py:871
  514.2 52.4 %collective-permute-start.67 = (bf16[4,512,512]{2,1,0:T(8,128)(2,1)}, bf16[4,512,512]{2,1,0:T(8,128)(2,1)}, u32[]{:S(2)}, u32[]{:S(2)}) collective-permute-start(bf16[4,512,512]{2,1,0:T(8,128)(2,1)} %get-tuple-element.572.pair_ref), channel_id=1, source_target_pairs={{8,16},{16,8},{9,17},{17,9},{10,18},{18,10},{11,19},{19,11},{12,20... | collective-permute-start | bytes 6291464 | tf_op jit(solution)/shard_map/ppermute | solution.py:871
  516.2 52.0 %collective-permute-start.66 = (bf16[4,512,512]{2,1,0:T(8,128)(2,1)S(1)}, bf16[4,512,512]{2,1,0:T(8,128)(2,1)S(1)}, u32[]{:S(2)}, u32[]{:S(2)}) collective-permute-start(bf16[4,512,512]{2,1,0:T(8,128)(2,1)S(1)} %get-tuple-element.558.middle_ref), channel_id=1, source_target_pairs={{0,8},{24,16},{8,0},{16,24},{1,9},{25,17},{9,1},{17,25},{2,10},{26... | collective-permute-start | bytes 6291464 | tf_op jit(solution)/shard_map/ppermute | solution.py:867
  525.8 47.0 %collective-permute-start.65 = (bf16[2,1024,512]{2,1,0:T(8,128)(2,1)}, bf16[2,1024,512]{2,1,0:T(8,128)(2,1)}, u32[]{:S(2)}, u32[]{:S(2)}) collective-permute-start(bf16[2,1024,512]{2,1,0:T(8,128)(2,1)} %add.189), channel_id=1, source_target_pairs={{0,4},{4,0},{1,5},{5,1},{2,6},{6,2},{3,7},{7,3},{8,12},{12,8},{9,1... | collective-permute-start | bytes 6291464 | tf_op jit(solution)/shard_map/ppermute | solution.py:592
  540.7 40.8 %collective-permute-start.70 = (bf16[2,512,768]{2,1,0:T(8,128)(2,1)}, bf16[2,512,768]{2,1,0:T(8,128)(2,1)S(1)}, u32[]{:S(2)}, u32[]{:S(2)}) collective-permute-start(bf16[2,512,768]{2,1,0:T(8,128)(2,1)} %pick.14), channel_id=1, source_target_pairs={{0,2},{1,3},{2,0},{3,1},{4,6},{5,7},{6,4},{7,5},{8,10},{9,11},{10,... | collective-permute-start | bytes 4718600 | tf_op jit(solution)/shard_map/ppermute | solution.py:588
  577.0 57.2 %collective-permute-start.73 = (bf16[4,512,512]{2,1,0:T(8,128)(2,1)}, bf16[4,512,512]{2,1,0:T(8,128)(2,1)}, u32[]{:S(2)}, u32[]{:S(2)}) collective-permute-start(bf16[4,512,512]{2,1,0:T(8,128)(2,1)} %get-tuple-element.590.pair_ref), channel_id=1, source_target_pairs={{8,16},{16,8},{9,17},{17,9},{10,18},{18,10},{11,19},{19,11},{12,20... | collective-permute-start | bytes 6291464 | tf_op jit(solution)/shard_map/ppermute | solution.py:871
  578.9 55.2 %collective-permute-start.72 = (bf16[4,512,512]{2,1,0:T(8,128)(2,1)}, bf16[4,512,512]{2,1,0:T(8,128)(2,1)S(1)}, u32[]{:S(2)}, u32[]{:S(2)}) collective-permute-start(bf16[4,512,512]{2,1,0:T(8,128)(2,1)} %get-tuple-element.576.middle_ref), channel_id=1, source_target_pairs={{0,8},{24,16},{8,0},{16,24},{1,9},{25,17},{9,1},{17,25},{2,10},{26... | collective-permute-start | bytes 6291464 | tf_op jit(solution)/shard_map/ppermute | solution.py:867
  583.2 50.9 %collective-permute-start.71 = (bf16[2,512,768]{2,1,0:T(8,128)(2,1)}, bf16[2,512,768]{2,1,0:T(8,128)(2,1)}, u32[]{:S(2)}, u32[]{:S(2)}) collective-permute-start(bf16[2,512,768]{2,1,0:T(8,128)(2,1)} %pick.15), channel_id=1, source_target_pairs={{0,1},{1,0},{2,3},{3,2},{4,5},{5,4},{6,7},{7,6},{8,9},{9,8},{10,11... | collective-permute-start | bytes 4718600 | tf_op jit(solution)/shard_map/ppermute | solution.py:588
  585.9 43.4 %collective-permute-start.68 = (bf16[1024,512]{1,0:T(8,128)(2,1)}, bf16[1024,512]{1,0:T(8,128)(2,1)}, u32[]{:S(2)}, u32[]{:S(2)}) collective-permute-start(bf16[1024,512]{1,0:T(8,128)(2,1)} %add_three.1), channel_id=1, source_target_pairs={{0,2},{1,3},{2,0},{3,1},{4,6},{5,7},{6,4},{7,5},{8,10},{9,11},{10,... | collective-permute-start | bytes 3145736 | tf_op jit(solution)/shard_map/ppermute | solution.py:588
  588.8 45.3 %collective-permute-start.69 = (bf16[2,512,512]{2,1,0:T(8,128)(2,1)}, bf16[2,512,512]{2,1,0:T(8,128)(2,1)}, u32[]{:S(2)}, u32[]{:S(2)}) collective-permute-start(bf16[2,512,512]{2,1,0:T(8,128)(2,1)} %pick_chosen.12), channel_id=1, source_target_pairs={{0,2},{1,3},{2,0},{3,1},{4,6},{5,7},{6,4},{7,5},{8,10},{9,11},{10,... | collective-permute-start | bytes 3145736 | tf_op jit(solution)/shard_map/ppermute | solution.py:588
  648.5 40.6 %collective-permute-start.81 = (bf16[4,512,512]{2,1,0:T(8,128)(2,1)}, bf16[4,512,512]{2,1,0:T(8,128)(2,1)}, u32[]{:S(2)}, u32[]{:S(2)}) collective-permute-start(bf16[4,512,512]{2,1,0:T(8,128)(2,1)} %get-tuple-element.613.pair_ref), channel_id=1, source_target_pairs={{8,16},{16,8},{9,17},{17,9},{10,18},{18,10},{11,19},{19,11},{12,20... | collective-permute-start | bytes 6291464 | tf_op jit(solution)/shard_map/ppermute | solution.py:871
  650.7 49.0 %collective-permute-start.80 = (bf16[4,512,512]{2,1,0:T(8,128)(2,1)}, bf16[4,512,512]{2,1,0:T(8,128)(2,1)}, u32[]{:S(2)}, u32[]{:S(2)}) collective-permute-start(bf16[4,512,512]{2,1,0:T(8,128)(2,1)} %get-tuple-element.612.middle_ref), channel_id=1, source_target_pairs={{0,8},{24,16},{8,0},{16,24},{1,9},{25,17},{9,1},{17,25},{2,10},{26... | collective-permute-start | bytes 6291464 | tf_op jit(solution)/shard_map/ppermute | solution.py:867
  706.9 56.8 %collective-permute-start.86 = (bf16[4,512,512]{2,1,0:T(8,128)(2,1)}, bf16[4,512,512]{2,1,0:T(8,128)(2,1)}, u32[]{:S(2)}, u32[]{:S(2)}) collective-permute-start(bf16[4,512,512]{2,1,0:T(8,128)(2,1)} %get-tuple-element.631.pair_ref), channel_id=1, source_target_pairs={{8,16},{16,8},{9,17},{17,9},{10,18},{18,10},{11,19},{19,11},{12,20... | collective-permute-start | bytes 6291464 | tf_op jit(solution)/shard_map/ppermute | solution.py:871
  708.9 54.8 %collective-permute-start.85 = (bf16[4,512,512]{2,1,0:T(8,128)(2,1)S(1)}, bf16[4,512,512]{2,1,0:T(8,128)(2,1)S(1)}, u32[]{:S(2)}, u32[]{:S(2)}) collective-permute-start(bf16[4,512,512]{2,1,0:T(8,128)(2,1)S(1)} %get-tuple-element.621.middle_ref), channel_id=1, source_target_pairs={{0,8},{24,16},{8,0},{16,24},{1,9},{25,17},{9,1},{17,25},{2,10},{26... | collective-permute-start | bytes 6291464 | tf_op jit(solution)/shard_map/ppermute | solution.py:867
  719.8 43.9 %collective-permute-start.84 = (bf16[2,512,512]{2,1,0:T(8,128)(2,1)}, bf16[2,512,512]{2,1,0:T(8,128)(2,1)}, u32[]{:S(2)}, u32[]{:S(2)}) collective-permute-start(bf16[2,512,512]{2,1,0:T(8,128)(2,1)} %pick_chosen.15), channel_id=1, source_target_pairs={{0,2},{1,3},{2,0},{3,1},{4,6},{5,7},{6,4},{7,5},{8,10},{9,11},{10,... | collective-permute-start | bytes 3145736 | tf_op jit(solution)/shard_map/ppermute | solution.py:588
  769.4 50.4 %collective-permute-start.96 = (bf16[4,512,512]{2,1,0:T(8,128)(2,1)S(1)}, bf16[4,512,512]{2,1,0:T(8,128)(2,1)S(1)}, u32[]{:S(2)}, u32[]{:S(2)}) collective-permute-start(bf16[4,512,512]{2,1,0:T(8,128)(2,1)S(1)} %get-tuple-element.638.total_ref), channel_id=1, source_target_pairs={{0,8},{24,16},{8,0},{16,24},{1,9},{25,17},{9,1},{17,25},{2,10},{26... | collective-permute-start | bytes 6291464 | tf_op jit(solution)/shard_map/ppermute | solution.py:867
  823.5 54.1 %collective-permute-start.104 = (bf16[4,512,512]{2,1,0:T(8,128)(2,1)}, bf16[4,512,512]{2,1,0:T(8,128)(2,1)}, u32[]{:S(2)}, u32[]{:S(2)}) collective-permute-start(bf16[4,512,512]{2,1,0:T(8,128)(2,1)} %add.191.total_ref), channel_id=1, source_target_pairs={{0,8},{24,16},{8,0},{16,24},{1,9},{25,17},{9,1},{17,25},{2,10},{26... | collective-permute-start | bytes 6291464 | tf_op jit(solution)/shard_map/ppermute | solution.py:867
  (275 other events, 2908.0 us)
Sparse Core Ops, SparseCore 0:
  32.2 45.2 all-gather.4
  157.0 44.5 all-gather.8
  203.2 64.3 all-gather.6

commit v6 on v5

--- a/solution.py
+++ b/solution.py
@@ -1834,17 +1834,17 @@
     own = fold(near, far, True)
     own_got = col_swap(own[1], 2)
     down = weight_grad(after(hidden, own), cot, width)
-    low_got, other_got, inner_row, down, own = together(low_got, other_got, inner_row, down, own)
+    gate = weight_grad(after(normed2, down), grad_in, width, 0, [units])
+    low_got, other_got, own_got, inner_row, down, own, gate = together(
+        low_got, other_got, own_got, inner_row, down, own, gate
+    )
     top_last = row_swap(add_low(top_near, other_got))
     low_last = col_swap(add_low(own[3], low_got[1]), 2)
     inner = inner[0] + inner_row
     inner_core = col_swap(inner, 1)
     line.advance(down)
-    gate = weight_grad(after(normed2, line.sent), grad_in, width, 0, [units])
-    up = weight_grad(after(normed2, gate), grad_in, width, 1, [units])
-    top_last, low_last, own_got, inner_core, up, gate = together(
-        top_last, low_last, own_got, inner_core, up, gate
-    )
+    up = weight_grad(after(normed2, line.sent), grad_in, width, 1, [units])
+    top_last, low_last, inner_core, up = together(top_last, low_last, inner_core, up)
     inner = inner + inner_core
     inner = inner + col_swap(inner, 2)
     inner2 = inner.reshape(length, 1)

time: 913 us -> 904 us (level)
    ppermute x20, waiting for transfers between devices: 61.1 us -> 51.9 us  [row_swap(): return lax.ppermute(values, 'row', [(0, 1), (1, 0)])]
    unnamed x380 -> x384, local copies, waits for them, and re-layouts: 64.5 us -> 64.5 us
  transfers between devices with their start and end apart: 109 -> 109, of which waited for: 45 -> 46; matrix products, arithmetic and copies ran while one was open for 6% -> 6% of each run, Pallas kernels for 40% -> 41%
where the time goes in v6:
time: 904 us; the launch traced here: 891 us
  Pallas kernels  411 us (45%)
  waiting for transfers between devices  238 us (26%)
  starting transfers between devices  104 us (12%)
  local copies, waits for them, and re-layouts  81 us (9%)
  other arithmetic  40.5 us (4%)
  between operations  16.3 us (2%)
    ppermute x70, waiting for transfers between devices, col_swap(): lax.ppermute(values, 'col', [(i, i ^ distance) for i in range(count)])  141 us
    pallas_call x7, Pallas kernels, tiled_call(): pl.pallas_call(partial(kernel, split=split), grid=(tiles,), in_specs=spec...  72.3 us
    pallas_call x8, Pallas kernels, spread(): pl.pallas_call(partial(spread_kernel, transposed=transposed), grid=(4,),...  70.8 us
    unnamed x384, local copies, waits for them, and re-layouts  64.5 us
    pallas_call x6, Pallas kernels, weight_grad(): pl.pallas_call(weight_grad_kernel, grid=(4,), in_specs=[left, left, right...  59.5 us
    ppermute x20, waiting for transfers between devices, row_swap(): return lax.ppermute(values, 'row', [(0, 1), (1, 0)])  51.9 us
    pallas_call x2, Pallas kernels, mamba_backward(): pl.pallas_call(partial(mamba_backward_kernel, head_width=head_width, plac...  49.1 us
    ppermute x8, waiting for transfers between devices, _start(): move = lax.ppermute(self.sent, 'dp', [(0, 1), (3, 2), (1, 0), (2, 3)])  42.1 us
  transfers between devices with their start and end apart: 109, of which 46 were waited for; matrix products, arithmetic and copies ran while one was open for 6% of the time, Pallas kernels for 41%

profile of v6, /device:TPU:0, one launch (start us, length us, event | category | flops | bytes accessed | tf_op | source)
XLA Modules:
  0.0 890.8 jit_solution(6516292062612882607)
XLA Ops:
  47.4 16.5 %collective-permute-done.4.refs_0_ = bf16[1024,512]{1,0:T(8,128)(2,1)S(1)} collective-permute-done((bf16[1024,512]{1,0:T(8,128)(2,1)S(1)}, bf16[1024,512]{1,0:T(8,128)(2,1)S(1)}, u32[]{:S(2)}, u32[]{:S(2)}) %collective-permute-start.4) | collective-permute-done | bytes 1048608 | tf_op jit(solution)/shard_map/ppermute | solution.py:592
  73.3 11.9 %collective-permute-done.11.refs_3_ = bf16[1,512,768]{2,1,0:T(8,128)(2,1)S(1)} collective-permute-done((bf16[1,512,768]{2,1,0:T(8,128)(2,1)S(1)}, bf16[1,512,768]{2,1,0:T(8,128)(2,1)S(1)}, u32[]{:S(2)}, u32[]{:S(2)}) %collective-permute-start.11) | collective-permute-done | bytes 786464 | tf_op jit(solution)/shard_map/ppermute | solution.py:588
  86.0 9.5 %collective-permute-done.7.refs_1_ = bf16[512,512]{1,0:T(8,128)(2,1)S(1)} collective-permute-done((bf16[512,512]{1,0:T(8,128)(2,1)S(1)}, bf16[512,512]{1,0:T(8,128)(2,1)S(1)}, u32[]{:S(2)}, u32[]{:S(2)}) %collective-permute-start.7) | collective-permute-done | bytes 524320 | tf_op jit(solution)/shard_map/ppermute | solution.py:588
  114.8 14.7 %project.2 = (bf16[1024,2048]{1,0:T(8,128)(2,1)}, f32[1024,128]{1,0:T(8,128)}, bf16[1024,1664]{1,0:T(8,128)(2,1)}, f32[1024,128]{1,0:T(8,128)}) custom-call(bf16[1024,512]{1,0:T(8,128)(2,1)} %copy-done.145, bf16[512,512]{1,0:T(8,128)(2,1)} %copy-done.164, bf16[512,512]{1,0:T(8,128)(2,1)} %copy-done.162, bf16[1024,512]{1,0:T(8,128)(2,1)} %copy-done.152, ...), custom_call_target="tpu_custom_call" | custom-call | flops 1 | bytes 1 | tf_op jit(solution)/shard_map/project/pallas_call | solution.py:1155
  180.6 13.9 %project.3 = (bf16[1024,2048]{1,0:T(8,128)(2,1)}, f32[1024,128]{1,0:T(8,128)}, bf16[1024,1664]{1,0:T(8,128)(2,1)}, f32[1024,128]{1,0:T(8,128)}) custom-call(bf16[1024,512]{1,0:T(8,128)(2,1)} %base_ref.1, bf16[1024,512]{1,0:T(8,128)(2,1)} %copy-done.144, bf16[1024,512]{1,0:T(8,128)(2,1)} %copy-done.150, bf16[1024,512]{1,0:T(8,128)(2,1)} %collective-permute-done.9.refs_3_, ...), custom_call_target="tpu_custom_call" | custom-call | flops 1 | bytes 1 | tf_op jit(solution)/shard_map/project/pallas_call | solution.py:1155
  239.5 12.8 %collective-permute-done.26.refs_1_ = bf16[512,512]{1,0:T(8,128)(2,1)S(1)} collective-permute-done((bf16[512,512]{1,0:T(8,128)(2,1)S(1)}, bf16[512,512]{1,0:T(8,128)(2,1)S(1)}, u32[]{:S(2)}, u32[]{:S(2)}) %collective-permute-start.26) | collective-permute-done | bytes 524320 | tf_op jit(solution)/shard_map/ppermute | solution.py:588
  252.3 10.1 %collective-permute-done.27.refs_5_ = bf16[512,512]{1,0:T(8,128)(2,1)S(1)} collective-permute-done((bf16[512,512]{1,0:T(8,128)(2,1)S(1)}, bf16[512,512]{1,0:T(8,128)(2,1)S(1)}, u32[]{:S(2)}, u32[]{:S(2)}) %collective-permute-start.27) | collective-permute-done | bytes 524320 | tf_op jit(solution)/shard_map/ppermute | solution.py:588
  317.3 11.5 %ffn.2 = (bf16[1024,2048]{1,0:T(8,128)(2,1)}, f32[1024,128]{1,0:T(8,128)}, bf16[1024,512]{1,0:T(8,128)(2,1)}, bf16[1024,1024]{1,0:T(8,128)(2,1)}, f32[1024,128]{1,0:T(8,128)}) custom-call(bf16[1024,512]{1,0:T(8,128)(2,1)} %copy-done.147, bf16[512,512]{1,0:T(8,128)(2,1)} %copy-done.171, bf16[512,512]{1,0:T(8,128)(2,1)} %copy-done.172, ...), custom_call_target="tpu_custom_call" | custom-call | flops 1 | bytes 1 | tf_op jit(solution)/shard_map/ffn/pallas_call | solution.py:1155
  328.8 9.1 %spread.10 = (bf16[2,1024,512]{2,1,0:T(8,128)(2,1)}, bf16[2,1024,512]{2,1,0:T(8,128)(2,1)}) custom-call(bf16[1024,1024]{1,0:T(8,128)(2,1)} %get-tuple-element.508.refs_0_.latter_1, bf16[2048,1024]{1,0:T(8,128)(2,1)} %bitcast.109), custom_call_target="tpu_custom_call" | custom-call | flops 1 | bytes 1 | tf_op jit(solution)/shard_map/spread/pallas_call | solution.py:1232
  338.1 11.2 %ffn.3 = (bf16[1024,2048]{1,0:T(8,128)(2,1)}, f32[1024,128]{1,0:T(8,128)}, bf16[1024,512]{1,0:T(8,128)(2,1)}, bf16[1024,1024]{1,0:T(8,128)(2,1)}, f32[1024,128]{1,0:T(8,128)}) custom-call(bf16[1024,512]{1,0:T(8,128)(2,1)} %copy-done.103, bf16[1024,512]{1,0:T(8,128)(2,1)} %copy-done.146, bf16[1024,512]{1,0:T(8,128)(2,1)} %copy-done.151, ...), custom_call_target="tpu_custom_call" | custom-call | flops 1 | bytes 1 | tf_op jit(solution)/shard_map/ffn/pallas_call | solution.py:1155
  352.9 9.2 %spread.11 = (bf16[2,1024,512]{2,1,0:T(8,128)(2,1)}, bf16[2,1024,512]{2,1,0:T(8,128)(2,1)}) custom-call(bf16[1024,1024]{1,0:T(8,128)(2,1)} %get-tuple-element.488.refs_0_.latter_0, bf16[2048,1024]{1,0:T(8,128)(2,1)} %bitcast.111), custom_call_target="tpu_custom_call" | custom-call | flops 1 | bytes 1 | tf_op jit(solution)/shard_map/spread/pallas_call | solution.py:1232
  391.8 9.1 %weight_grad.8.later_ref.now_ref = bf16[4,512,512]{2,1,0:T(8,128)(2,1)} custom-call(bf16[1024,2048]{1,0:T(8,128)(2,1)} %get-tuple-element.518.former_0, bf16[1024,2048]{1,0:T(8,128)(2,1)} %get-tuple-element.519.former_1, bf16[1024,1024]{1,0:T(8,128)(2,1)} %get-tuple-element.488.refs_0_.latter_0, bf16[1024,1024]{1,0:T(8,128)(2,1)} %get-tuple-element.508.refs_0_.latter_1), custom_call_target="tpu_custom_call" | custom-call | flops 1 | bytes 1 | tf_op jit(solution)/shard_map/weight_grad/pallas_call | solution.py:1185
  428.6 10.0 %collective-permute-done.52.refs_0_ = bf16[1024,512]{1,0:T(8,128)(2,1)S(1)} collective-permute-done((bf16[1024,512]{1,0:T(8,128)(2,1)S(1)}, bf16[1024,512]{1,0:T(8,128)(2,1)S(1)}, u32[]{:S(2)}, u32[]{:S(2)}) %collective-permute-start.52) | collective-permute-done | bytes 1048608 | tf_op jit(solution)/shard_map/ppermute | solution.py:592
  518.1 10.8 %weight_grad.10.refs_0_.refs_1_ = bf16[4,512,768]{2,1,0:T(8,128)(2,1)} custom-call(bf16[1024,2048]{1,0:T(8,128)(2,1)} %get-tuple-element.562.former_0, bf16[1024,2048]{1,0:T(8,128)(2,1)} %get-tuple-element.563.former_1, bf16[1024,768]{1,0:T(8,128)(2,1)} %copy-done.55, bf16[1024,768]{1,0:T(8,128)(2,1)} %copy-done.56), custom_call_target="tpu_custom_call" | custom-call | flops 1 | bytes 1 | tf_op jit(solution)/shard_map/weight_grad/pallas_call | solution.py:1185
  533.3 24.6 %mamba_backward.2 = (bf16[1024,1024]{1,0:T(8,128)(2,1)}, f32[1024,128]{1,0:T(8,128)S(1)}, f32[16,512]{1,0:T(8,128)S(1)}) custom-call(bf16[1024,1664]{1,0:T(8,128)(2,1)} %get-tuple-element.380.query_ref.key_ref.value_ref.raw_ref.tail_ref, bf16[1024,1664]{1,0:T(8,128)(2,1)} %get-tuple-element.380.query_ref.key_ref.value_ref.raw_ref.tail_ref, ...), custom_call_target="tpu_custom_call" | custom-call | flops 1 | bytes 1 | tf_op jit(solution)/shard_map/mamba_backward/pallas_call | solution.py:538
  581.9 24.5 %mamba_backward.3 = (bf16[1024,1024]{1,0:T(8,128)(2,1)}, f32[1024,128]{1,0:T(8,128)S(1)}, f32[16,512]{1,0:T(8,128)S(1)}) custom-call(bf16[1024,1664]{1,0:T(8,128)(2,1)} %get-tuple-element.416.query_ref.key_ref.value_ref.raw_ref.tail_ref, bf16[1024,1664]{1,0:T(8,128)(2,1)} %get-tuple-element.416.query_ref.key_ref.value_ref.raw_ref.tail_ref, ...), custom_call_target="tpu_custom_call" | custom-call | flops 1 | bytes 1 | tf_op jit(solution)/shard_map/mamba_backward/pallas_call | solution.py:538
  607.2 13.3 %weight_grad.11 = (bf16[4,512,512]{2,1,0:T(8,128)(2,1)}, bf16[4,512,512]{2,1,0:T(8,128)(2,1)}) custom-call(bf16[1024,2048]{1,0:T(8,128)(2,1)} %get-tuple-element.562.former_0, bf16[1024,2048]{1,0:T(8,128)(2,1)} %get-tuple-element.563.former_1, bf16[1024,1024]{1,0:T(8,128)(2,1)} %get-tuple-element.626.latter_0.refs_1_, ...), custom_call_target="tpu_custom_call" | custom-call | flops 1 | bytes 1 | tf_op jit(solution)/shard_map/weight_grad/pallas_call | solution.py:1185
  646.8 9.7 %collective-permute-done.74.refs_1_ = bf16[2,512,512]{2,1,0:T(8,128)(2,1)} collective-permute-done((bf16[2,512,512]{2,1,0:T(8,128)(2,1)}, bf16[2,512,512]{2,1,0:T(8,128)(2,1)}, u32[]{:S(2)}, u32[]{:S(2)}) %collective-permute-start.74) | collective-permute-done | bytes 1048608 | tf_op jit(solution)/shard_map/ppermute | solution.py:588
  670.9 9.4 %collective-permute-done.77.refs_1_.refs_5_ = bf16[2,512,256]{2,1,0:T(8,128)(2,1)S(1)} collective-permute-done((bf16[2,512,256]{2,1,0:T(8,128)(2,1)S(1)}, bf16[2,512,256]{2,1,0:T(8,128)(2,1)S(1)}, u32[]{:S(2)}, u32[]{:S(2)}) %collective-permute-start.77) | collective-permute-done | bytes 524320 | tf_op jit(solution)/shard_map/ppermute | solution.py:588
  680.4 10.6 %collective-permute-done.80.got_ref.end_ref = bf16[4,512,512]{2,1,0:T(8,128)(2,1)} collective-permute-done((bf16[4,512,512]{2,1,0:T(8,128)(2,1)}, bf16[4,512,512]{2,1,0:T(8,128)(2,1)}, u32[]{:S(2)}, u32[]{:S(2)}) %collective-permute-start.80) | collective-permute-done | bytes 2097184 | tf_op jit(solution)/shard_map/ppermute | solution.py:867
  712.4 12.9 %spread.14 = (bf16[2,1024,512]{2,1,0:T(8,128)(2,1)}, bf16[2,1024,512]{2,1,0:T(8,128)(2,1)}) custom-call(bf16[1024,768]{1,0:T(8,128)(2,1)} %copy-done.56, bf16[1024,1024]{1,0:T(8,128)(2,1)} %get-tuple-element.622.latter_1.refs_1_, bf16[2048,1792]{1,0:T(8,128)(2,1)} %bitcast.119), custom_call_target="tpu_custom_call" | custom-call | flops 1 | bytes 1 | tf_op jit(solution)/shard_map/spread/pallas_call | solution.py:1232
  725.3 12.9 %spread.15 = (bf16[2,1024,512]{2,1,0:T(8,128)(2,1)}, bf16[2,1024,512]{2,1,0:T(8,128)(2,1)}) custom-call(bf16[1024,768]{1,0:T(8,128)(2,1)} %copy-done.55, bf16[1024,1024]{1,0:T(8,128)(2,1)} %get-tuple-element.626.latter_0.refs_1_, bf16[2048,1792]{1,0:T(8,128)(2,1)} %bitcast.120), custom_call_target="tpu_custom_call" | custom-call | flops 1 | bytes 1 | tf_op jit(solution)/shard_map/spread/pallas_call | solution.py:1232
  738.2 16.7 %collective-permute-done.84.refs_1_ = bf16[2,512,512]{2,1,0:T(8,128)(2,1)} collective-permute-done((bf16[2,512,512]{2,1,0:T(8,128)(2,1)}, bf16[2,512,512]{2,1,0:T(8,128)(2,1)}, u32[]{:S(2)}, u32[]{:S(2)}) %collective-permute-start.84) | collective-permute-done | bytes 1048608 | tf_op jit(solution)/shard_map/ppermute | solution.py:588
  781.2 29.9 %collective-permute-done.96.last_ref = bf16[4,512,512]{2,1,0:T(8,128)(2,1)S(1)} collective-permute-done((bf16[4,512,512]{2,1,0:T(8,128)(2,1)S(1)}, bf16[4,512,512]{2,1,0:T(8,128)(2,1)S(1)}, u32[]{:S(2)}, u32[]{:S(2)}) %collective-permute-start.96) | collective-permute-done | bytes 2097184 | tf_op jit(solution)/shard_map/ppermute | solution.py:867
  (776 shorter events, 549.6 us)
Async XLA Ops:
  7.2 90.1 %all-gather.5.cloned.1.call-start = ((), (), s32[]{:S(2)}) async-start(), calls=%async_computation | async-start | bytes 2621440 | tf_op jit(solution)/shard_map/all_gather | solution.py:1663
  32.0 197.9 %all-gather.9.cloned.1.call-start = ((), (), s32[]{:S(2)}) async-start(), calls=%async_computation.2 | async-start | bytes 5242880 | tf_op jit(solution)/shard_map/all_gather | solution.py:1761
  157.0 110.8 %all-gather.7.cloned.1.call-start = ((), (), s32[]{:S(2)}) async-start(), calls=%async_computation.1 | async-start | bytes 3932160 | tf_op jit(solution)/shard_map/all_gather | solution.py:1663
  391.2 48.5 %collective-permute-start.54 = (bf16[4,512,512]{2,1,0:T(8,128)(2,1)}, bf16[4,512,512]{2,1,0:T(8,128)(2,1)}, u32[]{:S(2)}, u32[]{:S(2)}) collective-permute-start(bf16[4,512,512]{2,1,0:T(8,128)(2,1)} %weight_grad.6.former_ref), channel_id=1, source_target_pairs={{0,8},{24,16},{8,0},{16,24},{1,9},{25,17},{9,1},{17,25},{2,10},{26... | collective-permute-start | bytes 6291464 | tf_op jit(solution)/shard_map/ppermute | solution.py:867
  441.3 60.9 %collective-permute-start.63 = (bf16[4,512,512]{2,1,0:T(8,128)(2,1)S(1)}, bf16[4,512,512]{2,1,0:T(8,128)(2,1)}, u32[]{:S(2)}, u32[]{:S(2)}) collective-permute-start(bf16[4,512,512]{2,1,0:T(8,128)(2,1)S(1)} %copy-done.43), channel_id=1, source_target_pairs={{0,8},{24,16},{8,0},{16,24},{1,9},{25,17},{9,1},{17,25},{2,10},{26... | collective-permute-start | bytes 6291464 | tf_op jit(solution)/shard_map/ppermute | solution.py:867
  454.1 48.1 %collective-permute-start.61 = (bf16[2,1024,512]{2,1,0:T(8,128)(2,1)}, bf16[2,1024,512]{2,1,0:T(8,128)(2,1)}, u32[]{:S(2)}, u32[]{:S(2)}) collective-permute-start(bf16[2,1024,512]{2,1,0:T(8,128)(2,1)} %get-tuple-element.549), channel_id=1, source_target_pairs={{0,1},{1,0},{2,3},{3,2},{4,5},{5,4},{6,7},{7,6},{8,9},{9,8},{10,11... | collective-permute-start | bytes 6291464 | tf_op jit(solution)/shard_map/ppermute | solution.py:588
  454.8 47.4 %collective-permute-start.62 = (bf16[2,1024,512]{2,1,0:T(8,128)(2,1)}, bf16[2,1024,512]{2,1,0:T(8,128)(2,1)}, u32[]{:S(2)}, u32[]{:S(2)}) collective-permute-start(bf16[2,1024,512]{2,1,0:T(8,128)(2,1)} %get-tuple-element.550), channel_id=1, source_target_pairs={{0,1},{1,0},{2,3},{3,2},{4,5},{5,4},{6,7},{7,6},{8,9},{9,8},{10,11... | collective-permute-start | bytes 6291464 | tf_op jit(solution)/shard_map/ppermute | solution.py:588
  454.8 47.4 %collective-permute-start.64 = (bf16[4,512,512]{2,1,0:T(8,128)(2,1)S(1)}, bf16[4,512,512]{2,1,0:T(8,128)(2,1)}, u32[]{:S(2)}, u32[]{:S(2)}) collective-permute-start(bf16[4,512,512]{2,1,0:T(8,128)(2,1)S(1)} %add.188.pair_ref), channel_id=1, source_target_pairs={{8,16},{16,8},{9,17},{17,9},{10,18},{18,10},{11,19},{19,11},{12,20... | collective-permute-start | bytes 6291464 | tf_op jit(solution)/shard_map/ppermute | solution.py:871
  505.9 52.1 %collective-permute-start.67 = (bf16[4,512,512]{2,1,0:T(8,128)(2,1)}, bf16[4,512,512]{2,1,0:T(8,128)(2,1)}, u32[]{:S(2)}, u32[]{:S(2)}) collective-permute-start(bf16[4,512,512]{2,1,0:T(8,128)(2,1)} %get-tuple-element.572.pair_ref), channel_id=1, source_target_pairs={{8,16},{16,8},{9,17},{17,9},{10,18},{18,10},{11,19},{19,11},{12,20... | collective-permute-start | bytes 6291464 | tf_op jit(solution)/shard_map/ppermute | solution.py:871
  507.9 51.5 %collective-permute-start.66 = (bf16[4,512,512]{2,1,0:T(8,128)(2,1)S(1)}, bf16[4,512,512]{2,1,0:T(8,128)(2,1)S(1)}, u32[]{:S(2)}, u32[]{:S(2)}) collective-permute-start(bf16[4,512,512]{2,1,0:T(8,128)(2,1)S(1)} %get-tuple-element.558.middle_ref), channel_id=1, source_target_pairs={{0,8},{24,16},{8,0},{16,24},{1,9},{25,17},{9,1},{17,25},{2,10},{26... | collective-permute-start | bytes 6291464 | tf_op jit(solution)/shard_map/ppermute | solution.py:867
  517.0 47.0 %collective-permute-start.65 = (bf16[2,1024,512]{2,1,0:T(8,128)(2,1)}, bf16[2,1024,512]{2,1,0:T(8,128)(2,1)}, u32[]{:S(2)}, u32[]{:S(2)}) collective-permute-start(bf16[2,1024,512]{2,1,0:T(8,128)(2,1)} %add.189), channel_id=1, source_target_pairs={{0,4},{4,0},{1,5},{5,1},{2,6},{6,2},{3,7},{7,3},{8,12},{12,8},{9,1... | collective-permute-start | bytes 6291464 | tf_op jit(solution)/shard_map/ppermute | solution.py:592
  532.0 40.8 %collective-permute-start.70 = (bf16[2,512,768]{2,1,0:T(8,128)(2,1)}, bf16[2,512,768]{2,1,0:T(8,128)(2,1)S(1)}, u32[]{:S(2)}, u32[]{:S(2)}) collective-permute-start(bf16[2,512,768]{2,1,0:T(8,128)(2,1)} %pick.14), channel_id=1, source_target_pairs={{0,2},{1,3},{2,0},{3,1},{4,6},{5,7},{6,4},{7,5},{8,10},{9,11},{10,... | collective-permute-start | bytes 4718600 | tf_op jit(solution)/shard_map/ppermute | solution.py:588
  568.2 57.2 %collective-permute-start.73 = (bf16[4,512,512]{2,1,0:T(8,128)(2,1)}, bf16[4,512,512]{2,1,0:T(8,128)(2,1)}, u32[]{:S(2)}, u32[]{:S(2)}) collective-permute-start(bf16[4,512,512]{2,1,0:T(8,128)(2,1)} %get-tuple-element.590.pair_ref), channel_id=1, source_target_pairs={{8,16},{16,8},{9,17},{17,9},{10,18},{18,10},{11,19},{19,11},{12,20... | collective-permute-start | bytes 6291464 | tf_op jit(solution)/shard_map/ppermute | solution.py:871
  570.1 55.3 %collective-permute-start.72 = (bf16[4,512,512]{2,1,0:T(8,128)(2,1)}, bf16[4,512,512]{2,1,0:T(8,128)(2,1)S(1)}, u32[]{:S(2)}, u32[]{:S(2)}) collective-permute-start(bf16[4,512,512]{2,1,0:T(8,128)(2,1)} %get-tuple-element.576.middle_ref), channel_id=1, source_target_pairs={{0,8},{24,16},{8,0},{16,24},{1,9},{25,17},{9,1},{17,25},{2,10},{26... | collective-permute-start | bytes 6291464 | tf_op jit(solution)/shard_map/ppermute | solution.py:867
  574.5 50.9 %collective-permute-start.71 = (bf16[2,512,768]{2,1,0:T(8,128)(2,1)}, bf16[2,512,768]{2,1,0:T(8,128)(2,1)}, u32[]{:S(2)}, u32[]{:S(2)}) collective-permute-start(bf16[2,512,768]{2,1,0:T(8,128)(2,1)} %pick.15), channel_id=1, source_target_pairs={{0,1},{1,0},{2,3},{3,2},{4,5},{5,4},{6,7},{7,6},{8,9},{9,8},{10,11... | collective-permute-start | bytes 4718600 | tf_op jit(solution)/shard_map/ppermute | solution.py:588
  577.2 43.3 %collective-permute-start.68 = (bf16[1024,512]{1,0:T(8,128)(2,1)}, bf16[1024,512]{1,0:T(8,128)(2,1)}, u32[]{:S(2)}, u32[]{:S(2)}) collective-permute-start(bf16[1024,512]{1,0:T(8,128)(2,1)} %add_three.1), channel_id=1, source_target_pairs={{0,2},{1,3},{2,0},{3,1},{4,6},{5,7},{6,4},{7,5},{8,10},{9,11},{10,... | collective-permute-start | bytes 3145736 | tf_op jit(solution)/shard_map/ppermute | solution.py:588
  580.0 45.3 %collective-permute-start.69 = (bf16[2,512,512]{2,1,0:T(8,128)(2,1)}, bf16[2,512,512]{2,1,0:T(8,128)(2,1)}, u32[]{:S(2)}, u32[]{:S(2)}) collective-permute-start(bf16[2,512,512]{2,1,0:T(8,128)(2,1)} %pick_chosen.12), channel_id=1, source_target_pairs={{0,2},{1,3},{2,0},{3,1},{4,6},{5,7},{6,4},{7,5},{8,10},{9,11},{10,... | collective-permute-start | bytes 3145736 | tf_op jit(solution)/shard_map/ppermute | solution.py:588
  639.8 40.5 %collective-permute-start.81 = (bf16[4,512,512]{2,1,0:T(8,128)(2,1)}, bf16[4,512,512]{2,1,0:T(8,128)(2,1)}, u32[]{:S(2)}, u32[]{:S(2)}) collective-permute-start(bf16[4,512,512]{2,1,0:T(8,128)(2,1)} %get-tuple-element.613.pair_ref), channel_id=1, source_target_pairs={{8,16},{16,8},{9,17},{17,9},{10,18},{18,10},{11,19},{19,11},{12,20... | collective-permute-start | bytes 6291464 | tf_op jit(solution)/shard_map/ppermute | solution.py:871
  642.0 49.0 %collective-permute-start.80 = (bf16[4,512,512]{2,1,0:T(8,128)(2,1)}, bf16[4,512,512]{2,1,0:T(8,128)(2,1)}, u32[]{:S(2)}, u32[]{:S(2)}) collective-permute-start(bf16[4,512,512]{2,1,0:T(8,128)(2,1)} %get-tuple-element.612.middle_ref), channel_id=1, source_target_pairs={{0,8},{24,16},{8,0},{16,24},{1,9},{25,17},{9,1},{17,25},{2,10},{26... | collective-permute-start | bytes 6291464 | tf_op jit(solution)/shard_map/ppermute | solution.py:867
  698.2 56.8 %collective-permute-start.86 = (bf16[4,512,512]{2,1,0:T(8,128)(2,1)}, bf16[4,512,512]{2,1,0:T(8,128)(2,1)}, u32[]{:S(2)}, u32[]{:S(2)}) collective-permute-start(bf16[4,512,512]{2,1,0:T(8,128)(2,1)} %get-tuple-element.631.pair_ref), channel_id=1, source_target_pairs={{8,16},{16,8},{9,17},{17,9},{10,18},{18,10},{11,19},{19,11},{12,20... | collective-permute-start | bytes 6291464 | tf_op jit(solution)/shard_map/ppermute | solution.py:871
  700.2 54.8 %collective-permute-start.85 = (bf16[4,512,512]{2,1,0:T(8,128)(2,1)S(1)}, bf16[4,512,512]{2,1,0:T(8,128)(2,1)S(1)}, u32[]{:S(2)}, u32[]{:S(2)}) collective-permute-start(bf16[4,512,512]{2,1,0:T(8,128)(2,1)S(1)} %get-tuple-element.621.middle_ref), channel_id=1, source_target_pairs={{0,8},{24,16},{8,0},{16,24},{1,9},{25,17},{9,1},{17,25},{2,10},{26... | collective-permute-start | bytes 6291464 | tf_op jit(solution)/shard_map/ppermute | solution.py:867
  711.0 43.9 %collective-permute-start.84 = (bf16[2,512,512]{2,1,0:T(8,128)(2,1)}, bf16[2,512,512]{2,1,0:T(8,128)(2,1)}, u32[]{:S(2)}, u32[]{:S(2)}) collective-permute-start(bf16[2,512,512]{2,1,0:T(8,128)(2,1)} %pick_chosen.15), channel_id=1, source_target_pairs={{0,2},{1,3},{2,0},{3,1},{4,6},{5,7},{6,4},{7,5},{8,10},{9,11},{10,... | collective-permute-start | bytes 3145736 | tf_op jit(solution)/shard_map/ppermute | solution.py:588
  760.7 50.4 %collective-permute-start.96 = (bf16[4,512,512]{2,1,0:T(8,128)(2,1)S(1)}, bf16[4,512,512]{2,1,0:T(8,128)(2,1)S(1)}, u32[]{:S(2)}, u32[]{:S(2)}) collective-permute-start(bf16[4,512,512]{2,1,0:T(8,128)(2,1)S(1)} %get-tuple-element.638.total_ref), channel_id=1, source_target_pairs={{0,8},{24,16},{8,0},{16,24},{1,9},{25,17},{9,1},{17,25},{2,10},{26... | collective-permute-start | bytes 6291464 | tf_op jit(solution)/shard_map/ppermute | solution.py:867
  814.8 54.1 %collective-permute-start.104 = (bf16[4,512,512]{2,1,0:T(8,128)(2,1)}, bf16[4,512,512]{2,1,0:T(8,128)(2,1)}, u32[]{:S(2)}, u32[]{:S(2)}) collective-permute-start(bf16[4,512,512]{2,1,0:T(8,128)(2,1)} %add.191.total_ref), channel_id=1, source_target_pairs={{0,8},{24,16},{8,0},{16,24},{1,9},{25,17},{9,1},{17,25},{2,10},{26... | collective-permute-start | bytes 6291464 | tf_op jit(solution)/shard_map/ppermute | solution.py:867
  (277 other events, 2878.9 us)
Sparse Core Ops, SparseCore 0:
  32.2 45.2 all-gather.4
  157.1 44.5 all-gather.8
  203.3 64.3 all-gather.6
